TPU v7x, 32 devices: a whole 2x2x4 slice. The times are simulated.
32 devices in a mesh: groups: 2 (over y), cell: 8 (over z, x), gene: 2 (over core).
Axes of the slice: x: 2, y: 2, z: 4, core: 2. Of those that a mesh axis runs over, the one named last changes fastest.
Arguments:
- block_values: bfloat16 [16, 2, 64, 128, 128], P(('groups', 'cell'), 'gene'), parts along dimension 0, may hold values from 0 to 5632, as said below
- block_rows: int32 [16, 2, 64], P(('groups', 'cell'), 'gene'), parts along dimension 0, may hold values from 0 to 7
- block_cols: int32 [16, 2, 64], P(('groups', 'cell'), 'gene'), parts along dimension 0, may hold values from 0 to 15
- block_count: int32 [16, 2], P(('groups', 'cell'), 'gene'), parts along dimension 0, may hold values from 32 to 64, as said below
- cell_factor: float32 [512, 8192], P(('groups', 'gene'), 'cell'), parts along dimension 0, may hold values from 0 to 1
- gene_factor: float32 [512, 4096], P(('groups', 'cell'), 'gene'), parts along dimension 0, may hold values from 0 to 1
Outputs:
- cell_next: float32 [512, 8192], P(('groups', 'gene'), 'cell'), parts along dimension 0
- gene_next: float32 [512, 4096], P(('groups', 'cell'), 'gene'), parts along dimension 0
There are 2 independent parts, one for each index of `groups`. A program takes and returns all parts, laid end to end along the dimension named above; each array names one. Nothing has to cross between parts.
Inputs may be any that keep to these rules, and one draw needn't show every extreme that they name: Within a tile, the first block_count entries of block_rows and block_cols name distinct blocks; every tile's later entries are valid indices too. block_count reaches 64 on some tile of every draw. `block_values`: Positive.
All inputs are finite; a program needn't handle non-finite values.
Results may differ from a plain program's by a relative error of at most 0.0014.
Values may be sent and summed in bfloat16 or wider, within the bound.
No kernel may reach another device: no remote copies, remote signals or barrier semaphores. Data moves between devices by JAX's collectives and lax.ppermute only.
A program may use at most 64 MiB of HBM per device.

v0:
```python
import jax
import jax.numpy as jnp
from jax import lax
from jax.sharding import PartitionSpec as P

BLK = 128
CELL_DEV = 1024
GENE_DEV = 2048


def live_values(values, count):
    live = (jnp.arange(values.shape[0]) < count).astype(jnp.bfloat16)
    return values * live[:, None, None]


def tile_data_gene(vals, rows, cols, panel):
    kdim = panel.shape[0]
    col_blocks = panel.shape[1] // BLK
    row_blocks = CELL_DEV // BLK
    row_pick = (rows[:, None] == jnp.arange(row_blocks)[None, :]).astype(jnp.bfloat16)
    col_pick = (cols[:, None] == jnp.arange(col_blocks)[None, :]).astype(jnp.bfloat16)
    picked = jnp.einsum(
        "ng,kgc->nkc",
        col_pick,
        panel.reshape(kdim, col_blocks, BLK),
        preferred_element_type=jnp.float32,
    ).astype(jnp.bfloat16)
    partial_rows = jnp.einsum("nrc,nkc->nkr", vals, picked, preferred_element_type=jnp.float32)
    return jnp.einsum("nkr,nb->kbr", partial_rows, row_pick.astype(jnp.float32)).reshape(
        kdim, row_blocks * BLK
    )


def tile_data_cell(vals, rows, cols, panel):
    kdim = panel.shape[0]
    row_blocks = panel.shape[1] // BLK
    col_blocks = GENE_DEV // BLK
    row_pick = (rows[:, None] == jnp.arange(row_blocks)[None, :]).astype(jnp.bfloat16)
    col_pick = (cols[:, None] == jnp.arange(col_blocks)[None, :]).astype(jnp.float32)
    picked = jnp.einsum(
        "nb,kbr->nkr",
        row_pick,
        panel.reshape(kdim, row_blocks, BLK),
        preferred_element_type=jnp.float32,
    ).astype(jnp.bfloat16)
    partial_cols = jnp.einsum("nrc,nkr->nkc", vals, picked, preferred_element_type=jnp.float32)
    return jnp.einsum("nkc,ng->kgc", partial_cols, col_pick).reshape(kdim, col_blocks * BLK)


def gram_of(panel):
    return lax.dot_general(
        panel, panel, (((1,), (1,)), ((), ())), preferred_element_type=jnp.float32
    )


def shards(block_values, block_rows, block_cols, block_count, cell_factor, gene_factor):
    vals = live_values(block_values[0, 0], block_count[0, 0])
    rows = block_rows[0, 0]
    cols = block_cols[0, 0]
    gene_panel = lax.all_gather(gene_factor.astype(jnp.bfloat16), "cell", axis=0, tiled=True)
    cell_panel = lax.all_gather(cell_factor.astype(jnp.bfloat16), "gene", axis=0, tiled=True)
    gene_gram = lax.psum(gram_of(gene_panel).astype(jnp.bfloat16), "gene").astype(jnp.float32)
    rate_cell = 1.0 / (jnp.sqrt(jnp.sum(gene_gram * gene_gram)) + 1e-06)
    data_gene = tile_data_gene(vals, rows, cols, gene_panel)
    own_rows = lax.psum_scatter(data_gene, "gene", scatter_dimension=0, tiled=True)
    cell_share = cell_factor.shape[0]
    gram_rows = lax.dynamic_slice_in_dim(
        gene_gram, lax.axis_index("gene") * cell_share, cell_share, 0
    )
    stepped = jnp.dot(gram_rows, cell_panel.astype(jnp.float32), precision=lax.Precision.HIGHEST)
    cell_next = jnp.maximum(cell_factor - rate_cell * (stepped - own_rows), 0.0)
    next_panel = lax.all_gather(cell_next.astype(jnp.bfloat16), "gene", axis=0, tiled=True)
    local_gram = gram_of(next_panel)
    data_cell = tile_data_cell(vals, rows, cols, next_panel)
    gene_share = gene_factor.shape[0]
    cell_gram = lax.psum(local_gram, "cell")
    own_cols = lax.psum_scatter(data_cell, "cell", scatter_dimension=0, tiled=True)
    gram_part = lax.dynamic_slice_in_dim(
        cell_gram, lax.axis_index("cell") * gene_share, gene_share, 0
    )
    total = jnp.sum(cell_gram * cell_gram)
    rate_gene = 1.0 / (jnp.sqrt(total) + 1e-06)
    stepped_gene = jnp.dot(
        gram_part, gene_panel.astype(jnp.float32), precision=lax.Precision.HIGHEST
    )
    gene_next = jnp.maximum(gene_factor - rate_gene * (stepped_gene - own_cols), 0.0)
    return (cell_next, gene_next)


def solution(mesh):
    return jax.shard_map(
        shards,
        mesh=mesh,
        in_specs=(
            P(("groups", "cell"), "gene", None, None, None),
            P(("groups", "cell"), "gene", None),
            P(("groups", "cell"), "gene", None),
            P(("groups", "cell"), "gene"),
            P(("groups", "gene"), "cell"),
            P(("groups", "cell"), "gene"),
        ),
        out_specs=(P(("groups", "gene"), "cell"), P(("groups", "cell"), "gene")),
        check_vma=False,
    )
```

profile of v0, /device:TPU:0, one launch (start us, length us, event | category | flops | bytes accessed | tf_op | source)
XLA Modules:
  0.0 241.6 jit_solution(3348596650288630485)
XLA Ops:
  7.2 0.0 all-gather.2.cloned.1.call-start
  7.2 1.6 convert_element_type.35
  8.8 0.0 all-gather.2.cloned.1.call-update
  8.9 0.0 all-reduce.3.cloned.1.call-start
  9.6 44.0 %all-gather.2.cloned.1.call-done = bf16[256,2048]{1,0:T(8,128)(2,1)} async-done(((bf16[32,2048]{1,0:T(8,128)(2,1)}), bf16[256,2048]{1,0:T(8,128)(2,1)}) %all-gather.2.cloned.1.call-update) | async-done | bytes 1048592 | tf_op jit(solution)/shard_map/all_gather | solution.py:60
  53.6 2.7 %convolution_convert_fusion = bf16[256,256]{1,0:T(8,128)(2,1)} fusion(bf16[256,2048]{1,0:T(8,128)(2,1)} %all-gather.2.cloned.1.call-done), kind=kOutput, calls=%fused_computation.18 | convolution fusion | flops 268500992 | bytes 1179648 | tf_op jit(solution)/shard_map/dot_general | solution.py:51
  56.3 0.0 reduce-scatter.3.cloned.1.call-start
  56.4 1.6 copy.12
  58.0 1.3 fusion.18
  59.3 4.2 %fusion.4 = bf16[64,256,128]{2,1,0:T(8,128)(2,1)S(1)} fusion(bf16[64,256,128]{2,0,1:T(8,128)(2,1)S(1)} %fusion.18, bf16[1,1,64,128,128]{4,3,2,1,0:T(8,128)(2,1)S(1)} %copy-done.1, bf16[64]{0:T(256)(128)(2,1)S(1)} %compare_convert_fusion), kind=kOutput, calls=%fused_computation.6 | convolution fusion | flops 537919488 | bytes 10485888 | tf_op jit(solution)/shard_map/nrc,nkc->nkr/dot_general | solution.py:28
  63.5 2.3 fusion.2
  65.8 1.2 copy.27
  67.0 0.0 reduce-scatter.3.cloned.1.call-update
  67.0 0.0 all-reduce.5.cloned.1.call-start
  67.1 2.2 all_gather.10
  69.3 3.9 %all-reduce.3.cloned.1.call-done = bf16[256,256]{1,0:T(8,128)(2,1)} async-done(((bf16[256,256]{1,0:T(8,128)(2,1)}), bf16[256,256]{1,0:T(8,128)(2,1)}) %all-reduce.3.cloned.1.call-update) | async-done | bytes 131088 | tf_op jit(solution)/shard_map/psum | solution.py:62
  73.2 1.6 multiply_reduce_fusion.1
  75.5 9.7 %reduce-scatter.3.cloned.1.call-done = f32[128,1024]{1,0:T(8,128)} async-done(((f32[256,1024]{1,0:T(8,128)}), f32[128,1024]{1,0:T(8,128)}) %reduce-scatter.3.cloned.1.call-update) | async-done | bytes 524304 | tf_op jit(solution)/shard_map/reduce_scatter | solution.py:65
  85.2 2.1 fusion.30
  87.3 2.2 all_gather.11
  89.5 1.0 fusion.31
  90.5 0.0 all-reduce.5.cloned.1.call-update
  90.5 0.2 reduce-scatter.5.cloned.1.call-start
  90.8 0.1 copy.14
  90.9 1.3 fusion.23
  92.1 4.2 %fusion.5 = bf16[64,256,128]{2,1,0:T(8,128)(2,1)S(1)} fusion(bf16[64,256,128]{2,0,1:T(8,128)(2,1)S(1)} %fusion.23, bf16[1,1,64,128,128]{4,3,2,1,0:T(8,128)(2,1)S(1)} %copy-done.1, bf16[64]{0:T(256)(128)(2,1)S(1)} %compare_convert_fusion), kind=kOutput, calls=%fused_computation.7 | convolution fusion | flops 537919488 | bytes 10485888 | tf_op jit(solution)/shard_map/nrc,nkr->nkc/dot_general | solution.py:46
  96.3 2.4 fusion
  98.7 2.2 copy.26
  100.9 61.5 %all-reduce.5.cloned.1.call-done = f32[256,256]{1,0:T(8,128)} async-done(((f32[256,256]{1,0:T(8,128)}), f32[256,256]{1,0:T(8,128)}) %all-reduce.5.cloned.1.call-update) | async-done | bytes 262160 | tf_op jit(solution)/shard_map/psum | solution.py:76
  162.4 1.6 multiply_reduce_fusion
  164.8 68.0 %reduce-scatter.5.cloned.1.call-done = f32[32,2048]{1,0:T(8,128)} async-done(((f32[256,2048]{1,0:T(8,128)}), f32[32,2048]{1,0:T(8,128)}) %reduce-scatter.5.cloned.1.call-update) | async-done | bytes 262160 | tf_op jit(solution)/shard_map/reduce_scatter | solution.py:77
  232.8 2.3 fusion.8
  (16 shorter events, 0.1 us)
Async XLA Ops:
  7.2 50.8 %copy-start.5 = (s32[1,1,64]{2,1,0:T(1,128)S(1)}, s32[1,1,64]{2,1,0:T(1,128)}, u32[]{:S(2)}) copy-start(s32[1,1,64]{2,1,0:T(1,128)} %param.8) | copy-start | bytes 772
  7.2 46.4 %all-gather.2.cloned.1.call-start = ((), (), s32[]{:S(2)}) async-start(), calls=%async_computation.2 | async-start | bytes 1179648 | tf_op jit(solution)/shard_map/all_gather | solution.py:60
  8.9 64.3 %all-reduce.3.cloned.1.call-start = ((), (), s32[]{:S(2)}) async-start(), calls=%async_computation.3 | async-start | bytes 262144 | tf_op jit(solution)/shard_map/psum | solution.py:62
  56.3 3.0 %copy-start.1 = (bf16[1,1,64,128,128]{4,3,2,1,0:T(8,128)(2,1)S(1)}, bf16[1,1,64,128,128]{4,3,2,1,0:T(8,128)(2,1)}, u32[]{:S(2)}) copy-start(bf16[1,1,64,128,128]{4,3,2,1,0:T(8,128)(2,1)} %param.6) | copy-start | bytes 6291460
  56.3 28.8 %reduce-scatter.3.cloned.1.call-start = ((), (), s32[]{:S(2)}) async-start(), calls=%async_computation.4 | async-start | bytes 1572864 | tf_op jit(solution)/shard_map/reduce_scatter | solution.py:65
  59.3 4.2 %copy-start.4 = (s32[1,1,64]{2,1,0:T(1,128)S(1)}, s32[1,1,64]{2,1,0:T(1,128)}, u32[]{:S(2)}) copy-start(s32[1,1,64]{2,1,0:T(1,128)} %param.7) | copy-start | bytes 772
  63.5 3.6 %copy-start.2 = (f32[128,1024]{1,0:T(8,128)S(1)}, f32[128,1024]{1,0:T(8,128)}, u32[]{:S(2)}) copy-start(f32[128,1024]{1,0:T(8,128)} %param.10) | copy-start | bytes 1572868
  67.0 95.4 %all-reduce.5.cloned.1.call-start = ((), (), s32[]{:S(2)}) async-start(), calls=%async_computation.5 | async-start | bytes 524288 | tf_op jit(solution)/shard_map/psum | solution.py:76
  90.5 142.3 %reduce-scatter.5.cloned.1.call-start = ((), (), s32[]{:S(2)}) async-start(), calls=%async_computation.6 | async-start | bytes 2359296 | tf_op jit(solution)/shard_map/reduce_scatter | solution.py:77
  98.7 134.1 %copy-start = (bf16[256,2048]{1,0:T(8,128)(2,1)S(1)}, bf16[256,2048]{1,0:T(8,128)(2,1)}, u32[]{:S(2)}) copy-start(bf16[256,2048]{1,0:T(8,128)(2,1)} %all-gather.2.cloned.1.call-done) | copy-start | bytes 3145732
  98.7 134.1 %copy-start.3 = (f32[32,2048]{1,0:T(8,128)S(1)}, f32[32,2048]{1,0:T(8,128)}, u32[]{:S(2)}) copy-start(f32[32,2048]{1,0:T(8,128)} %param.11) | copy-start | bytes 786436
Sparse Core Ops, SparseCore 0:
  10.7 42.8 all-gather.1
  56.5 16.6 all-reduce.2
  75.4 9.6 reduce-scatter.2
  90.6 71.7 all-reduce.4
  165.8 66.9 reduce-scatter.4
where the time goes:
time: 242 us
  waiting for transfers between devices  187 us (77%)
  matrix products  23.8 us (10%)
  between operations  16 us (7%)
  local copies, waits for them, and re-layouts  5.09 us (2%)
  other arithmetic  4.85 us (2%)
  blocking collectives  4.35 us (2%)
    reduce_scatter x1, waiting for transfers between devices, shards(): lax.psum_scatter(data_cell, 'cell', scatter_dimension=0, tiled=True)  68 us
    psum x1, waiting for transfers between devices, shards(): cell_gram = lax.psum(local_gram, 'cell')  61.5 us
    all_gather x1, waiting for transfers between devices, shards(): lax.all_gather(gene_factor.astype(jnp.bfloat16), 'cell', axis=0, tiled=True)  44 us
    reduce_scatter x1, waiting for transfers between devices, shards(): lax.psum_scatter(data_gene, 'gene', scatter_dimension=0, tiled=True)  9.68 us
    unnamed x16, local copies, waits for them, and re-layouts  5.09 us
  transfers between devices with their start and end apart: 5, of which 5 were waited for; matrix products, arithmetic and copies ran while one was open for 10% of the time, Pallas kernels for 0%

commit v1 on v0

v1 whole, which is shorter than its diff:
```python
import functools

import jax
import jax.numpy as jnp
from jax import lax
from jax.experimental import pallas as pl
from jax.experimental.pallas import tpu as pltpu
from jax.sharding import PartitionSpec as P

BLK = 128
CELL_DEV = 1024
GENE_DEV = 2048
VMEM_BYTES = 48 * 2**20

NT = (((1,), (1,)), ((), ()))
NN = (((1,), (0,)), ((), ()))
SMEM_SPEC = pl.BlockSpec(memory_space=pltpu.SMEM)
VMEM_SPEC = pl.BlockSpec(memory_space=pltpu.VMEM)


def dot(a, b, dims=NN):
    return lax.dot_general(a, b, dims, preferred_element_type=jnp.float32)


def split_dot(a, b):
    high = a.astype(jnp.bfloat16)
    rest = a - high.astype(jnp.float32)
    mid = rest.astype(jnp.bfloat16)
    low = (rest - mid.astype(jnp.float32)).astype(jnp.bfloat16)
    return dot(high, b) + (dot(mid, b) + dot(low, b))


def call(body, outs, n_smem, n_vmem, flops, traffic, scratch=()):
    return pl.pallas_call(
        body,
        out_shape=outs,
        in_specs=[SMEM_SPEC] * n_smem + [VMEM_SPEC] * n_vmem,
        out_specs=jax.tree.map(lambda _: VMEM_SPEC, outs),
        scratch_shapes=list(scratch),
        compiler_params=pltpu.CompilerParams(vmem_limit_bytes=VMEM_BYTES),
        cost_estimate=pl.CostEstimate(flops=flops, bytes_accessed=traffic, transcendentals=0),
    )


def shape(dims, dtype):
    return jax.ShapeDtypeStruct(dims, dtype)


def dense_body(rows, cols, count, values, tile):
    tile[...] = jnp.zeros_like(tile)

    def place(n, carry):
        row = pl.multiple_of(rows[n] * BLK, BLK)
        col = pl.multiple_of(cols[n] * BLK, BLK)
        tile[pl.ds(row, BLK), pl.ds(col, BLK)] = values[n]
        return carry

    lax.fori_loop(0, count[0], place, 0)


def dense_tile(values, rows, cols, count):
    return call(
        dense_body,
        shape((CELL_DEV, GENE_DEV), jnp.bfloat16),
        3,
        1,
        0,
        2 * 2**20 + 4 * 2**20,
    )(rows, cols, count, values)


def gene_body(owners, tile, *refs):
    shares, panel, message = refs[:-2], refs[-2], refs[-1]
    for n, part in enumerate(shares):
        size = part.shape[0]
        panel[pl.ds(pl.multiple_of(owners[n] * size, size), size)] = part[...]
    low = panel[...]
    message[:, :CELL_DEV] = dot(low, tile[...], NT)
    message[:, CELL_DEV:] = dot(low, low, NT)


def cell_body(picks, at, tile, mine, other, factor_mine, factor_other, cell_next, low_out, *rest):
    sends, (factor, updated, chosen) = rest[:-3], rest[-3:]
    share = factor_mine.shape[0]
    own = pl.multiple_of(at[0] * share, share)
    theirs = pl.multiple_of((1 - at[0]) * share, share)
    factor[pl.ds(own, share)] = factor_mine[...]
    factor[pl.ds(theirs, share)] = factor_other[...]
    gram = mine[:, CELL_DEV:] + other[:, CELL_DEV:]
    norm = jnp.sum(jnp.sum(gram * gram, axis=1, keepdims=True), axis=0, keepdims=True)
    rate = 1.0 / (jnp.sqrt(norm) + 1e-06)
    data = mine[:, :CELL_DEV] + other[:, :CELL_DEV]
    held = factor[...]
    stepped = split_dot(gram, held.astype(jnp.bfloat16))
    updated[...] = jnp.maximum(held - rate * (stepped - data), 0.0)
    cell_next[...] = updated[pl.ds(own, share)]
    low_out[...] = updated[...].astype(jnp.bfloat16)
    if sends:
        size = sends[0].shape[0]
        for n in range(len(sends)):
            row = pl.multiple_of(picks[n] * size, size)
            chosen[n * size : (n + 1) * size] = low_out[pl.ds(row, size)]
        product = dot(chosen[...], tile[...])
        for n, out in enumerate(sends):
            out[...] = product[n * size : (n + 1) * size].astype(out.dtype)


def keep_body(picks, low, tile, gram, *rest):
    keeps, chosen = rest[:-1], rest[-1]
    panel = low[...]
    gram[...] = dot(panel, panel, NT).astype(gram.dtype)
    size = keeps[0].shape[0]
    for n in range(len(keeps)):
        row = pl.multiple_of(picks[n] * size, size)
        chosen[n * size : (n + 1) * size] = low[pl.ds(row, size)]
    product = dot(chosen[...], tile[...])
    for n, out in enumerate(keeps):
        out[...] = product[n * size : (n + 1) * size]


def gram_body(partials, panel, stepped, square):
    size = stepped.shape[0]
    gram = partials[:size].astype(jnp.float32)
    for n in range(1, partials.shape[0] // size):
        gram = gram + partials[n * size : (n + 1) * size].astype(jnp.float32)
    stepped[...] = split_dot(gram, panel[...])
    norm = jnp.sum(jnp.sum(gram * gram, axis=1, keepdims=True), axis=0, keepdims=True)
    square[...] = jnp.broadcast_to(norm, square.shape)


def gram_of(panel):
    return dot(panel, panel, NT)


def shards(block_values, block_rows, block_cols, block_count, cell_factor, gene_factor):
    n_cell = lax.axis_size("cell")
    kdim = cell_factor.shape[0] * lax.axis_size("gene")
    size = gene_factor.shape[0]
    cell_share = cell_factor.shape[0]
    paired = size % 16 == 0 and n_cell >= 4 and n_cell & (n_cell - 1) == 0
    cell_at = lax.axis_index("cell")
    gene_at = lax.axis_index("gene")

    def swap(value, bits):
        return lax.ppermute(value, "cell", [(n, n ^ bits) for n in range(n_cell)])

    def swap_core(value):
        return lax.ppermute(value, "gene", [(0, 1), (1, 0)])

    low_share = gene_factor.astype(jnp.bfloat16)
    if paired:
        offsets = list(range(2, n_cell, 2))
        offsets.sort(key=lambda bits: -bits)
        near = swap(low_share, 1)
        far = [swap(low_share, bits) for bits in offsets]
        shares = [low_share, near] + far + [swap(part, 1) for part in far]
        owners = [0, 1] + offsets + [bits ^ 1 for bits in offsets]
        owners = jnp.stack([cell_at ^ bits for bits in owners]).astype(jnp.int32)
    else:
        shares = [lax.all_gather(low_share, "cell", axis=0, tiled=True)]
        owners = jnp.zeros((1,), jnp.int32)
    factor_other = swap_core(cell_factor)
    tile = dense_tile(block_values[0, 0], block_rows[0, 0], block_cols[0, 0], block_count[0])

    panel, message = call(
        gene_body,
        (shape((kdim, GENE_DEV), jnp.bfloat16), shape((kdim, CELL_DEV + kdim), jnp.float32)),
        1,
        1 + len(shares),
        2 * kdim * GENE_DEV * (CELL_DEV + kdim),
        8 * 2**20,
    )(owners, tile, *shares)
    other = swap_core(message)

    sent = [bits ^ 1 for bits in offsets] + [1] if paired else []
    kept = offsets + [0] if paired else []
    picks = jnp.stack([cell_at ^ bits for bits in sent or [0]]).astype(jnp.int32)
    outs = call(
        cell_body,
        (
            shape(cell_factor.shape, jnp.float32),
            shape((kdim, CELL_DEV), jnp.bfloat16),
            *[shape((size, GENE_DEV), jnp.bfloat16) for _ in sent],
        ),
        2,
        5,
        2 * kdim * CELL_DEV * 3 * kdim + kdim * CELL_DEV * GENE_DEV,
        10 * 2**20,
        [
            pltpu.VMEM((kdim, CELL_DEV), jnp.float32),
            pltpu.VMEM((kdim, CELL_DEV), jnp.float32),
            pltpu.VMEM((kdim // 2, CELL_DEV), jnp.bfloat16),
        ],
    )(picks, gene_at[None].astype(jnp.int32), tile, message, other, cell_factor, factor_other)
    cell_next, next_low, sends = outs[0], outs[1], outs[2:]

    if not paired:
        cell_gram = lax.psum(gram_of(next_low), "cell")
        own_cols = lax.psum_scatter(dot(next_low, tile), "cell", scatter_dimension=0, tiled=True)
        gram_part = lax.dynamic_slice_in_dim(cell_gram, cell_at * size, size, 0)
        rate_gene = 1.0 / (jnp.sqrt(jnp.sum(cell_gram * cell_gram)) + 1e-06)
        stepped = jnp.dot(
            gram_part, panel.astype(jnp.float32), precision=lax.Precision.HIGHEST
        )
        return (cell_next, jnp.maximum(gene_factor - rate_gene * (stepped - own_cols), 0.0))

    arrived = [swap(part, 1) for part in sends]
    picks = jnp.stack([cell_at ^ bits for bits in kept]).astype(jnp.int32)
    gram, *keeps = call(
        keep_body,
        (
            shape((kdim, kdim), jnp.bfloat16),
            *[shape((size, GENE_DEV), jnp.float32) for _ in kept],
        ),
        1,
        2,
        2 * kdim * CELL_DEV * kdim + kdim * CELL_DEV * GENE_DEV,
        6 * 2**20,
        [pltpu.VMEM((kdim // 2, CELL_DEV), jnp.bfloat16)],
    )(picks, next_low, tile)
    partials = lax.all_to_all(gram, "cell", 0, 0, tiled=True)
    stepped, square = call(
        gram_body,
        (shape((size, GENE_DEV), jnp.float32), shape((8, 128), jnp.float32)),
        0,
        2,
        2 * size * kdim * GENE_DEV * 3,
        2 * 2**20,
    )(partials, panel)
    squares = lax.all_to_all(
        jnp.broadcast_to(square[None], (n_cell, 8, 128)), "cell", 0, 0, tiled=True
    )
    rate_gene = 1.0 / (jnp.sqrt(jnp.sum(squares[:, 0, 0])) + 1e-06)
    pairs = [mine + part.astype(jnp.float32) for mine, part in zip(keeps, arrived)]
    own_cols = pairs[-1]
    for bits, pair in zip(offsets, pairs):
        own_cols = own_cols + swap(pair.astype(jnp.bfloat16), bits).astype(jnp.float32)
    return (cell_next, jnp.maximum(gene_factor - rate_gene * (stepped - own_cols), 0.0))


def solution(mesh):
    return jax.shard_map(
        shards,
        mesh=mesh,
        in_specs=(
            P(("groups", "cell"), "gene", None, None, None),
            P(("groups", "cell"), "gene", None),
            P(("groups", "cell"), "gene", None),
            P(("groups", "cell"), "gene"),
            P(("groups", "gene"), "cell"),
            P(("groups", "cell"), "gene"),
        ),
        out_specs=(P(("groups", "gene"), "cell"), P(("groups", "cell"), "gene")),
        check_vma=False,
    )
```

time: 242 us -> 73.9 us (0.31)
  waiting for transfers between devices: 187 us -> 18 us
  starting transfers between devices: 0.39 us -> 31.8 us
  matrix products: 23.8 us -> 0 us
  Pallas kernels: 0 us -> 14.4 us
  between operations: 16 us -> 2.16 us
  blocking collectives: 4.35 us -> 0 us
    reduce_scatter x2 -> x0, waiting for transfers between devices: 77.7 us -> none  [the longest x1 68 us: shards(): lax.psum_scatter(data_cell, 'cell', scatter_dimension=0, tiled=True)]
    psum x2 -> x0, waiting for transfers between devices: 65.4 us -> none  [the longest x1 61.5 us: shards(): cell_gram = lax.psum(local_gram, 'cell')]
    all_gather x1 -> x0, waiting for transfers between devices: 44 us -> none  [shards(): lax.all_gather(gene_factor.astype(jnp.bfloat16), 'cell', axis=0, tiled=True)]
    ppermute x0 -> x16, starting transfers between devices: none -> 24.5 us  [the longest x14 24 us: swap(): return lax.ppermute(value, 'cell', [(n, n ^ bits) for n in range(n_cell)])]
    dot_general x10 -> x0, matrix products: 23.8 us -> none  [the longest x1 4.18 us: tile_data_gene(): jnp.einsum('nrc,nkc->nkr', vals, picked, preferred_element_type=jnp.float32)]
    pallas_call x0 -> x5, Pallas kernels: none -> 14.4 us  [the longest x1 4.56 us: shards(): call(cell_body, (shape(cell_factor.shape, jnp.float32), shape((kdim, CELL...]
    ppermute x0 -> x16, waiting for transfers between devices: none -> 13.4 us  [the longest x14 10.2 us: swap(): return lax.ppermute(value, 'cell', [(n, n ^ bits) for n in range(n_cell)])]
    all_to_all x0 -> x2, starting transfers between devices: none -> 7.27 us  [the longest x1 3.93 us: shards(): partials = lax.all_to_all(gram, 'cell', 0, 0, tiled=True)]
  transfers between devices with their start and end apart: 5 -> 18, of which waited for: 5 -> 6; matrix products, arithmetic and copies ran while one was open for 10% -> 2% of each run, Pallas kernels for 0% -> 8%
where the time goes in v1:
time: 73.9 us; the launch traced here: 73.6 us
  starting transfers between devices  31.8 us (43%)
  waiting for transfers between devices  18 us (24%)
  Pallas kernels  14.4 us (19%)
  local copies, waits for them, and re-layouts  4.62 us (6%)
  other arithmetic  2.63 us (4%)
  between operations  2.16 us (3%)
    ppermute x14, starting transfers between devices, swap(): return lax.ppermute(value, 'cell', [(n, n ^ bits) for n in range(n_cell)])  24 us
    ppermute x14, waiting for transfers between devices, swap(): return lax.ppermute(value, 'cell', [(n, n ^ bits) for n in range(n_cell)])  10.2 us
    all_to_all x1, waiting for transfers between devices, shards(): lax.all_to_all(jnp.broadcast_to(square[None], (n_cell, 8, 128)), 'cell',...  4.58 us
    pallas_call x1, Pallas kernels, shards(): call(cell_body, (shape(cell_factor.shape, jnp.float32), shape((kdim, CELL...  4.56 us
    all_to_all x1, starting transfers between devices, shards(): partials = lax.all_to_all(gram, 'cell', 0, 0, tiled=True)  3.93 us
    unnamed x16, local copies, waits for them, and re-layouts  3.91 us
    pallas_call x1, Pallas kernels, shards(): call(gene_body, (shape((kdim, GENE_DEV), jnp.bfloat16), shape((kdim, CELL...  3.89 us
    pallas_call x1, Pallas kernels, dense_tile(): call(dense_body, shape((CELL_DEV, GENE_DEV), jnp.bfloat16), 3, 1, 0, 2 *...  3.45 us
  transfers between devices with their start and end apart: 18, of which 6 were waited for; matrix products, arithmetic and copies ran while one was open for 2% of the time, Pallas kernels for 8%

profile of v1, /device:TPU:0, one launch (start us, length us, event | category | flops | bytes accessed | tf_op | source)
XLA Modules:
  0.0 73.6 jit_solution(7191650738687762687)
XLA Ops:
  0.6 1.0 %convert_element_type.33.refs_0_ = bf16[32,2048]{1,0:T(8,128)(2,1)S(1)} convert(f32[32,2048]{1,0:T(8,128)} %param.11) | non-fusion elementwise | flops 65536 | bytes 393216 | tf_op jit(solution)/shard_map/convert_element_type | solution.py:150
  1.6 3.1 %collective-permute-start.3 = (bf16[32,2048]{1,0:T(8,128)(2,1)S(1)}, bf16[32,2048]{1,0:T(8,128)(2,1)S(1)}, u32[]{:S(2)}, u32[]{:S(2)}) collective-permute-start(bf16[32,2048]{1,0:T(8,128)(2,1)S(1)} %convert_element_type.33.refs_0_), channel_id=1, source_target_pairs={{0,4},{2,6},{4,0},{6,2},{8,12},{10,14},{12,8},{14,10},{1,5},{3,7},... | collective-permute-start | bytes 393224 | tf_op jit(solution)/shard_map/ppermute | solution.py:145
  4.7 2.6 %collective-permute-start.2 = (bf16[32,2048]{1,0:T(8,128)(2,1)S(1)}, bf16[32,2048]{1,0:T(8,128)(2,1)S(1)}, u32[]{:S(2)}, u32[]{:S(2)}) collective-permute-start(bf16[32,2048]{1,0:T(8,128)(2,1)S(1)} %convert_element_type.33.refs_0_), channel_id=1, source_target_pairs={{0,8},{2,10},{4,12},{6,14},{8,0},{10,2},{12,4},{14,6},{1,9},{3,11}... | collective-permute-start | bytes 393224 | tf_op jit(solution)/shard_map/ppermute | solution.py:145
  7.3 1.7 %collective-permute-start = (bf16[32,2048]{1,0:T(8,128)(2,1)S(1)}, bf16[32,2048]{1,0:T(8,128)(2,1)S(1)}, u32[]{:S(2)}, u32[]{:S(2)}) collective-permute-start(bf16[32,2048]{1,0:T(8,128)(2,1)S(1)} %convert_element_type.33.refs_0_), channel_id=1, source_target_pairs={{0,2},{2,0},{4,6},{6,4},{8,10},{10,8},{12,14},{14,12},{1,3},{3,1},... | collective-permute-start | bytes 393224 | tf_op jit(solution)/shard_map/ppermute | solution.py:145
  9.0 0.7 collective-permute-done.3.refs_4_
  9.7 1.7 %collective-permute-start.6 = (bf16[32,2048]{1,0:T(8,128)(2,1)S(1)}, bf16[32,2048]{1,0:T(8,128)(2,1)S(1)}, u32[]{:S(2)}, u32[]{:S(2)}) collective-permute-start(bf16[32,2048]{1,0:T(8,128)(2,1)S(1)} %collective-permute-done.3.refs_4_), channel_id=1, source_target_pairs={{0,2},{2,0},{4,6},{6,4},{8,10},{10,8},{12,14},{14,12},{1,3},{3,1},... | collective-permute-start | bytes 393224 | tf_op jit(solution)/shard_map/ppermute | solution.py:145
  11.4 6.2 %collective-permute-done.2.refs_3_ = bf16[32,2048]{1,0:T(8,128)(2,1)S(1)} collective-permute-done((bf16[32,2048]{1,0:T(8,128)(2,1)S(1)}, bf16[32,2048]{1,0:T(8,128)(2,1)S(1)}, u32[]{:S(2)}, u32[]{:S(2)}) %collective-permute-start.2) | collective-permute-done | bytes 131104 | tf_op jit(solution)/shard_map/ppermute | solution.py:145
  17.6 1.5 %collective-permute-start.5 = (bf16[32,2048]{1,0:T(8,128)(2,1)S(1)}, bf16[32,2048]{1,0:T(8,128)(2,1)S(1)}, u32[]{:S(2)}, u32[]{:S(2)}) collective-permute-start(bf16[32,2048]{1,0:T(8,128)(2,1)S(1)} %collective-permute-done.2.refs_3_), channel_id=1, source_target_pairs={{0,2},{2,0},{4,6},{6,4},{8,10},{10,8},{12,14},{14,12},{1,3},{3,1},... | collective-permute-start | bytes 393224 | tf_op jit(solution)/shard_map/ppermute | solution.py:145
  19.1 0.5 collective-permute-start.4
  20.3 1.6 %copy-done.1 = bf16[1,1,64,128,128]{4,3,2,1,0:T(8,128)(2,1)S(1)} copy-done((bf16[1,1,64,128,128]{4,3,2,1,0:T(8,128)(2,1)S(1)}, bf16[1,1,64,128,128]{4,3,2,1,0:T(8,128)(2,1)}, u32[]{:S(2)}) %copy-start.1) | copy-done | bytes 2097176
  21.9 0.7 copy-done.5
  22.6 0.7 copy-done.6
  23.2 3.4 %shard_map.77.tile = bf16[1024,2048]{1,0:T(8,128)(2,1)} custom-call(s32[64]{0:T(128)S(1)} %bitcast.18, s32[64]{0:T(128)S(1)} %bitcast.19, s32[1]{0:T(128)} %bitcast.15.count, bf16[64,128,128]{2,1,0:T(8,128)(2,1)S(1)} %bitcast.16), custom_call_target="tpu_custom_call" | custom-call | bytes 6291456 | tf_op jit(solution)/shard_map/pallas_call | solution.py:62
  26.8 3.9 %shard_map.78 = (bf16[256,2048]{1,0:T(8,128)(2,1)S(1)}, f32[256,1280]{1,0:T(8,128)S(1)}) custom-call(s32[8]{0:T(128)S(1)} %stack.50.owners, bf16[1024,2048]{1,0:T(8,128)(2,1)} %shard_map.77.tile, bf16[32,2048]{1,0:T(8,128)(2,1)S(1)} %convert_element_type.33.refs_0_, bf16[32,2048]{1,0:T(8,128)(2,1)S(1)} %collective-permute-done.refs_1_, ...), custom_call_target="tpu_custom_call" | custom-call | flops 1342177280 | bytes 8388608 | tf_op jit(solution)/shard_map/pallas_call | solution.py:165
  30.7 1.0 %copy-done.2 = bf16[256,2048]{1,0:T(8,128)(2,1)} copy-done((bf16[256,2048]{1,0:T(8,128)(2,1)}, bf16[256,2048]{1,0:T(8,128)(2,1)S(1)}, u32[]{:S(2)}) %copy-start.2) | copy-done | bytes 1048600
  32.3 3.0 %collective-permute-done.8.factor_other = f32[128,1024]{1,0:T(8,128)} collective-permute-done((f32[128,1024]{1,0:T(8,128)S(1)}, f32[128,1024]{1,0:T(8,128)}, u32[]{:S(2)}, u32[]{:S(2)}) %collective-permute-start.8) | collective-permute-done | bytes 524320 | tf_op jit(solution)/shard_map/ppermute | solution.py:148
  35.5 4.6 %shard_map.79 = (f32[128,1024]{1,0:T(8,128)}, bf16[256,1024]{1,0:T(8,128)(2,1)S(1)}, bf16[32,2048]{1,0:T(8,128)(2,1)}, bf16[32,2048]{1,0:T(8,128)(2,1)S(1)}, bf1...) custom-call(s32[4]{0:T(128)S(1)} %pad_add_fusion.picks, s32[1]{0:T(128)} %bitcast.4.at, ...), custom_call_target="tpu_custom_call" | custom-call | flops 939524096 | bytes 10485760 | tf_op jit(solution)/shard_map/pallas_call | solution.py:178
  40.0 1.2 %collective-permute-start.10 = (bf16[32,2048]{1,0:T(8,128)(2,1)}, bf16[32,2048]{1,0:T(8,128)(2,1)S(1)}, u32[]{:S(2)}, u32[]{:S(2)}) collective-permute-start(bf16[32,2048]{1,0:T(8,128)(2,1)} %get-tuple-element.27), channel_id=1, source_target_pairs={{0,2},{2,0},{4,6},{6,4},{8,10},{10,8},{12,14},{14,12},{1,3},{3,1},... | collective-permute-start | bytes 393224 | tf_op jit(solution)/shard_map/ppermute | solution.py:145
  41.3 1.9 %shard_map.80 = (bf16[256,256]{1,0:T(8,128)(2,1)}, f32[32,2048]{1,0:T(8,128)S(1)}, f32[32,2048]{1,0:T(8,128)S(1)}, f32[32,2048]{1,0:T(8,128)S(1)}, f32[32,2048]{1,0:T(8,128)S(1)}) custom-call(s32[4]{0:T(128)S(1)} %pad_add_fusion.1.picks, bf16[256,1024]{1,0:T(8,128)(2,1)S(1)} %get-tuple-element.19.low, bf16[1024,2048]{1,0:T(8,128)(2,1)S(1)} %copy-done), custom_call_target="tpu_custom_call" | custom-call | flops 671088640 | bytes 6291456 | tf_op jit(solution)/shard_map/pallas_call | solution.py:209
  43.2 3.9 %all-to-all-start = ((bf16[8,32,256]{2,1,0:T(8,128)(2,1)}), bf16[8,32,256]{2,1,0:T(8,128)(2,1)S(1)}, u32[]{:S(2)}, u32[]{:S(2)}) async-start(bf16[8,32,256]{2,1,0:T(8,128)(2,1)} %bitcast.13), calls=%async_computation | async-start | bytes 262144 | tf_op jit(solution)/shard_map/all_to_all | solution.py:221
  47.2 2.0 %collective-permute-start.9 = (bf16[32,2048]{1,0:T(8,128)(2,1)S(1)}, bf16[32,2048]{1,0:T(8,128)(2,1)S(1)}, u32[]{:S(2)}, u32[]{:S(2)}) collective-permute-start(bf16[32,2048]{1,0:T(8,128)(2,1)S(1)} %get-tuple-element.25), channel_id=1, source_target_pairs={{0,2},{2,0},{4,6},{6,4},{8,10},{10,8},{12,14},{14,12},{1,3},{3,1},... | collective-permute-start | bytes 393224 | tf_op jit(solution)/shard_map/ppermute | solution.py:145
  49.2 2.0 %collective-permute-start.14 = (bf16[32,2048]{1,0:T(8,128)(2,1)S(1)}, bf16[32,2048]{1,0:T(8,128)(2,1)S(1)}, u32[]{:S(2)}, u32[]{:S(2)}) collective-permute-start(bf16[32,2048]{1,0:T(8,128)(2,1)S(1)} %get-tuple-element.31), channel_id=1, source_target_pairs={{0,2},{2,0},{4,6},{6,4},{8,10},{10,8},{12,14},{14,12},{1,3},{3,1},... | collective-permute-start | bytes 393224 | tf_op jit(solution)/shard_map/ppermute | solution.py:145
  51.2 3.3 %collective-permute-start.11 = (bf16[32,2048]{1,0:T(8,128)(2,1)S(1)}, bf16[32,2048]{1,0:T(8,128)(2,1)S(1)}, u32[]{:S(2)}, u32[]{:S(2)}) collective-permute-start(bf16[32,2048]{1,0:T(8,128)(2,1)S(1)} %add_convert_fusion.2), channel_id=1, source_target_pairs={{0,12},{2,14},{4,8},{6,10},{8,4},{10,6},{12,0},{14,2},{1,13},{3,15... | collective-permute-start | bytes 393224 | tf_op jit(solution)/shard_map/ppermute | solution.py:145
  54.6 3.3 %collective-permute-done.12 = bf16[32,2048]{1,0:T(8,128)(2,1)S(1)} collective-permute-done((bf16[32,2048]{1,0:T(8,128)(2,1)S(1)}, bf16[32,2048]{1,0:T(8,128)(2,1)S(1)}, u32[]{:S(2)}, u32[]{:S(2)}) %collective-permute-start.12) | collective-permute-done | bytes 131104 | tf_op jit(solution)/shard_map/ppermute | solution.py:145
  57.9 2.3 %collective-permute-start.13 = (bf16[32,2048]{1,0:T(8,128)(2,1)S(1)}, bf16[32,2048]{1,0:T(8,128)(2,1)S(1)}, u32[]{:S(2)}, u32[]{:S(2)}) collective-permute-start(bf16[32,2048]{1,0:T(8,128)(2,1)S(1)} %add_convert_fusion.1), channel_id=1, source_target_pairs={{0,8},{2,10},{4,12},{6,14},{8,0},{10,2},{12,4},{14,6},{1,9},{3,11}... | collective-permute-start | bytes 393224 | tf_op jit(solution)/shard_map/ppermute | solution.py:145
  60.1 0.6 shard_map.81
  60.7 0.6 broadcast_in_dim.10
  61.4 3.3 %all-to-all-start.1 = ((f32[8,8,128]{2,1,0:T(8,128)}), f32[8,8,128]{2,1,0:T(8,128)S(1)}, u32[]{:S(2)}, u32[]{:S(2)}) async-start(f32[8,8,128]{2,1,0:T(8,128)} %broadcast_in_dim.10), calls=%async_computation.1 | async-start | bytes 65536 | tf_op jit(solution)/shard_map/all_to_all | solution.py:230
  64.8 2.0 %collective-permute-start.15 = (bf16[32,2048]{1,0:T(8,128)(2,1)S(1)}, bf16[32,2048]{1,0:T(8,128)(2,1)S(1)}, u32[]{:S(2)}, u32[]{:S(2)}) collective-permute-start(bf16[32,2048]{1,0:T(8,128)(2,1)S(1)} %add_convert_fusion), channel_id=1, source_target_pairs={{0,4},{2,6},{4,0},{6,2},{8,12},{10,14},{12,8},{14,10},{1,5},{3,7},... | collective-permute-start | bytes 393224 | tf_op jit(solution)/shard_map/ppermute | solution.py:145
  66.8 4.6 %all-to-all-done.1 = f32[8,8,128]{2,1,0:T(8,128)S(1)} async-done(((f32[8,8,128]{2,1,0:T(8,128)}), f32[8,8,128]{2,1,0:T(8,128)S(1)}, u32[]{:S(2)}, u32[]{:S(2)}) %all-to-all-start.1) | async-done | bytes 32800 | tf_op jit(solution)/shard_map/all_to_all | solution.py:230
  71.4 0.6 slice_reduce_fusion
  72.8 0.8 %subtract_maximum_fusion = f32[32,2048]{1,0:T(8,128)} fusion(f32[32,2048]{1,0:T(8,128)S(1)} %copy-done.7, f32[32,2048]{1,0:T(8,128)S(1)} %get-tuple-element.23, bf16[32,2048]{1,0:T(8,128)(2,1)S(1)} %collective-permute-done.15, bf16[32,2048]{1,0:T(8,128)(2,1)S(1)} %collective-permute-done.13, bf16[32,2048]{1,0:T(8,128)(2,1)S(1)} %collective-permute-done.11, ...), kind=kLoop, calls=%fused_computation | loop fusion | flops 786432 | bytes 1572868 | tf_op jit(solution)/shard_map/max | solution.py:238
  (35 shorter events, 1.2 us)
Async XLA Ops:
  1.6 8.1 %collective-permute-start.3 = (bf16[32,2048]{1,0:T(8,128)(2,1)S(1)}, bf16[32,2048]{1,0:T(8,128)(2,1)S(1)}, u32[]{:S(2)}, u32[]{:S(2)}) collective-permute-start(bf16[32,2048]{1,0:T(8,128)(2,1)S(1)} %convert_element_type.33.refs_0_), channel_id=1, source_target_pairs={{0,4},{2,6},{4,0},{6,2},{8,12},{10,14},{12,8},{14,10},{1,5},{3,7},... | collective-permute-start | bytes 393224 | tf_op jit(solution)/shard_map/ppermute | solution.py:145
  4.7 12.9 %collective-permute-start.2 = (bf16[32,2048]{1,0:T(8,128)(2,1)S(1)}, bf16[32,2048]{1,0:T(8,128)(2,1)S(1)}, u32[]{:S(2)}, u32[]{:S(2)}) collective-permute-start(bf16[32,2048]{1,0:T(8,128)(2,1)S(1)} %convert_element_type.33.refs_0_), channel_id=1, source_target_pairs={{0,8},{2,10},{4,12},{6,14},{8,0},{10,2},{12,4},{14,6},{1,9},{3,11}... | collective-permute-start | bytes 393224 | tf_op jit(solution)/shard_map/ppermute | solution.py:145
  7.3 11.8 %collective-permute-start.1 = (bf16[32,2048]{1,0:T(8,128)(2,1)S(1)}, bf16[32,2048]{1,0:T(8,128)(2,1)S(1)}, u32[]{:S(2)}, u32[]{:S(2)}) collective-permute-start(bf16[32,2048]{1,0:T(8,128)(2,1)S(1)} %convert_element_type.33.refs_0_), channel_id=1, source_target_pairs={{0,12},{2,14},{4,8},{6,10},{8,4},{10,6},{12,0},{14,2},{1,13},{3,15... | collective-permute-start | bytes 393224 | tf_op jit(solution)/shard_map/ppermute | solution.py:145
  7.3 19.5 %collective-permute-start = (bf16[32,2048]{1,0:T(8,128)(2,1)S(1)}, bf16[32,2048]{1,0:T(8,128)(2,1)S(1)}, u32[]{:S(2)}, u32[]{:S(2)}) collective-permute-start(bf16[32,2048]{1,0:T(8,128)(2,1)S(1)} %convert_element_type.33.refs_0_), channel_id=1, source_target_pairs={{0,2},{2,0},{4,6},{6,4},{8,10},{10,8},{12,14},{14,12},{1,3},{3,1},... | collective-permute-start | bytes 393224 | tf_op jit(solution)/shard_map/ppermute | solution.py:145
  9.7 17.0 %collective-permute-start.6 = (bf16[32,2048]{1,0:T(8,128)(2,1)S(1)}, bf16[32,2048]{1,0:T(8,128)(2,1)S(1)}, u32[]{:S(2)}, u32[]{:S(2)}) collective-permute-start(bf16[32,2048]{1,0:T(8,128)(2,1)S(1)} %collective-permute-done.3.refs_4_), channel_id=1, source_target_pairs={{0,2},{2,0},{4,6},{6,4},{8,10},{10,8},{12,14},{14,12},{1,3},{3,1},... | collective-permute-start | bytes 393224 | tf_op jit(solution)/shard_map/ppermute | solution.py:145
  17.6 9.1 %collective-permute-start.5 = (bf16[32,2048]{1,0:T(8,128)(2,1)S(1)}, bf16[32,2048]{1,0:T(8,128)(2,1)S(1)}, u32[]{:S(2)}, u32[]{:S(2)}) collective-permute-start(bf16[32,2048]{1,0:T(8,128)(2,1)S(1)} %collective-permute-done.2.refs_3_), channel_id=1, source_target_pairs={{0,2},{2,0},{4,6},{6,4},{8,10},{10,8},{12,14},{14,12},{1,3},{3,1},... | collective-permute-start | bytes 393224 | tf_op jit(solution)/shard_map/ppermute | solution.py:145
  19.1 7.7 %collective-permute-start.4 = (bf16[32,2048]{1,0:T(8,128)(2,1)S(1)}, bf16[32,2048]{1,0:T(8,128)(2,1)S(1)}, u32[]{:S(2)}, u32[]{:S(2)}) collective-permute-start(bf16[32,2048]{1,0:T(8,128)(2,1)S(1)} %collective-permute-done.1.refs_2_), channel_id=1, source_target_pairs={{0,2},{2,0},{4,6},{6,4},{8,10},{10,8},{12,14},{14,12},{1,3},{3,1},... | collective-permute-start | bytes 393224 | tf_op jit(solution)/shard_map/ppermute | solution.py:145
  20.3 1.6 %copy-start.1 = (bf16[1,1,64,128,128]{4,3,2,1,0:T(8,128)(2,1)S(1)}, bf16[1,1,64,128,128]{4,3,2,1,0:T(8,128)(2,1)}, u32[]{:S(2)}) copy-start(bf16[1,1,64,128,128]{4,3,2,1,0:T(8,128)(2,1)} %param.6) | copy-start | bytes 6291460
  21.9 0.7 copy-start.5
  22.5 0.7 copy-start.6
  26.7 5.0 %copy-start.4 = (f32[128,1024]{1,0:T(8,128)S(1)}, f32[128,1024]{1,0:T(8,128)}, u32[]{:S(2)}) copy-start(f32[128,1024]{1,0:T(8,128)} %factor_mine.1) | copy-start | bytes 1572868
  30.7 1.0 %copy-start.2 = (bf16[256,2048]{1,0:T(8,128)(2,1)}, bf16[256,2048]{1,0:T(8,128)(2,1)S(1)}, u32[]{:S(2)}) copy-start(bf16[256,2048]{1,0:T(8,128)(2,1)S(1)} %get-tuple-element.21.panel) | copy-start | bytes 3145732
  31.7 3.8 %collective-permute-start.7 = (f32[256,1280]{1,0:T(8,128)S(1)}, f32[256,1280]{1,0:T(8,128)S(1)}, u32[]{:S(2)}, u32[]{:S(2)}) collective-permute-start(f32[256,1280]{1,0:T(8,128)S(1)} %get-tuple-element.17.mine), channel_id=1, source_target_pairs={{0,1},{1,0},{2,3},{3,2},{4,5},{5,4},{6,7},{7,6},{8,9},{9,8},{10,11... | collective-permute-start | bytes 3932168 | tf_op jit(solution)/shard_map/ppermute | solution.py:148
  31.7 3.5 %collective-permute-start.8 = (f32[128,1024]{1,0:T(8,128)S(1)}, f32[128,1024]{1,0:T(8,128)}, u32[]{:S(2)}, u32[]{:S(2)}) collective-permute-start(f32[128,1024]{1,0:T(8,128)S(1)} %copy-done.4), channel_id=1, source_target_pairs={{0,1},{1,0},{2,3},{3,2},{4,5},{5,4},{6,7},{7,6},{8,9},{9,8},{10,11... | collective-permute-start | bytes 1572872 | tf_op jit(solution)/shard_map/ppermute | solution.py:148
  35.5 5.8 %copy-start = (bf16[1024,2048]{1,0:T(8,128)(2,1)S(1)}, bf16[1024,2048]{1,0:T(8,128)(2,1)}, u32[]{:S(2)}) copy-start(bf16[1024,2048]{1,0:T(8,128)(2,1)} %shard_map.77.tile) | copy-start | bytes 12582916
  40.0 11.2 %collective-permute-start.10 = (bf16[32,2048]{1,0:T(8,128)(2,1)}, bf16[32,2048]{1,0:T(8,128)(2,1)S(1)}, u32[]{:S(2)}, u32[]{:S(2)}) collective-permute-start(bf16[32,2048]{1,0:T(8,128)(2,1)} %get-tuple-element.27), channel_id=1, source_target_pairs={{0,2},{2,0},{4,6},{6,4},{8,10},{10,8},{12,14},{14,12},{1,3},{3,1},... | collective-permute-start | bytes 393224 | tf_op jit(solution)/shard_map/ppermute | solution.py:145
  41.3 18.8 %copy-start.3 = (bf16[256,2048]{1,0:T(8,128)(2,1)S(1)}, bf16[256,2048]{1,0:T(8,128)(2,1)}, u32[]{:S(2)}) copy-start(bf16[256,2048]{1,0:T(8,128)(2,1)} %copy-done.2) | copy-start | bytes 3145732
  43.2 29.5 %copy-start.7 = (f32[32,2048]{1,0:T(8,128)S(1)}, f32[32,2048]{1,0:T(8,128)}, u32[]{:S(2)}) copy-start(f32[32,2048]{1,0:T(8,128)} %param.11) | copy-start | bytes 786436
  43.2 16.9 %all-to-all-start = ((bf16[8,32,256]{2,1,0:T(8,128)(2,1)}), bf16[8,32,256]{2,1,0:T(8,128)(2,1)S(1)}, u32[]{:S(2)}, u32[]{:S(2)}) async-start(bf16[8,32,256]{2,1,0:T(8,128)(2,1)} %bitcast.13), calls=%async_computation | async-start | bytes 262144 | tf_op jit(solution)/shard_map/all_to_all | solution.py:221
  47.2 25.5 %collective-permute-start.9 = (bf16[32,2048]{1,0:T(8,128)(2,1)S(1)}, bf16[32,2048]{1,0:T(8,128)(2,1)S(1)}, u32[]{:S(2)}, u32[]{:S(2)}) collective-permute-start(bf16[32,2048]{1,0:T(8,128)(2,1)S(1)} %get-tuple-element.25), channel_id=1, source_target_pairs={{0,2},{2,0},{4,6},{6,4},{8,10},{10,8},{12,14},{14,12},{1,3},{3,1},... | collective-permute-start | bytes 393224 | tf_op jit(solution)/shard_map/ppermute | solution.py:145
  49.2 8.6 %collective-permute-start.12 = (bf16[32,2048]{1,0:T(8,128)(2,1)S(1)}, bf16[32,2048]{1,0:T(8,128)(2,1)S(1)}, u32[]{:S(2)}, u32[]{:S(2)}) collective-permute-start(bf16[32,2048]{1,0:T(8,128)(2,1)S(1)} %get-tuple-element.29), channel_id=1, source_target_pairs={{0,2},{2,0},{4,6},{6,4},{8,10},{10,8},{12,14},{14,12},{1,3},{3,1},... | collective-permute-start | bytes 393224 | tf_op jit(solution)/shard_map/ppermute | solution.py:145
  49.2 15.5 %collective-permute-start.14 = (bf16[32,2048]{1,0:T(8,128)(2,1)S(1)}, bf16[32,2048]{1,0:T(8,128)(2,1)S(1)}, u32[]{:S(2)}, u32[]{:S(2)}) collective-permute-start(bf16[32,2048]{1,0:T(8,128)(2,1)S(1)} %get-tuple-element.31), channel_id=1, source_target_pairs={{0,2},{2,0},{4,6},{6,4},{8,10},{10,8},{12,14},{14,12},{1,3},{3,1},... | collective-permute-start | bytes 393224 | tf_op jit(solution)/shard_map/ppermute | solution.py:145
  51.2 21.5 %collective-permute-start.11 = (bf16[32,2048]{1,0:T(8,128)(2,1)S(1)}, bf16[32,2048]{1,0:T(8,128)(2,1)S(1)}, u32[]{:S(2)}, u32[]{:S(2)}) collective-permute-start(bf16[32,2048]{1,0:T(8,128)(2,1)S(1)} %add_convert_fusion.2), channel_id=1, source_target_pairs={{0,12},{2,14},{4,8},{6,10},{8,4},{10,6},{12,0},{14,2},{1,13},{3,15... | collective-permute-start | bytes 393224 | tf_op jit(solution)/shard_map/ppermute | solution.py:145
  57.9 14.9 %collective-permute-start.13 = (bf16[32,2048]{1,0:T(8,128)(2,1)S(1)}, bf16[32,2048]{1,0:T(8,128)(2,1)S(1)}, u32[]{:S(2)}, u32[]{:S(2)}) collective-permute-start(bf16[32,2048]{1,0:T(8,128)(2,1)S(1)} %add_convert_fusion.1), channel_id=1, source_target_pairs={{0,8},{2,10},{4,12},{6,14},{8,0},{10,2},{12,4},{14,6},{1,9},{3,11}... | collective-permute-start | bytes 393224 | tf_op jit(solution)/shard_map/ppermute | solution.py:145
  61.4 10.0 %all-to-all-start.1 = ((f32[8,8,128]{2,1,0:T(8,128)}), f32[8,8,128]{2,1,0:T(8,128)S(1)}, u32[]{:S(2)}, u32[]{:S(2)}) async-start(f32[8,8,128]{2,1,0:T(8,128)} %broadcast_in_dim.10), calls=%async_computation.1 | async-start | bytes 65536 | tf_op jit(solution)/shard_map/all_to_all | solution.py:230
  64.8 8.0 %collective-permute-start.15 = (bf16[32,2048]{1,0:T(8,128)(2,1)S(1)}, bf16[32,2048]{1,0:T(8,128)(2,1)S(1)}, u32[]{:S(2)}, u32[]{:S(2)}) collective-permute-start(bf16[32,2048]{1,0:T(8,128)(2,1)S(1)} %add_convert_fusion), channel_id=1, source_target_pairs={{0,4},{2,6},{4,0},{6,2},{8,12},{10,14},{12,8},{14,10},{1,5},{3,7},... | collective-permute-start | bytes 393224 | tf_op jit(solution)/shard_map/ppermute | solution.py:145

commit v2 on v1

v2 whole, which is shorter than its diff:
```python
import functools

import jax
import jax.numpy as jnp
from jax import lax
from jax.experimental import pallas as pl
from jax.experimental.pallas import tpu as pltpu
from jax.sharding import PartitionSpec as P

BLK = 128
CELL_DEV = 1024
GENE_DEV = 2048
VMEM_BYTES = 24 * 2**20

NT = (((1,), (1,)), ((), ()))
NN = (((1,), (0,)), ((), ()))
SMEM_SPEC = pl.BlockSpec(memory_space=pltpu.SMEM)
VMEM_SPEC = pl.BlockSpec(memory_space=pltpu.VMEM)


def dot(a, b, dims=NN):
    return lax.dot_general(a, b, dims, preferred_element_type=jnp.float32)


def split_dot(a, b):
    high = a.astype(jnp.bfloat16)
    low = (a - high.astype(jnp.float32)).astype(jnp.bfloat16)
    rows = a.shape[0]
    both = dot(jnp.concatenate([high, low], axis=0), b)
    return both[:rows] + both[rows:]


def call(body, outs, n_smem, n_vmem, flops, traffic, scratch=()):
    return pl.pallas_call(
        body,
        out_shape=outs,
        in_specs=[SMEM_SPEC] * n_smem + [VMEM_SPEC] * n_vmem,
        out_specs=jax.tree.map(lambda _: VMEM_SPEC, outs),
        scratch_shapes=list(scratch),
        compiler_params=pltpu.CompilerParams(vmem_limit_bytes=VMEM_BYTES),
        cost_estimate=pl.CostEstimate(flops=flops, bytes_accessed=traffic, transcendentals=0),
    )


def shape(dims, dtype):
    return jax.ShapeDtypeStruct(dims, dtype)


def dense_body(rows, cols, count, values, tile, turned):
    tile[...] = jnp.zeros_like(tile)
    turned[...] = jnp.zeros_like(turned)

    def place(n, carry):
        row = pl.multiple_of(rows[n] * BLK, BLK)
        col = pl.multiple_of(cols[n] * BLK, BLK)
        block = values[n]
        tile[pl.ds(row, BLK), pl.ds(col, BLK)] = block
        turned[pl.ds(col, BLK), pl.ds(row, BLK)] = block.T
        return carry

    lax.fori_loop(0, count[0], place, 0)


def dense_tile(values, rows, cols, count):
    return call(
        dense_body,
        (
            shape((CELL_DEV, GENE_DEV), jnp.bfloat16),
            shape((GENE_DEV, CELL_DEV), jnp.bfloat16),
        ),
        3,
        1,
        0,
        0,
    )(rows, cols, count, values)


def first_body(turned, *refs):
    shares, panel, message = refs[:-2], refs[-2], refs[-1]
    size = shares[0].shape[0]
    for n, part in enumerate(shares):
        panel[n * size : (n + 1) * size] = part[...]
    message[...] = dot(panel[...], turned[...])


def second_body(owners, turned, first, *refs):
    shares, panel, message, chosen = refs[:-3], refs[-3], refs[-2], refs[-1]
    size, half = shares[0].shape[0], first.shape[0]
    for n, part in enumerate(shares):
        chosen[n * size : (n + 1) * size] = part[...]
    for n in range(half // size):
        row = pl.multiple_of(owners[n] * size, size)
        panel[pl.ds(row, size)] = first[n * size : (n + 1) * size]
    for n, part in enumerate(shares):
        row = pl.multiple_of(owners[half // size + n] * size, size)
        panel[pl.ds(row, size)] = part[...]
    message[:, :CELL_DEV] = dot(chosen[...], turned[...])
    low = panel[...]
    gram = dot(low, low, NT)
    kdim = low.shape[0]
    message[:, CELL_DEV : CELL_DEV + kdim] = gram[:half]
    message[:, CELL_DEV + kdim :] = gram[half:]


def cell_body(
    at, owners, picks, tile, mine_first, other_first, mine, other, factor_mine, factor_other,
    cell_next, low, gram_out, *rest
):
    parts, (factor, data, updated, chosen) = rest[:-4], rest[-4:]
    share = factor_mine.shape[0]
    kdim = factor.shape[0]
    half = mine.shape[0]
    own = pl.multiple_of(at[0] * share, share)
    theirs = pl.multiple_of((1 - at[0]) * share, share)
    factor[pl.ds(own, share)] = factor_mine[...]
    factor[pl.ds(theirs, share)] = factor_other[...]
    size = kdim // owners.shape[0]
    for n in range(owners.shape[0]):
        row = pl.multiple_of(owners[n] * size, size)
        if n * size < half:
            rows = pl.ds(n * size, size)
            data[pl.ds(row, size)] = mine_first[rows] + other_first[rows]
        else:
            rows = pl.ds(n * size - half, size)
            data[pl.ds(row, size)] = mine[rows, :CELL_DEV] + other[rows, :CELL_DEV]
    gram = mine[:, CELL_DEV:] + other[:, CELL_DEV:]
    gram = jnp.concatenate([gram[:, :kdim], gram[:, kdim:]], axis=0)
    norm = jnp.sum(jnp.sum(gram * gram, axis=1, keepdims=True), axis=0, keepdims=True)
    rate = 1.0 / (jnp.sqrt(norm) + 1e-06)
    held = factor[...]
    stepped = split_dot(gram, held.astype(jnp.bfloat16))
    updated[...] = jnp.maximum(held - rate * (stepped - data[...]), 0.0)
    cell_next[...] = updated[pl.ds(own, share)]
    low[...] = updated[...].astype(jnp.bfloat16)
    if not parts:
        return
    panel = low[...]
    gram_out[...] = dot(panel, panel, NT).astype(gram_out.dtype)
    for n in range(picks.shape[0]):
        row = pl.multiple_of(picks[n] * size, size)
        chosen[n * size : (n + 1) * size] = low[pl.ds(row, size)]
    product = dot(chosen[...], tile[...])
    row = 0
    for out in parts:
        out[...] = product[row : row + out.shape[0]].astype(out.dtype)
        row += out.shape[0]


def gram_body(partials, panel, stepped, square):
    size = stepped.shape[0]
    gram = partials[:size].astype(jnp.float32)
    for n in range(1, partials.shape[0] // size):
        gram = gram + partials[n * size : (n + 1) * size].astype(jnp.float32)
    stepped[...] = split_dot(gram, panel[...])
    norm = jnp.sum(jnp.sum(gram * gram, axis=1, keepdims=True), axis=0, keepdims=True)
    square[...] = jnp.broadcast_to(norm, square.shape)


def gram_of(panel):
    return dot(panel, panel, NT)


def shards(block_values, block_rows, block_cols, block_count, cell_factor, gene_factor):
    n_cell = lax.axis_size("cell")
    kdim = cell_factor.shape[0] * lax.axis_size("gene")
    size = gene_factor.shape[0]
    paired = size % 16 == 0 and n_cell >= 4 and n_cell & (n_cell - 1) == 0
    cell_at = lax.axis_index("cell")
    gene_at = lax.axis_index("gene")

    def swap(value, bits):
        return lax.ppermute(value, "cell", [(n, n ^ bits) for n in range(n_cell)])

    def swap_core(value):
        return lax.ppermute(value, "gene", [(0, 1), (1, 0)])

    def ints(values):
        return jnp.stack(values).astype(jnp.int32)

    low_share = gene_factor.astype(jnp.bfloat16)
    factor_other = swap_core(cell_factor)
    values = block_values[0, 0]
    tile, turned = dense_tile(values, block_rows[0, 0], block_cols[0, 0], block_count[0])
    half = kdim // 2
    if paired:
        lines = [1 << bit for bit in range(1, n_cell.bit_length() - 1)][::-1]
        far = {0: low_share}
        for bits in lines + [1]:
            far[bits] = swap(low_share, bits)
        first = sorted(range(n_cell), key=lambda bits: (bits.bit_count(), bits))
        first, second = first[: n_cell // 2], first[n_cell // 2 :]
        far[lines[0]], tile, turned, factor_other = lax.optimization_barrier(
            (far[lines[0]], tile, turned, factor_other)
        )
        for at, bits in enumerate(lines):
            for held in sorted(far):
                if held and held not in (1, bits) and held ^ bits not in far and held % (2 * bits) == 0:
                    far[held ^ bits] = swap(far[held], bits)
        for bits in range(2, n_cell, 2):
            far[bits ^ 1] = swap(far[bits], 1)
        owners = ints([cell_at ^ bits for bits in first + second])
        twice = [bits for bits in second if bits % 2 == 0]
        first_shares = [far[bits] for bits in first]
        first_shares[0], *ahead = lax.optimization_barrier((low_share, *[far[bits] for bits in twice]))
        far.update(zip(twice, ahead))
        second_shares = [far[bits] for bits in second]
    else:
        whole = lax.all_gather(low_share, "cell", axis=0, tiled=True)
        owners = jnp.arange(2, dtype=jnp.int32)
        first_shares, second_shares = [whole[:half]], [whole[half:]]

    panel_first, message_first = call(
        first_body,
        (shape((half, GENE_DEV), jnp.bfloat16), shape((half, CELL_DEV), jnp.float32)),
        0,
        1 + len(first_shares),
        0,
        0,
    )(turned, *first_shares)
    other_first = swap_core(message_first)
    if paired:
        other_first, *second_shares = lax.optimization_barrier((other_first, *second_shares))
    panel, message = call(
        second_body,
        (
            shape((kdim, GENE_DEV), jnp.bfloat16),
            shape((half, CELL_DEV + 2 * kdim), jnp.float32),
        ),
        1,
        2 + len(second_shares),
        2 * half * GENE_DEV * (CELL_DEV + 2 * kdim),
        8 * 2**20,
        [pltpu.VMEM((half, GENE_DEV), jnp.bfloat16)],
    )(owners, turned, panel_first, *second_shares)
    other = swap_core(message)

    through = list(range(n_cell - 2, 2, -2)) if paired else []
    order = [bits ^ 1 for bits in through] + [2, 3] + through + [1, 0] if paired else [0]
    rows = [size] * len(through) + [2 * size] if paired else []
    keeps = [size] * (len(through) + 2) if paired else []
    cell_next, next_low, gram, *parts = call(
        cell_body,
        (
            shape(cell_factor.shape, jnp.float32),
            shape((kdim, CELL_DEV), jnp.bfloat16),
            shape((kdim, kdim), jnp.bfloat16),
            *[shape((count, GENE_DEV), jnp.bfloat16) for count in rows],
            *[shape((count, GENE_DEV), jnp.float32) for count in keeps],
        ),
        3,
        7,
        2 * kdim * CELL_DEV * 3 * kdim + 2 * kdim * CELL_DEV * GENE_DEV,
        14 * 2**20,
        [
            pltpu.VMEM((kdim, CELL_DEV), jnp.float32),
            pltpu.VMEM((kdim, CELL_DEV), jnp.float32),
            pltpu.VMEM((kdim, CELL_DEV), jnp.float32),
            pltpu.VMEM((kdim, CELL_DEV), jnp.bfloat16),
        ],
    )(
        ints([gene_at]), owners, ints([cell_at ^ bits for bits in order]),
        tile, message_first, other_first, message, other, cell_factor, factor_other,
    )

    if not paired:
        cell_gram = lax.psum(gram_of(next_low), "cell")
        own_cols = lax.psum_scatter(dot(next_low, tile), "cell", scatter_dimension=0, tiled=True)
        gram_part = lax.dynamic_slice_in_dim(cell_gram, cell_at * size, size, 0)
        rate_gene = 1.0 / (jnp.sqrt(jnp.sum(cell_gram * cell_gram)) + 1e-06)
        stepped = jnp.dot(
            gram_part, panel.astype(jnp.float32), precision=lax.Precision.HIGHEST
        )
        return (cell_next, jnp.maximum(gene_factor - rate_gene * (stepped - own_cols), 0.0))

    sends, keeps = parts[: len(rows)], parts[len(rows) :]
    arrived = [swap(part, 1) for part in sends[:-1]]
    beside = swap(sends[-1], 2).astype(jnp.float32)
    moved = [(mine + part.astype(jnp.float32)).astype(jnp.bfloat16) for mine, part in zip(keeps, arrived)]
    near = (keeps[-2] + beside[size:]).astype(jnp.bfloat16)
    moved[0], gram = lax.optimization_barrier((moved[0], gram))
    partials = lax.all_to_all(gram, "cell", 0, 0, tiled=True)
    stepped, square = call(
        gram_body,
        (shape((size, GENE_DEV), jnp.float32), shape((8, 128), jnp.float32)),
        0,
        2,
        2 * size * kdim * GENE_DEV * 3,
        2 * 2**20,
    )(partials, panel)
    squares = lax.all_to_all(
        jnp.broadcast_to(square[None], (n_cell, 8, 128)), "cell", 0, 0, tiled=True
    )
    rate_gene = 1.0 / (jnp.sqrt(jnp.sum(squares[:, 0, 0])) + 1e-06)
    own_cols = keeps[-1] + beside[:size]
    for part, bits in zip(moved + [near], through + [1]):
        own_cols = own_cols + swap(part, bits).astype(jnp.float32)
    return (cell_next, jnp.maximum(gene_factor - rate_gene * (stepped - own_cols), 0.0))


def solution(mesh):
    return jax.shard_map(
        shards,
        mesh=mesh,
        in_specs=(
            P(("groups", "cell"), "gene", None, None, None),
            P(("groups", "cell"), "gene", None),
            P(("groups", "cell"), "gene", None),
            P(("groups", "cell"), "gene"),
            P(("groups", "gene"), "cell"),
            P(("groups", "cell"), "gene"),
        ),
        out_specs=(P(("groups", "gene"), "cell"), P(("groups", "cell"), "gene")),
        check_vma=False,
    )
```

time: 73.9 us -> 94 us (1.27)
  local copies, waits for them, and re-layouts: 4.62 us -> 18.2 us
  waiting for transfers between devices: 18 us -> 30.4 us
  starting transfers between devices: 31.8 us -> 26.1 us
  Pallas kernels: 14.4 us -> 11.7 us
  other arithmetic: 2.63 us -> 4.44 us
    unnamed x16 -> x34, local copies, waits for them, and re-layouts: 3.91 us -> 17.4 us
    ppermute x14 -> x13, waiting for transfers between devices: 10.2 us -> 17.6 us  [swap(): return lax.ppermute(value, 'cell', [(n, n ^ bits) for n in range(n_cell)])]
    all_to_all x1, waiting for transfers between devices: 0.01 us -> 7.05 us  [shards(): partials = lax.all_to_all(gram, 'cell', 0, 0, tiled=True)]
    ppermute x14 -> x13, starting transfers between devices: 24 us -> 18 us  [swap(): return lax.ppermute(value, 'cell', [(n, n ^ bits) for n in range(n_cell)])]
    convert_element_type x3 -> x4, other arithmetic: 0.08 us -> 2.04 us  [the longest x2 1.01 us: shards(): (mine + part.astype(jnp.float32)).astype(jnp.bfloat16)]
    pallas_call x1, Pallas kernels: 4.56 us -> 3.28 us  [shards(): call(cell_body, (shape(cell_factor.shape, jnp.float32), shape((kdim, CELL...]
    pallas_call x3, Pallas kernels: 9.26 us -> 8.12 us  [the longest x1 5.76 us: dense_tile(): call(dense_body, (shape((CELL_DEV, GENE_DEV), jnp.bfloat16), shape((GENE_...]
    ppermute x2 -> x3, waiting for transfers between devices: 3.19 us -> 2.19 us  [swap_core(): return lax.ppermute(value, 'gene', [(0, 1), (1, 0)])]
  transfers between devices with their start and end apart: 18 -> 18, of which waited for: 6 -> 9; matrix products, arithmetic and copies ran while one was open for 2% -> 5% of each run, Pallas kernels for 8% -> 7%
where the time goes in v2:
time: 94 us; the launch traced here: 93 us
  waiting for transfers between devices  30.4 us (32%)
  starting transfers between devices  26.1 us (28%)
  local copies, waits for them, and re-layouts  18.2 us (19%)
  Pallas kernels  11.7 us (12%)
  other arithmetic  4.44 us (5%)
  between operations  2.19 us (2%)
    ppermute x13, starting transfers between devices, swap(): return lax.ppermute(value, 'cell', [(n, n ^ bits) for n in range(n_cell)])  18 us
    ppermute x13, waiting for transfers between devices, swap(): return lax.ppermute(value, 'cell', [(n, n ^ bits) for n in range(n_cell)])  17.6 us
    unnamed x34, local copies, waits for them, and re-layouts  17.4 us
    all_to_all x1, waiting for transfers between devices, shards(): partials = lax.all_to_all(gram, 'cell', 0, 0, tiled=True)  7.05 us
    pallas_call x1, Pallas kernels, dense_tile(): call(dense_body, (shape((CELL_DEV, GENE_DEV), jnp.bfloat16), shape((GENE_...  5.76 us
    all_to_all x1, starting transfers between devices, shards(): lax.all_to_all(jnp.broadcast_to(square[None], (n_cell, 8, 128)), 'cell',...  4.07 us
    all_to_all x1, waiting for transfers between devices, shards(): lax.all_to_all(jnp.broadcast_to(square[None], (n_cell, 8, 128)), 'cell',...  3.61 us
    all_to_all x1, starting transfers between devices, shards(): partials = lax.all_to_all(gram, 'cell', 0, 0, tiled=True)  3.38 us
  transfers between devices with their start and end apart: 18, of which 9 were waited for; matrix products, arithmetic and copies ran while one was open for 5% of the time, Pallas kernels for 7%

profile of v2, /device:TPU:0, one launch (start us, length us, event | category | flops | bytes accessed | tf_op | source)
XLA Modules:
  0.0 93.0 jit_solution(3561321505017223759)
XLA Ops:
  1.1 1.0 %convert_element_type.30.refs_0_ = bf16[32,2048]{1,0:T(8,128)(2,1)S(1)} convert(f32[32,2048]{1,0:T(8,128)} %param.11) | non-fusion elementwise | flops 65536 | bytes 393216 | tf_op jit(solution)/shard_map/convert_element_type | solution.py:180
  2.1 3.7 %collective-permute-start = (bf16[32,2048]{1,0:T(8,128)(2,1)S(1)}, bf16[32,2048]{1,0:T(8,128)(2,1)S(1)}, u32[]{:S(2)}, u32[]{:S(2)}) collective-permute-start(bf16[32,2048]{1,0:T(8,128)(2,1)S(1)} %convert_element_type.30.refs_0_), channel_id=1, source_target_pairs={{0,8},{2,10},{4,12},{6,14},{8,0},{10,2},{12,4},{14,6},{1,9},{3,11}... | collective-permute-start | bytes 393224 | tf_op jit(solution)/shard_map/ppermute | solution.py:172
  6.4 1.6 %copy-done.4 = bf16[1,1,64,128,128]{4,3,2,1,0:T(8,128)(2,1)S(1)} copy-done((bf16[1,1,64,128,128]{4,3,2,1,0:T(8,128)(2,1)S(1)}, bf16[1,1,64,128,128]{4,3,2,1,0:T(8,128)(2,1)}, u32[]{:S(2)}) %copy-start.4) | copy-done | bytes 2097176
  9.3 5.8 %shard_map.77 = (bf16[1024,2048]{1,0:T(8,128)(2,1)S(1)}, bf16[2048,1024]{1,0:T(8,128)(2,1)S(1)}) custom-call(s32[64]{0:T(128)S(1)} %bitcast.18, s32[64]{0:T(128)S(1)} %bitcast.19, s32[1]{0:T(128)} %bitcast.15.count, bf16[64,128,128]{2,1,0:T(8,128)(2,1)S(1)} %bitcast.16), custom_call_target="tpu_custom_call" | custom-call | tf_op jit(solution)/shard_map/pallas_call | solution.py:65
  15.1 2.0 %copy-done.2 = bf16[1024,2048]{1,0:T(8,128)(2,1)} copy-done((bf16[1024,2048]{1,0:T(8,128)(2,1)}, bf16[1024,2048]{1,0:T(8,128)(2,1)S(1)}, u32[]{:S(2)}) %copy-start.2) | copy-done | bytes 4194328
  17.4 1.8 %collective-permute-start.4 = (bf16[32,2048]{1,0:T(8,128)(2,1)S(1)}, bf16[32,2048]{1,0:T(8,128)(2,1)S(1)}, u32[]{:S(2)}, u32[]{:S(2)}) collective-permute-start(bf16[32,2048]{1,0:T(8,128)(2,1)S(1)} %convert_element_type.30.refs_0_), channel_id=1, source_target_pairs={{0,4},{2,6},{4,0},{6,2},{8,12},{10,14},{12,8},{14,10},{1,5},{3,7},... | collective-permute-start | bytes 393224 | tf_op jit(solution)/shard_map/ppermute | solution.py:172
  19.4 4.1 %collective-permute-done.2.refs_2_ = bf16[32,2048]{1,0:T(8,128)(2,1)S(1)} collective-permute-done((bf16[32,2048]{1,0:T(8,128)(2,1)S(1)}, bf16[32,2048]{1,0:T(8,128)(2,1)S(1)}, u32[]{:S(2)}, u32[]{:S(2)}) %collective-permute-start.2) | collective-permute-done | bytes 131104 | tf_op jit(solution)/shard_map/ppermute | solution.py:172
  23.5 1.8 %collective-permute-done.4.refs_2_ = bf16[32,2048]{1,0:T(8,128)(2,1)S(1)} collective-permute-done((bf16[32,2048]{1,0:T(8,128)(2,1)S(1)}, bf16[32,2048]{1,0:T(8,128)(2,1)S(1)}, u32[]{:S(2)}, u32[]{:S(2)}) %collective-permute-start.4) | collective-permute-done | bytes 131104 | tf_op jit(solution)/shard_map/ppermute | solution.py:172
  26.1 2.0 %copy-done = bf16[2048,1024]{1,0:T(8,128)(2,1)} copy-done((bf16[2048,1024]{1,0:T(8,128)(2,1)}, bf16[2048,1024]{1,0:T(8,128)(2,1)S(1)}, u32[]{:S(2)}) %copy-start) | copy-done | bytes 4194328
  29.0 1.2 %collective-permute-start.6 = (bf16[32,2048]{1,0:T(8,128)(2,1)S(1)}, bf16[32,2048]{1,0:T(8,128)(2,1)S(1)}, u32[]{:S(2)}, u32[]{:S(2)}) collective-permute-start(bf16[32,2048]{1,0:T(8,128)(2,1)S(1)} %collective-permute-done.4.refs_2_), channel_id=1, source_target_pairs={{0,2},{2,0},{4,6},{6,4},{8,10},{10,8},{12,14},{14,12},{1,3},{3,1},... | collective-permute-start | bytes 393224 | tf_op jit(solution)/shard_map/ppermute | solution.py:172
  31.0 1.2 %collective-permute-start.8 = (bf16[32,2048]{1,0:T(8,128)(2,1)S(1)}, bf16[32,2048]{1,0:T(8,128)(2,1)S(1)}, u32[]{:S(2)}, u32[]{:S(2)}) collective-permute-start(bf16[32,2048]{1,0:T(8,128)(2,1)S(1)} %collective-permute-done.2.refs_2_), channel_id=1, source_target_pairs={{0,2},{2,0},{4,6},{6,4},{8,10},{10,8},{12,14},{14,12},{1,3},{3,1},... | collective-permute-start | bytes 393224 | tf_op jit(solution)/shard_map/ppermute | solution.py:172
  32.3 3.0 %collective-permute-done.6.refs_0_ = bf16[32,2048]{1,0:T(8,128)(2,1)S(1)} collective-permute-done((bf16[32,2048]{1,0:T(8,128)(2,1)S(1)}, bf16[32,2048]{1,0:T(8,128)(2,1)S(1)}, u32[]{:S(2)}, u32[]{:S(2)}) %collective-permute-start.6) | collective-permute-done | bytes 131104 | tf_op jit(solution)/shard_map/ppermute | solution.py:172
  35.3 2.8 %collective-permute-done.7.refs_1_ = bf16[32,2048]{1,0:T(8,128)(2,1)S(1)} collective-permute-done((bf16[32,2048]{1,0:T(8,128)(2,1)S(1)}, bf16[32,2048]{1,0:T(8,128)(2,1)S(1)}, u32[]{:S(2)}, u32[]{:S(2)}) %collective-permute-start.7) | collective-permute-done | bytes 131104 | tf_op jit(solution)/shard_map/ppermute | solution.py:172
  38.1 2.4 %collective-permute-done.8.refs_3_ = bf16[32,2048]{1,0:T(8,128)(2,1)S(1)} collective-permute-done((bf16[32,2048]{1,0:T(8,128)(2,1)S(1)}, bf16[32,2048]{1,0:T(8,128)(2,1)S(1)}, u32[]{:S(2)}, u32[]{:S(2)}) %collective-permute-start.8) | collective-permute-done | bytes 131104 | tf_op jit(solution)/shard_map/ppermute | solution.py:172
  41.3 2.2 %copy-done.1 = bf16[2048,1024]{1,0:T(8,128)(2,1)S(1)} copy-done((bf16[2048,1024]{1,0:T(8,128)(2,1)S(1)}, bf16[2048,1024]{1,0:T(8,128)(2,1)}, u32[]{:S(2)}) %copy-start.1) | copy-done | bytes 4194328
  43.5 1.6 %shard_map.79 = (bf16[256,2048]{1,0:T(8,128)(2,1)S(1)}, f32[128,1536]{1,0:T(8,128)S(1)}) custom-call(s32[8]{0:T(128)S(1)} %stack.50.owners, bf16[2048,1024]{1,0:T(8,128)(2,1)S(1)} %copy-done.1, bf16[128,2048]{1,0:T(8,128)(2,1)S(1)} %get-tuple-element.41.first, bf16[32,2048]{1,0:T(8,128)(2,1)S(1)} %collective-permute-done.6.refs_0_, ...), custom_call_target="tpu_custom_call" | custom-call | flops 805306368 | bytes 8388608 | tf_op jit(solution)/shard_map/pallas_call | solution.py:223
  45.3 2.2 %collective-permute-done.9.other = f32[128,1536]{1,0:T(8,128)S(1)} collective-permute-done((f32[128,1536]{1,0:T(8,128)S(1)}, f32[128,1536]{1,0:T(8,128)S(1)}, u32[]{:S(2)}, u32[]{:S(2)}) %collective-permute-start.9) | collective-permute-done | bytes 786464 | tf_op jit(solution)/shard_map/ppermute | solution.py:175
  47.5 2.2 %copy-done.3 = bf16[1024,2048]{1,0:T(8,128)(2,1)S(1)} copy-done((bf16[1024,2048]{1,0:T(8,128)(2,1)S(1)}, bf16[1024,2048]{1,0:T(8,128)(2,1)}, u32[]{:S(2)}) %copy-start.3) | copy-done | bytes 4194328
  49.6 1.0 %copy-done.7 = f32[128,1024]{1,0:T(8,128)S(1)} copy-done((f32[128,1024]{1,0:T(8,128)S(1)}, f32[128,1024]{1,0:T(8,128)}, u32[]{:S(2)}) %copy-start.7) | copy-done | bytes 524312
  50.7 1.0 %copy-done.9 = f32[128,1024]{1,0:T(8,128)S(1)} copy-done((f32[128,1024]{1,0:T(8,128)S(1)}, f32[128,1024]{1,0:T(8,128)}, u32[]{:S(2)}) %copy-start.9) | copy-done | bytes 524312
  51.7 1.0 %copy-done.11 = f32[128,1024]{1,0:T(8,128)S(1)} copy-done((f32[128,1024]{1,0:T(8,128)S(1)}, f32[128,1024]{1,0:T(8,128)}, u32[]{:S(2)}) %copy-start.11) | copy-done | bytes 524312
  52.8 3.3 %shard_map.80 = (f32[128,1024]{1,0:T(8,128)}, bf16[256,1024]{1,0:T(8,128)(2,1)}, bf16[256,256]{1,0:T(8,128)(2,1)}, bf16[32,2048]{1,0:T(8,128)(2,1)S(1)}, bf16[32...) custom-call(s32[1]{0:T(128)} %bitcast.at, ...), custom_call_target="tpu_custom_call" | custom-call | flops 1476395008 | bytes 14680064 | tf_op jit(solution)/shard_map/pallas_call | solution.py:241
  57.4 1.2 %collective-permute-start.10 = (bf16[32,2048]{1,0:T(8,128)(2,1)S(1)}, bf16[32,2048]{1,0:T(8,128)(2,1)S(1)}, u32[]{:S(2)}, u32[]{:S(2)}) collective-permute-start(bf16[32,2048]{1,0:T(8,128)(2,1)S(1)} %get-tuple-element.50), channel_id=1, source_target_pairs={{0,2},{2,0},{4,6},{6,4},{8,10},{10,8},{12,14},{14,12},{1,3},{3,1},... | collective-permute-start | bytes 393224 | tf_op jit(solution)/shard_map/ppermute | solution.py:172
  60.3 3.5 %collective-permute-done.10 = bf16[32,2048]{1,0:T(8,128)(2,1)S(1)} collective-permute-done((bf16[32,2048]{1,0:T(8,128)(2,1)S(1)}, bf16[32,2048]{1,0:T(8,128)(2,1)S(1)}, u32[]{:S(2)}, u32[]{:S(2)}) %collective-permute-start.10) | collective-permute-done | bytes 131104 | tf_op jit(solution)/shard_map/ppermute | solution.py:172
  63.8 3.4 %all-to-all-start = ((bf16[8,32,256]{2,1,0:T(8,128)(2,1)}), bf16[8,32,256]{2,1,0:T(8,128)(2,1)S(1)}, u32[]{:S(2)}, u32[]{:S(2)}) async-start(bf16[8,32,256]{2,1,0:T(8,128)(2,1)} %bitcast.13), calls=%async_computation | async-start | bytes 262144 | tf_op jit(solution)/shard_map/all_to_all | solution.py:281
  67.2 3.8 %collective-permute-start.12 = (bf16[32,2048]{1,0:T(8,128)(2,1)S(1)}, bf16[32,2048]{1,0:T(8,128)(2,1)S(1)}, u32[]{:S(2)}, u32[]{:S(2)}) collective-permute-start(bf16[32,2048]{1,0:T(8,128)(2,1)S(1)} %add_convert_fusion.1), channel_id=1, source_target_pairs={{0,12},{2,14},{4,8},{6,10},{8,4},{10,6},{12,0},{14,2},{1,13},{3,15... | collective-permute-start | bytes 393224 | tf_op jit(solution)/shard_map/ppermute | solution.py:172
  71.0 1.0 %add_convert_fusion = bf16[32,2048]{1,0:T(8,128)(2,1)S(1)} fusion(f32[32,2048]{1,0:T(8,128)} %copy-done.13, bf16[32,2048]{1,0:T(8,128)(2,1)S(1)} %collective-permute-done.13), kind=kLoop, calls=%fused_computation.10 | loop fusion | flops 196608 | bytes 524288 | tf_op jit(solution)/shard_map/convert_element_type | solution.py:278
  72.1 7.1 %all-to-all-done = bf16[8,32,256]{2,1,0:T(8,128)(2,1)S(1)} async-done(((bf16[8,32,256]{2,1,0:T(8,128)(2,1)}), bf16[8,32,256]{2,1,0:T(8,128)(2,1)S(1)}, u32[]{:S(2)}, u32[]{:S(2)}) %all-to-all-start) | async-done | bytes 131104 | tf_op jit(solution)/shard_map/all_to_all | solution.py:281
  80.1 4.1 %all-to-all-start.1 = ((f32[8,8,128]{2,1,0:T(8,128)}), f32[8,8,128]{2,1,0:T(8,128)S(1)}, u32[]{:S(2)}, u32[]{:S(2)}) async-start(f32[8,8,128]{2,1,0:T(8,128)} %broadcast_in_dim.2), calls=%async_computation.1 | async-start | bytes 65536 | tf_op jit(solution)/shard_map/all_to_all | solution.py:290
  84.1 1.0 %fusion = bf16[32,2048]{1,0:T(8,128)(2,1)S(1)} fusion(f32[32,2048]{1,0:T(8,128)} %copy-done.12, f32[64,2048]{1,0:T(8,128)S(1)} %convert_element_type.33), kind=kLoop, calls=%fused_computation.1 | loop fusion | flops 131072 | bytes 655360 | tf_op jit(solution)/shard_map/convert_element_type | solution.py:279
  85.1 2.1 %collective-permute-start.15 = (bf16[32,2048]{1,0:T(8,128)(2,1)S(1)}, bf16[32,2048]{1,0:T(8,128)(2,1)S(1)}, u32[]{:S(2)}, u32[]{:S(2)}) collective-permute-start(bf16[32,2048]{1,0:T(8,128)(2,1)S(1)} %fusion), channel_id=1, source_target_pairs={{0,2},{2,0},{4,6},{6,4},{8,10},{10,8},{12,14},{14,12},{1,3},{3,1},... | collective-permute-start | bytes 393224 | tf_op jit(solution)/shard_map/ppermute | solution.py:172
  87.2 3.6 %all-to-all-done.1 = f32[8,8,128]{2,1,0:T(8,128)S(1)} async-done(((f32[8,8,128]{2,1,0:T(8,128)}), f32[8,8,128]{2,1,0:T(8,128)S(1)}, u32[]{:S(2)}, u32[]{:S(2)}) %all-to-all-start.1) | async-done | bytes 32800 | tf_op jit(solution)/shard_map/all_to_all | solution.py:290
  (53 shorter events, 11.4 us)
Async XLA Ops:
  0.6 16.5 %collective-permute-start.1 = (f32[128,1024]{1,0:T(8,128)}, f32[128,1024]{1,0:T(8,128)S(1)}, u32[]{:S(2)}, u32[]{:S(2)}) collective-permute-start(f32[128,1024]{1,0:T(8,128)} %factor_mine.1), channel_id=1, source_target_pairs={{0,1},{1,0},{2,3},{3,2},{4,5},{5,4},{6,7},{7,6},{8,9},{9,8},{10,11... | collective-permute-start | bytes 1572872 | tf_op jit(solution)/shard_map/ppermute | solution.py:175
  2.1 15.0 %collective-permute-start = (bf16[32,2048]{1,0:T(8,128)(2,1)S(1)}, bf16[32,2048]{1,0:T(8,128)(2,1)S(1)}, u32[]{:S(2)}, u32[]{:S(2)}) collective-permute-start(bf16[32,2048]{1,0:T(8,128)(2,1)S(1)} %convert_element_type.30.refs_0_), channel_id=1, source_target_pairs={{0,8},{2,10},{4,12},{6,14},{8,0},{10,2},{12,4},{14,6},{1,9},{3,11}... | collective-permute-start | bytes 393224 | tf_op jit(solution)/shard_map/ppermute | solution.py:172
  6.4 1.6 %copy-start.4 = (bf16[1,1,64,128,128]{4,3,2,1,0:T(8,128)(2,1)S(1)}, bf16[1,1,64,128,128]{4,3,2,1,0:T(8,128)(2,1)}, u32[]{:S(2)}) copy-start(bf16[1,1,64,128,128]{4,3,2,1,0:T(8,128)(2,1)} %param.6) | copy-start | bytes 6291460
  15.1 2.0 %copy-start.2 = (bf16[1024,2048]{1,0:T(8,128)(2,1)}, bf16[1024,2048]{1,0:T(8,128)(2,1)S(1)}, u32[]{:S(2)}) copy-start(bf16[1024,2048]{1,0:T(8,128)(2,1)S(1)} %get-tuple-element.34.tile) | copy-start | bytes 12582916
  17.1 9.0 %copy-start.6 = (f32[128,1024]{1,0:T(8,128)}, f32[128,1024]{1,0:T(8,128)S(1)}, u32[]{:S(2)}) copy-start(f32[128,1024]{1,0:T(8,128)S(1)} %collective-permute-done.1.factor_other) | copy-start | bytes 1572868
  17.1 30.4 %copy-start.5 = (f32[128,1024]{1,0:T(8,128)S(1)}, f32[128,1024]{1,0:T(8,128)}, u32[]{:S(2)}) copy-start(f32[128,1024]{1,0:T(8,128)} %factor_mine.1) | copy-start | bytes 1572868
  17.1 6.4 %collective-permute-start.2 = (bf16[32,2048]{1,0:T(8,128)(2,1)S(1)}, bf16[32,2048]{1,0:T(8,128)(2,1)S(1)}, u32[]{:S(2)}, u32[]{:S(2)}) collective-permute-start(bf16[32,2048]{1,0:T(8,128)(2,1)S(1)} %collective-permute-done.refs_3_), channel_id=1, source_target_pairs={{0,4},{2,6},{4,0},{6,2},{8,12},{10,14},{12,8},{14,10},{1,5},{3,7},... | collective-permute-start | bytes 393224 | tf_op jit(solution)/shard_map/ppermute | solution.py:172
  17.4 7.9 %collective-permute-start.4 = (bf16[32,2048]{1,0:T(8,128)(2,1)S(1)}, bf16[32,2048]{1,0:T(8,128)(2,1)S(1)}, u32[]{:S(2)}, u32[]{:S(2)}) collective-permute-start(bf16[32,2048]{1,0:T(8,128)(2,1)S(1)} %convert_element_type.30.refs_0_), channel_id=1, source_target_pairs={{0,4},{2,6},{4,0},{6,2},{8,12},{10,14},{12,8},{14,10},{1,5},{3,7},... | collective-permute-start | bytes 393224 | tf_op jit(solution)/shard_map/ppermute | solution.py:172
  19.2 6.2 %collective-permute-start.3 = (bf16[32,2048]{1,0:T(8,128)(2,1)S(1)}, bf16[32,2048]{1,0:T(8,128)(2,1)S(1)}, u32[]{:S(2)}, u32[]{:S(2)}) collective-permute-start(bf16[32,2048]{1,0:T(8,128)(2,1)S(1)} %convert_element_type.30.refs_0_), channel_id=1, source_target_pairs={{0,2},{2,0},{4,6},{6,4},{8,10},{10,8},{12,14},{14,12},{1,3},{3,1},... | collective-permute-start | bytes 393224 | tf_op jit(solution)/shard_map/ppermute | solution.py:172
  26.1 2.0 %copy-start = (bf16[2048,1024]{1,0:T(8,128)(2,1)}, bf16[2048,1024]{1,0:T(8,128)(2,1)S(1)}, u32[]{:S(2)}) copy-start(bf16[2048,1024]{1,0:T(8,128)(2,1)S(1)} %get-tuple-element.35.turned) | copy-start | bytes 12582916
  28.2 12.3 %collective-permute-start.5 = (f32[128,1024]{1,0:T(8,128)S(1)}, f32[128,1024]{1,0:T(8,128)S(1)}, u32[]{:S(2)}, u32[]{:S(2)}) collective-permute-start(f32[128,1024]{1,0:T(8,128)S(1)} %get-tuple-element.38.mine_first), channel_id=1, source_target_pairs={{0,1},{1,0},{2,3},{3,2},{4,5},{5,4},{6,7},{7,6},{8,9},{9,8},{10,11... | collective-permute-start | bytes 1572872 | tf_op jit(solution)/shard_map/ppermute | solution.py:175
  28.2 0.8 copy-start.8
  29.0 6.3 %collective-permute-start.6 = (bf16[32,2048]{1,0:T(8,128)(2,1)S(1)}, bf16[32,2048]{1,0:T(8,128)(2,1)S(1)}, u32[]{:S(2)}, u32[]{:S(2)}) collective-permute-start(bf16[32,2048]{1,0:T(8,128)(2,1)S(1)} %collective-permute-done.4.refs_2_), channel_id=1, source_target_pairs={{0,2},{2,0},{4,6},{6,4},{8,10},{10,8},{12,14},{14,12},{1,3},{3,1},... | collective-permute-start | bytes 393224 | tf_op jit(solution)/shard_map/ppermute | solution.py:172
  30.2 7.9 %collective-permute-start.7 = (bf16[32,2048]{1,0:T(8,128)(2,1)S(1)}, bf16[32,2048]{1,0:T(8,128)(2,1)S(1)}, u32[]{:S(2)}, u32[]{:S(2)}) collective-permute-start(bf16[32,2048]{1,0:T(8,128)(2,1)S(1)} %collective-permute-done.refs_3_), channel_id=1, source_target_pairs={{0,2},{2,0},{4,6},{6,4},{8,10},{10,8},{12,14},{14,12},{1,3},{3,1},... | collective-permute-start | bytes 393224 | tf_op jit(solution)/shard_map/ppermute | solution.py:172
  31.0 9.5 %collective-permute-start.8 = (bf16[32,2048]{1,0:T(8,128)(2,1)S(1)}, bf16[32,2048]{1,0:T(8,128)(2,1)S(1)}, u32[]{:S(2)}, u32[]{:S(2)}) collective-permute-start(bf16[32,2048]{1,0:T(8,128)(2,1)S(1)} %collective-permute-done.2.refs_2_), channel_id=1, source_target_pairs={{0,2},{2,0},{4,6},{6,4},{8,10},{10,8},{12,14},{14,12},{1,3},{3,1},... | collective-permute-start | bytes 393224 | tf_op jit(solution)/shard_map/ppermute | solution.py:172
  40.5 0.8 copy-start.10
  41.3 2.2 %copy-start.1 = (bf16[2048,1024]{1,0:T(8,128)(2,1)S(1)}, bf16[2048,1024]{1,0:T(8,128)(2,1)}, u32[]{:S(2)}) copy-start(bf16[2048,1024]{1,0:T(8,128)(2,1)} %copy-done) | copy-start | bytes 12582916
  45.1 2.4 %collective-permute-start.9 = (f32[128,1536]{1,0:T(8,128)S(1)}, f32[128,1536]{1,0:T(8,128)S(1)}, u32[]{:S(2)}, u32[]{:S(2)}) collective-permute-start(f32[128,1536]{1,0:T(8,128)S(1)} %get-tuple-element.46.mine), channel_id=1, source_target_pairs={{0,1},{1,0},{2,3},{3,2},{4,5},{5,4},{6,7},{7,6},{8,9},{9,8},{10,11... | collective-permute-start | bytes 2359304 | tf_op jit(solution)/shard_map/ppermute | solution.py:175
  47.5 2.2 %copy-start.3 = (bf16[1024,2048]{1,0:T(8,128)(2,1)S(1)}, bf16[1024,2048]{1,0:T(8,128)(2,1)}, u32[]{:S(2)}) copy-start(bf16[1024,2048]{1,0:T(8,128)(2,1)} %copy-done.2) | copy-start | bytes 12582916
  49.6 1.0 %copy-start.7 = (f32[128,1024]{1,0:T(8,128)S(1)}, f32[128,1024]{1,0:T(8,128)}, u32[]{:S(2)}) copy-start(f32[128,1024]{1,0:T(8,128)} %copy-done.6) | copy-start | bytes 1572868
  50.7 1.0 %copy-start.9 = (f32[128,1024]{1,0:T(8,128)S(1)}, f32[128,1024]{1,0:T(8,128)}, u32[]{:S(2)}) copy-start(f32[128,1024]{1,0:T(8,128)} %copy-done.8) | copy-start | bytes 1572868
  51.7 1.0 %copy-start.11 = (f32[128,1024]{1,0:T(8,128)S(1)}, f32[128,1024]{1,0:T(8,128)}, u32[]{:S(2)}) copy-start(f32[128,1024]{1,0:T(8,128)} %copy-done.10) | copy-start | bytes 1572868
  56.1 0.7 copy-start.12
  57.4 34.7 %copy-start.16 = (f32[32,2048]{1,0:T(8,128)S(1)}, f32[32,2048]{1,0:T(8,128)}, u32[]{:S(2)}) copy-start(f32[32,2048]{1,0:T(8,128)} %param.11) | copy-start | bytes 786436
  57.4 6.3 %collective-permute-start.10 = (bf16[32,2048]{1,0:T(8,128)(2,1)S(1)}, bf16[32,2048]{1,0:T(8,128)(2,1)S(1)}, u32[]{:S(2)}, u32[]{:S(2)}) collective-permute-start(bf16[32,2048]{1,0:T(8,128)(2,1)S(1)} %get-tuple-element.50), channel_id=1, source_target_pairs={{0,2},{2,0},{4,6},{6,4},{8,10},{10,8},{12,14},{14,12},{1,3},{3,1},... | collective-permute-start | bytes 393224 | tf_op jit(solution)/shard_map/ppermute | solution.py:172
  58.6 12.4 %collective-permute-start.13 = (bf16[32,2048]{1,0:T(8,128)(2,1)}, bf16[32,2048]{1,0:T(8,128)(2,1)S(1)}, u32[]{:S(2)}, u32[]{:S(2)}) collective-permute-start(bf16[32,2048]{1,0:T(8,128)(2,1)} %get-tuple-element.60), channel_id=1, source_target_pairs={{0,2},{2,0},{4,6},{6,4},{8,10},{10,8},{12,14},{14,12},{1,3},{3,1},... | collective-permute-start | bytes 393224 | tf_op jit(solution)/shard_map/ppermute | solution.py:172
  59.5 12.6 %collective-permute-start.11 = (bf16[64,2048]{1,0:T(8,128)(2,1)}, bf16[64,2048]{1,0:T(8,128)(2,1)S(1)}, u32[]{:S(2)}, u32[]{:S(2)}) collective-permute-start(bf16[64,2048]{1,0:T(8,128)(2,1)} %get-tuple-element.57), channel_id=1, source_target_pairs={{0,4},{2,6},{4,0},{6,2},{8,12},{10,14},{12,8},{14,10},{1,5},{3,7},... | collective-permute-start | bytes 786440 | tf_op jit(solution)/shard_map/ppermute | solution.py:172
  63.8 15.3 %all-to-all-start = ((bf16[8,32,256]{2,1,0:T(8,128)(2,1)}), bf16[8,32,256]{2,1,0:T(8,128)(2,1)S(1)}, u32[]{:S(2)}, u32[]{:S(2)}) async-start(bf16[8,32,256]{2,1,0:T(8,128)(2,1)} %bitcast.13), calls=%async_computation | async-start | bytes 262144 | tf_op jit(solution)/shard_map/all_to_all | solution.py:281
  67.2 24.9 %collective-permute-start.12 = (bf16[32,2048]{1,0:T(8,128)(2,1)S(1)}, bf16[32,2048]{1,0:T(8,128)(2,1)S(1)}, u32[]{:S(2)}, u32[]{:S(2)}) collective-permute-start(bf16[32,2048]{1,0:T(8,128)(2,1)S(1)} %add_convert_fusion.1), channel_id=1, source_target_pairs={{0,12},{2,14},{4,8},{6,10},{8,4},{10,6},{12,0},{14,2},{1,13},{3,15... | collective-permute-start | bytes 393224 | tf_op jit(solution)/shard_map/ppermute | solution.py:172
  72.0 20.2 %collective-permute-start.14 = (bf16[32,2048]{1,0:T(8,128)(2,1)S(1)}, bf16[32,2048]{1,0:T(8,128)(2,1)S(1)}, u32[]{:S(2)}, u32[]{:S(2)}) collective-permute-start(bf16[32,2048]{1,0:T(8,128)(2,1)S(1)} %add_convert_fusion), channel_id=1, source_target_pairs={{0,8},{2,10},{4,12},{6,14},{8,0},{10,2},{12,4},{14,6},{1,9},{3,11}... | collective-permute-start | bytes 393224 | tf_op jit(solution)/shard_map/ppermute | solution.py:172
  80.1 10.8 %all-to-all-start.1 = ((f32[8,8,128]{2,1,0:T(8,128)}), f32[8,8,128]{2,1,0:T(8,128)S(1)}, u32[]{:S(2)}, u32[]{:S(2)}) async-start(f32[8,8,128]{2,1,0:T(8,128)} %broadcast_in_dim.2), calls=%async_computation.1 | async-start | bytes 65536 | tf_op jit(solution)/shard_map/all_to_all | solution.py:290
  85.1 7.1 %collective-permute-start.15 = (bf16[32,2048]{1,0:T(8,128)(2,1)S(1)}, bf16[32,2048]{1,0:T(8,128)(2,1)S(1)}, u32[]{:S(2)}, u32[]{:S(2)}) collective-permute-start(bf16[32,2048]{1,0:T(8,128)(2,1)S(1)} %fusion), channel_id=1, source_target_pairs={{0,2},{2,0},{4,6},{6,4},{8,10},{10,8},{12,14},{14,12},{1,3},{3,1},... | collective-permute-start | bytes 393224 | tf_op jit(solution)/shard_map/ppermute | solution.py:172
  (3 other events, 2.0 us)

commit v3 on v2

v3 whole, which is shorter than its diff:
```python
import functools

import jax
import jax.numpy as jnp
from jax import lax
from jax.experimental import pallas as pl
from jax.experimental.pallas import tpu as pltpu
from jax.sharding import PartitionSpec as P

BLK = 128
CELL_DEV = 1024
GENE_DEV = 2048
VMEM_BYTES = 24 * 2**20

NT = (((1,), (1,)), ((), ()))
NN = (((1,), (0,)), ((), ()))
SMEM_SPEC = pl.BlockSpec(memory_space=pltpu.SMEM)
VMEM_SPEC = pl.BlockSpec(memory_space=pltpu.VMEM)


def dot(a, b, dims=NN):
    return lax.dot_general(a, b, dims, preferred_element_type=jnp.float32)


def split_dot(a, b):
    high = a.astype(jnp.bfloat16)
    low = (a - high.astype(jnp.float32)).astype(jnp.bfloat16)
    rows = a.shape[0]
    both = dot(jnp.concatenate([high, low], axis=0), b)
    return both[:rows] + both[rows:]


def call(body, outs, n_smem, n_vmem, flops, traffic, scratch=()):
    return pl.pallas_call(
        body,
        out_shape=outs,
        in_specs=[SMEM_SPEC] * n_smem + [VMEM_SPEC] * n_vmem,
        out_specs=jax.tree.map(lambda _: VMEM_SPEC, outs),
        scratch_shapes=list(scratch),
        compiler_params=pltpu.CompilerParams(vmem_limit_bytes=VMEM_BYTES),
        cost_estimate=pl.CostEstimate(flops=flops, bytes_accessed=traffic, transcendentals=0),
    )


def shape(dims, dtype):
    return jax.ShapeDtypeStruct(dims, dtype)


def dense_body(turn, rows, cols, count, values, tile):
    tile[...] = jnp.zeros_like(tile)

    def place(n, carry):
        row = pl.multiple_of(rows[n] * BLK, BLK)
        col = pl.multiple_of(cols[n] * BLK, BLK)
        if turn:
            tile[pl.ds(col, BLK), pl.ds(row, BLK)] = values[n].T
        else:
            tile[pl.ds(row, BLK), pl.ds(col, BLK)] = values[n]
        return carry

    lax.fori_loop(0, count[0], place, 0)


def dense_tile(turn, values, rows, cols, count):
    dims = (GENE_DEV, CELL_DEV) if turn else (CELL_DEV, GENE_DEV)
    body = functools.partial(dense_body, turn)
    return call(body, shape(dims, jnp.bfloat16), 3, 1, 0, 0)(rows, cols, count, values)


def first_body(turned, *refs):
    shares, panel, message = refs[:-2], refs[-2], refs[-1]
    size = shares[0].shape[0]
    for n, part in enumerate(shares):
        panel[n * size : (n + 1) * size] = part[...]
    message[...] = dot(panel[...], turned[...])


def owned(bits, size):
    return pl.ds(pl.multiple_of((lax.axis_index("cell") ^ bits) * size, size), size)


def second_body(order, turned, first, *refs):
    shares, panel, message, chosen = refs[:-3], refs[-3], refs[-2], refs[-1]
    size, half = shares[0].shape[0], first.shape[0]
    for n, part in enumerate(shares):
        chosen[n * size : (n + 1) * size] = part[...]
    if order is None:
        panel[:half] = first[...]
        panel[half:] = chosen[...]
    else:
        for n, bits in enumerate(order):
            source = first if n * size < half else chosen
            panel[owned(bits, size)] = source[n * size % half : n * size % half + size]
    message[:, :CELL_DEV] = dot(chosen[...], turned[...])
    low = panel[...]
    gram = dot(low, low, NT)
    kdim = low.shape[0]
    message[:, CELL_DEV : CELL_DEV + kdim] = gram[:half]
    message[:, CELL_DEV + kdim :] = gram[half:]


def cell_body(
    order, picks, tile, mine_first, other_first, mine, other, factor_mine, factor_other,
    cell_next, low, gram_out, *rest
):
    parts, (factor, data, updated, chosen) = rest[:-4], rest[-4:]
    share = factor_mine.shape[0]
    kdim = factor.shape[0]
    half = mine.shape[0]
    core = lax.axis_index("gene")
    own = pl.ds(pl.multiple_of(core * share, share), share)
    theirs = pl.ds(pl.multiple_of((1 - core) * share, share), share)
    factor[own] = factor_mine[...]
    factor[theirs] = factor_other[...]
    if order is None:
        data[:half] = mine_first[...] + other_first[...]
        data[half:] = mine[:, :CELL_DEV] + other[:, :CELL_DEV]
    else:
        size = kdim // len(order)
        for n, bits in enumerate(order):
            rows = slice(n * size % half, n * size % half + size)
            if n * size < half:
                data[owned(bits, size)] = mine_first[rows] + other_first[rows]
            else:
                data[owned(bits, size)] = mine[rows, :CELL_DEV] + other[rows, :CELL_DEV]
    gram = mine[:, CELL_DEV:] + other[:, CELL_DEV:]
    gram = jnp.concatenate([gram[:, :kdim], gram[:, kdim:]], axis=0)
    norm = jnp.sum(jnp.sum(gram * gram, axis=1, keepdims=True), axis=0, keepdims=True)
    rate = 1.0 / (jnp.sqrt(norm) + 1e-06)
    held = factor[...]
    stepped = split_dot(gram, held.astype(jnp.bfloat16))
    updated[...] = jnp.maximum(held - rate * (stepped - data[...]), 0.0)
    cell_next[...] = updated[own]
    low[...] = updated[...].astype(jnp.bfloat16)
    gram_out[...] = dot(low[own], low[...], NT).astype(gram_out.dtype)
    if not parts:
        return
    for n, bits in enumerate(picks):
        chosen[n * size : (n + 1) * size] = low[owned(bits, size)]
    product = dot(chosen[...], tile[...])
    row = 0
    for out in parts:
        out[...] = product[row : row + out.shape[0]].astype(out.dtype)
        row += out.shape[0]


def gram_body(mine, other, panel, factor, base, rate_out, gram):
    share = mine.shape[0]
    core = lax.axis_index("gene")
    gram[pl.ds(pl.multiple_of(core * share, share), share)] = mine[...]
    gram[pl.ds(pl.multiple_of((1 - core) * share, share), share)] = other[...]
    whole = gram[...]
    norm = jnp.sum(jnp.sum(whole * whole, axis=1, keepdims=True), axis=0, keepdims=True)
    rate = 1.0 / (jnp.sqrt(norm) + 1e-06)
    base[...] = factor[...] - rate * split_dot(gram[owned(0, factor.shape[0])], panel[...])
    rate_out[...] = jnp.broadcast_to(rate, rate_out.shape)


def last_body(rate, base, own, beside, *refs):
    size = own.shape[0]
    total = own[...] + beside[:size].astype(jnp.float32)
    for part in refs[:-1]:
        total = total + part[...].astype(jnp.float32)
    refs[-1][...] = jnp.maximum(base[...] + rate[0:1, 0:1] * total, 0.0)


def gram_of(panel):
    return dot(panel, panel, NT)


def shards(block_values, block_rows, block_cols, block_count, cell_factor, gene_factor):
    n_cell = lax.axis_size("cell")
    kdim = cell_factor.shape[0] * lax.axis_size("gene")
    size = gene_factor.shape[0]
    half = kdim // 2
    paired = size % 16 == 0 and n_cell >= 4 and n_cell & (n_cell - 1) == 0

    def swap(value, bits):
        return lax.ppermute(value, "cell", [(n, n ^ bits) for n in range(n_cell)])

    def swap_core(value):
        return lax.ppermute(value, "gene", [(0, 1), (1, 0)])

    low_share = gene_factor.astype(jnp.bfloat16)
    factor_other = swap_core(cell_factor)
    blocks = (block_values[0, 0], block_rows[0, 0], block_cols[0, 0], block_count[0])
    turned = dense_tile(True, *blocks)
    tile = dense_tile(False, *blocks)
    if paired:
        lines = [1 << bit for bit in range(1, n_cell.bit_length() - 1)][::-1]
        far = {0: low_share}
        for bits in lines + [1]:
            far[bits] = swap(low_share, bits)
        first = sorted(range(n_cell), key=lambda bits: (bits.bit_count(), bits))
        first, second = first[: n_cell // 2], first[n_cell // 2 :]
        far[lines[0]], turned, factor_other = lax.optimization_barrier(
            (far[lines[0]], turned, factor_other)
        )
        for at, bits in enumerate(lines):
            for held in sorted(far):
                if held and held not in (1, bits) and held ^ bits not in far and held % (2 * bits) == 0:
                    far[held ^ bits] = swap(far[held], bits)
        for bits in range(2, n_cell, 2):
            far[bits ^ 1] = swap(far[bits], 1)
        order = first + second
        first_shares = [far[bits] for bits in first]
        second_shares = [far[bits] for bits in second]
    else:
        whole = lax.all_gather(low_share, "cell", axis=0, tiled=True)
        order = None
        first_shares, second_shares = [whole[:half]], [whole[half:]]

    panel_first, message_first = call(
        first_body,
        (shape((half, GENE_DEV), jnp.bfloat16), shape((half, CELL_DEV), jnp.float32)),
        0,
        1 + len(first_shares),
        0,
        0,
    )(turned, *first_shares)
    other_first = swap_core(message_first)
    if paired:
        other_first, tile, *second_shares = lax.optimization_barrier(
            (other_first, tile, *second_shares)
        )
    panel, message = call(
        functools.partial(second_body, order),
        (
            shape((kdim, GENE_DEV), jnp.bfloat16),
            shape((half, CELL_DEV + 2 * kdim), jnp.float32),
        ),
        0,
        2 + len(second_shares),
        2 * half * GENE_DEV * (CELL_DEV + 2 * kdim),
        8 * 2**20,
        [pltpu.VMEM((half, GENE_DEV), jnp.bfloat16)],
    )(turned, panel_first, *second_shares)
    other = swap_core(message)

    through = list(range(n_cell - 2, 2, -2)) if paired else []
    picks = [bits ^ 1 for bits in through] + [2, 3] + through + [1, 0]
    rows = [size] * len(through) + [2 * size] if paired else []
    keeps = [size] * (len(through) + 2) if paired else []
    cell_next, next_low, gram, *parts = call(
        functools.partial(cell_body, order, picks),
        (
            shape(cell_factor.shape, jnp.float32),
            shape((kdim, CELL_DEV), jnp.bfloat16),
            shape((half, kdim), jnp.bfloat16),
            *[shape((count, GENE_DEV), jnp.bfloat16) for count in rows],
            *[shape((count, GENE_DEV), jnp.float32) for count in keeps],
        ),
        0,
        7,
        2 * kdim * CELL_DEV * 3 * kdim + 2 * kdim * CELL_DEV * GENE_DEV,
        14 * 2**20,
        [
            pltpu.VMEM((kdim, CELL_DEV), jnp.float32),
            pltpu.VMEM((kdim, CELL_DEV), jnp.float32),
            pltpu.VMEM((kdim, CELL_DEV), jnp.float32),
            pltpu.VMEM((kdim, CELL_DEV), jnp.bfloat16),
        ],
    )(tile, message_first, other_first, message, other, cell_factor, factor_other)

    if not paired:
        cell_gram = lax.psum(gram_of(next_low), "cell")
        own_cols = lax.psum_scatter(dot(next_low, tile), "cell", scatter_dimension=0, tiled=True)
        gram_part = lax.dynamic_slice_in_dim(cell_gram, lax.axis_index("cell") * size, size, 0)
        rate_gene = 1.0 / (jnp.sqrt(jnp.sum(cell_gram * cell_gram)) + 1e-06)
        stepped = jnp.dot(
            gram_part, panel.astype(jnp.float32), precision=lax.Precision.HIGHEST
        )
        return (cell_next, jnp.maximum(gene_factor - rate_gene * (stepped - own_cols), 0.0))

    sends, keeps = parts[: len(rows)], parts[len(rows) :]
    arrived = [swap(part, 1) for part in sends[:-1]]
    beside = swap(sends[-1], 2)
    moved = [(mine + part.astype(jnp.float32)).astype(jnp.bfloat16) for mine, part in zip(keeps, arrived)]
    near = (keeps[-2] + beside[size:].astype(jnp.float32)).astype(jnp.bfloat16)
    for bits in [1] + lines[::-1]:
        gram = gram.astype(jnp.bfloat16)
        partner = swap(gram, bits)
        if bits == 1:
            partner, moved[0] = lax.optimization_barrier((partner, moved[0]))
        gram = gram.astype(jnp.float32) + partner.astype(jnp.float32)
    base, rate = call(
        gram_body,
        (shape((size, GENE_DEV), jnp.float32), shape((8, 128), jnp.float32)),
        0,
        4,
        0,
        0,
        [pltpu.VMEM((kdim, kdim), jnp.float32)],
    )(gram, swap_core(gram), panel, gene_factor)
    sums = [swap(part, bits) for part, bits in zip(moved + [near], through + [1])]
    gene_next = call(
        last_body, shape((size, GENE_DEV), jnp.float32), 0, 4 + len(sums), 0, 0
    )(rate, base, keeps[-1], beside, *sums)
    return (cell_next, gene_next)


def solution(mesh):
    return jax.shard_map(
        shards,
        mesh=mesh,
        in_specs=(
            P(("groups", "cell"), "gene", None, None, None),
            P(("groups", "cell"), "gene", None),
            P(("groups", "cell"), "gene", None),
            P(("groups", "cell"), "gene"),
            P(("groups", "gene"), "cell"),
            P(("groups", "cell"), "gene"),
        ),
        out_specs=(P(("groups", "gene"), "cell"), P(("groups", "cell"), "gene")),
        check_vma=False,
    )
```

time: 94 us -> 67.9 us (0.72)
  local copies, waits for them, and re-layouts: 18.2 us -> 2.91 us
  starting transfers between devices: 26.1 us -> 18 us
  other arithmetic: 4.44 us -> 1.11 us
  waiting for transfers between devices: 30.4 us -> 31.6 us
    unnamed x34 -> x10, local copies, waits for them, and re-layouts: 17.4 us -> 2.91 us
    ppermute x13 -> x16, waiting for transfers between devices: 17.6 us -> 29.3 us  [swap(): return lax.ppermute(value, 'cell', [(n, n ^ bits) for n in range(n_cell)])]
    all_to_all x2 -> x0, waiting for transfers between devices: 10.7 us -> none  [the longest x1 7.05 us: shards(): partials = lax.all_to_all(gram, 'cell', 0, 0, tiled=True)]
    all_to_all x2 -> x0, starting transfers between devices: 7.45 us -> none  [the longest x1 4.07 us: shards(): lax.all_to_all(jnp.broadcast_to(square[None], (n_cell, 8, 128)), 'cell',...]
    convert_element_type x2 -> x3, other arithmetic: 1.02 us -> 0.07 us  [the longest x2 0.04 us: shards(): gram = gram.astype(jnp.bfloat16)]
    convert_element_type x2, other arithmetic: 1.01 us -> 0.06 us  [shards(): (mine + part.astype(jnp.float32)).astype(jnp.bfloat16)]
    pallas_call x3 -> x5, Pallas kernels: 10.7 us -> 11.5 us  [the longest x2 6.81 us: dense_tile(): call(body, shape(dims, jnp.bfloat16), 3, 1, 0, 0)(rows, cols, count, values)]
    ppermute x13 -> x16, starting transfers between devices: 18 us -> 17.2 us  [swap(): return lax.ppermute(value, 'cell', [(n, n ^ bits) for n in range(n_cell)])]
  transfers between devices with their start and end apart: 18 -> 20, of which waited for: 9 -> 10; matrix products, arithmetic and copies ran while one was open for 5% -> 2% of each run, Pallas kernels for 7% -> 11%
where the time goes in v3:
time: 67.9 us; the launch traced here: 67.7 us
  waiting for transfers between devices  31.6 us (47%)
  starting transfers between devices  18 us (27%)
  Pallas kernels  12.6 us (19%)
  local copies, waits for them, and re-layouts  2.91 us (4%)
  between operations  1.49 us (2%)
  other arithmetic  1.11 us (2%)
    ppermute x16, waiting for transfers between devices, swap(): return lax.ppermute(value, 'cell', [(n, n ^ bits) for n in range(n_cell)])  29.3 us
    ppermute x16, starting transfers between devices, swap(): return lax.ppermute(value, 'cell', [(n, n ^ bits) for n in range(n_cell)])  17.2 us
    pallas_call x2, Pallas kernels, dense_tile(): call(body, shape(dims, jnp.bfloat16), 3, 1, 0, 0)(rows, cols, count, values)  6.81 us
    unnamed x10, local copies, waits for them, and re-layouts  2.91 us
    pallas_call x1, Pallas kernels, shards(): call(functools.partial(cell_body, order, picks), (shape(cell_factor.shape...  2.78 us
    ppermute x4, waiting for transfers between devices, swap_core(): return lax.ppermute(value, 'gene', [(0, 1), (1, 0)])  2.28 us
  transfers between devices with their start and end apart: 20, of which 10 were waited for; matrix products, arithmetic and copies ran while one was open for 2% of the time, Pallas kernels for 11%

profile of v3, /device:TPU:0, one launch (start us, length us, event | category | flops | bytes accessed | tf_op | source)
XLA Modules:
  0.0 67.7 jit_solution(5136990088288806727)
XLA Ops:
  0.6 0.5 collective-permute-start.1
  1.1 1.0 %convert_element_type.45.refs_0_ = bf16[32,2048]{1,0:T(8,128)(2,1)S(1)} convert(f32[32,2048]{1,0:T(8,128)} %factor.1) | non-fusion elementwise | flops 65536 | bytes 393216 | tf_op jit(solution)/shard_map/convert_element_type | solution.py:184
  2.1 3.7 %collective-permute-start = (bf16[32,2048]{1,0:T(8,128)(2,1)S(1)}, bf16[32,2048]{1,0:T(8,128)(2,1)S(1)}, u32[]{:S(2)}, u32[]{:S(2)}) collective-permute-start(bf16[32,2048]{1,0:T(8,128)(2,1)S(1)} %convert_element_type.45.refs_0_), channel_id=1, source_target_pairs={{0,8},{2,10},{4,12},{6,14},{8,0},{10,2},{12,4},{14,6},{1,9},{3,11}... | collective-permute-start | bytes 393224 | tf_op jit(solution)/shard_map/ppermute | solution.py:179
  5.8 1.6 %collective-permute-start.3 = (bf16[32,2048]{1,0:T(8,128)(2,1)S(1)}, bf16[32,2048]{1,0:T(8,128)(2,1)S(1)}, u32[]{:S(2)}, u32[]{:S(2)}) collective-permute-start(bf16[32,2048]{1,0:T(8,128)(2,1)S(1)} %convert_element_type.45.refs_0_), channel_id=1, source_target_pairs={{0,4},{2,6},{4,0},{6,2},{8,12},{10,14},{12,8},{14,10},{1,5},{3,7},... | collective-permute-start | bytes 393224 | tf_op jit(solution)/shard_map/ppermute | solution.py:179
  7.4 1.5 %collective-permute-start.2 = (bf16[32,2048]{1,0:T(8,128)(2,1)S(1)}, bf16[32,2048]{1,0:T(8,128)(2,1)S(1)}, u32[]{:S(2)}, u32[]{:S(2)}) collective-permute-start(bf16[32,2048]{1,0:T(8,128)(2,1)S(1)} %convert_element_type.45.refs_0_), channel_id=1, source_target_pairs={{0,2},{2,0},{4,6},{6,4},{8,10},{10,8},{12,14},{14,12},{1,3},{3,1},... | collective-permute-start | bytes 393224 | tf_op jit(solution)/shard_map/ppermute | solution.py:179
  9.5 1.6 %copy-done = bf16[1,1,64,128,128]{4,3,2,1,0:T(8,128)(2,1)S(1)} copy-done((bf16[1,1,64,128,128]{4,3,2,1,0:T(8,128)(2,1)S(1)}, bf16[1,1,64,128,128]{4,3,2,1,0:T(8,128)(2,1)}, u32[]{:S(2)}) %copy-start) | copy-done | bytes 2097176
  11.1 0.7 copy-done.3
  11.8 0.7 copy-done.4
  12.4 5.3 %shard_map.77.turned = bf16[2048,1024]{1,0:T(8,128)(2,1)S(1)} custom-call(s32[64]{0:T(128)S(1)} %bitcast.8, s32[64]{0:T(128)S(1)} %bitcast.10, s32[1]{0:T(128)} %bitcast.4.count, bf16[64,128,128]{2,1,0:T(8,128)(2,1)S(1)} %bitcast.6), custom_call_target="tpu_custom_call" | custom-call | tf_op jit(solution)/shard_map/pallas_call | solution.py:67
  17.8 0.7 %shard_map.78 = (bf16[128,2048]{1,0:T(8,128)(2,1)S(1)}, f32[128,1024]{1,0:T(8,128)S(1)}) custom-call(bf16[2048,1024]{1,0:T(8,128)(2,1)S(1)} %shard_map.77.turned, bf16[32,2048]{1,0:T(8,128)(2,1)S(1)} %convert_element_type.45.refs_0_, bf16[32,2048]{1,0:T(8,128)(2,1)S(1)} %collective-permute-done.2.refs_1_, ...), custom_call_target="tpu_custom_call" | custom-call | tf_op jit(solution)/shard_map/pallas_call | solution.py:213
  18.8 2.0 %collective-permute-start.6 = (bf16[32,2048]{1,0:T(8,128)(2,1)S(1)}, bf16[32,2048]{1,0:T(8,128)(2,1)S(1)}, u32[]{:S(2)}, u32[]{:S(2)}) collective-permute-start(bf16[32,2048]{1,0:T(8,128)(2,1)S(1)} %collective-permute-done.refs_3_), channel_id=1, source_target_pairs={{0,2},{2,0},{4,6},{6,4},{8,10},{10,8},{12,14},{14,12},{1,3},{3,1},... | collective-permute-start | bytes 393224 | tf_op jit(solution)/shard_map/ppermute | solution.py:179
  20.8 3.7 %collective-permute-done.7.refs_2_ = bf16[32,2048]{1,0:T(8,128)(2,1)S(1)} collective-permute-done((bf16[32,2048]{1,0:T(8,128)(2,1)S(1)}, bf16[32,2048]{1,0:T(8,128)(2,1)S(1)}, u32[]{:S(2)}, u32[]{:S(2)}) %collective-permute-start.7) | collective-permute-done | bytes 131104 | tf_op jit(solution)/shard_map/ppermute | solution.py:179
  24.5 1.5 %shard_map.79.tile = bf16[1024,2048]{1,0:T(8,128)(2,1)S(1)} custom-call(s32[64]{0:T(128)S(1)} %bitcast.9, s32[64]{0:T(128)S(1)} %bitcast.11, s32[1]{0:T(128)} %bitcast.5.count, bf16[64,128,128]{2,1,0:T(8,128)(2,1)S(1)} %bitcast.7), custom_call_target="tpu_custom_call" | custom-call | tf_op jit(solution)/shard_map/pallas_call | solution.py:67
  26.0 1.8 %collective-permute-done.6.refs_1_ = bf16[32,2048]{1,0:T(8,128)(2,1)S(1)} collective-permute-done((bf16[32,2048]{1,0:T(8,128)(2,1)S(1)}, bf16[32,2048]{1,0:T(8,128)(2,1)S(1)}, u32[]{:S(2)}, u32[]{:S(2)}) %collective-permute-start.6) | collective-permute-done | bytes 131104 | tf_op jit(solution)/shard_map/ppermute | solution.py:179
  27.8 2.3 %collective-permute-done.8.refs_3_ = bf16[32,2048]{1,0:T(8,128)(2,1)S(1)} collective-permute-done((bf16[32,2048]{1,0:T(8,128)(2,1)S(1)}, bf16[32,2048]{1,0:T(8,128)(2,1)S(1)}, u32[]{:S(2)}, u32[]{:S(2)}) %collective-permute-start.8) | collective-permute-done | bytes 131104 | tf_op jit(solution)/shard_map/ppermute | solution.py:179
  30.1 1.1 %shard_map.80 = (bf16[256,2048]{1,0:T(8,128)(2,1)S(1)}, f32[128,1536]{1,0:T(8,128)S(1)}) custom-call(bf16[2048,1024]{1,0:T(8,128)(2,1)S(1)} %shard_map.77.turned, bf16[128,2048]{1,0:T(8,128)(2,1)S(1)} %get-tuple-element.33.first, bf16[32,2048]{1,0:T(8,128)(2,1)S(1)} %collective-permute-done.5.refs_0_, bf16[32,2048]{1,0:T(8,128)(2,1)S(1)} %collective-permute-done.6.refs_1_, ...), custom_call_target="tpu_custom_call" | custom-call | flops 805306368 | bytes 8388608 | tf_op jit(solution)/shard_map/pallas_call | solution.py:226
  31.3 2.3 %collective-permute-done.9.other = f32[128,1536]{1,0:T(8,128)S(1)} collective-permute-done((f32[128,1536]{1,0:T(8,128)S(1)}, f32[128,1536]{1,0:T(8,128)S(1)}, u32[]{:S(2)}, u32[]{:S(2)}) %collective-permute-start.9) | collective-permute-done | bytes 786464 | tf_op jit(solution)/shard_map/ppermute | solution.py:182
  33.6 2.8 %shard_map.81 = (f32[128,1024]{1,0:T(8,128)}, bf16[256,1024]{1,0:T(8,128)(2,1)}, bf16[128,256]{1,0:T(8,128)(2,1)S(1)}, bf16[32,2048]{1,0:T(8,128)(2,1)S(1)}, bf1...) custom-call(bf16[1024,2048]{1,0:T(8,128)(2,1)S(1)} %shard_map.79.til, ...), custom_call_target="tpu_custom_call" | custom-call | flops 1476395008 | bytes 14680064 | tf_op jit(solution)/shard_map/pallas_call | solution.py:244
  36.7 1.7 %collective-permute-start.10 = (bf16[128,256]{1,0:T(8,128)(2,1)S(1)}, bf16[128,256]{1,0:T(8,128)(2,1)S(1)}, u32[]{:S(2)}, u32[]{:S(2)}) collective-permute-start(bf16[128,256]{1,0:T(8,128)(2,1)S(1)} %get-tuple-element.41), channel_id=1, source_target_pairs={{0,2},{2,0},{4,6},{6,4},{8,10},{10,8},{12,14},{14,12},{1,3},{3,1},... | collective-permute-start | bytes 196616 | tf_op jit(solution)/shard_map/ppermute | solution.py:179
  38.4 4.2 %collective-permute-done.11 = bf16[32,2048]{1,0:T(8,128)(2,1)S(1)} collective-permute-done((bf16[32,2048]{1,0:T(8,128)(2,1)S(1)}, bf16[32,2048]{1,0:T(8,128)(2,1)S(1)}, u32[]{:S(2)}, u32[]{:S(2)}) %collective-permute-start.11) | collective-permute-done | bytes 131104 | tf_op jit(solution)/shard_map/ppermute | solution.py:179
  42.7 0.7 collective-permute-done.10
  43.4 1.8 %collective-permute-start.12 = (bf16[128,256]{1,0:T(8,128)(2,1)S(1)}, bf16[128,256]{1,0:T(8,128)(2,1)S(1)}, u32[]{:S(2)}, u32[]{:S(2)}) collective-permute-start(bf16[128,256]{1,0:T(8,128)(2,1)S(1)} %add_convert_fusion.4), channel_id=1, source_target_pairs={{0,4},{2,6},{4,0},{6,2},{8,12},{10,14},{12,8},{14,10},{1,5},{3,7},... | collective-permute-start | bytes 196616 | tf_op jit(solution)/shard_map/ppermute | solution.py:179
  45.2 0.3 collective-permute-start.17
  45.9 2.5 %collective-permute-done.12 = bf16[128,256]{1,0:T(8,128)(2,1)S(1)} collective-permute-done((bf16[128,256]{1,0:T(8,128)(2,1)S(1)}, bf16[128,256]{1,0:T(8,128)(2,1)S(1)}, u32[]{:S(2)}, u32[]{:S(2)}) %collective-permute-start.12) | collective-permute-done | bytes 65568 | tf_op jit(solution)/shard_map/ppermute | solution.py:179
  48.4 0.6 collective-permute-start.13
  49.1 1.1 %collective-permute-done.17 = bf16[32,2048]{1,0:T(8,128)(2,1)S(1)} collective-permute-done((bf16[32,2048]{1,0:T(8,128)(2,1)S(1)}, bf16[32,2048]{1,0:T(8,128)(2,1)S(1)}, u32[]{:S(2)}, u32[]{:S(2)}) %collective-permute-start.17) | collective-permute-done | bytes 131104 | tf_op jit(solution)/shard_map/ppermute | solution.py:179
  50.2 1.3 %collective-permute-start.18 = (bf16[32,2048]{1,0:T(8,128)(2,1)S(1)}, bf16[32,2048]{1,0:T(8,128)(2,1)S(1)}, u32[]{:S(2)}, u32[]{:S(2)}) collective-permute-start(bf16[32,2048]{1,0:T(8,128)(2,1)S(1)} %add_convert_fusion.1), channel_id=1, source_target_pairs={{0,8},{2,10},{4,12},{6,14},{8,0},{10,2},{12,4},{14,6},{1,9},{3,11}... | collective-permute-start | bytes 393224 | tf_op jit(solution)/shard_map/ppermute | solution.py:179
  51.5 9.2 %collective-permute-done.13 = bf16[128,256]{1,0:T(8,128)(2,1)S(1)} collective-permute-done((bf16[128,256]{1,0:T(8,128)(2,1)S(1)}, bf16[128,256]{1,0:T(8,128)(2,1)S(1)}, u32[]{:S(2)}, u32[]{:S(2)}) %collective-permute-start.13) | collective-permute-done | bytes 65568 | tf_op jit(solution)/shard_map/ppermute | solution.py:179
  60.8 1.8 %collective-permute-start.19 = (bf16[32,2048]{1,0:T(8,128)(2,1)S(1)}, bf16[32,2048]{1,0:T(8,128)(2,1)S(1)}, u32[]{:S(2)}, u32[]{:S(2)}) collective-permute-start(bf16[32,2048]{1,0:T(8,128)(2,1)S(1)} %add_convert_fusion), channel_id=1, source_target_pairs={{0,2},{2,0},{4,6},{6,4},{8,10},{10,8},{12,14},{14,12},{1,3},{3,1},... | collective-permute-start | bytes 393224 | tf_op jit(solution)/shard_map/ppermute | solution.py:179
  62.7 0.3 shard_map.82
  63.0 3.8 %collective-permute-done.19.refs_2_ = bf16[32,2048]{1,0:T(8,128)(2,1)S(1)} collective-permute-done((bf16[32,2048]{1,0:T(8,128)(2,1)S(1)}, bf16[32,2048]{1,0:T(8,128)(2,1)S(1)}, u32[]{:S(2)}, u32[]{:S(2)}) %collective-permute-start.19) | collective-permute-done | bytes 131104 | tf_op jit(solution)/shard_map/ppermute | solution.py:179
  66.8 0.8 %shard_map.83 = f32[32,2048]{1,0:T(8,128)} custom-call(f32[8,128]{1,0:T(8,128)S(1)} %get-tuple-element.46.rate, f32[32,2048]{1,0:T(8,128)S(1)} %get-tuple-element.47.base, f32[32,2048]{1,0:T(8,128)S(1)} %get-tuple-element.48.own, bf16[64,2048]{1,0:T(8,128)(2,1)S(1)} %collective-permute-done.15.beside, bf16[32,2048]{1,0:T(8,128)(2,1)S(1)} %collective-permute-done.16.refs_0_, ...), custom_call_target="tpu_custom_call" | custom-call | tf_op jit(solution)/shard_map/pallas_call | solution.py:296
  (32 shorter events, 1.2 us)
Async XLA Ops:
  0.6 17.1 %collective-permute-start.1 = (f32[128,1024]{1,0:T(8,128)}, f32[128,1024]{1,0:T(8,128)S(1)}, u32[]{:S(2)}, u32[]{:S(2)}) collective-permute-start(f32[128,1024]{1,0:T(8,128)} %factor_mine.1), channel_id=1, source_target_pairs={{0,1},{1,0},{2,3},{3,2},{4,5},{5,4},{6,7},{7,6},{8,9},{9,8},{10,11... | collective-permute-start | bytes 1572872 | tf_op jit(solution)/shard_map/ppermute | solution.py:182
  2.1 15.6 %collective-permute-start = (bf16[32,2048]{1,0:T(8,128)(2,1)S(1)}, bf16[32,2048]{1,0:T(8,128)(2,1)S(1)}, u32[]{:S(2)}, u32[]{:S(2)}) collective-permute-start(bf16[32,2048]{1,0:T(8,128)(2,1)S(1)} %convert_element_type.45.refs_0_), channel_id=1, source_target_pairs={{0,8},{2,10},{4,12},{6,14},{8,0},{10,2},{12,4},{14,6},{1,9},{3,11}... | collective-permute-start | bytes 393224 | tf_op jit(solution)/shard_map/ppermute | solution.py:179
  5.8 12.0 %collective-permute-start.3 = (bf16[32,2048]{1,0:T(8,128)(2,1)S(1)}, bf16[32,2048]{1,0:T(8,128)(2,1)S(1)}, u32[]{:S(2)}, u32[]{:S(2)}) collective-permute-start(bf16[32,2048]{1,0:T(8,128)(2,1)S(1)} %convert_element_type.45.refs_0_), channel_id=1, source_target_pairs={{0,4},{2,6},{4,0},{6,2},{8,12},{10,14},{12,8},{14,10},{1,5},{3,7},... | collective-permute-start | bytes 393224 | tf_op jit(solution)/shard_map/ppermute | solution.py:179
  7.4 10.4 %collective-permute-start.2 = (bf16[32,2048]{1,0:T(8,128)(2,1)S(1)}, bf16[32,2048]{1,0:T(8,128)(2,1)S(1)}, u32[]{:S(2)}, u32[]{:S(2)}) collective-permute-start(bf16[32,2048]{1,0:T(8,128)(2,1)S(1)} %convert_element_type.45.refs_0_), channel_id=1, source_target_pairs={{0,2},{2,0},{4,6},{6,4},{8,10},{10,8},{12,14},{14,12},{1,3},{3,1},... | collective-permute-start | bytes 393224 | tf_op jit(solution)/shard_map/ppermute | solution.py:179
  9.5 1.6 %copy-start = (bf16[1,1,64,128,128]{4,3,2,1,0:T(8,128)(2,1)S(1)}, bf16[1,1,64,128,128]{4,3,2,1,0:T(8,128)(2,1)}, u32[]{:S(2)}) copy-start(bf16[1,1,64,128,128]{4,3,2,1,0:T(8,128)(2,1)} %param.6) | copy-start | bytes 6291460
  11.1 0.7 copy-start.3
  11.8 0.7 copy-start.4
  18.5 11.6 %collective-permute-start.4 = (f32[128,1024]{1,0:T(8,128)S(1)}, f32[128,1024]{1,0:T(8,128)S(1)}, u32[]{:S(2)}, u32[]{:S(2)}) collective-permute-start(f32[128,1024]{1,0:T(8,128)S(1)} %get-tuple-element.30.mine_first), channel_id=1, source_target_pairs={{0,1},{1,0},{2,3},{3,2},{4,5},{5,4},{6,7},{7,6},{8,9},{9,8},{10,11... | collective-permute-start | bytes 1572872 | tf_op jit(solution)/shard_map/ppermute | solution.py:182
  18.6 5.9 %collective-permute-start.7 = (bf16[32,2048]{1,0:T(8,128)(2,1)S(1)}, bf16[32,2048]{1,0:T(8,128)(2,1)S(1)}, u32[]{:S(2)}, u32[]{:S(2)}) collective-permute-start(bf16[32,2048]{1,0:T(8,128)(2,1)S(1)} %collective-permute-done.refs_3_), channel_id=1, source_target_pairs={{0,4},{2,6},{4,0},{6,2},{8,12},{10,14},{12,8},{14,10},{1,5},{3,7},... | collective-permute-start | bytes 393224 | tf_op jit(solution)/shard_map/ppermute | solution.py:179
  18.7 7.3 %collective-permute-start.5 = (bf16[32,2048]{1,0:T(8,128)(2,1)S(1)}, bf16[32,2048]{1,0:T(8,128)(2,1)S(1)}, u32[]{:S(2)}, u32[]{:S(2)}) collective-permute-start(bf16[32,2048]{1,0:T(8,128)(2,1)S(1)} %collective-permute-done.3.refs_2_), channel_id=1, source_target_pairs={{0,2},{2,0},{4,6},{6,4},{8,10},{10,8},{12,14},{14,12},{1,3},{3,1},... | collective-permute-start | bytes 393224 | tf_op jit(solution)/shard_map/ppermute | solution.py:179
  18.8 9.0 %collective-permute-start.6 = (bf16[32,2048]{1,0:T(8,128)(2,1)S(1)}, bf16[32,2048]{1,0:T(8,128)(2,1)S(1)}, u32[]{:S(2)}, u32[]{:S(2)}) collective-permute-start(bf16[32,2048]{1,0:T(8,128)(2,1)S(1)} %collective-permute-done.refs_3_), channel_id=1, source_target_pairs={{0,2},{2,0},{4,6},{6,4},{8,10},{10,8},{12,14},{14,12},{1,3},{3,1},... | collective-permute-start | bytes 393224 | tf_op jit(solution)/shard_map/ppermute | solution.py:179
  24.5 5.6 %collective-permute-start.8 = (bf16[32,2048]{1,0:T(8,128)(2,1)S(1)}, bf16[32,2048]{1,0:T(8,128)(2,1)S(1)}, u32[]{:S(2)}, u32[]{:S(2)}) collective-permute-start(bf16[32,2048]{1,0:T(8,128)(2,1)S(1)} %collective-permute-done.7.refs_2_), channel_id=1, source_target_pairs={{0,2},{2,0},{4,6},{6,4},{8,10},{10,8},{12,14},{14,12},{1,3},{3,1},... | collective-permute-start | bytes 393224 | tf_op jit(solution)/shard_map/ppermute | solution.py:179
  26.0 7.6 %copy-start.2 = (f32[128,1024]{1,0:T(8,128)S(1)}, f32[128,1024]{1,0:T(8,128)}, u32[]{:S(2)}) copy-start(f32[128,1024]{1,0:T(8,128)} %factor_mine.1) | copy-start | bytes 1572868
  31.2 31.4 %copy-start.1 = (f32[32,2048]{1,0:T(8,128)S(1)}, f32[32,2048]{1,0:T(8,128)}, u32[]{:S(2)}) copy-start(f32[32,2048]{1,0:T(8,128)} %factor.1) | copy-start | bytes 786436
  31.3 2.4 %collective-permute-start.9 = (f32[128,1536]{1,0:T(8,128)S(1)}, f32[128,1536]{1,0:T(8,128)S(1)}, u32[]{:S(2)}, u32[]{:S(2)}) collective-permute-start(f32[128,1536]{1,0:T(8,128)S(1)} %get-tuple-element.38.mine), channel_id=1, source_target_pairs={{0,1},{1,0},{2,3},{3,2},{4,5},{5,4},{6,7},{7,6},{8,9},{9,8},{10,11... | collective-permute-start | bytes 2359304 | tf_op jit(solution)/shard_map/ppermute | solution.py:182
  36.4 6.3 %collective-permute-start.11 = (bf16[32,2048]{1,0:T(8,128)(2,1)S(1)}, bf16[32,2048]{1,0:T(8,128)(2,1)S(1)}, u32[]{:S(2)}, u32[]{:S(2)}) collective-permute-start(bf16[32,2048]{1,0:T(8,128)(2,1)S(1)} %get-tuple-element.43), channel_id=1, source_target_pairs={{0,2},{2,0},{4,6},{6,4},{8,10},{10,8},{12,14},{14,12},{1,3},{3,1},... | collective-permute-start | bytes 393224 | tf_op jit(solution)/shard_map/ppermute | solution.py:179
  36.7 6.7 %collective-permute-start.10 = (bf16[128,256]{1,0:T(8,128)(2,1)S(1)}, bf16[128,256]{1,0:T(8,128)(2,1)S(1)}, u32[]{:S(2)}, u32[]{:S(2)}) collective-permute-start(bf16[128,256]{1,0:T(8,128)(2,1)S(1)} %get-tuple-element.41), channel_id=1, source_target_pairs={{0,2},{2,0},{4,6},{6,4},{8,10},{10,8},{12,14},{14,12},{1,3},{3,1},... | collective-permute-start | bytes 196616 | tf_op jit(solution)/shard_map/ppermute | solution.py:179
  43.4 5.0 %collective-permute-start.12 = (bf16[128,256]{1,0:T(8,128)(2,1)S(1)}, bf16[128,256]{1,0:T(8,128)(2,1)S(1)}, u32[]{:S(2)}, u32[]{:S(2)}) collective-permute-start(bf16[128,256]{1,0:T(8,128)(2,1)S(1)} %add_convert_fusion.4), channel_id=1, source_target_pairs={{0,4},{2,6},{4,0},{6,2},{8,12},{10,14},{12,8},{14,10},{1,5},{3,7},... | collective-permute-start | bytes 196616 | tf_op jit(solution)/shard_map/ppermute | solution.py:179
  45.2 5.0 %collective-permute-start.17 = (bf16[32,2048]{1,0:T(8,128)(2,1)S(1)}, bf16[32,2048]{1,0:T(8,128)(2,1)S(1)}, u32[]{:S(2)}, u32[]{:S(2)}) collective-permute-start(bf16[32,2048]{1,0:T(8,128)(2,1)S(1)} %get-tuple-element.52), channel_id=1, source_target_pairs={{0,2},{2,0},{4,6},{6,4},{8,10},{10,8},{12,14},{14,12},{1,3},{3,1},... | collective-permute-start | bytes 393224 | tf_op jit(solution)/shard_map/ppermute | solution.py:179
  45.5 15.3 %collective-permute-start.15 = (bf16[64,2048]{1,0:T(8,128)(2,1)S(1)}, bf16[64,2048]{1,0:T(8,128)(2,1)S(1)}, u32[]{:S(2)}, u32[]{:S(2)}) collective-permute-start(bf16[64,2048]{1,0:T(8,128)(2,1)S(1)} %get-tuple-element.49), channel_id=1, source_target_pairs={{0,4},{2,6},{4,0},{6,2},{8,12},{10,14},{12,8},{14,10},{1,5},{3,7},... | collective-permute-start | bytes 786440 | tf_op jit(solution)/shard_map/ppermute | solution.py:179
  45.7 17.3 %collective-permute-start.16 = (bf16[32,2048]{1,0:T(8,128)(2,1)S(1)}, bf16[32,2048]{1,0:T(8,128)(2,1)S(1)}, u32[]{:S(2)}, u32[]{:S(2)}) collective-permute-start(bf16[32,2048]{1,0:T(8,128)(2,1)S(1)} %add_convert_fusion.2), channel_id=1, source_target_pairs={{0,12},{2,14},{4,8},{6,10},{8,4},{10,6},{12,0},{14,2},{1,13},{3,15... | collective-permute-start | bytes 393224 | tf_op jit(solution)/shard_map/ppermute | solution.py:179
  48.4 12.3 %collective-permute-start.13 = (bf16[128,256]{1,0:T(8,128)(2,1)S(1)}, bf16[128,256]{1,0:T(8,128)(2,1)S(1)}, u32[]{:S(2)}, u32[]{:S(2)}) collective-permute-start(bf16[128,256]{1,0:T(8,128)(2,1)S(1)} %add_convert_fusion.3), channel_id=1, source_target_pairs={{0,8},{2,10},{4,12},{6,14},{8,0},{10,2},{12,4},{14,6},{1,9},{3,11}... | collective-permute-start | bytes 196616 | tf_op jit(solution)/shard_map/ppermute | solution.py:179
  50.2 12.8 %collective-permute-start.18 = (bf16[32,2048]{1,0:T(8,128)(2,1)S(1)}, bf16[32,2048]{1,0:T(8,128)(2,1)S(1)}, u32[]{:S(2)}, u32[]{:S(2)}) collective-permute-start(bf16[32,2048]{1,0:T(8,128)(2,1)S(1)} %add_convert_fusion.1), channel_id=1, source_target_pairs={{0,8},{2,10},{4,12},{6,14},{8,0},{10,2},{12,4},{14,6},{1,9},{3,11}... | collective-permute-start | bytes 393224 | tf_op jit(solution)/shard_map/ppermute | solution.py:179
  60.7 2.0 %collective-permute-start.14 = (f32[128,256]{1,0:T(8,128)S(1)}, f32[128,256]{1,0:T(8,128)S(1)}, u32[]{:S(2)}, u32[]{:S(2)}) collective-permute-start(f32[128,256]{1,0:T(8,128)S(1)} %convert_add_fusion.mine), channel_id=1, source_target_pairs={{0,1},{1,0},{2,3},{3,2},{4,5},{5,4},{6,7},{7,6},{8,9},{9,8},{10,11... | collective-permute-start | bytes 393224 | tf_op jit(solution)/shard_map/ppermute | solution.py:182
  60.8 6.0 %collective-permute-start.19 = (bf16[32,2048]{1,0:T(8,128)(2,1)S(1)}, bf16[32,2048]{1,0:T(8,128)(2,1)S(1)}, u32[]{:S(2)}, u32[]{:S(2)}) collective-permute-start(bf16[32,2048]{1,0:T(8,128)(2,1)S(1)} %add_convert_fusion), channel_id=1, source_target_pairs={{0,2},{2,0},{4,6},{6,4},{8,10},{10,8},{12,14},{14,12},{1,3},{3,1},... | collective-permute-start | bytes 393224 | tf_op jit(solution)/shard_map/ppermute | solution.py:179

commit v4 on v3

v4 whole, which is shorter than its diff:
```python
import functools

import jax
import jax.numpy as jnp
from jax import lax
from jax.experimental import pallas as pl
from jax.experimental.pallas import tpu as pltpu
from jax.sharding import PartitionSpec as P

BLK = 128
CELL_DEV = 1024
GENE_DEV = 2048
VMEM_BYTES = 24 * 2**20

NT = (((1,), (1,)), ((), ()))
NN = (((1,), (0,)), ((), ()))
SMEM_SPEC = pl.BlockSpec(memory_space=pltpu.SMEM)
VMEM_SPEC = pl.BlockSpec(memory_space=pltpu.VMEM)


def dot(a, b, dims=NN):
    return lax.dot_general(a, b, dims, preferred_element_type=jnp.float32)


def split_dot(a, b):
    high = a.astype(jnp.bfloat16)
    low = (a - high.astype(jnp.float32)).astype(jnp.bfloat16)
    rows = a.shape[0]
    both = dot(jnp.concatenate([high, low], axis=0), b)
    return both[:rows] + both[rows:]


def call(body, outs, n_smem, n_vmem, flops, traffic, scratch=()):
    return pl.pallas_call(
        body,
        out_shape=outs,
        in_specs=[SMEM_SPEC] * n_smem + [VMEM_SPEC] * n_vmem,
        out_specs=jax.tree.map(lambda _: VMEM_SPEC, outs),
        scratch_shapes=list(scratch),
        compiler_params=pltpu.CompilerParams(vmem_limit_bytes=VMEM_BYTES),
        cost_estimate=pl.CostEstimate(flops=flops, bytes_accessed=traffic, transcendentals=0),
    )


def shape(dims, dtype):
    return jax.ShapeDtypeStruct(dims, dtype)


def dense_body(rows_in, cols_in, count, values, tile, rows, cols, sems, index_sems):
    copies = [
        pltpu.make_async_copy(rows_in, rows, index_sems.at[0]),
        pltpu.make_async_copy(cols_in, cols, index_sems.at[1]),
    ]
    for copy in copies:
        copy.start()
    tile[...] = jnp.zeros_like(tile)
    for copy in copies:
        copy.wait()

    def block(n):
        row = pl.multiple_of(rows[n] * BLK, BLK)
        col = pl.multiple_of(cols[n] * BLK, BLK)
        place = tile.at[pl.ds(row, BLK), pl.ds(col, BLK)]
        return pltpu.make_async_copy(values.at[n], place, sems.at[n])

    def start(n, carry):
        block(n).start()
        return carry

    def wait(n, carry):
        block(n).wait()
        return carry

    lax.fori_loop(0, count[0], start, 0)
    lax.fori_loop(0, count[0], wait, 0)


def dense_tile(values, rows, cols, count):
    anywhere = pl.BlockSpec(memory_space=pl.ANY)
    n_blocks = values.shape[0]
    return pl.pallas_call(
        dense_body,
        out_shape=shape((CELL_DEV, GENE_DEV), jnp.bfloat16),
        in_specs=[anywhere, anywhere, SMEM_SPEC, anywhere],
        out_specs=VMEM_SPEC,
        scratch_shapes=[
            pltpu.SMEM((n_blocks,), jnp.int32),
            pltpu.SMEM((n_blocks,), jnp.int32),
            pltpu.SemaphoreType.DMA((n_blocks,)),
            pltpu.SemaphoreType.DMA((2,)),
        ],
        compiler_params=pltpu.CompilerParams(vmem_limit_bytes=VMEM_BYTES),
        cost_estimate=pl.CostEstimate(flops=0, bytes_accessed=0, transcendentals=0),
    )(rows, cols, count, values)


def owned(bits, size):
    return pl.ds(pl.multiple_of((lax.axis_index("cell") ^ bits) * size, size), size)


def join_body(*refs):
    row = 0
    for part in refs[:-1]:
        refs[-1][row : row + part.shape[0]] = part[...]
        row += part.shape[0]


def gene_body(order, tile, *refs):
    shares, (panel, mine, message) = refs[:-3], refs[-3:]
    if order is None:
        panel[...] = shares[0][...]
    else:
        size = panel.shape[0] // len(order)
        row = 0
        for part in shares:
            for at in range(0, part.shape[0], size):
                panel[owned(order[row], size)] = part[at : at + size]
                row += 1
    low = panel[...]
    mine[:, :CELL_DEV] = dot(low, tile[...], NT)
    mine[:, CELL_DEV:] = dot(low, low, NT)
    message[...] = mine[...].astype(message.dtype)


def cell_body(picks, tile, mine, other, factor_mine, factor_other, cell_next, low, *rest):
    (first, *sends, gram_out), (factor, updated, chosen) = rest[:-3] or (None, None), rest[-3:]
    share = factor_mine.shape[0]
    core = lax.axis_index("gene")
    own = pl.ds(pl.multiple_of(core * share, share), share)
    theirs = pl.ds(pl.multiple_of((1 - core) * share, share), share)
    factor[own] = factor_mine[...]
    factor[theirs] = factor_other[...]
    gram = mine[:, CELL_DEV:] + other[:, CELL_DEV:].astype(jnp.float32)
    norm = jnp.sum(jnp.sum(gram * gram, axis=1, keepdims=True), axis=0, keepdims=True)
    rate = 1.0 / (jnp.sqrt(norm) + 1e-06)
    held = factor[...]
    stepped = split_dot(gram, held.astype(jnp.bfloat16))
    data = mine[:, :CELL_DEV] + other[:, :CELL_DEV].astype(jnp.float32)
    updated[...] = jnp.maximum(held - rate * (stepped - data), 0.0)
    cell_next[...] = updated[own]
    low[...] = updated[...].astype(jnp.bfloat16)
    if not sends:
        return
    size = chosen.shape[0] // len(picks)
    picked_product(picks, low, tile, chosen, [first.at[:size], *sends])
    own_gram = dot(low[own], low[...], NT)
    rows, width = gram_out.shape[0], own_gram.shape[1]
    for n in range(share // rows):
        gram_out[:, n * width : (n + 1) * width] = own_gram[n * rows : (n + 1) * rows]
    first[size:] = gram_out[...].astype(first.dtype)


def picked_product(picks, low, tile, chosen, parts):
    size = chosen.shape[0] // len(picks)
    for n, bits in enumerate(picks):
        chosen[n * size : (n + 1) * size] = low[owned(bits, size)]
    product = dot(chosen[...], tile[...])
    row = 0
    for out in parts:
        out[...] = product[row : row + out.shape[0]].astype(out.dtype)
        row += out.shape[0]


def keep_body(picks, low, tile, *rest):
    picked_product(picks, low, tile, rest[-1], rest[:-1])


def pass_body(keep, arrived, gram, gram_arrived, out):
    size = keep.shape[0]
    out[:size] = (keep[...] + arrived[...].astype(jnp.float32)).astype(out.dtype)
    gram_sum = gram[...].astype(jnp.float32) + gram_arrived[...].astype(jnp.float32)
    out[size:] = gram_sum.astype(out.dtype)


def gram_body(mine, other, panel, factor, base, rate_out, gram):
    rows, width = mine.shape[0], gram.shape[1]
    core = lax.axis_index("gene")
    for half, part in ((core, mine), (1 - core, other)):
        for n in range(part.shape[1] // width):
            row = pl.multiple_of(half * (gram.shape[0] // 2) + n * rows, rows)
            gram[pl.ds(row, rows)] = part[:, n * width : (n + 1) * width]
    whole = gram[...]
    norm = jnp.sum(jnp.sum(whole * whole, axis=1, keepdims=True), axis=0, keepdims=True)
    rate = 1.0 / (jnp.sqrt(norm) + 1e-06)
    base[...] = factor[...] - rate * split_dot(gram[owned(0, factor.shape[0])], panel[...])
    rate_out[...] = jnp.broadcast_to(rate, rate_out.shape)


def last_body(rate, base, own, beside, third, second, last, out):
    size = own.shape[0]
    total = own[...]
    for part in (beside, third, second, last):
        total = total + part[:size].astype(jnp.float32)
    out[...] = jnp.maximum(base[...] + rate[0:1, 0:1] * total, 0.0)


def gram_of(panel):
    return dot(panel, panel, NT)


def shards(block_values, block_rows, block_cols, block_count, cell_factor, gene_factor):
    n_cell = lax.axis_size("cell")
    kdim = cell_factor.shape[0] * lax.axis_size("gene")
    size = gene_factor.shape[0]
    half = kdim // 2
    gram_rows = half * kdim // GENE_DEV
    paired = n_cell == 8 and size % 16 == 0 and gram_rows % 16 == 0

    def swap(value, bits):
        return lax.ppermute(value, "cell", [(n, n ^ bits) for n in range(n_cell)])

    def swap_core(value):
        return lax.ppermute(value, "gene", [(0, 1), (1, 0)])

    def wide(rows, dtype):
        return shape((rows, GENE_DEV), dtype)

    low_share = gene_factor.astype(jnp.bfloat16)
    factor_other = swap_core(cell_factor)
    tile = dense_tile(block_values[0, 0], block_rows[0, 0], block_cols[0, 0], block_count[0])
    if paired:
        near = [swap(low_share, bits) for bits in (1, 2, 4)]
        beside, second, fourth, tile, factor_other = lax.optimization_barrier((*near, tile, factor_other))
        sixth = swap(fourth, 2)
        both = call(join_body, wide(2 * size, jnp.bfloat16), 0, 2, 0, 0)(second, fourth)
        shares = [low_share, beside, both, swap(both, 1), sixth, swap(sixth, 1)]
        order = [0, 1, 2, 4, 3, 5, 6, 7]
    else:
        shares = [lax.all_gather(low_share, "cell", axis=0, tiled=True)]
        order = None

    panel, mine, message = call(
        functools.partial(gene_body, order),
        (
            wide(kdim, jnp.bfloat16),
            shape((kdim, CELL_DEV + kdim), jnp.float32),
            shape((kdim, CELL_DEV + kdim), jnp.bfloat16),
        ),
        0,
        1 + len(shares),
        0,
        0,
    )(tile, *shares)
    other = swap_core(message)

    sent = [7, 5, 2, 3]
    kept = [6, 4, 1, 0]
    cell_next, next_low, *sends = call(
        functools.partial(cell_body, sent),
        (
            shape(cell_factor.shape, jnp.float32),
            shape((kdim, CELL_DEV), jnp.bfloat16),
            *(
                [
                    wide(size + gram_rows, jnp.bfloat16),
                    wide(size, jnp.bfloat16),
                    wide(2 * size, jnp.bfloat16),
                    wide(gram_rows, jnp.float32),
                ]
                if paired
                else []
            ),
        ),
        0,
        5,
        0,
        0,
        [
            pltpu.VMEM((kdim, CELL_DEV), jnp.float32),
            pltpu.VMEM((kdim, CELL_DEV), jnp.float32),
            pltpu.VMEM((half, CELL_DEV), jnp.bfloat16),
        ],
    )(tile, mine, other, cell_factor, factor_other)

    if not paired:
        cell_gram = lax.psum(gram_of(next_low), "cell")
        own_cols = lax.psum_scatter(dot(next_low, tile), "cell", scatter_dimension=0, tiled=True)
        gram_part = lax.dynamic_slice_in_dim(cell_gram, lax.axis_index("cell") * size, size, 0)
        rate_gene = 1.0 / (jnp.sqrt(jnp.sum(cell_gram * cell_gram)) + 1e-06)
        stepped = jnp.dot(
            gram_part, panel.astype(jnp.float32), precision=lax.Precision.HIGHEST
        )
        return (cell_next, jnp.maximum(gene_factor - rate_gene * (stepped - own_cols), 0.0))

    arrived_third, arrived_second = swap(sends[0], 1), swap(sends[1], 1)
    beside = swap(sends[2], 2)
    keeps = call(
        functools.partial(keep_body, kept),
        tuple(wide(size, jnp.float32) for _ in kept),
        0,
        2,
        0,
        0,
        [pltpu.VMEM((half, CELL_DEV), jnp.bfloat16)],
    )(next_low, tile)
    third = swap((keeps[0] + arrived_third[:size].astype(jnp.float32)).astype(jnp.bfloat16), 6)
    gram = (sends[3] + arrived_third[size:].astype(jnp.float32)).astype(jnp.bfloat16)
    message = call(pass_body, wide(size + gram_rows, jnp.bfloat16), 0, 4, 0, 0)(
        keeps[1], arrived_second, gram, swap(gram, 2)
    )
    second = swap(message, 4)
    last = swap((keeps[2] + beside[size:].astype(jnp.float32)).astype(jnp.bfloat16), 1)
    last, second, third = lax.optimization_barrier((last, second, third))
    gram = message[size:].astype(jnp.float32) + second[size:].astype(jnp.float32)
    base, rate = call(
        gram_body,
        (wide(size, jnp.float32), shape((8, 128), jnp.float32)),
        0,
        4,
        0,
        0,
        [pltpu.VMEM((kdim, kdim), jnp.float32)],
    )(gram, swap_core(gram), panel, gene_factor)
    gene_next = call(last_body, wide(size, jnp.float32), 0, 7, 0, 0)(
        rate, base, keeps[3], beside, third, second, last
    )
    return (cell_next, gene_next)


def solution(mesh):
    return jax.shard_map(
        shards,
        mesh=mesh,
        in_specs=(
            P(("groups", "cell"), "gene", None, None, None),
            P(("groups", "cell"), "gene", None),
            P(("groups", "cell"), "gene", None),
            P(("groups", "cell"), "gene"),
            P(("groups", "gene"), "cell"),
            P(("groups", "cell"), "gene"),
        ),
        out_specs=(P(("groups", "gene"), "cell"), P(("groups", "cell"), "gene")),
        check_vma=False,
    )
```

time: 67.9 us -> 59.9 us (0.88)
  waiting for transfers between devices: 31.6 us -> 23.6 us
  Pallas kernels: 12.6 us -> 8.55 us
  starting transfers between devices: 18 us -> 22 us
    ppermute x16 -> x13, waiting for transfers between devices: 29.3 us -> 20.2 us  [swap(): return lax.ppermute(value, 'cell', [(n, n ^ bits) for n in range(n_cell)])]
    ppermute x16 -> x13, starting transfers between devices: 17.2 us -> 21.3 us  [swap(): return lax.ppermute(value, 'cell', [(n, n ^ bits) for n in range(n_cell)])]
    pallas_call x7 -> x8, Pallas kernels: 12.6 us -> 8.55 us  [the longest x1 2.56 us: dense_tile(): pl.pallas_call(dense_body, out_shape=shape((CELL_DEV, GENE_DEV), jnp.bflo...]
    ppermute x4 -> x3, waiting for transfers between devices: 2.28 us -> 3.42 us  [swap_core(): return lax.ppermute(value, 'gene', [(0, 1), (1, 0)])]
  transfers between devices with their start and end apart: 20 -> 16, of which waited for: 10 -> 10; matrix products, arithmetic and copies ran while one was open for 2% -> 2% of each run, Pallas kernels for 11% -> 6%
where the time goes in v4:
time: 59.9 us; the launch traced here: 59.6 us
  waiting for transfers between devices  23.6 us (39%)
  starting transfers between devices  22 us (37%)
  Pallas kernels  8.55 us (14%)
  local copies, waits for them, and re-layouts  2.91 us (5%)
  between operations  1.42 us (2%)
  other arithmetic  1.05 us (2%)
    ppermute x13, starting transfers between devices, swap(): return lax.ppermute(value, 'cell', [(n, n ^ bits) for n in range(n_cell)])  21.3 us
    ppermute x13, waiting for transfers between devices, swap(): return lax.ppermute(value, 'cell', [(n, n ^ bits) for n in range(n_cell)])  20.2 us
    ppermute x3, waiting for transfers between devices, swap_core(): return lax.ppermute(value, 'gene', [(0, 1), (1, 0)])  3.42 us
    unnamed x10, local copies, waits for them, and re-layouts  2.91 us
    pallas_call x1, Pallas kernels, dense_tile(): pl.pallas_call(dense_body, out_shape=shape((CELL_DEV, GENE_DEV), jnp.bflo...  2.56 us
    pallas_call x1, Pallas kernels, shards(): call(functools.partial(cell_body, sent), (shape(cell_factor.shape, jnp.fl...  2.43 us
    pallas_call x1, Pallas kernels, shards(): call(functools.partial(gene_body, order), (wide(kdim, jnp.bfloat16), shap...  1.61 us
  transfers between devices with their start and end apart: 16, of which 10 were waited for; matrix products, arithmetic and copies ran while one was open for 2% of the time, Pallas kernels for 6%

profile of v4, /device:TPU:0, one launch (start us, length us, event | category | flops | bytes accessed | tf_op | source)
XLA Modules:
  0.0 59.6 jit_solution(16837403044382039073)
XLA Ops:
  0.6 0.5 collective-permute-start.3
  1.1 1.0 %convert_element_type.27.refs_0_ = bf16[32,2048]{1,0:T(8,128)(2,1)S(1)} convert(f32[32,2048]{1,0:T(8,128)} %factor.1) | non-fusion elementwise | flops 65536 | bytes 393216 | tf_op jit(solution)/shard_map/convert_element_type | solution.py:218
  2.1 3.7 %collective-permute-start.2 = (bf16[32,2048]{1,0:T(8,128)(2,1)S(1)}, bf16[32,2048]{1,0:T(8,128)(2,1)S(1)}, u32[]{:S(2)}, u32[]{:S(2)}) collective-permute-start(bf16[32,2048]{1,0:T(8,128)(2,1)S(1)} %convert_element_type.27.refs_0_), channel_id=1, source_target_pairs={{0,8},{2,10},{4,12},{6,14},{8,0},{10,2},{12,4},{14,6},{1,9},{3,11}... | collective-permute-start | bytes 393224 | tf_op jit(solution)/shard_map/ppermute | solution.py:210
  5.8 1.6 %collective-permute-start.1 = (bf16[32,2048]{1,0:T(8,128)(2,1)S(1)}, bf16[32,2048]{1,0:T(8,128)(2,1)S(1)}, u32[]{:S(2)}, u32[]{:S(2)}) collective-permute-start(bf16[32,2048]{1,0:T(8,128)(2,1)S(1)} %convert_element_type.27.refs_0_), channel_id=1, source_target_pairs={{0,4},{2,6},{4,0},{6,2},{8,12},{10,14},{12,8},{14,10},{1,5},{3,7},... | collective-permute-start | bytes 393224 | tf_op jit(solution)/shard_map/ppermute | solution.py:210
  7.4 1.5 %collective-permute-start = (bf16[32,2048]{1,0:T(8,128)(2,1)S(1)}, bf16[32,2048]{1,0:T(8,128)(2,1)S(1)}, u32[]{:S(2)}, u32[]{:S(2)}) collective-permute-start(bf16[32,2048]{1,0:T(8,128)(2,1)S(1)} %convert_element_type.27.refs_0_), channel_id=1, source_target_pairs={{0,2},{2,0},{4,6},{6,4},{8,10},{10,8},{12,14},{14,12},{1,3},{3,1},... | collective-permute-start | bytes 393224 | tf_op jit(solution)/shard_map/ppermute | solution.py:210
  9.5 1.6 %copy-done = bf16[1,1,64,128,128]{4,3,2,1,0:T(8,128)(2,1)S(1)} copy-done((bf16[1,1,64,128,128]{4,3,2,1,0:T(8,128)(2,1)S(1)}, bf16[1,1,64,128,128]{4,3,2,1,0:T(8,128)(2,1)}, u32[]{:S(2)}) %copy-start) | copy-done | bytes 2097176
  11.1 0.7 %copy-done.3 = s32[1,1,64]{2,1,0:T(1,128)S(1)} copy-done((s32[1,1,64]{2,1,0:T(1,128)S(1)}, s32[1,1,64]{2,1,0:T(1,128)}, u32[]{:S(2)}) %copy-start.3) | copy-done | bytes 280
  11.8 0.7 %copy-done.4 = s32[1,1,64]{2,1,0:T(1,128)S(1)} copy-done((s32[1,1,64]{2,1,0:T(1,128)S(1)}, s32[1,1,64]{2,1,0:T(1,128)}, u32[]{:S(2)}) %copy-start.4) | copy-done | bytes 280
  12.4 2.6 %shard_map.77.tile = bf16[1024,2048]{1,0:T(8,128)(2,1)S(1)} custom-call(s32[64]{0:T(128)S(1)} %bitcast.6, s32[64]{0:T(128)S(1)} %bitcast.7, s32[1]{0:T(128)} %bitcast.4.count, bf16[64,128,128]{2,1,0:T(8,128)(2,1)S(1)} %bitcast.5), custom_call_target="tpu_custom_call" | custom-call | tf_op jit(solution)/shard_map/pallas_call | solution.py:81
  15.0 0.4 collective-permute-start.5
  15.5 0.7 %collective-permute-start.4 = (bf16[64,2048]{1,0:T(8,128)(2,1)S(1)}, bf16[64,2048]{1,0:T(8,128)(2,1)S(1)}, u32[]{:S(2)}, u32[]{:S(2)}) collective-permute-start(bf16[64,2048]{1,0:T(8,128)(2,1)S(1)} %shard_map.78.refs_2_), channel_id=1, source_target_pairs={{0,2},{2,0},{4,6},{6,4},{8,10},{10,8},{12,14},{14,12},{1,3},{3,1},... | collective-permute-start | bytes 786440 | tf_op jit(solution)/shard_map/ppermute | solution.py:210
  16.1 3.9 %collective-permute-done.5.refs_4_ = bf16[32,2048]{1,0:T(8,128)(2,1)S(1)} collective-permute-done((bf16[32,2048]{1,0:T(8,128)(2,1)S(1)}, bf16[32,2048]{1,0:T(8,128)(2,1)S(1)}, u32[]{:S(2)}, u32[]{:S(2)}) %collective-permute-start.5) | collective-permute-done | bytes 131104 | tf_op jit(solution)/shard_map/ppermute | solution.py:210
  20.1 0.6 collective-permute-start.6
  20.6 3.4 %collective-permute-done.4.refs_3_ = bf16[64,2048]{1,0:T(8,128)(2,1)S(1)} collective-permute-done((bf16[64,2048]{1,0:T(8,128)(2,1)S(1)}, bf16[64,2048]{1,0:T(8,128)(2,1)S(1)}, u32[]{:S(2)}, u32[]{:S(2)}) %collective-permute-start.4) | collective-permute-done | bytes 262176 | tf_op jit(solution)/shard_map/ppermute | solution.py:210
  24.0 1.4 %collective-permute-done.6.refs_5_ = bf16[32,2048]{1,0:T(8,128)(2,1)S(1)} collective-permute-done((bf16[32,2048]{1,0:T(8,128)(2,1)S(1)}, bf16[32,2048]{1,0:T(8,128)(2,1)S(1)}, u32[]{:S(2)}, u32[]{:S(2)}) %collective-permute-start.6) | collective-permute-done | bytes 131104 | tf_op jit(solution)/shard_map/ppermute | solution.py:210
  25.4 1.6 %shard_map.79 = (bf16[256,2048]{1,0:T(8,128)(2,1)S(1)}, f32[256,1280]{1,0:T(8,128)S(1)}, bf16[256,1280]{1,0:T(8,128)(2,1)S(1)}) custom-call(bf16[1024,2048]{1,0:T(8,128)(2,1)S(1)} %shard_map.77.tile, bf16[32,2048]{1,0:T(8,128)(2,1)S(1)} %convert_element_type.27.refs_0_, bf16[32,2048]{1,0:T(8,128)(2,1)S(1)} %collective-permute-done.refs_1_, ...), custom_call_target="tpu_custom_call" | custom-call | tf_op jit(solution)/shard_map/pallas_call | solution.py:232
  27.1 2.1 %collective-permute-done.7.other = bf16[256,1280]{1,0:T(8,128)(2,1)S(1)} collective-permute-done((bf16[256,1280]{1,0:T(8,128)(2,1)S(1)}, bf16[256,1280]{1,0:T(8,128)(2,1)S(1)}, u32[]{:S(2)}, u32[]{:S(2)}) %collective-permute-start.7) | collective-permute-done | bytes 655392 | tf_op jit(solution)/shard_map/ppermute | solution.py:213
  29.2 2.4 %shard_map.80 = (f32[128,1024]{1,0:T(8,128)}, bf16[256,1024]{1,0:T(8,128)(2,1)S(1)}, bf16[48,2048]{1,0:T(8,128)(2,1)S(1)}, bf16[32,2048]{1,0:T(8,128)(2,1)S(1)},...) custom-call(bf16[1024,2048]{1,0:T(8,128)(2,1)S(1)} %shard_map.77.tile, f32[256,1280]{1,0:T(8,128)S(1)} %get-tuple-element.29.mine, ...), custom_call_target="tpu_custom_call" | custom-call | tf_op jit(solution)/shard_map/pallas_call | solution.py:248
  31.6 1.1 %collective-permute-start.9 = (bf16[48,2048]{1,0:T(8,128)(2,1)S(1)}, bf16[48,2048]{1,0:T(8,128)(2,1)S(1)}, u32[]{:S(2)}, u32[]{:S(2)}) collective-permute-start(bf16[48,2048]{1,0:T(8,128)(2,1)S(1)} %get-tuple-element.37), channel_id=1, source_target_pairs={{0,2},{2,0},{4,6},{6,4},{8,10},{10,8},{12,14},{14,12},{1,3},{3,1},... | collective-permute-start | bytes 589832 | tf_op jit(solution)/shard_map/ppermute | solution.py:210
  32.8 0.7 %shard_map.81 = (f32[32,2048]{1,0:T(8,128)S(1)}, f32[32,2048]{1,0:T(8,128)S(1)}, f32[32,2048]{1,0:T(8,128)S(1)}, f32[32,2048]{1,0:T(8,128)S(1)}) custom-call(bf16[256,1024]{1,0:T(8,128)(2,1)S(1)} %get-tuple-element.33.low, bf16[1024,2048]{1,0:T(8,128)(2,1)S(1)} %shard_map.77.tile), custom_call_target="tpu_custom_call" | custom-call | tf_op jit(solution)/shard_map/pallas_call | solution.py:287
  33.5 0.9 %collective-permute-start.8 = (bf16[32,2048]{1,0:T(8,128)(2,1)S(1)}, bf16[32,2048]{1,0:T(8,128)(2,1)S(1)}, u32[]{:S(2)}, u32[]{:S(2)}) collective-permute-start(bf16[32,2048]{1,0:T(8,128)(2,1)S(1)} %get-tuple-element.35), channel_id=1, source_target_pairs={{0,2},{2,0},{4,6},{6,4},{8,10},{10,8},{12,14},{14,12},{1,3},{3,1},... | collective-permute-start | bytes 393224 | tf_op jit(solution)/shard_map/ppermute | solution.py:210
  34.5 1.7 %collective-permute-start.11 = (bf16[64,2048]{1,0:T(8,128)(2,1)S(1)}, bf16[64,2048]{1,0:T(8,128)(2,1)S(1)}, u32[]{:S(2)}, u32[]{:S(2)}) collective-permute-start(bf16[64,2048]{1,0:T(8,128)(2,1)S(1)} %get-tuple-element.39), channel_id=1, source_target_pairs={{0,4},{2,6},{4,0},{6,2},{8,12},{10,14},{12,8},{14,10},{1,5},{3,7},... | collective-permute-start | bytes 786440 | tf_op jit(solution)/shard_map/ppermute | solution.py:210
  36.2 3.2 %collective-permute-done.9 = bf16[48,2048]{1,0:T(8,128)(2,1)S(1)} collective-permute-done((bf16[48,2048]{1,0:T(8,128)(2,1)S(1)}, bf16[48,2048]{1,0:T(8,128)(2,1)S(1)}, u32[]{:S(2)}, u32[]{:S(2)}) %collective-permute-start.9) | collective-permute-done | bytes 196640 | tf_op jit(solution)/shard_map/ppermute | solution.py:210
  39.4 1.8 %collective-permute-start.10 = (bf16[16,2048]{1,0:T(8,128)(2,1)S(1)}, bf16[16,2048]{1,0:T(8,128)(2,1)S(1)}, u32[]{:S(2)}, u32[]{:S(2)}) collective-permute-start(bf16[16,2048]{1,0:T(8,128)(2,1)S(1)} %add_convert_fusion.2.gram), channel_id=1, source_target_pairs={{0,4},{2,6},{4,0},{6,2},{8,12},{10,14},{12,8},{14,10},{1,5},{3,7},... | collective-permute-start | bytes 196616 | tf_op jit(solution)/shard_map/ppermute | solution.py:210
  41.2 2.2 %collective-permute-start.14 = (bf16[32,2048]{1,0:T(8,128)(2,1)S(1)}, bf16[32,2048]{1,0:T(8,128)(2,1)S(1)}, u32[]{:S(2)}, u32[]{:S(2)}) collective-permute-start(bf16[32,2048]{1,0:T(8,128)(2,1)S(1)} %add_convert_fusion), channel_id=1, source_target_pairs={{0,12},{2,14},{4,8},{6,10},{8,4},{10,6},{12,0},{14,2},{1,13},{3,15... | collective-permute-start | bytes 393224 | tf_op jit(solution)/shard_map/ppermute | solution.py:210
  43.4 0.6 collective-permute-done.10.gram_arrived
  44.0 3.5 %collective-permute-start.13 = (bf16[48,2048]{1,0:T(8,128)(2,1)S(1)}, bf16[48,2048]{1,0:T(8,128)(2,1)S(1)}, u32[]{:S(2)}, u32[]{:S(2)}) collective-permute-start(bf16[48,2048]{1,0:T(8,128)(2,1)S(1)} %shard_map.82), channel_id=1, source_target_pairs={{0,8},{2,10},{4,12},{6,14},{8,0},{10,2},{12,4},{14,6},{1,9},{3,11}... | collective-permute-start | bytes 589832 | tf_op jit(solution)/shard_map/ppermute | solution.py:210
  47.6 1.6 %collective-permute-start.12 = (bf16[32,2048]{1,0:T(8,128)(2,1)S(1)}, bf16[32,2048]{1,0:T(8,128)(2,1)S(1)}, u32[]{:S(2)}, u32[]{:S(2)}) collective-permute-start(bf16[32,2048]{1,0:T(8,128)(2,1)S(1)} %add_convert_fusion.1), channel_id=1, source_target_pairs={{0,2},{2,0},{4,6},{6,4},{8,10},{10,8},{12,14},{14,12},{1,3},{3,1},... | collective-permute-start | bytes 393224 | tf_op jit(solution)/shard_map/ppermute | solution.py:210
  49.6 3.1 %collective-permute-done.12.last = bf16[32,2048]{1,0:T(8,128)(2,1)S(1)} collective-permute-done((bf16[32,2048]{1,0:T(8,128)(2,1)S(1)}, bf16[32,2048]{1,0:T(8,128)(2,1)S(1)}, u32[]{:S(2)}, u32[]{:S(2)}) %collective-permute-start.12) | collective-permute-done | bytes 131104 | tf_op jit(solution)/shard_map/ppermute | solution.py:210
  52.7 4.3 %collective-permute-done.13.second = bf16[48,2048]{1,0:T(8,128)(2,1)S(1)} collective-permute-done((bf16[48,2048]{1,0:T(8,128)(2,1)S(1)}, bf16[48,2048]{1,0:T(8,128)(2,1)S(1)}, u32[]{:S(2)}, u32[]{:S(2)}) %collective-permute-start.13) | collective-permute-done | bytes 196640 | tf_op jit(solution)/shard_map/ppermute | solution.py:210
  57.1 1.3 %collective-permute-done.15.other = f32[16,2048]{1,0:T(8,128)S(1)} collective-permute-done((f32[16,2048]{1,0:T(8,128)S(1)}, f32[16,2048]{1,0:T(8,128)S(1)}, u32[]{:S(2)}, u32[]{:S(2)}) %collective-permute-start.15) | collective-permute-done | bytes 131104 | tf_op jit(solution)/shard_map/ppermute | solution.py:213
  58.7 0.8 %shard_map.84 = f32[32,2048]{1,0:T(8,128)} custom-call(f32[8,128]{1,0:T(8,128)S(1)} %get-tuple-element.43.rate, f32[32,2048]{1,0:T(8,128)S(1)} %get-tuple-element.44.base, f32[32,2048]{1,0:T(8,128)S(1)} %get-tuple-element.45.own, bf16[64,2048]{1,0:T(8,128)(2,1)S(1)} %collective-permute-done.11.beside, bf16[32,2048]{1,0:T(8,128)(2,1)S(1)} %collective-permute-done.14.third, ...), custom_call_target="tpu_custom_call" | custom-call | tf_op jit(solution)/shard_map/pallas_call | solution.py:314
  (23 shorter events, 1.0 us)
Async XLA Ops:
  0.6 14.4 %collective-permute-start.3 = (f32[128,1024]{1,0:T(8,128)}, f32[128,1024]{1,0:T(8,128)S(1)}, u32[]{:S(2)}, u32[]{:S(2)}) collective-permute-start(f32[128,1024]{1,0:T(8,128)} %factor_mine.1), channel_id=1, source_target_pairs={{0,1},{1,0},{2,3},{3,2},{4,5},{5,4},{6,7},{7,6},{8,9},{9,8},{10,11... | collective-permute-start | bytes 1572872 | tf_op jit(solution)/shard_map/ppermute | solution.py:213
  2.1 12.9 %collective-permute-start.2 = (bf16[32,2048]{1,0:T(8,128)(2,1)S(1)}, bf16[32,2048]{1,0:T(8,128)(2,1)S(1)}, u32[]{:S(2)}, u32[]{:S(2)}) collective-permute-start(bf16[32,2048]{1,0:T(8,128)(2,1)S(1)} %convert_element_type.27.refs_0_), channel_id=1, source_target_pairs={{0,8},{2,10},{4,12},{6,14},{8,0},{10,2},{12,4},{14,6},{1,9},{3,11}... | collective-permute-start | bytes 393224 | tf_op jit(solution)/shard_map/ppermute | solution.py:210
  5.8 9.2 %collective-permute-start.1 = (bf16[32,2048]{1,0:T(8,128)(2,1)S(1)}, bf16[32,2048]{1,0:T(8,128)(2,1)S(1)}, u32[]{:S(2)}, u32[]{:S(2)}) collective-permute-start(bf16[32,2048]{1,0:T(8,128)(2,1)S(1)} %convert_element_type.27.refs_0_), channel_id=1, source_target_pairs={{0,4},{2,6},{4,0},{6,2},{8,12},{10,14},{12,8},{14,10},{1,5},{3,7},... | collective-permute-start | bytes 393224 | tf_op jit(solution)/shard_map/ppermute | solution.py:210
  7.4 7.6 %collective-permute-start = (bf16[32,2048]{1,0:T(8,128)(2,1)S(1)}, bf16[32,2048]{1,0:T(8,128)(2,1)S(1)}, u32[]{:S(2)}, u32[]{:S(2)}) collective-permute-start(bf16[32,2048]{1,0:T(8,128)(2,1)S(1)} %convert_element_type.27.refs_0_), channel_id=1, source_target_pairs={{0,2},{2,0},{4,6},{6,4},{8,10},{10,8},{12,14},{14,12},{1,3},{3,1},... | collective-permute-start | bytes 393224 | tf_op jit(solution)/shard_map/ppermute | solution.py:210
  9.5 1.6 %copy-start = (bf16[1,1,64,128,128]{4,3,2,1,0:T(8,128)(2,1)S(1)}, bf16[1,1,64,128,128]{4,3,2,1,0:T(8,128)(2,1)}, u32[]{:S(2)}) copy-start(bf16[1,1,64,128,128]{4,3,2,1,0:T(8,128)(2,1)} %param.6) | copy-start | bytes 6291460
  11.1 0.7 %copy-start.3 = (s32[1,1,64]{2,1,0:T(1,128)S(1)}, s32[1,1,64]{2,1,0:T(1,128)}, u32[]{:S(2)}) copy-start(s32[1,1,64]{2,1,0:T(1,128)} %param.7) | copy-start | bytes 772
  11.8 0.7 %copy-start.4 = (s32[1,1,64]{2,1,0:T(1,128)S(1)}, s32[1,1,64]{2,1,0:T(1,128)}, u32[]{:S(2)}) copy-start(s32[1,1,64]{2,1,0:T(1,128)} %param.8) | copy-start | bytes 772
  15.0 5.0 %collective-permute-start.5 = (bf16[32,2048]{1,0:T(8,128)(2,1)S(1)}, bf16[32,2048]{1,0:T(8,128)(2,1)S(1)}, u32[]{:S(2)}, u32[]{:S(2)}) collective-permute-start(bf16[32,2048]{1,0:T(8,128)(2,1)S(1)} %collective-permute-done.2.refs_1_), channel_id=1, source_target_pairs={{0,4},{2,6},{4,0},{6,2},{8,12},{10,14},{12,8},{14,10},{1,5},{3,7},... | collective-permute-start | bytes 393224 | tf_op jit(solution)/shard_map/ppermute | solution.py:210
  15.4 13.8 %copy-start.2 = (f32[128,1024]{1,0:T(8,128)S(1)}, f32[128,1024]{1,0:T(8,128)}, u32[]{:S(2)}) copy-start(f32[128,1024]{1,0:T(8,128)} %factor_mine.1) | copy-start | bytes 1572868
  15.5 8.6 %collective-permute-start.4 = (bf16[64,2048]{1,0:T(8,128)(2,1)S(1)}, bf16[64,2048]{1,0:T(8,128)(2,1)S(1)}, u32[]{:S(2)}, u32[]{:S(2)}) collective-permute-start(bf16[64,2048]{1,0:T(8,128)(2,1)S(1)} %shard_map.78.refs_2_), channel_id=1, source_target_pairs={{0,2},{2,0},{4,6},{6,4},{8,10},{10,8},{12,14},{14,12},{1,3},{3,1},... | collective-permute-start | bytes 786440 | tf_op jit(solution)/shard_map/ppermute | solution.py:210
  20.1 5.4 %collective-permute-start.6 = (bf16[32,2048]{1,0:T(8,128)(2,1)S(1)}, bf16[32,2048]{1,0:T(8,128)(2,1)S(1)}, u32[]{:S(2)}, u32[]{:S(2)}) collective-permute-start(bf16[32,2048]{1,0:T(8,128)(2,1)S(1)} %collective-permute-done.5.refs_4_), channel_id=1, source_target_pairs={{0,2},{2,0},{4,6},{6,4},{8,10},{10,8},{12,14},{14,12},{1,3},{3,1},... | collective-permute-start | bytes 393224 | tf_op jit(solution)/shard_map/ppermute | solution.py:210
  27.0 2.2 %collective-permute-start.7 = (bf16[256,1280]{1,0:T(8,128)(2,1)S(1)}, bf16[256,1280]{1,0:T(8,128)(2,1)S(1)}, u32[]{:S(2)}, u32[]{:S(2)}) collective-permute-start(bf16[256,1280]{1,0:T(8,128)(2,1)S(1)} %get-tuple-element.30), channel_id=1, source_target_pairs={{0,1},{1,0},{2,3},{3,2},{4,5},{5,4},{6,7},{7,6},{8,9},{9,8},{10,11... | collective-permute-start | bytes 1966088 | tf_op jit(solution)/shard_map/ppermute | solution.py:213
  31.6 7.7 %collective-permute-start.9 = (bf16[48,2048]{1,0:T(8,128)(2,1)S(1)}, bf16[48,2048]{1,0:T(8,128)(2,1)S(1)}, u32[]{:S(2)}, u32[]{:S(2)}) collective-permute-start(bf16[48,2048]{1,0:T(8,128)(2,1)S(1)} %get-tuple-element.37), channel_id=1, source_target_pairs={{0,2},{2,0},{4,6},{6,4},{8,10},{10,8},{12,14},{14,12},{1,3},{3,1},... | collective-permute-start | bytes 589832 | tf_op jit(solution)/shard_map/ppermute | solution.py:210
  33.5 24.9 %copy-start.1 = (f32[32,2048]{1,0:T(8,128)S(1)}, f32[32,2048]{1,0:T(8,128)}, u32[]{:S(2)}) copy-start(f32[32,2048]{1,0:T(8,128)} %factor.1) | copy-start | bytes 786436
  33.5 9.9 %collective-permute-start.8 = (bf16[32,2048]{1,0:T(8,128)(2,1)S(1)}, bf16[32,2048]{1,0:T(8,128)(2,1)S(1)}, u32[]{:S(2)}, u32[]{:S(2)}) collective-permute-start(bf16[32,2048]{1,0:T(8,128)(2,1)S(1)} %get-tuple-element.35), channel_id=1, source_target_pairs={{0,2},{2,0},{4,6},{6,4},{8,10},{10,8},{12,14},{14,12},{1,3},{3,1},... | collective-permute-start | bytes 393224 | tf_op jit(solution)/shard_map/ppermute | solution.py:210
  34.5 13.1 %collective-permute-start.11 = (bf16[64,2048]{1,0:T(8,128)(2,1)S(1)}, bf16[64,2048]{1,0:T(8,128)(2,1)S(1)}, u32[]{:S(2)}, u32[]{:S(2)}) collective-permute-start(bf16[64,2048]{1,0:T(8,128)(2,1)S(1)} %get-tuple-element.39), channel_id=1, source_target_pairs={{0,4},{2,6},{4,0},{6,2},{8,12},{10,14},{12,8},{14,10},{1,5},{3,7},... | collective-permute-start | bytes 786440 | tf_op jit(solution)/shard_map/ppermute | solution.py:210
  39.4 4.6 %collective-permute-start.10 = (bf16[16,2048]{1,0:T(8,128)(2,1)S(1)}, bf16[16,2048]{1,0:T(8,128)(2,1)S(1)}, u32[]{:S(2)}, u32[]{:S(2)}) collective-permute-start(bf16[16,2048]{1,0:T(8,128)(2,1)S(1)} %add_convert_fusion.2.gram), channel_id=1, source_target_pairs={{0,4},{2,6},{4,0},{6,2},{8,12},{10,14},{12,8},{14,10},{1,5},{3,7},... | collective-permute-start | bytes 196616 | tf_op jit(solution)/shard_map/ppermute | solution.py:210
  41.2 8.3 %collective-permute-start.14 = (bf16[32,2048]{1,0:T(8,128)(2,1)S(1)}, bf16[32,2048]{1,0:T(8,128)(2,1)S(1)}, u32[]{:S(2)}, u32[]{:S(2)}) collective-permute-start(bf16[32,2048]{1,0:T(8,128)(2,1)S(1)} %add_convert_fusion), channel_id=1, source_target_pairs={{0,12},{2,14},{4,8},{6,10},{8,4},{10,6},{12,0},{14,2},{1,13},{3,15... | collective-permute-start | bytes 393224 | tf_op jit(solution)/shard_map/ppermute | solution.py:210
  44.0 12.9 %collective-permute-start.13 = (bf16[48,2048]{1,0:T(8,128)(2,1)S(1)}, bf16[48,2048]{1,0:T(8,128)(2,1)S(1)}, u32[]{:S(2)}, u32[]{:S(2)}) collective-permute-start(bf16[48,2048]{1,0:T(8,128)(2,1)S(1)} %shard_map.82), channel_id=1, source_target_pairs={{0,8},{2,10},{4,12},{6,14},{8,0},{10,2},{12,4},{14,6},{1,9},{3,11}... | collective-permute-start | bytes 589832 | tf_op jit(solution)/shard_map/ppermute | solution.py:210
  47.6 5.0 %collective-permute-start.12 = (bf16[32,2048]{1,0:T(8,128)(2,1)S(1)}, bf16[32,2048]{1,0:T(8,128)(2,1)S(1)}, u32[]{:S(2)}, u32[]{:S(2)}) collective-permute-start(bf16[32,2048]{1,0:T(8,128)(2,1)S(1)} %add_convert_fusion.1), channel_id=1, source_target_pairs={{0,2},{2,0},{4,6},{6,4},{8,10},{10,8},{12,14},{14,12},{1,3},{3,1},... | collective-permute-start | bytes 393224 | tf_op jit(solution)/shard_map/ppermute | solution.py:210
  57.0 1.4 %collective-permute-start.15 = (f32[16,2048]{1,0:T(8,128)S(1)}, f32[16,2048]{1,0:T(8,128)S(1)}, u32[]{:S(2)}, u32[]{:S(2)}) collective-permute-start(f32[16,2048]{1,0:T(8,128)S(1)} %convert_add_fusion.mine), channel_id=1, source_target_pairs={{0,1},{1,0},{2,3},{3,2},{4,5},{5,4},{6,7},{7,6},{8,9},{9,8},{10,11... | collective-permute-start | bytes 393224 | tf_op jit(solution)/shard_map/ppermute | solution.py:213

commit v5 on v4

--- a/solution.py
+++ b/solution.py
@@ -123,7 +123,7 @@
 
 
 def cell_body(picks, tile, mine, other, factor_mine, factor_other, cell_next, low, *rest):
-    (first, *sends, gram_out), (factor, updated, chosen) = rest[:-3] or (None, None), rest[-3:]
+    sends, (factor, updated, chosen) = rest[:-3], rest[-3:]
     share = factor_mine.shape[0]
     core = lax.axis_index("gene")
     own = pl.ds(pl.multiple_of(core * share, share), share)
@@ -141,13 +141,7 @@
     low[...] = updated[...].astype(jnp.bfloat16)
     if not sends:
         return
-    size = chosen.shape[0] // len(picks)
-    picked_product(picks, low, tile, chosen, [first.at[:size], *sends])
-    own_gram = dot(low[own], low[...], NT)
-    rows, width = gram_out.shape[0], own_gram.shape[1]
-    for n in range(share // rows):
-        gram_out[:, n * width : (n + 1) * width] = own_gram[n * rows : (n + 1) * rows]
-    first[size:] = gram_out[...].astype(first.dtype)
+    picked_product(picks, low, tile, chosen, sends)
 
 
 def picked_product(picks, low, tile, chosen, parts):
@@ -161,18 +155,27 @@
         row += out.shape[0]
 
 
-def keep_body(picks, low, tile, *rest):
+def keep_body(picks, low, tile, gram, *rest):
     picked_product(picks, low, tile, rest[-1], rest[:-1])
-
-
-def pass_body(keep, arrived, gram, gram_arrived, out):
-    size = keep.shape[0]
-    out[:size] = (keep[...] + arrived[...].astype(jnp.float32)).astype(out.dtype)
-    gram_sum = gram[...].astype(jnp.float32) + gram_arrived[...].astype(jnp.float32)
-    out[size:] = gram_sum.astype(out.dtype)
-
-
-def gram_body(mine, other, panel, factor, base, rate_out, gram):
+    share = low.shape[0] // 2
+    own = pl.ds(pl.multiple_of(lax.axis_index("gene") * share, share), share)
+    half = dot(low[own], low[...], NT).astype(gram.dtype)
+    rows, width = gram.shape[0], half.shape[1]
+    for n in range(share // rows):
+        gram[:, n * width : (n + 1) * width] = half[n * rows : (n + 1) * rows]
+
+
+def sum_body(keep, arrived, out):
+    out[...] = (keep[...] + arrived[...].astype(jnp.float32)).astype(out.dtype)
+
+
+def turn_body(keep, own, beside, third, out, partial):
+    size = own.shape[0]
+    out[...] = (keep[...] + beside[size:].astype(jnp.float32)).astype(out.dtype)
+    partial[...] = own[...] + beside[:size].astype(jnp.float32) + third[...].astype(jnp.float32)
+
+
+def last_body(mine, other, panel, factor, partial, second, last, out, gram):
     rows, width = mine.shape[0], gram.shape[1]
     core = lax.axis_index("gene")
     for half, part in ((core, mine), (1 - core, other)):
@@ -182,16 +185,9 @@
     whole = gram[...]
     norm = jnp.sum(jnp.sum(whole * whole, axis=1, keepdims=True), axis=0, keepdims=True)
     rate = 1.0 / (jnp.sqrt(norm) + 1e-06)
-    base[...] = factor[...] - rate * split_dot(gram[owned(0, factor.shape[0])], panel[...])
-    rate_out[...] = jnp.broadcast_to(rate, rate_out.shape)
-
-
-def last_body(rate, base, own, beside, third, second, last, out):
-    size = own.shape[0]
-    total = own[...]
-    for part in (beside, third, second, last):
-        total = total + part[:size].astype(jnp.float32)
-    out[...] = jnp.maximum(base[...] + rate[0:1, 0:1] * total, 0.0)
+    stepped = split_dot(gram[owned(0, factor.shape[0])], panel[...])
+    data = partial[...] + second[...].astype(jnp.float32) + last[...].astype(jnp.float32)
+    out[...] = jnp.maximum(factor[...] - rate * (stepped - data), 0.0)
 
 
 def gram_of(panel):
@@ -216,19 +212,21 @@
         return shape((rows, GENE_DEV), dtype)
 
     low_share = gene_factor.astype(jnp.bfloat16)
-    factor_other = swap_core(cell_factor)
     tile = dense_tile(block_values[0, 0], block_rows[0, 0], block_cols[0, 0], block_count[0])
     if paired:
         near = [swap(low_share, bits) for bits in (1, 2, 4)]
-        beside, second, fourth, tile, factor_other = lax.optimization_barrier((*near, tile, factor_other))
+        beside, second, fourth = lax.optimization_barrier(near)
         sixth = swap(fourth, 2)
         both = call(join_body, wide(2 * size, jnp.bfloat16), 0, 2, 0, 0)(second, fourth)
+        both, factor = lax.optimization_barrier((both, cell_factor))
         shares = [low_share, beside, both, swap(both, 1), sixth, swap(sixth, 1)]
         order = [0, 1, 2, 4, 3, 5, 6, 7]
     else:
         shares = [lax.all_gather(low_share, "cell", axis=0, tiled=True)]
-        order = None
-
+        order, factor = None, cell_factor
+    factor_other = swap_core(factor)
+
+    shares[0], factor_other = lax.optimization_barrier((shares[0], factor_other))
     panel, mine, message = call(
         functools.partial(gene_body, order),
         (
@@ -252,10 +250,9 @@
             shape((kdim, CELL_DEV), jnp.bfloat16),
             *(
                 [
-                    wide(size + gram_rows, jnp.bfloat16),
+                    wide(size, jnp.bfloat16),
                     wide(size, jnp.bfloat16),
                     wide(2 * size, jnp.bfloat16),
-                    wide(gram_rows, jnp.float32),
                 ]
                 if paired
                 else []
@@ -284,36 +281,41 @@
 
     arrived_third, arrived_second = swap(sends[0], 1), swap(sends[1], 1)
     beside = swap(sends[2], 2)
-    keeps = call(
+    gram, *keeps = call(
         functools.partial(keep_body, kept),
-        tuple(wide(size, jnp.float32) for _ in kept),
+        (wide(gram_rows, jnp.bfloat16), *[wide(size, jnp.float32) for _ in kept]),
         0,
         2,
         0,
-        0,
+        16 * 2**20,
         [pltpu.VMEM((half, CELL_DEV), jnp.bfloat16)],
     )(next_low, tile)
-    third = swap((keeps[0] + arrived_third[:size].astype(jnp.float32)).astype(jnp.bfloat16), 6)
-    gram = (sends[3] + arrived_third[size:].astype(jnp.float32)).astype(jnp.bfloat16)
-    message = call(pass_body, wide(size + gram_rows, jnp.bfloat16), 0, 4, 0, 0)(
-        keeps[1], arrived_second, gram, swap(gram, 2)
-    )
-    second = swap(message, 4)
-    last = swap((keeps[2] + beside[size:].astype(jnp.float32)).astype(jnp.bfloat16), 1)
-    last, second, third = lax.optimization_barrier((last, second, third))
-    gram = message[size:].astype(jnp.float32) + second[size:].astype(jnp.float32)
-    base, rate = call(
-        gram_body,
-        (wide(size, jnp.float32), shape((8, 128), jnp.float32)),
-        0,
-        4,
+    gram_arrived = swap(gram, 4)
+    third = call(sum_body, wide(size, jnp.bfloat16), 0, 2, 0, 16 * 2**20)(keeps[0], arrived_third)
+    gram_arrived, third = lax.optimization_barrier((gram_arrived, third))
+    third = swap(third, 6)
+    gram = (gram.astype(jnp.float32) + gram_arrived.astype(jnp.float32)).astype(jnp.bfloat16)
+    gram_arrived = swap(gram, 2)
+    beside, arrived_second = lax.optimization_barrier((beside, arrived_second))
+    second = call(sum_body, wide(size, jnp.bfloat16), 0, 2, 0, 16 * 2**20)(keeps[1], arrived_second)
+    gram_arrived, second = lax.optimization_barrier((gram_arrived, second))
+    second = swap(second, 4)
+    gram = (gram.astype(jnp.float32) + gram_arrived.astype(jnp.float32)).astype(jnp.bfloat16)
+    message, partial = call(
+        turn_body, (wide(size, jnp.bfloat16), wide(size, jnp.float32)), 0, 4, 0, 16 * 2**20
+    )(keeps[2], keeps[3], beside, third)
+    last = swap(message, 1)
+    gram_arrived, second = lax.optimization_barrier((swap(gram, 1), second))
+    gram = gram.astype(jnp.float32) + gram_arrived.astype(jnp.float32)
+    gene_next = call(
+        last_body,
+        wide(size, jnp.float32),
+        0,
+        7,
         0,
         0,
         [pltpu.VMEM((kdim, kdim), jnp.float32)],
-    )(gram, swap_core(gram), panel, gene_factor)
-    gene_next = call(last_body, wide(size, jnp.float32), 0, 7, 0, 0)(
-        rate, base, keeps[3], beside, third, second, last
-    )
+    )(gram, swap_core(gram), panel, gene_factor, partial, second, last)
     return (cell_next, gene_next)
 
 

time: 59.9 us -> 57.3 us (0.957)
  waiting for transfers between devices: 23.6 us -> 19.6 us
  starting transfers between devices: 22 us -> 23.9 us
    ppermute x13 -> x15, waiting for transfers between devices: 20.2 us -> 16.1 us  [swap(): return lax.ppermute(value, 'cell', [(n, n ^ bits) for n in range(n_cell)])]
    ppermute x13 -> x15, starting transfers between devices: 21.3 us -> 23.7 us  [swap(): return lax.ppermute(value, 'cell', [(n, n ^ bits) for n in range(n_cell)])]
    pallas_call x4 -> x5, Pallas kernels: 1.94 us -> 2.01 us  [the longest x1 1.02 us: shards(): call(last_body, wide(size, jnp.float32), 0, 7, 0, 0, [pltpu.VMEM((kdim, k...]
  transfers between devices with their start and end apart: 16 -> 18, of which waited for: 10 -> 11; matrix products, arithmetic and copies ran while one was open for 2% -> 0% of each run, Pallas kernels for 6% -> 6%
where the time goes in v5:
time: 57.3 us; the launch traced here: 57 us
  starting transfers between devices  23.9 us (42%)
  waiting for transfers between devices  19.6 us (34%)
  Pallas kernels  8.18 us (14%)
  local copies, waits for them, and re-layouts  2.91 us (5%)
  between operations  1.44 us (3%)
  other arithmetic  1.02 us (2%)
    ppermute x15, starting transfers between devices, swap(): return lax.ppermute(value, 'cell', [(n, n ^ bits) for n in range(n_cell)])  23.7 us
    ppermute x15, waiting for transfers between devices, swap(): return lax.ppermute(value, 'cell', [(n, n ^ bits) for n in range(n_cell)])  16.1 us
    ppermute x3, waiting for transfers between devices, swap_core(): return lax.ppermute(value, 'gene', [(0, 1), (1, 0)])  3.41 us
    unnamed x10, local copies, waits for them, and re-layouts  2.91 us
    pallas_call x1, Pallas kernels, dense_tile(): pl.pallas_call(dense_body, out_shape=shape((CELL_DEV, GENE_DEV), jnp.bflo...  2.56 us
    pallas_call x1, Pallas kernels, shards(): call(functools.partial(cell_body, sent), (shape(cell_factor.shape, jnp.fl...  2.03 us
    pallas_call x1, Pallas kernels, shards(): call(functools.partial(gene_body, order), (wide(kdim, jnp.bfloat16), shap...  1.57 us
  transfers between devices with their start and end apart: 18, of which 11 were waited for; matrix products, arithmetic and copies ran while one was open for 0% of the time, Pallas kernels for 6%

profile of v5, /device:TPU:0, one launch (start us, length us, event | category | flops | bytes accessed | tf_op | source)
XLA Modules:
  0.0 57.0 jit_solution(9456361125471305858)
XLA Ops:
  0.6 1.0 %convert_element_type.27.refs_0_ = bf16[32,2048]{1,0:T(8,128)(2,1)S(1)} convert(f32[32,2048]{1,0:T(8,128)} %factor.1) | non-fusion elementwise | flops 65536 | bytes 393216 | tf_op jit(solution)/shard_map/convert_element_type | solution.py:214
  1.6 4.1 %collective-permute-start.2 = (bf16[32,2048]{1,0:T(8,128)(2,1)S(1)}, bf16[32,2048]{1,0:T(8,128)(2,1)S(1)}, u32[]{:S(2)}, u32[]{:S(2)}) collective-permute-start(bf16[32,2048]{1,0:T(8,128)(2,1)S(1)} %convert_element_type.27.refs_0_), channel_id=1, source_target_pairs={{0,8},{2,10},{4,12},{6,14},{8,0},{10,2},{12,4},{14,6},{1,9},{3,11}... | collective-permute-start | bytes 393224 | tf_op jit(solution)/shard_map/ppermute | solution.py:206
  5.7 1.6 %collective-permute-start.1 = (bf16[32,2048]{1,0:T(8,128)(2,1)S(1)}, bf16[32,2048]{1,0:T(8,128)(2,1)S(1)}, u32[]{:S(2)}, u32[]{:S(2)}) collective-permute-start(bf16[32,2048]{1,0:T(8,128)(2,1)S(1)} %convert_element_type.27.refs_0_), channel_id=1, source_target_pairs={{0,4},{2,6},{4,0},{6,2},{8,12},{10,14},{12,8},{14,10},{1,5},{3,7},... | collective-permute-start | bytes 393224 | tf_op jit(solution)/shard_map/ppermute | solution.py:206
  7.3 1.5 %collective-permute-start = (bf16[32,2048]{1,0:T(8,128)(2,1)S(1)}, bf16[32,2048]{1,0:T(8,128)(2,1)S(1)}, u32[]{:S(2)}, u32[]{:S(2)}) collective-permute-start(bf16[32,2048]{1,0:T(8,128)(2,1)S(1)} %convert_element_type.27.refs_0_), channel_id=1, source_target_pairs={{0,2},{2,0},{4,6},{6,4},{8,10},{10,8},{12,14},{14,12},{1,3},{3,1},... | collective-permute-start | bytes 393224 | tf_op jit(solution)/shard_map/ppermute | solution.py:206
  8.8 3.3 %collective-permute-done.2.refs_1_ = bf16[32,2048]{1,0:T(8,128)(2,1)S(1)} collective-permute-done((bf16[32,2048]{1,0:T(8,128)(2,1)S(1)}, bf16[32,2048]{1,0:T(8,128)(2,1)S(1)}, u32[]{:S(2)}, u32[]{:S(2)}) %collective-permute-start.2) | collective-permute-done | bytes 131104 | tf_op jit(solution)/shard_map/ppermute | solution.py:206
  12.4 1.5 %collective-permute-start.5 = (bf16[32,2048]{1,0:T(8,128)(2,1)S(1)}, bf16[32,2048]{1,0:T(8,128)(2,1)S(1)}, u32[]{:S(2)}, u32[]{:S(2)}) collective-permute-start(bf16[32,2048]{1,0:T(8,128)(2,1)S(1)} %collective-permute-done.2.refs_1_), channel_id=1, source_target_pairs={{0,4},{2,6},{4,0},{6,2},{8,12},{10,14},{12,8},{14,10},{1,5},{3,7},... | collective-permute-start | bytes 393224 | tf_op jit(solution)/shard_map/ppermute | solution.py:206
  13.9 1.5 %collective-permute-start.4 = (bf16[64,2048]{1,0:T(8,128)(2,1)S(1)}, bf16[64,2048]{1,0:T(8,128)(2,1)S(1)}, u32[]{:S(2)}, u32[]{:S(2)}) collective-permute-start(bf16[64,2048]{1,0:T(8,128)(2,1)S(1)} %shard_map.78.refs_2_), channel_id=1, source_target_pairs={{0,2},{2,0},{4,6},{6,4},{8,10},{10,8},{12,14},{14,12},{1,3},{3,1},... | collective-permute-start | bytes 786440 | tf_op jit(solution)/shard_map/ppermute | solution.py:206
  15.4 2.9 %collective-permute-done.5.refs_4_ = bf16[32,2048]{1,0:T(8,128)(2,1)S(1)} collective-permute-done((bf16[32,2048]{1,0:T(8,128)(2,1)S(1)}, bf16[32,2048]{1,0:T(8,128)(2,1)S(1)}, u32[]{:S(2)}, u32[]{:S(2)}) %collective-permute-start.5) | collective-permute-done | bytes 131104 | tf_op jit(solution)/shard_map/ppermute | solution.py:206
  18.3 1.5 %collective-permute-start.6 = (bf16[32,2048]{1,0:T(8,128)(2,1)S(1)}, bf16[32,2048]{1,0:T(8,128)(2,1)S(1)}, u32[]{:S(2)}, u32[]{:S(2)}) collective-permute-start(bf16[32,2048]{1,0:T(8,128)(2,1)S(1)} %collective-permute-done.5.refs_4_), channel_id=1, source_target_pairs={{0,2},{2,0},{4,6},{6,4},{8,10},{10,8},{12,14},{14,12},{1,3},{3,1},... | collective-permute-start | bytes 393224 | tf_op jit(solution)/shard_map/ppermute | solution.py:206
  20.5 1.6 %copy-done = bf16[1,1,64,128,128]{4,3,2,1,0:T(8,128)(2,1)S(1)} copy-done((bf16[1,1,64,128,128]{4,3,2,1,0:T(8,128)(2,1)S(1)}, bf16[1,1,64,128,128]{4,3,2,1,0:T(8,128)(2,1)}, u32[]{:S(2)}) %copy-start) | copy-done | bytes 2097176
  22.1 0.7 %copy-done.3 = s32[1,1,64]{2,1,0:T(1,128)S(1)} copy-done((s32[1,1,64]{2,1,0:T(1,128)S(1)}, s32[1,1,64]{2,1,0:T(1,128)}, u32[]{:S(2)}) %copy-start.3) | copy-done | bytes 280
  22.8 0.7 %copy-done.4 = s32[1,1,64]{2,1,0:T(1,128)S(1)} copy-done((s32[1,1,64]{2,1,0:T(1,128)S(1)}, s32[1,1,64]{2,1,0:T(1,128)}, u32[]{:S(2)}) %copy-start.4) | copy-done | bytes 280
  23.4 2.6 %shard_map.77.tile = bf16[1024,2048]{1,0:T(8,128)(2,1)S(1)} custom-call(s32[64]{0:T(128)S(1)} %bitcast.6, s32[64]{0:T(128)S(1)} %bitcast.7, s32[1]{0:T(128)} %bitcast.4.count, bf16[64,128,128]{2,1,0:T(8,128)(2,1)S(1)} %bitcast.5), custom_call_target="tpu_custom_call" | custom-call | tf_op jit(solution)/shard_map/pallas_call | solution.py:81
  26.0 1.6 %shard_map.79 = (bf16[256,2048]{1,0:T(8,128)(2,1)S(1)}, f32[256,1280]{1,0:T(8,128)S(1)}, bf16[256,1280]{1,0:T(8,128)(2,1)S(1)}) custom-call(bf16[1024,2048]{1,0:T(8,128)(2,1)S(1)} %shard_map.77.tile, bf16[32,2048]{1,0:T(8,128)(2,1)S(1)} %convert_element_type.27.refs_0_, bf16[32,2048]{1,0:T(8,128)(2,1)S(1)} %collective-permute-done.refs_1_, ...), custom_call_target="tpu_custom_call" | custom-call | tf_op jit(solution)/shard_map/pallas_call | solution.py:230
  27.7 2.1 %collective-permute-done.7.other = bf16[256,1280]{1,0:T(8,128)(2,1)S(1)} collective-permute-done((bf16[256,1280]{1,0:T(8,128)(2,1)S(1)}, bf16[256,1280]{1,0:T(8,128)(2,1)S(1)}, u32[]{:S(2)}, u32[]{:S(2)}) %collective-permute-start.7) | collective-permute-done | bytes 655392 | tf_op jit(solution)/shard_map/ppermute | solution.py:209
  29.8 2.0 %shard_map.80 = (f32[128,1024]{1,0:T(8,128)}, bf16[256,1024]{1,0:T(8,128)(2,1)S(1)}, bf16[32,2048]{1,0:T(8,128)(2,1)S(1)}, bf16[32,2048]{1,0:T(8,128)(2,1)S(1)}, bf16[64,2048]{1,0:T(8,128)(2,1)S(1)}) custom-call(bf16[1024,2048]{1,0:T(8,128)(2,1)S(1)} %shard_map.77.tile, f32[256,1280]{1,0:T(8,128)S(1)} %get-tuple-element.38.mine, ...), custom_call_target="tpu_custom_call" | custom-call | tf_op jit(solution)/shard_map/pallas_call | solution.py:246
  31.8 0.6 collective-permute-start.9
  32.4 0.9 %shard_map.81 = (bf16[16,2048]{1,0:T(8,128)(2,1)S(1)}, f32[32,2048]{1,0:T(8,128)S(1)}, f32[32,2048]{1,0:T(8,128)S(1)}, f32[32,2048]{1,0:T(8,128)S(1)}, f32[32,2048]{1,0:T(8,128)S(1)}) custom-call(bf16[256,1024]{1,0:T(8,128)(2,1)S(1)} %get-tuple-element.42.low, bf16[1024,2048]{1,0:T(8,128)(2,1)S(1)} %shard_map.77.tile), custom_call_target="tpu_custom_call" | custom-call | bytes 16777216 | tf_op jit(solution)/shard_map/pallas_call | solution.py:284
  33.3 2.4 %collective-permute-start.8 = (bf16[16,2048]{1,0:T(8,128)(2,1)S(1)}, bf16[16,2048]{1,0:T(8,128)(2,1)S(1)}, u32[]{:S(2)}, u32[]{:S(2)}) collective-permute-start(bf16[16,2048]{1,0:T(8,128)(2,1)S(1)} %get-tuple-element.43), channel_id=1, source_target_pairs={{0,8},{2,10},{4,12},{6,14},{8,0},{10,2},{12,4},{14,6},{1,9},{3,11}... | collective-permute-start | bytes 196616 | tf_op jit(solution)/shard_map/ppermute | solution.py:206
  35.7 0.5 collective-permute-start.12
  36.2 1.6 %collective-permute-start.11 = (bf16[64,2048]{1,0:T(8,128)(2,1)S(1)}, bf16[64,2048]{1,0:T(8,128)(2,1)S(1)}, u32[]{:S(2)}, u32[]{:S(2)}) collective-permute-start(bf16[64,2048]{1,0:T(8,128)(2,1)S(1)} %get-tuple-element.48), channel_id=1, source_target_pairs={{0,4},{2,6},{4,0},{6,2},{8,12},{10,14},{12,8},{14,10},{1,5},{3,7},... | collective-permute-start | bytes 786440 | tf_op jit(solution)/shard_map/ppermute | solution.py:206
  37.9 1.7 %collective-permute-done.8 = bf16[16,2048]{1,0:T(8,128)(2,1)S(1)} collective-permute-done((bf16[16,2048]{1,0:T(8,128)(2,1)S(1)}, bf16[16,2048]{1,0:T(8,128)(2,1)S(1)}, u32[]{:S(2)}, u32[]{:S(2)}) %collective-permute-start.8) | collective-permute-done | bytes 65568 | tf_op jit(solution)/shard_map/ppermute | solution.py:206
  39.7 2.9 %collective-permute-start.16 = (bf16[32,2048]{1,0:T(8,128)(2,1)S(1)}, bf16[32,2048]{1,0:T(8,128)(2,1)S(1)}, u32[]{:S(2)}, u32[]{:S(2)}) collective-permute-start(bf16[32,2048]{1,0:T(8,128)(2,1)S(1)} %shard_map.82), channel_id=1, source_target_pairs={{0,12},{2,14},{4,8},{6,10},{8,4},{10,6},{12,0},{14,2},{1,13},{3,15... | collective-permute-start | bytes 393224 | tf_op jit(solution)/shard_map/ppermute | solution.py:206
  42.7 3.2 %collective-permute-done.11.beside = bf16[64,2048]{1,0:T(8,128)(2,1)S(1)} collective-permute-done((bf16[64,2048]{1,0:T(8,128)(2,1)S(1)}, bf16[64,2048]{1,0:T(8,128)(2,1)S(1)}, u32[]{:S(2)}, u32[]{:S(2)}) %collective-permute-start.11) | collective-permute-done | bytes 262176 | tf_op jit(solution)/shard_map/ppermute | solution.py:206
  45.9 1.3 %collective-permute-done.10 = bf16[16,2048]{1,0:T(8,128)(2,1)S(1)} collective-permute-done((bf16[16,2048]{1,0:T(8,128)(2,1)S(1)}, bf16[16,2048]{1,0:T(8,128)(2,1)S(1)}, u32[]{:S(2)}, u32[]{:S(2)}) %collective-permute-start.10) | collective-permute-done | bytes 65568 | tf_op jit(solution)/shard_map/ppermute | solution.py:206
  47.2 0.8 %collective-permute-start.14 = (bf16[32,2048]{1,0:T(8,128)(2,1)S(1)}, bf16[32,2048]{1,0:T(8,128)(2,1)S(1)}, u32[]{:S(2)}, u32[]{:S(2)}) collective-permute-start(bf16[32,2048]{1,0:T(8,128)(2,1)S(1)} %shard_map.83), channel_id=1, source_target_pairs={{0,8},{2,10},{4,12},{6,14},{8,0},{10,2},{12,4},{14,6},{1,9},{3,11}... | collective-permute-start | bytes 393224 | tf_op jit(solution)/shard_map/ppermute | solution.py:206
  48.1 1.1 %collective-permute-start.13 = (bf16[16,2048]{1,0:T(8,128)(2,1)S(1)}, bf16[16,2048]{1,0:T(8,128)(2,1)S(1)}, u32[]{:S(2)}, u32[]{:S(2)}) collective-permute-start(bf16[16,2048]{1,0:T(8,128)(2,1)S(1)} %add_convert_fusion), channel_id=1, source_target_pairs={{0,2},{2,0},{4,6},{6,4},{8,10},{10,8},{12,14},{14,12},{1,3},{3,1},... | collective-permute-start | bytes 196616 | tf_op jit(solution)/shard_map/ppermute | solution.py:206
  49.4 1.9 %collective-permute-start.17 = (bf16[32,2048]{1,0:T(8,128)(2,1)S(1)}, bf16[32,2048]{1,0:T(8,128)(2,1)S(1)}, u32[]{:S(2)}, u32[]{:S(2)}) collective-permute-start(bf16[32,2048]{1,0:T(8,128)(2,1)S(1)} %get-tuple-element.61), channel_id=1, source_target_pairs={{0,2},{2,0},{4,6},{6,4},{8,10},{10,8},{12,14},{14,12},{1,3},{3,1},... | collective-permute-start | bytes 393224 | tf_op jit(solution)/shard_map/ppermute | solution.py:206
  51.2 1.2 %collective-permute-done.13 = bf16[16,2048]{1,0:T(8,128)(2,1)S(1)} collective-permute-done((bf16[16,2048]{1,0:T(8,128)(2,1)S(1)}, bf16[16,2048]{1,0:T(8,128)(2,1)S(1)}, u32[]{:S(2)}, u32[]{:S(2)}) %collective-permute-start.13) | collective-permute-done | bytes 65568 | tf_op jit(solution)/shard_map/ppermute | solution.py:206
  52.4 2.1 %collective-permute-done.14.second = bf16[32,2048]{1,0:T(8,128)(2,1)S(1)} collective-permute-done((bf16[32,2048]{1,0:T(8,128)(2,1)S(1)}, bf16[32,2048]{1,0:T(8,128)(2,1)S(1)}, u32[]{:S(2)}, u32[]{:S(2)}) %collective-permute-start.14) | collective-permute-done | bytes 131104 | tf_op jit(solution)/shard_map/ppermute | solution.py:206
  54.6 1.3 %collective-permute-done.15.other = f32[16,2048]{1,0:T(8,128)S(1)} collective-permute-done((f32[16,2048]{1,0:T(8,128)S(1)}, f32[16,2048]{1,0:T(8,128)S(1)}, u32[]{:S(2)}, u32[]{:S(2)}) %collective-permute-start.15) | collective-permute-done | bytes 131104 | tf_op jit(solution)/shard_map/ppermute | solution.py:209
  56.0 1.0 %shard_map.85 = f32[32,2048]{1,0:T(8,128)} custom-call(f32[16,2048]{1,0:T(8,128)S(1)} %convert_add_fusion.mine, f32[16,2048]{1,0:T(8,128)S(1)} %collective-permute-done.15.other, bf16[256,2048]{1,0:T(8,128)(2,1)S(1)} %get-tuple-element.54.panel, f32[32,2048]{1,0:T(8,128)S(1)} %copy-done.1, f32[32,2048]{1,0:T(8,128)S(1)} %get-tuple-element.59.partial, ...), custom_call_target="tpu_custom_call" | custom-call | tf_op jit(solution)/shard_map/pallas_call | solution.py:310
  (27 shorter events, 0.9 us)
Async XLA Ops:
  1.6 10.5 %collective-permute-start.2 = (bf16[32,2048]{1,0:T(8,128)(2,1)S(1)}, bf16[32,2048]{1,0:T(8,128)(2,1)S(1)}, u32[]{:S(2)}, u32[]{:S(2)}) collective-permute-start(bf16[32,2048]{1,0:T(8,128)(2,1)S(1)} %convert_element_type.27.refs_0_), channel_id=1, source_target_pairs={{0,8},{2,10},{4,12},{6,14},{8,0},{10,2},{12,4},{14,6},{1,9},{3,11}... | collective-permute-start | bytes 393224 | tf_op jit(solution)/shard_map/ppermute | solution.py:206
  5.7 6.6 %collective-permute-start.1 = (bf16[32,2048]{1,0:T(8,128)(2,1)S(1)}, bf16[32,2048]{1,0:T(8,128)(2,1)S(1)}, u32[]{:S(2)}, u32[]{:S(2)}) collective-permute-start(bf16[32,2048]{1,0:T(8,128)(2,1)S(1)} %convert_element_type.27.refs_0_), channel_id=1, source_target_pairs={{0,4},{2,6},{4,0},{6,2},{8,12},{10,14},{12,8},{14,10},{1,5},{3,7},... | collective-permute-start | bytes 393224 | tf_op jit(solution)/shard_map/ppermute | solution.py:206
  7.3 5.0 %collective-permute-start = (bf16[32,2048]{1,0:T(8,128)(2,1)S(1)}, bf16[32,2048]{1,0:T(8,128)(2,1)S(1)}, u32[]{:S(2)}, u32[]{:S(2)}) collective-permute-start(bf16[32,2048]{1,0:T(8,128)(2,1)S(1)} %convert_element_type.27.refs_0_), channel_id=1, source_target_pairs={{0,2},{2,0},{4,6},{6,4},{8,10},{10,8},{12,14},{14,12},{1,3},{3,1},... | collective-permute-start | bytes 393224 | tf_op jit(solution)/shard_map/ppermute | solution.py:206
  12.3 13.7 %collective-permute-start.3 = (f32[128,1024]{1,0:T(8,128)}, f32[128,1024]{1,0:T(8,128)S(1)}, u32[]{:S(2)}, u32[]{:S(2)}) collective-permute-start(f32[128,1024]{1,0:T(8,128)} %factor_mine.1), channel_id=1, source_target_pairs={{0,1},{1,0},{2,3},{3,2},{4,5},{5,4},{6,7},{7,6},{8,9},{9,8},{10,11... | collective-permute-start | bytes 1572872 | tf_op jit(solution)/shard_map/ppermute | solution.py:209
  12.4 5.9 %collective-permute-start.5 = (bf16[32,2048]{1,0:T(8,128)(2,1)S(1)}, bf16[32,2048]{1,0:T(8,128)(2,1)S(1)}, u32[]{:S(2)}, u32[]{:S(2)}) collective-permute-start(bf16[32,2048]{1,0:T(8,128)(2,1)S(1)} %collective-permute-done.2.refs_1_), channel_id=1, source_target_pairs={{0,4},{2,6},{4,0},{6,2},{8,12},{10,14},{12,8},{14,10},{1,5},{3,7},... | collective-permute-start | bytes 393224 | tf_op jit(solution)/shard_map/ppermute | solution.py:206
  13.9 12.1 %collective-permute-start.4 = (bf16[64,2048]{1,0:T(8,128)(2,1)S(1)}, bf16[64,2048]{1,0:T(8,128)(2,1)S(1)}, u32[]{:S(2)}, u32[]{:S(2)}) collective-permute-start(bf16[64,2048]{1,0:T(8,128)(2,1)S(1)} %shard_map.78.refs_2_), channel_id=1, source_target_pairs={{0,2},{2,0},{4,6},{6,4},{8,10},{10,8},{12,14},{14,12},{1,3},{3,1},... | collective-permute-start | bytes 786440 | tf_op jit(solution)/shard_map/ppermute | solution.py:206
  18.3 7.7 %collective-permute-start.6 = (bf16[32,2048]{1,0:T(8,128)(2,1)S(1)}, bf16[32,2048]{1,0:T(8,128)(2,1)S(1)}, u32[]{:S(2)}, u32[]{:S(2)}) collective-permute-start(bf16[32,2048]{1,0:T(8,128)(2,1)S(1)} %collective-permute-done.5.refs_4_), channel_id=1, source_target_pairs={{0,2},{2,0},{4,6},{6,4},{8,10},{10,8},{12,14},{14,12},{1,3},{3,1},... | collective-permute-start | bytes 393224 | tf_op jit(solution)/shard_map/ppermute | solution.py:206
  20.5 1.6 %copy-start = (bf16[1,1,64,128,128]{4,3,2,1,0:T(8,128)(2,1)S(1)}, bf16[1,1,64,128,128]{4,3,2,1,0:T(8,128)(2,1)}, u32[]{:S(2)}) copy-start(bf16[1,1,64,128,128]{4,3,2,1,0:T(8,128)(2,1)} %param.6) | copy-start | bytes 6291460
  22.1 0.7 %copy-start.3 = (s32[1,1,64]{2,1,0:T(1,128)S(1)}, s32[1,1,64]{2,1,0:T(1,128)}, u32[]{:S(2)}) copy-start(s32[1,1,64]{2,1,0:T(1,128)} %param.7) | copy-start | bytes 772
  22.8 0.7 %copy-start.4 = (s32[1,1,64]{2,1,0:T(1,128)S(1)}, s32[1,1,64]{2,1,0:T(1,128)}, u32[]{:S(2)}) copy-start(s32[1,1,64]{2,1,0:T(1,128)} %param.8) | copy-start | bytes 772
  26.0 3.8 %copy-start.2 = (f32[128,1024]{1,0:T(8,128)S(1)}, f32[128,1024]{1,0:T(8,128)}, u32[]{:S(2)}) copy-start(f32[128,1024]{1,0:T(8,128)} %factor_mine.1) | copy-start | bytes 1572868
  27.6 2.2 %collective-permute-start.7 = (bf16[256,1280]{1,0:T(8,128)(2,1)S(1)}, bf16[256,1280]{1,0:T(8,128)(2,1)S(1)}, u32[]{:S(2)}, u32[]{:S(2)}) collective-permute-start(bf16[256,1280]{1,0:T(8,128)(2,1)S(1)} %get-tuple-element.39), channel_id=1, source_target_pairs={{0,1},{1,0},{2,3},{3,2},{4,5},{5,4},{6,7},{7,6},{8,9},{9,8},{10,11... | collective-permute-start | bytes 1966088 | tf_op jit(solution)/shard_map/ppermute | solution.py:209
  31.8 6.1 %collective-permute-start.9 = (bf16[32,2048]{1,0:T(8,128)(2,1)S(1)}, bf16[32,2048]{1,0:T(8,128)(2,1)S(1)}, u32[]{:S(2)}, u32[]{:S(2)}) collective-permute-start(bf16[32,2048]{1,0:T(8,128)(2,1)S(1)} %get-tuple-element.45), channel_id=1, source_target_pairs={{0,2},{2,0},{4,6},{6,4},{8,10},{10,8},{12,14},{14,12},{1,3},{3,1},... | collective-permute-start | bytes 393224 | tf_op jit(solution)/shard_map/ppermute | solution.py:206
  33.3 22.7 %copy-start.1 = (f32[32,2048]{1,0:T(8,128)S(1)}, f32[32,2048]{1,0:T(8,128)}, u32[]{:S(2)}) copy-start(f32[32,2048]{1,0:T(8,128)} %factor.1) | copy-start | bytes 786436
  33.3 6.3 %collective-permute-start.8 = (bf16[16,2048]{1,0:T(8,128)(2,1)S(1)}, bf16[16,2048]{1,0:T(8,128)(2,1)S(1)}, u32[]{:S(2)}, u32[]{:S(2)}) collective-permute-start(bf16[16,2048]{1,0:T(8,128)(2,1)S(1)} %get-tuple-element.43), channel_id=1, source_target_pairs={{0,8},{2,10},{4,12},{6,14},{8,0},{10,2},{12,4},{14,6},{1,9},{3,11}... | collective-permute-start | bytes 196616 | tf_op jit(solution)/shard_map/ppermute | solution.py:206
  35.7 7.0 %collective-permute-start.12 = (bf16[32,2048]{1,0:T(8,128)(2,1)S(1)}, bf16[32,2048]{1,0:T(8,128)(2,1)S(1)}, u32[]{:S(2)}, u32[]{:S(2)}) collective-permute-start(bf16[32,2048]{1,0:T(8,128)(2,1)S(1)} %get-tuple-element.49), channel_id=1, source_target_pairs={{0,2},{2,0},{4,6},{6,4},{8,10},{10,8},{12,14},{14,12},{1,3},{3,1},... | collective-permute-start | bytes 393224 | tf_op jit(solution)/shard_map/ppermute | solution.py:206
  36.2 9.6 %collective-permute-start.11 = (bf16[64,2048]{1,0:T(8,128)(2,1)S(1)}, bf16[64,2048]{1,0:T(8,128)(2,1)S(1)}, u32[]{:S(2)}, u32[]{:S(2)}) collective-permute-start(bf16[64,2048]{1,0:T(8,128)(2,1)S(1)} %get-tuple-element.48), channel_id=1, source_target_pairs={{0,4},{2,6},{4,0},{6,2},{8,12},{10,14},{12,8},{14,10},{1,5},{3,7},... | collective-permute-start | bytes 786440 | tf_op jit(solution)/shard_map/ppermute | solution.py:206
  39.6 7.6 %collective-permute-start.10 = (bf16[16,2048]{1,0:T(8,128)(2,1)S(1)}, bf16[16,2048]{1,0:T(8,128)(2,1)S(1)}, u32[]{:S(2)}, u32[]{:S(2)}) collective-permute-start(bf16[16,2048]{1,0:T(8,128)(2,1)S(1)} %add_convert_fusion.1), channel_id=1, source_target_pairs={{0,4},{2,6},{4,0},{6,2},{8,12},{10,14},{12,8},{14,10},{1,5},{3,7},... | collective-permute-start | bytes 196616 | tf_op jit(solution)/shard_map/ppermute | solution.py:206
  39.7 9.6 %collective-permute-start.16 = (bf16[32,2048]{1,0:T(8,128)(2,1)S(1)}, bf16[32,2048]{1,0:T(8,128)(2,1)S(1)}, u32[]{:S(2)}, u32[]{:S(2)}) collective-permute-start(bf16[32,2048]{1,0:T(8,128)(2,1)S(1)} %shard_map.82), channel_id=1, source_target_pairs={{0,12},{2,14},{4,8},{6,10},{8,4},{10,6},{12,0},{14,2},{1,13},{3,15... | collective-permute-start | bytes 393224 | tf_op jit(solution)/shard_map/ppermute | solution.py:206
  47.2 7.3 %collective-permute-start.14 = (bf16[32,2048]{1,0:T(8,128)(2,1)S(1)}, bf16[32,2048]{1,0:T(8,128)(2,1)S(1)}, u32[]{:S(2)}, u32[]{:S(2)}) collective-permute-start(bf16[32,2048]{1,0:T(8,128)(2,1)S(1)} %shard_map.83), channel_id=1, source_target_pairs={{0,8},{2,10},{4,12},{6,14},{8,0},{10,2},{12,4},{14,6},{1,9},{3,11}... | collective-permute-start | bytes 393224 | tf_op jit(solution)/shard_map/ppermute | solution.py:206
  48.1 4.3 %collective-permute-start.13 = (bf16[16,2048]{1,0:T(8,128)(2,1)S(1)}, bf16[16,2048]{1,0:T(8,128)(2,1)S(1)}, u32[]{:S(2)}, u32[]{:S(2)}) collective-permute-start(bf16[16,2048]{1,0:T(8,128)(2,1)S(1)} %add_convert_fusion), channel_id=1, source_target_pairs={{0,2},{2,0},{4,6},{6,4},{8,10},{10,8},{12,14},{14,12},{1,3},{3,1},... | collective-permute-start | bytes 196616 | tf_op jit(solution)/shard_map/ppermute | solution.py:206
  49.4 5.2 %collective-permute-start.17 = (bf16[32,2048]{1,0:T(8,128)(2,1)S(1)}, bf16[32,2048]{1,0:T(8,128)(2,1)S(1)}, u32[]{:S(2)}, u32[]{:S(2)}) collective-permute-start(bf16[32,2048]{1,0:T(8,128)(2,1)S(1)} %get-tuple-element.61), channel_id=1, source_target_pairs={{0,2},{2,0},{4,6},{6,4},{8,10},{10,8},{12,14},{14,12},{1,3},{3,1},... | collective-permute-start | bytes 393224 | tf_op jit(solution)/shard_map/ppermute | solution.py:206
  54.5 1.4 %collective-permute-start.15 = (f32[16,2048]{1,0:T(8,128)S(1)}, f32[16,2048]{1,0:T(8,128)S(1)}, u32[]{:S(2)}, u32[]{:S(2)}) collective-permute-start(f32[16,2048]{1,0:T(8,128)S(1)} %convert_add_fusion.mine), channel_id=1, source_target_pairs={{0,1},{1,0},{2,3},{3,2},{4,5},{5,4},{6,7},{7,6},{8,9},{9,8},{10,11... | collective-permute-start | bytes 393224 | tf_op jit(solution)/shard_map/ppermute | solution.py:209

commit v6 on v5

--- a/solution.py
+++ b/solution.py
@@ -11,6 +11,7 @@
 CELL_DEV = 1024
 GENE_DEV = 2048
 VMEM_BYTES = 24 * 2**20
+AHEAD = 16 * 2**20
 
 NT = (((1,), (1,)), ((), ()))
 NN = (((1,), (0,)), ((), ()))
@@ -75,8 +76,12 @@
     lax.fori_loop(0, count[0], wait, 0)
 
 
+def pinned(array):
+    return pltpu.with_memory_space_constraint(array, pltpu.HBM)
+
+
 def dense_tile(values, rows, cols, count):
-    anywhere = pl.BlockSpec(memory_space=pl.ANY)
+    anywhere = pl.BlockSpec(memory_space=pltpu.HBM)
     n_blocks = values.shape[0]
     return pl.pallas_call(
         dense_body,
@@ -90,8 +95,8 @@
             pltpu.SemaphoreType.DMA((2,)),
         ],
         compiler_params=pltpu.CompilerParams(vmem_limit_bytes=VMEM_BYTES),
-        cost_estimate=pl.CostEstimate(flops=0, bytes_accessed=0, transcendentals=0),
-    )(rows, cols, count, values)
+        cost_estimate=pl.CostEstimate(flops=0, bytes_accessed=AHEAD, transcendentals=0),
+    )(pinned(rows), pinned(cols), count, pinned(values))
 
 
 def owned(bits, size):
@@ -169,13 +174,17 @@
     out[...] = (keep[...] + arrived[...].astype(jnp.float32)).astype(out.dtype)
 
 
-def turn_body(keep, own, beside, third, out, partial):
+def turn_body(keep, own, arrived, third, out, partial):
     size = own.shape[0]
-    out[...] = (keep[...] + beside[size:].astype(jnp.float32)).astype(out.dtype)
-    partial[...] = own[...] + beside[:size].astype(jnp.float32) + third[...].astype(jnp.float32)
-
-
-def last_body(mine, other, panel, factor, partial, second, last, out, gram):
+    out[...] = (keep[...] + arrived[:size].astype(jnp.float32)).astype(out.dtype)
+    partial[...] = own[...] + arrived[size:].astype(jnp.float32) + third[...].astype(jnp.float32)
+
+
+def add_body(partial, arrived, out):
+    out[...] = partial[...] + arrived[...].astype(jnp.float32)
+
+
+def last_body(mine, other, panel, factor, partial, last, out, gram):
     rows, width = mine.shape[0], gram.shape[1]
     core = lax.axis_index("gene")
     for half, part in ((core, mine), (1 - core, other)):
@@ -186,7 +195,7 @@
     norm = jnp.sum(jnp.sum(whole * whole, axis=1, keepdims=True), axis=0, keepdims=True)
     rate = 1.0 / (jnp.sqrt(norm) + 1e-06)
     stepped = split_dot(gram[owned(0, factor.shape[0])], panel[...])
-    data = partial[...] + second[...].astype(jnp.float32) + last[...].astype(jnp.float32)
+    data = partial[...] + last[...].astype(jnp.float32)
     out[...] = jnp.maximum(factor[...] - rate * (stepped - data), 0.0)
 
 
@@ -212,19 +221,21 @@
         return shape((rows, GENE_DEV), dtype)
 
     low_share = gene_factor.astype(jnp.bfloat16)
-    tile = dense_tile(block_values[0, 0], block_rows[0, 0], block_cols[0, 0], block_count[0])
+    values = block_values[0, 0]
     if paired:
         near = [swap(low_share, bits) for bits in (1, 2, 4)]
         beside, second, fourth = lax.optimization_barrier(near)
         sixth = swap(fourth, 2)
         both = call(join_body, wide(2 * size, jnp.bfloat16), 0, 2, 0, 0)(second, fourth)
         both, factor = lax.optimization_barrier((both, cell_factor))
-        shares = [low_share, beside, both, swap(both, 1), sixth, swap(sixth, 1)]
+        both_beside, values = lax.optimization_barrier((swap(both, 1), values))
+        shares = [low_share, beside, both, both_beside, sixth, swap(sixth, 1)]
         order = [0, 1, 2, 4, 3, 5, 6, 7]
     else:
         shares = [lax.all_gather(low_share, "cell", axis=0, tiled=True)]
         order, factor = None, cell_factor
     factor_other = swap_core(factor)
+    tile = dense_tile(values, block_rows[0, 0], block_cols[0, 0], block_count[0])
 
     shares[0], factor_other = lax.optimization_barrier((shares[0], factor_other))
     panel, mine, message = call(
@@ -241,8 +252,8 @@
     )(tile, *shares)
     other = swap_core(message)
 
-    sent = [7, 5, 2, 3]
-    kept = [6, 4, 1, 0]
+    sent = [7, 5, 3, 1]
+    kept = [6, 4, 2, 0]
     cell_next, next_low, *sends = call(
         functools.partial(cell_body, sent),
         (
@@ -279,43 +290,43 @@
         )
         return (cell_next, jnp.maximum(gene_factor - rate_gene * (stepped - own_cols), 0.0))
 
-    arrived_third, arrived_second = swap(sends[0], 1), swap(sends[1], 1)
-    beside = swap(sends[2], 2)
+    arrived = [swap(part, 1) for part in sends]
     gram, *keeps = call(
         functools.partial(keep_body, kept),
         (wide(gram_rows, jnp.bfloat16), *[wide(size, jnp.float32) for _ in kept]),
         0,
         2,
         0,
-        16 * 2**20,
+        AHEAD,
         [pltpu.VMEM((half, CELL_DEV), jnp.bfloat16)],
     )(next_low, tile)
     gram_arrived = swap(gram, 4)
-    third = call(sum_body, wide(size, jnp.bfloat16), 0, 2, 0, 16 * 2**20)(keeps[0], arrived_third)
-    gram_arrived, third = lax.optimization_barrier((gram_arrived, third))
+    third = call(sum_body, wide(size, jnp.bfloat16), 0, 2, 0, AHEAD)(keeps[0], arrived[0])
+    second = call(sum_body, wide(size, jnp.bfloat16), 0, 2, 0, AHEAD)(keeps[1], arrived[1])
+    gram_arrived, second, third = lax.optimization_barrier((gram_arrived, second, third))
     third = swap(third, 6)
+    second = swap(second, 4)
     gram = (gram.astype(jnp.float32) + gram_arrived.astype(jnp.float32)).astype(jnp.bfloat16)
     gram_arrived = swap(gram, 2)
-    beside, arrived_second = lax.optimization_barrier((beside, arrived_second))
-    second = call(sum_body, wide(size, jnp.bfloat16), 0, 2, 0, 16 * 2**20)(keeps[1], arrived_second)
-    gram_arrived, second = lax.optimization_barrier((gram_arrived, second))
-    second = swap(second, 4)
+    message, partial = call(
+        turn_body, (wide(size, jnp.bfloat16), wide(size, jnp.float32)), 0, 4, 0, 0
+    )(keeps[2], keeps[3], arrived[2], third)
+    last = swap(message, 2)
+    gram_arrived, partial = lax.optimization_barrier((gram_arrived, partial))
     gram = (gram.astype(jnp.float32) + gram_arrived.astype(jnp.float32)).astype(jnp.bfloat16)
-    message, partial = call(
-        turn_body, (wide(size, jnp.bfloat16), wide(size, jnp.float32)), 0, 4, 0, 16 * 2**20
-    )(keeps[2], keeps[3], beside, third)
-    last = swap(message, 1)
-    gram_arrived, second = lax.optimization_barrier((swap(gram, 1), second))
+    gram_arrived = swap(gram, 1)
+    partial = call(add_body, wide(size, jnp.float32), 0, 2, 0, AHEAD)(partial, second)
+    gram_arrived, partial = lax.optimization_barrier((gram_arrived, partial))
     gram = gram.astype(jnp.float32) + gram_arrived.astype(jnp.float32)
     gene_next = call(
         last_body,
         wide(size, jnp.float32),
         0,
-        7,
+        6,
         0,
         0,
         [pltpu.VMEM((kdim, kdim), jnp.float32)],
-    )(gram, swap_core(gram), panel, gene_factor, partial, second, last)
+    )(gram, swap_core(gram), panel, gene_factor, partial, last)
     return (cell_next, gene_next)
 
 

time: 57.3 us -> 56.9 us (level)
  local copies, waits for them, and re-layouts: 2.91 us -> 0.01 us
  starting transfers between devices: 23.9 us -> 25.2 us
  waiting for transfers between devices: 19.6 us -> 20.5 us
    unnamed x10 -> x4, local copies, waits for them, and re-layouts: 2.91 us -> 0.01 us
    ppermute x15, waiting for transfers between devices: 16.1 us -> 18.4 us  [swap(): return lax.ppermute(value, 'cell', [(n, n ^ bits) for n in range(n_cell)])]
    ppermute x3, waiting for transfers between devices: 3.41 us -> 2.09 us  [swap_core(): return lax.ppermute(value, 'gene', [(0, 1), (1, 0)])]
    ppermute x15, starting transfers between devices: 23.7 us -> 24.9 us  [swap(): return lax.ppermute(value, 'cell', [(n, n ^ bits) for n in range(n_cell)])]
  transfers between devices with their start and end apart: 18 -> 18, of which waited for: 11 -> 12; matrix products, arithmetic and copies ran while one was open for 0% -> 0% of each run, Pallas kernels for 6% -> 7%
where the time goes in v6:
time: 56.9 us; the launch traced here: 56.6 us
  starting transfers between devices  25.2 us (44%)
  waiting for transfers between devices  20.5 us (36%)
  Pallas kernels  8.5 us (15%)
  between operations  1.43 us (3%)
  other arithmetic  1.02 us (2%)
    ppermute x15, starting transfers between devices, swap(): return lax.ppermute(value, 'cell', [(n, n ^ bits) for n in range(n_cell)])  24.9 us
    ppermute x15, waiting for transfers between devices, swap(): return lax.ppermute(value, 'cell', [(n, n ^ bits) for n in range(n_cell)])  18.4 us
    pallas_call x1, Pallas kernels, dense_tile(): pl.pallas_call(dense_body, out_shape=shape((CELL_DEV, GENE_DEV), jnp.bflo...  2.84 us
    ppermute x3, waiting for transfers between devices, swap_core(): return lax.ppermute(value, 'gene', [(0, 1), (1, 0)])  2.09 us
    pallas_call x1, Pallas kernels, shards(): call(functools.partial(cell_body, sent), (shape(cell_factor.shape, jnp.fl...  2.03 us
    pallas_call x1, Pallas kernels, shards(): call(functools.partial(gene_body, order), (wide(kdim, jnp.bfloat16), shap...  1.57 us
  transfers between devices with their start and end apart: 18, of which 12 were waited for; matrix products, arithmetic and copies ran while one was open for 0% of the time, Pallas kernels for 7%

profile of v6, /device:TPU:0, one launch (start us, length us, event | category | flops | bytes accessed | tf_op | source)
XLA Modules:
  0.0 56.6 jit_solution(8525070065953286881)
XLA Ops:
  0.6 1.0 %convert_element_type.27.refs_0_ = bf16[32,2048]{1,0:T(8,128)(2,1)S(1)} convert(f32[32,2048]{1,0:T(8,128)} %factor.1) | non-fusion elementwise | flops 65536 | bytes 393216 | tf_op jit(solution)/shard_map/convert_element_type | solution.py:223
  1.6 4.1 %collective-permute-start.2 = (bf16[32,2048]{1,0:T(8,128)(2,1)S(1)}, bf16[32,2048]{1,0:T(8,128)(2,1)S(1)}, u32[]{:S(2)}, u32[]{:S(2)}) collective-permute-start(bf16[32,2048]{1,0:T(8,128)(2,1)S(1)} %convert_element_type.27.refs_0_), channel_id=1, source_target_pairs={{0,8},{2,10},{4,12},{6,14},{8,0},{10,2},{12,4},{14,6},{1,9},{3,11}... | collective-permute-start | bytes 393224 | tf_op jit(solution)/shard_map/ppermute | solution.py:215
  5.7 1.6 %collective-permute-start.1 = (bf16[32,2048]{1,0:T(8,128)(2,1)S(1)}, bf16[32,2048]{1,0:T(8,128)(2,1)S(1)}, u32[]{:S(2)}, u32[]{:S(2)}) collective-permute-start(bf16[32,2048]{1,0:T(8,128)(2,1)S(1)} %convert_element_type.27.refs_0_), channel_id=1, source_target_pairs={{0,4},{2,6},{4,0},{6,2},{8,12},{10,14},{12,8},{14,10},{1,5},{3,7},... | collective-permute-start | bytes 393224 | tf_op jit(solution)/shard_map/ppermute | solution.py:215
  7.3 1.5 %collective-permute-start = (bf16[32,2048]{1,0:T(8,128)(2,1)S(1)}, bf16[32,2048]{1,0:T(8,128)(2,1)S(1)}, u32[]{:S(2)}, u32[]{:S(2)}) collective-permute-start(bf16[32,2048]{1,0:T(8,128)(2,1)S(1)} %convert_element_type.27.refs_0_), channel_id=1, source_target_pairs={{0,2},{2,0},{4,6},{6,4},{8,10},{10,8},{12,14},{14,12},{1,3},{3,1},... | collective-permute-start | bytes 393224 | tf_op jit(solution)/shard_map/ppermute | solution.py:215
  8.8 3.3 %collective-permute-done.2.refs_1_ = bf16[32,2048]{1,0:T(8,128)(2,1)S(1)} collective-permute-done((bf16[32,2048]{1,0:T(8,128)(2,1)S(1)}, bf16[32,2048]{1,0:T(8,128)(2,1)S(1)}, u32[]{:S(2)}, u32[]{:S(2)}) %collective-permute-start.2) | collective-permute-done | bytes 131104 | tf_op jit(solution)/shard_map/ppermute | solution.py:215
  12.1 0.2 collective-permute-done.1.refs_0_
  12.4 1.6 %collective-permute-start.3 = (bf16[64,2048]{1,0:T(8,128)(2,1)S(1)}, bf16[64,2048]{1,0:T(8,128)(2,1)S(1)}, u32[]{:S(2)}, u32[]{:S(2)}) collective-permute-start(bf16[64,2048]{1,0:T(8,128)(2,1)S(1)} %shard_map.77.refs_2_), channel_id=1, source_target_pairs={{0,2},{2,0},{4,6},{6,4},{8,10},{10,8},{12,14},{14,12},{1,3},{3,1},... | collective-permute-start | bytes 786440 | tf_op jit(solution)/shard_map/ppermute | solution.py:215
  14.0 1.4 %collective-permute-start.5 = (bf16[32,2048]{1,0:T(8,128)(2,1)S(1)}, bf16[32,2048]{1,0:T(8,128)(2,1)S(1)}, u32[]{:S(2)}, u32[]{:S(2)}) collective-permute-start(bf16[32,2048]{1,0:T(8,128)(2,1)S(1)} %collective-permute-done.2.refs_1_), channel_id=1, source_target_pairs={{0,4},{2,6},{4,0},{6,2},{8,12},{10,14},{12,8},{14,10},{1,5},{3,7},... | collective-permute-start | bytes 393224 | tf_op jit(solution)/shard_map/ppermute | solution.py:215
  15.4 4.2 %collective-permute-done.5.refs_4_ = bf16[32,2048]{1,0:T(8,128)(2,1)S(1)} collective-permute-done((bf16[32,2048]{1,0:T(8,128)(2,1)S(1)}, bf16[32,2048]{1,0:T(8,128)(2,1)S(1)}, u32[]{:S(2)}, u32[]{:S(2)}) %collective-permute-start.5) | collective-permute-done | bytes 131104 | tf_op jit(solution)/shard_map/ppermute | solution.py:215
  19.6 0.5 collective-permute-start.6
  20.7 0.4 collective-permute-done.3.refs_3_
  21.1 2.8 %shard_map.78.tile = bf16[1024,2048]{1,0:T(8,128)(2,1)S(1)} custom-call(s32[64]{0:T(128)} %bitcast.6, s32[64]{0:T(128)} %bitcast.7, s32[1]{0:T(128)} %bitcast.4.count, bf16[64,128,128]{2,1,0:T(8,128)(2,1)} %bitcast.5), custom_call_target="tpu_custom_call" | custom-call | bytes 16777216 | tf_op jit(solution)/shard_map/pallas_call | solution.py:86
  24.0 0.5 collective-permute-done.6.refs_5_
  24.6 1.6 %shard_map.79 = (bf16[256,2048]{1,0:T(8,128)(2,1)S(1)}, f32[256,1280]{1,0:T(8,128)S(1)}, bf16[256,1280]{1,0:T(8,128)(2,1)S(1)}) custom-call(bf16[1024,2048]{1,0:T(8,128)(2,1)S(1)} %shard_map.78.tile, bf16[32,2048]{1,0:T(8,128)(2,1)S(1)} %convert_element_type.27.refs_0_, bf16[32,2048]{1,0:T(8,128)(2,1)S(1)} %collective-permute-done.refs_1_, ...), custom_call_target="tpu_custom_call" | custom-call | tf_op jit(solution)/shard_map/pallas_call | solution.py:241
  26.2 2.1 %collective-permute-done.7.other = bf16[256,1280]{1,0:T(8,128)(2,1)S(1)} collective-permute-done((bf16[256,1280]{1,0:T(8,128)(2,1)S(1)}, bf16[256,1280]{1,0:T(8,128)(2,1)S(1)}, u32[]{:S(2)}, u32[]{:S(2)}) %collective-permute-start.7) | collective-permute-done | bytes 655392 | tf_op jit(solution)/shard_map/ppermute | solution.py:218
  28.3 2.0 %shard_map.80 = (f32[128,1024]{1,0:T(8,128)}, bf16[256,1024]{1,0:T(8,128)(2,1)S(1)}, bf16[32,2048]{1,0:T(8,128)(2,1)S(1)}, bf16[32,2048]{1,0:T(8,128)(2,1)S(1)}, bf16[64,2048]{1,0:T(8,128)(2,1)S(1)}) custom-call(bf16[1024,2048]{1,0:T(8,128)(2,1)S(1)} %shard_map.78.tile, f32[256,1280]{1,0:T(8,128)S(1)} %get-tuple-element.41.mine, ...), custom_call_target="tpu_custom_call" | custom-call | tf_op jit(solution)/shard_map/pallas_call | solution.py:257
  30.3 1.1 %collective-permute-start.9 = (bf16[32,2048]{1,0:T(8,128)(2,1)S(1)}, bf16[32,2048]{1,0:T(8,128)(2,1)S(1)}, u32[]{:S(2)}, u32[]{:S(2)}) collective-permute-start(bf16[32,2048]{1,0:T(8,128)(2,1)S(1)} %get-tuple-element.48), channel_id=1, source_target_pairs={{0,2},{2,0},{4,6},{6,4},{8,10},{10,8},{12,14},{14,12},{1,3},{3,1},... | collective-permute-start | bytes 393224 | tf_op jit(solution)/shard_map/ppermute | solution.py:215
  31.4 0.9 %collective-permute-start.10 = (bf16[32,2048]{1,0:T(8,128)(2,1)S(1)}, bf16[32,2048]{1,0:T(8,128)(2,1)S(1)}, u32[]{:S(2)}, u32[]{:S(2)}) collective-permute-start(bf16[32,2048]{1,0:T(8,128)(2,1)S(1)} %get-tuple-element.50), channel_id=1, source_target_pairs={{0,2},{2,0},{4,6},{6,4},{8,10},{10,8},{12,14},{14,12},{1,3},{3,1},... | collective-permute-start | bytes 393224 | tf_op jit(solution)/shard_map/ppermute | solution.py:215
  32.4 0.9 %shard_map.81 = (bf16[16,2048]{1,0:T(8,128)(2,1)S(1)}, f32[32,2048]{1,0:T(8,128)S(1)}, f32[32,2048]{1,0:T(8,128)S(1)}, f32[32,2048]{1,0:T(8,128)S(1)}, f32[32,2048]{1,0:T(8,128)S(1)}) custom-call(bf16[256,1024]{1,0:T(8,128)(2,1)S(1)} %get-tuple-element.45.low, bf16[1024,2048]{1,0:T(8,128)(2,1)S(1)} %shard_map.78.tile), custom_call_target="tpu_custom_call" | custom-call | bytes 16777216 | tf_op jit(solution)/shard_map/pallas_call | solution.py:294
  33.3 2.2 %collective-permute-start.8 = (bf16[16,2048]{1,0:T(8,128)(2,1)S(1)}, bf16[16,2048]{1,0:T(8,128)(2,1)S(1)}, u32[]{:S(2)}, u32[]{:S(2)}) collective-permute-start(bf16[16,2048]{1,0:T(8,128)(2,1)S(1)} %get-tuple-element.46), channel_id=1, source_target_pairs={{0,8},{2,10},{4,12},{6,14},{8,0},{10,2},{12,4},{14,6},{1,9},{3,11}... | collective-permute-start | bytes 196616 | tf_op jit(solution)/shard_map/ppermute | solution.py:215
  35.4 0.5 collective-permute-start.12
  36.0 0.7 %collective-permute-done.9.arrived = bf16[32,2048]{1,0:T(8,128)(2,1)S(1)} collective-permute-done((bf16[32,2048]{1,0:T(8,128)(2,1)S(1)}, bf16[32,2048]{1,0:T(8,128)(2,1)S(1)}, u32[]{:S(2)}, u32[]{:S(2)}) %collective-permute-start.9) | collective-permute-done | bytes 131104 | tf_op jit(solution)/shard_map/ppermute | solution.py:215
  36.7 2.8 %collective-permute-done.10.arrived = bf16[32,2048]{1,0:T(8,128)(2,1)S(1)} collective-permute-done((bf16[32,2048]{1,0:T(8,128)(2,1)S(1)}, bf16[32,2048]{1,0:T(8,128)(2,1)S(1)}, u32[]{:S(2)}, u32[]{:S(2)}) %collective-permute-start.10) | collective-permute-done | bytes 131104 | tf_op jit(solution)/shard_map/ppermute | solution.py:215
  39.5 3.2 %collective-permute-start.13 = (bf16[32,2048]{1,0:T(8,128)(2,1)S(1)}, bf16[32,2048]{1,0:T(8,128)(2,1)S(1)}, u32[]{:S(2)}, u32[]{:S(2)}) collective-permute-start(bf16[32,2048]{1,0:T(8,128)(2,1)S(1)} %shard_map.83), channel_id=1, source_target_pairs={{0,12},{2,14},{4,8},{6,10},{8,4},{10,6},{12,0},{14,2},{1,13},{3,15... | collective-permute-start | bytes 393224 | tf_op jit(solution)/shard_map/ppermute | solution.py:215
  42.9 1.2 %collective-permute-start.15 = (bf16[32,2048]{1,0:T(8,128)(2,1)S(1)}, bf16[32,2048]{1,0:T(8,128)(2,1)S(1)}, u32[]{:S(2)}, u32[]{:S(2)}) collective-permute-start(bf16[32,2048]{1,0:T(8,128)(2,1)S(1)} %shard_map.82), channel_id=1, source_target_pairs={{0,8},{2,10},{4,12},{6,14},{8,0},{10,2},{12,4},{14,6},{1,9},{3,11}... | collective-permute-start | bytes 393224 | tf_op jit(solution)/shard_map/ppermute | solution.py:215
  44.1 3.0 %collective-permute-done.13.third = bf16[32,2048]{1,0:T(8,128)(2,1)S(1)} collective-permute-done((bf16[32,2048]{1,0:T(8,128)(2,1)S(1)}, bf16[32,2048]{1,0:T(8,128)(2,1)S(1)}, u32[]{:S(2)}, u32[]{:S(2)}) %collective-permute-start.13) | collective-permute-done | bytes 131104 | tf_op jit(solution)/shard_map/ppermute | solution.py:215
  47.1 0.4 collective-permute-done.11
  47.6 1.4 %collective-permute-start.14 = (bf16[16,2048]{1,0:T(8,128)(2,1)S(1)}, bf16[16,2048]{1,0:T(8,128)(2,1)S(1)}, u32[]{:S(2)}, u32[]{:S(2)}) collective-permute-start(bf16[16,2048]{1,0:T(8,128)(2,1)S(1)} %add_convert_fusion), channel_id=1, source_target_pairs={{0,2},{2,0},{4,6},{6,4},{8,10},{10,8},{12,14},{14,12},{1,3},{3,1},... | collective-permute-start | bytes 196616 | tf_op jit(solution)/shard_map/ppermute | solution.py:215
  49.0 3.6 %collective-permute-start.17 = (bf16[32,2048]{1,0:T(8,128)(2,1)S(1)}, bf16[32,2048]{1,0:T(8,128)(2,1)S(1)}, u32[]{:S(2)}, u32[]{:S(2)}) collective-permute-start(bf16[32,2048]{1,0:T(8,128)(2,1)S(1)} %get-tuple-element.63), channel_id=1, source_target_pairs={{0,4},{2,6},{4,0},{6,2},{8,12},{10,14},{12,8},{14,10},{1,5},{3,7},... | collective-permute-start | bytes 393224 | tf_op jit(solution)/shard_map/ppermute | solution.py:215
  52.6 0.1 collective-permute-done.15.arrived
  52.9 2.7 %collective-permute-done.17.last = bf16[32,2048]{1,0:T(8,128)(2,1)S(1)} collective-permute-done((bf16[32,2048]{1,0:T(8,128)(2,1)S(1)}, bf16[32,2048]{1,0:T(8,128)(2,1)S(1)}, u32[]{:S(2)}, u32[]{:S(2)}) %collective-permute-start.17) | collective-permute-done | bytes 131104 | tf_op jit(solution)/shard_map/ppermute | solution.py:215
  55.6 1.0 %shard_map.86 = f32[32,2048]{1,0:T(8,128)} custom-call(f32[16,2048]{1,0:T(8,128)S(1)} %convert_add_fusion.mine, f32[16,2048]{1,0:T(8,128)S(1)} %collective-permute-done.16.other, bf16[256,2048]{1,0:T(8,128)(2,1)S(1)} %get-tuple-element.61.panel, f32[32,2048]{1,0:T(8,128)S(1)} %copy-done, f32[32,2048]{1,0:T(8,128)S(1)} %shard_map.85.partial, ...), custom_call_target="tpu_custom_call" | custom-call | tf_op jit(solution)/shard_map/pallas_call | solution.py:321
  (22 shorter events, 0.5 us)
Async XLA Ops:
  1.6 10.5 %collective-permute-start.2 = (bf16[32,2048]{1,0:T(8,128)(2,1)S(1)}, bf16[32,2048]{1,0:T(8,128)(2,1)S(1)}, u32[]{:S(2)}, u32[]{:S(2)}) collective-permute-start(bf16[32,2048]{1,0:T(8,128)(2,1)S(1)} %convert_element_type.27.refs_0_), channel_id=1, source_target_pairs={{0,8},{2,10},{4,12},{6,14},{8,0},{10,2},{12,4},{14,6},{1,9},{3,11}... | collective-permute-start | bytes 393224 | tf_op jit(solution)/shard_map/ppermute | solution.py:215
  5.7 6.6 %collective-permute-start.1 = (bf16[32,2048]{1,0:T(8,128)(2,1)S(1)}, bf16[32,2048]{1,0:T(8,128)(2,1)S(1)}, u32[]{:S(2)}, u32[]{:S(2)}) collective-permute-start(bf16[32,2048]{1,0:T(8,128)(2,1)S(1)} %convert_element_type.27.refs_0_), channel_id=1, source_target_pairs={{0,4},{2,6},{4,0},{6,2},{8,12},{10,14},{12,8},{14,10},{1,5},{3,7},... | collective-permute-start | bytes 393224 | tf_op jit(solution)/shard_map/ppermute | solution.py:215
  7.3 5.0 %collective-permute-start = (bf16[32,2048]{1,0:T(8,128)(2,1)S(1)}, bf16[32,2048]{1,0:T(8,128)(2,1)S(1)}, u32[]{:S(2)}, u32[]{:S(2)}) collective-permute-start(bf16[32,2048]{1,0:T(8,128)(2,1)S(1)} %convert_element_type.27.refs_0_), channel_id=1, source_target_pairs={{0,2},{2,0},{4,6},{6,4},{8,10},{10,8},{12,14},{14,12},{1,3},{3,1},... | collective-permute-start | bytes 393224 | tf_op jit(solution)/shard_map/ppermute | solution.py:215
  12.3 11.7 %collective-permute-start.4 = (f32[128,1024]{1,0:T(8,128)}, f32[128,1024]{1,0:T(8,128)S(1)}, u32[]{:S(2)}, u32[]{:S(2)}) collective-permute-start(f32[128,1024]{1,0:T(8,128)} %factor_mine.1), channel_id=1, source_target_pairs={{0,1},{1,0},{2,3},{3,2},{4,5},{5,4},{6,7},{7,6},{8,9},{9,8},{10,11... | collective-permute-start | bytes 1572872 | tf_op jit(solution)/shard_map/ppermute | solution.py:218
  12.4 8.7 %collective-permute-start.3 = (bf16[64,2048]{1,0:T(8,128)(2,1)S(1)}, bf16[64,2048]{1,0:T(8,128)(2,1)S(1)}, u32[]{:S(2)}, u32[]{:S(2)}) collective-permute-start(bf16[64,2048]{1,0:T(8,128)(2,1)S(1)} %shard_map.77.refs_2_), channel_id=1, source_target_pairs={{0,2},{2,0},{4,6},{6,4},{8,10},{10,8},{12,14},{14,12},{1,3},{3,1},... | collective-permute-start | bytes 786440 | tf_op jit(solution)/shard_map/ppermute | solution.py:215
  14.0 5.6 %collective-permute-start.5 = (bf16[32,2048]{1,0:T(8,128)(2,1)S(1)}, bf16[32,2048]{1,0:T(8,128)(2,1)S(1)}, u32[]{:S(2)}, u32[]{:S(2)}) collective-permute-start(bf16[32,2048]{1,0:T(8,128)(2,1)S(1)} %collective-permute-done.2.refs_1_), channel_id=1, source_target_pairs={{0,4},{2,6},{4,0},{6,2},{8,12},{10,14},{12,8},{14,10},{1,5},{3,7},... | collective-permute-start | bytes 393224 | tf_op jit(solution)/shard_map/ppermute | solution.py:215
  19.6 5.0 %collective-permute-start.6 = (bf16[32,2048]{1,0:T(8,128)(2,1)S(1)}, bf16[32,2048]{1,0:T(8,128)(2,1)S(1)}, u32[]{:S(2)}, u32[]{:S(2)}) collective-permute-start(bf16[32,2048]{1,0:T(8,128)(2,1)S(1)} %collective-permute-done.5.refs_4_), channel_id=1, source_target_pairs={{0,2},{2,0},{4,6},{6,4},{8,10},{10,8},{12,14},{14,12},{1,3},{3,1},... | collective-permute-start | bytes 393224 | tf_op jit(solution)/shard_map/ppermute | solution.py:215
  24.0 4.3 %copy-start.1 = (f32[128,1024]{1,0:T(8,128)S(1)}, f32[128,1024]{1,0:T(8,128)}, u32[]{:S(2)}) copy-start(f32[128,1024]{1,0:T(8,128)} %factor_mine.1) | copy-start | bytes 1572868
  26.1 2.2 %collective-permute-start.7 = (bf16[256,1280]{1,0:T(8,128)(2,1)S(1)}, bf16[256,1280]{1,0:T(8,128)(2,1)S(1)}, u32[]{:S(2)}, u32[]{:S(2)}) collective-permute-start(bf16[256,1280]{1,0:T(8,128)(2,1)S(1)} %get-tuple-element.42), channel_id=1, source_target_pairs={{0,1},{1,0},{2,3},{3,2},{4,5},{5,4},{6,7},{7,6},{8,9},{9,8},{10,11... | collective-permute-start | bytes 1966088 | tf_op jit(solution)/shard_map/ppermute | solution.py:218
  30.3 6.3 %collective-permute-start.9 = (bf16[32,2048]{1,0:T(8,128)(2,1)S(1)}, bf16[32,2048]{1,0:T(8,128)(2,1)S(1)}, u32[]{:S(2)}, u32[]{:S(2)}) collective-permute-start(bf16[32,2048]{1,0:T(8,128)(2,1)S(1)} %get-tuple-element.48), channel_id=1, source_target_pairs={{0,2},{2,0},{4,6},{6,4},{8,10},{10,8},{12,14},{14,12},{1,3},{3,1},... | collective-permute-start | bytes 393224 | tf_op jit(solution)/shard_map/ppermute | solution.py:215
  31.4 8.0 %collective-permute-start.10 = (bf16[32,2048]{1,0:T(8,128)(2,1)S(1)}, bf16[32,2048]{1,0:T(8,128)(2,1)S(1)}, u32[]{:S(2)}, u32[]{:S(2)}) collective-permute-start(bf16[32,2048]{1,0:T(8,128)(2,1)S(1)} %get-tuple-element.50), channel_id=1, source_target_pairs={{0,2},{2,0},{4,6},{6,4},{8,10},{10,8},{12,14},{14,12},{1,3},{3,1},... | collective-permute-start | bytes 393224 | tf_op jit(solution)/shard_map/ppermute | solution.py:215
  33.3 22.3 %copy-start = (f32[32,2048]{1,0:T(8,128)S(1)}, f32[32,2048]{1,0:T(8,128)}, u32[]{:S(2)}) copy-start(f32[32,2048]{1,0:T(8,128)} %factor.1) | copy-start | bytes 786436
  33.3 6.3 %collective-permute-start.8 = (bf16[16,2048]{1,0:T(8,128)(2,1)S(1)}, bf16[16,2048]{1,0:T(8,128)(2,1)S(1)}, u32[]{:S(2)}, u32[]{:S(2)}) collective-permute-start(bf16[16,2048]{1,0:T(8,128)(2,1)S(1)} %get-tuple-element.46), channel_id=1, source_target_pairs={{0,8},{2,10},{4,12},{6,14},{8,0},{10,2},{12,4},{14,6},{1,9},{3,11}... | collective-permute-start | bytes 196616 | tf_op jit(solution)/shard_map/ppermute | solution.py:215
  35.4 11.6 %collective-permute-start.12 = (bf16[64,2048]{1,0:T(8,128)(2,1)S(1)}, bf16[64,2048]{1,0:T(8,128)(2,1)S(1)}, u32[]{:S(2)}, u32[]{:S(2)}) collective-permute-start(bf16[64,2048]{1,0:T(8,128)(2,1)S(1)} %get-tuple-element.54), channel_id=1, source_target_pairs={{0,2},{2,0},{4,6},{6,4},{8,10},{10,8},{12,14},{14,12},{1,3},{3,1},... | collective-permute-start | bytes 786440 | tf_op jit(solution)/shard_map/ppermute | solution.py:215
  39.5 7.5 %collective-permute-start.13 = (bf16[32,2048]{1,0:T(8,128)(2,1)S(1)}, bf16[32,2048]{1,0:T(8,128)(2,1)S(1)}, u32[]{:S(2)}, u32[]{:S(2)}) collective-permute-start(bf16[32,2048]{1,0:T(8,128)(2,1)S(1)} %shard_map.83), channel_id=1, source_target_pairs={{0,12},{2,14},{4,8},{6,10},{8,4},{10,6},{12,0},{14,2},{1,13},{3,15... | collective-permute-start | bytes 393224 | tf_op jit(solution)/shard_map/ppermute | solution.py:215
  42.8 4.8 %collective-permute-start.11 = (bf16[16,2048]{1,0:T(8,128)(2,1)S(1)}, bf16[16,2048]{1,0:T(8,128)(2,1)S(1)}, u32[]{:S(2)}, u32[]{:S(2)}) collective-permute-start(bf16[16,2048]{1,0:T(8,128)(2,1)S(1)} %add_convert_fusion.1), channel_id=1, source_target_pairs={{0,4},{2,6},{4,0},{6,2},{8,12},{10,14},{12,8},{14,10},{1,5},{3,7},... | collective-permute-start | bytes 196616 | tf_op jit(solution)/shard_map/ppermute | solution.py:215
  42.9 9.9 %collective-permute-start.15 = (bf16[32,2048]{1,0:T(8,128)(2,1)S(1)}, bf16[32,2048]{1,0:T(8,128)(2,1)S(1)}, u32[]{:S(2)}, u32[]{:S(2)}) collective-permute-start(bf16[32,2048]{1,0:T(8,128)(2,1)S(1)} %shard_map.82), channel_id=1, source_target_pairs={{0,8},{2,10},{4,12},{6,14},{8,0},{10,2},{12,4},{14,6},{1,9},{3,11}... | collective-permute-start | bytes 393224 | tf_op jit(solution)/shard_map/ppermute | solution.py:215
  47.6 5.2 %collective-permute-start.14 = (bf16[16,2048]{1,0:T(8,128)(2,1)S(1)}, bf16[16,2048]{1,0:T(8,128)(2,1)S(1)}, u32[]{:S(2)}, u32[]{:S(2)}) collective-permute-start(bf16[16,2048]{1,0:T(8,128)(2,1)S(1)} %add_convert_fusion), channel_id=1, source_target_pairs={{0,2},{2,0},{4,6},{6,4},{8,10},{10,8},{12,14},{14,12},{1,3},{3,1},... | collective-permute-start | bytes 196616 | tf_op jit(solution)/shard_map/ppermute | solution.py:215
  49.0 6.6 %collective-permute-start.17 = (bf16[32,2048]{1,0:T(8,128)(2,1)S(1)}, bf16[32,2048]{1,0:T(8,128)(2,1)S(1)}, u32[]{:S(2)}, u32[]{:S(2)}) collective-permute-start(bf16[32,2048]{1,0:T(8,128)(2,1)S(1)} %get-tuple-element.63), channel_id=1, source_target_pairs={{0,4},{2,6},{4,0},{6,2},{8,12},{10,14},{12,8},{14,10},{1,5},{3,7},... | collective-permute-start | bytes 393224 | tf_op jit(solution)/shard_map/ppermute | solution.py:215
  52.8 2.8 %collective-permute-start.16 = (f32[16,2048]{1,0:T(8,128)S(1)}, f32[16,2048]{1,0:T(8,128)S(1)}, u32[]{:S(2)}, u32[]{:S(2)}) collective-permute-start(f32[16,2048]{1,0:T(8,128)S(1)} %convert_add_fusion.mine), channel_id=1, source_target_pairs={{0,1},{1,0},{2,3},{3,2},{4,5},{5,4},{6,7},{7,6},{8,9},{9,8},{10,11... | collective-permute-start | bytes 393224 | tf_op jit(solution)/shard_map/ppermute | solution.py:218

commit v7 on v6

--- a/solution.py
+++ b/solution.py
@@ -101,13 +101,6 @@
 
 def owned(bits, size):
     return pl.ds(pl.multiple_of((lax.axis_index("cell") ^ bits) * size, size), size)
-
-
-def join_body(*refs):
-    row = 0
-    for part in refs[:-1]:
-        refs[-1][row : row + part.shape[0]] = part[...]
-        row += part.shape[0]
 
 
 def gene_body(order, tile, *refs):
@@ -171,20 +164,17 @@
 
 
 def sum_body(keep, arrived, out):
-    out[...] = (keep[...] + arrived[...].astype(jnp.float32)).astype(out.dtype)
-
-
-def turn_body(keep, own, arrived, third, out, partial):
-    size = own.shape[0]
-    out[...] = (keep[...] + arrived[:size].astype(jnp.float32)).astype(out.dtype)
-    partial[...] = own[...] + arrived[size:].astype(jnp.float32) + third[...].astype(jnp.float32)
-
-
-def add_body(partial, arrived, out):
-    out[...] = partial[...] + arrived[...].astype(jnp.float32)
-
-
-def last_body(mine, other, panel, factor, partial, last, out, gram):
+    out[...] = (keep[...] + arrived[: keep.shape[0]].astype(jnp.float32)).astype(out.dtype)
+
+
+def total_body(own, arrived, third, second, last, out):
+    total = own[...] + arrived[own.shape[0] :].astype(jnp.float32)
+    for part in (third, second, last):
+        total = total + part[...].astype(jnp.float32)
+    out[...] = total
+
+
+def last_body(mine, other, panel, factor, data, out, gram):
     rows, width = mine.shape[0], gram.shape[1]
     core = lax.axis_index("gene")
     for half, part in ((core, mine), (1 - core, other)):
@@ -195,8 +185,7 @@
     norm = jnp.sum(jnp.sum(whole * whole, axis=1, keepdims=True), axis=0, keepdims=True)
     rate = 1.0 / (jnp.sqrt(norm) + 1e-06)
     stepped = split_dot(gram[owned(0, factor.shape[0])], panel[...])
-    data = partial[...] + last[...].astype(jnp.float32)
-    out[...] = jnp.maximum(factor[...] - rate * (stepped - data), 0.0)
+    out[...] = jnp.maximum(factor[...] - rate * (stepped - data[...]), 0.0)
 
 
 def gram_of(panel):
@@ -224,13 +213,12 @@
     values = block_values[0, 0]
     if paired:
         near = [swap(low_share, bits) for bits in (1, 2, 4)]
-        beside, second, fourth = lax.optimization_barrier(near)
-        sixth = swap(fourth, 2)
-        both = call(join_body, wide(2 * size, jnp.bfloat16), 0, 2, 0, 0)(second, fourth)
-        both, factor = lax.optimization_barrier((both, cell_factor))
-        both_beside, values = lax.optimization_barrier((swap(both, 1), values))
-        shares = [low_share, beside, both, both_beside, sixth, swap(sixth, 1)]
-        order = [0, 1, 2, 4, 3, 5, 6, 7]
+        beside, second, fourth, factor = lax.optimization_barrier((*near, cell_factor))
+        sixth, third, fifth = swap(fourth, 2), swap(beside, 2), swap(fourth, 1)
+        seventh = swap(sixth, 1)
+        fifth, values = lax.optimization_barrier((fifth, values))
+        shares = [low_share, beside, second, third, fourth, fifth, sixth, seventh]
+        order = range(n_cell)
     else:
         shares = [lax.all_gather(low_share, "cell", axis=0, tiled=True)]
         order, factor = None, cell_factor
@@ -306,27 +294,21 @@
     gram_arrived, second, third = lax.optimization_barrier((gram_arrived, second, third))
     third = swap(third, 6)
     second = swap(second, 4)
+    last = swap(call(sum_body, wide(size, jnp.bfloat16), 0, 2, 0, 0)(keeps[2], arrived[2]), 2)
     gram = (gram.astype(jnp.float32) + gram_arrived.astype(jnp.float32)).astype(jnp.bfloat16)
-    gram_arrived = swap(gram, 2)
-    message, partial = call(
-        turn_body, (wide(size, jnp.bfloat16), wide(size, jnp.float32)), 0, 4, 0, 0
-    )(keeps[2], keeps[3], arrived[2], third)
-    last = swap(message, 2)
-    gram_arrived, partial = lax.optimization_barrier((gram_arrived, partial))
-    gram = (gram.astype(jnp.float32) + gram_arrived.astype(jnp.float32)).astype(jnp.bfloat16)
-    gram_arrived = swap(gram, 1)
-    partial = call(add_body, wide(size, jnp.float32), 0, 2, 0, AHEAD)(partial, second)
-    gram_arrived, partial = lax.optimization_barrier((gram_arrived, partial))
+    gram = (gram.astype(jnp.float32) + swap(gram, 2).astype(jnp.float32)).astype(jnp.bfloat16)
+    total = call(total_body, wide(size, jnp.float32), 0, 5, 0, AHEAD)(keeps[3], arrived[2], third, second, last)
+    gram_arrived, total = lax.optimization_barrier((swap(gram, 1), total))
     gram = gram.astype(jnp.float32) + gram_arrived.astype(jnp.float32)
     gene_next = call(
         last_body,
         wide(size, jnp.float32),
         0,
-        6,
+        5,
         0,
         0,
         [pltpu.VMEM((kdim, kdim), jnp.float32)],
-    )(gram, swap_core(gram), panel, gene_factor, partial, last)
+    )(gram, swap_core(gram), panel, gene_factor, total)
     return (cell_next, gene_next)
 
 

time: 56.9 us -> 55.7 us (0.979)
  waiting for transfers between devices: 20.5 us -> 19.9 us
  starting transfers between devices: 25.2 us -> 24.6 us
    ppermute x15 -> x16, waiting for transfers between devices: 18.4 us -> 16.4 us  [swap(): return lax.ppermute(value, 'cell', [(n, n ^ bits) for n in range(n_cell)])]
    ppermute x3, waiting for transfers between devices: 2.09 us -> 3.42 us  [swap_core(): return lax.ppermute(value, 'gene', [(0, 1), (1, 0)])]
    ppermute x15 -> x16, starting transfers between devices: 24.9 us -> 24.4 us  [swap(): return lax.ppermute(value, 'cell', [(n, n ^ bits) for n in range(n_cell)])]
  transfers between devices with their start and end apart: 18 -> 19, of which waited for: 12 -> 9; matrix products, arithmetic and copies ran while one was open for 0% -> 0% of each run, Pallas kernels for 7% -> 7%
where the time goes in v7:
time: 55.7 us; the launch traced here: 55.4 us
  starting transfers between devices  24.6 us (44%)
  waiting for transfers between devices  19.9 us (36%)
  Pallas kernels  8.51 us (15%)
  between operations  1.44 us (3%)
  other arithmetic  1.02 us (2%)
    ppermute x16, starting transfers between devices, swap(): return lax.ppermute(value, 'cell', [(n, n ^ bits) for n in range(n_cell)])  24.4 us
    ppermute x16, waiting for transfers between devices, swap(): return lax.ppermute(value, 'cell', [(n, n ^ bits) for n in range(n_cell)])  16.4 us
    ppermute x3, waiting for transfers between devices, swap_core(): return lax.ppermute(value, 'gene', [(0, 1), (1, 0)])  3.42 us
    pallas_call x1, Pallas kernels, dense_tile(): pl.pallas_call(dense_body, out_shape=shape((CELL_DEV, GENE_DEV), jnp.bflo...  2.84 us
    pallas_call x1, Pallas kernels, shards(): call(functools.partial(cell_body, sent), (shape(cell_factor.shape, jnp.fl...  2.03 us
    pallas_call x1, Pallas kernels, shards(): call(functools.partial(gene_body, order), (wide(kdim, jnp.bfloat16), shap...  1.57 us
  transfers between devices with their start and end apart: 19, of which 9 were waited for; matrix products, arithmetic and copies ran while one was open for 0% of the time, Pallas kernels for 7%

profile of v7, /device:TPU:0, one launch (start us, length us, event | category | flops | bytes accessed | tf_op | source)
XLA Modules:
  0.0 55.4 jit_solution(12711636935353491565)
XLA Ops:
  0.6 1.0 %convert_element_type.27.refs_0_ = bf16[32,2048]{1,0:T(8,128)(2,1)S(1)} convert(f32[32,2048]{1,0:T(8,128)} %factor.1) | non-fusion elementwise | flops 65536 | bytes 393216 | tf_op jit(solution)/shard_map/convert_element_type | solution.py:212
  1.6 4.1 %collective-permute-start.2 = (bf16[32,2048]{1,0:T(8,128)(2,1)S(1)}, bf16[32,2048]{1,0:T(8,128)(2,1)S(1)}, u32[]{:S(2)}, u32[]{:S(2)}) collective-permute-start(bf16[32,2048]{1,0:T(8,128)(2,1)S(1)} %convert_element_type.27.refs_0_), channel_id=1, source_target_pairs={{0,8},{2,10},{4,12},{6,14},{8,0},{10,2},{12,4},{14,6},{1,9},{3,11}... | collective-permute-start | bytes 393224 | tf_op jit(solution)/shard_map/ppermute | solution.py:204
  5.7 1.6 %collective-permute-start.1 = (bf16[32,2048]{1,0:T(8,128)(2,1)S(1)}, bf16[32,2048]{1,0:T(8,128)(2,1)S(1)}, u32[]{:S(2)}, u32[]{:S(2)}) collective-permute-start(bf16[32,2048]{1,0:T(8,128)(2,1)S(1)} %convert_element_type.27.refs_0_), channel_id=1, source_target_pairs={{0,4},{2,6},{4,0},{6,2},{8,12},{10,14},{12,8},{14,10},{1,5},{3,7},... | collective-permute-start | bytes 393224 | tf_op jit(solution)/shard_map/ppermute | solution.py:204
  7.3 1.5 %collective-permute-start = (bf16[32,2048]{1,0:T(8,128)(2,1)S(1)}, bf16[32,2048]{1,0:T(8,128)(2,1)S(1)}, u32[]{:S(2)}, u32[]{:S(2)}) collective-permute-start(bf16[32,2048]{1,0:T(8,128)(2,1)S(1)} %convert_element_type.27.refs_0_), channel_id=1, source_target_pairs={{0,2},{2,0},{4,6},{6,4},{8,10},{10,8},{12,14},{14,12},{1,3},{3,1},... | collective-permute-start | bytes 393224 | tf_op jit(solution)/shard_map/ppermute | solution.py:204
  8.8 3.3 %collective-permute-done.2.refs_4_ = bf16[32,2048]{1,0:T(8,128)(2,1)S(1)} collective-permute-done((bf16[32,2048]{1,0:T(8,128)(2,1)S(1)}, bf16[32,2048]{1,0:T(8,128)(2,1)S(1)}, u32[]{:S(2)}, u32[]{:S(2)}) %collective-permute-start.2) | collective-permute-done | bytes 131104 | tf_op jit(solution)/shard_map/ppermute | solution.py:204
  12.1 0.2 collective-permute-done.1.refs_2_
  12.3 1.4 %collective-permute-start.6 = (bf16[32,2048]{1,0:T(8,128)(2,1)S(1)}, bf16[32,2048]{1,0:T(8,128)(2,1)S(1)}, u32[]{:S(2)}, u32[]{:S(2)}) collective-permute-start(bf16[32,2048]{1,0:T(8,128)(2,1)S(1)} %collective-permute-done.2.refs_4_), channel_id=1, source_target_pairs={{0,4},{2,6},{4,0},{6,2},{8,12},{10,14},{12,8},{14,10},{1,5},{3,7},... | collective-permute-start | bytes 393224 | tf_op jit(solution)/shard_map/ppermute | solution.py:204
  13.8 1.5 %collective-permute-start.3 = (bf16[32,2048]{1,0:T(8,128)(2,1)S(1)}, bf16[32,2048]{1,0:T(8,128)(2,1)S(1)}, u32[]{:S(2)}, u32[]{:S(2)}) collective-permute-start(bf16[32,2048]{1,0:T(8,128)(2,1)S(1)} %collective-permute-done.2.refs_4_), channel_id=1, source_target_pairs={{0,2},{2,0},{4,6},{6,4},{8,10},{10,8},{12,14},{14,12},{1,3},{3,1},... | collective-permute-start | bytes 393224 | tf_op jit(solution)/shard_map/ppermute | solution.py:204
  15.3 0.6 %collective-permute-start.5 = (bf16[32,2048]{1,0:T(8,128)(2,1)S(1)}, bf16[32,2048]{1,0:T(8,128)(2,1)S(1)}, u32[]{:S(2)}, u32[]{:S(2)}) collective-permute-start(bf16[32,2048]{1,0:T(8,128)(2,1)S(1)} %collective-permute-done.refs_1_), channel_id=1, source_target_pairs={{0,4},{2,6},{4,0},{6,2},{8,12},{10,14},{12,8},{14,10},{1,5},{3,7},... | collective-permute-start | bytes 393224 | tf_op jit(solution)/shard_map/ppermute | solution.py:204
  15.9 2.7 %collective-permute-done.6.refs_6_ = bf16[32,2048]{1,0:T(8,128)(2,1)S(1)} collective-permute-done((bf16[32,2048]{1,0:T(8,128)(2,1)S(1)}, bf16[32,2048]{1,0:T(8,128)(2,1)S(1)}, u32[]{:S(2)}, u32[]{:S(2)}) %collective-permute-start.6) | collective-permute-done | bytes 131104 | tf_op jit(solution)/shard_map/ppermute | solution.py:204
  18.6 1.5 %collective-permute-start.7 = (bf16[32,2048]{1,0:T(8,128)(2,1)S(1)}, bf16[32,2048]{1,0:T(8,128)(2,1)S(1)}, u32[]{:S(2)}, u32[]{:S(2)}) collective-permute-start(bf16[32,2048]{1,0:T(8,128)(2,1)S(1)} %collective-permute-done.6.refs_6_), channel_id=1, source_target_pairs={{0,2},{2,0},{4,6},{6,4},{8,10},{10,8},{12,14},{14,12},{1,3},{3,1},... | collective-permute-start | bytes 393224 | tf_op jit(solution)/shard_map/ppermute | solution.py:204
  20.8 2.8 %shard_map.77.tile = bf16[1024,2048]{1,0:T(8,128)(2,1)S(1)} custom-call(s32[64]{0:T(128)} %bitcast.6, s32[64]{0:T(128)} %bitcast.7, s32[1]{0:T(128)} %bitcast.4.count, bf16[64,128,128]{2,1,0:T(8,128)(2,1)} %bitcast.5), custom_call_target="tpu_custom_call" | custom-call | bytes 16777216 | tf_op jit(solution)/shard_map/pallas_call | solution.py:86
  23.7 1.6 %shard_map.78 = (bf16[256,2048]{1,0:T(8,128)(2,1)S(1)}, f32[256,1280]{1,0:T(8,128)S(1)}, bf16[256,1280]{1,0:T(8,128)(2,1)S(1)}) custom-call(bf16[1024,2048]{1,0:T(8,128)(2,1)S(1)} %shard_map.77.tile, bf16[32,2048]{1,0:T(8,128)(2,1)S(1)} %convert_element_type.27.refs_0_, bf16[32,2048]{1,0:T(8,128)(2,1)S(1)} %collective-permute-done.refs_1_, ...), custom_call_target="tpu_custom_call" | custom-call | tf_op jit(solution)/shard_map/pallas_call | solution.py:229
  25.4 2.1 %collective-permute-done.8.other = bf16[256,1280]{1,0:T(8,128)(2,1)S(1)} collective-permute-done((bf16[256,1280]{1,0:T(8,128)(2,1)S(1)}, bf16[256,1280]{1,0:T(8,128)(2,1)S(1)}, u32[]{:S(2)}, u32[]{:S(2)}) %collective-permute-start.8) | collective-permute-done | bytes 655392 | tf_op jit(solution)/shard_map/ppermute | solution.py:207
  27.5 2.0 %shard_map.79 = (f32[128,1024]{1,0:T(8,128)}, bf16[256,1024]{1,0:T(8,128)(2,1)S(1)}, bf16[32,2048]{1,0:T(8,128)(2,1)S(1)}, bf16[32,2048]{1,0:T(8,128)(2,1)S(1)}, bf16[64,2048]{1,0:T(8,128)(2,1)S(1)}) custom-call(bf16[1024,2048]{1,0:T(8,128)(2,1)S(1)} %shard_map.77.tile, f32[256,1280]{1,0:T(8,128)S(1)} %get-tuple-element.35.mine, ...), custom_call_target="tpu_custom_call" | custom-call | tf_op jit(solution)/shard_map/pallas_call | solution.py:245
  29.5 1.4 %collective-permute-start.10 = (bf16[32,2048]{1,0:T(8,128)(2,1)S(1)}, bf16[32,2048]{1,0:T(8,128)(2,1)S(1)}, u32[]{:S(2)}, u32[]{:S(2)}) collective-permute-start(bf16[32,2048]{1,0:T(8,128)(2,1)S(1)} %get-tuple-element.42), channel_id=1, source_target_pairs={{0,2},{2,0},{4,6},{6,4},{8,10},{10,8},{12,14},{14,12},{1,3},{3,1},... | collective-permute-start | bytes 393224 | tf_op jit(solution)/shard_map/ppermute | solution.py:204
  30.9 0.6 %collective-permute-start.11 = (bf16[32,2048]{1,0:T(8,128)(2,1)S(1)}, bf16[32,2048]{1,0:T(8,128)(2,1)S(1)}, u32[]{:S(2)}, u32[]{:S(2)}) collective-permute-start(bf16[32,2048]{1,0:T(8,128)(2,1)S(1)} %get-tuple-element.44), channel_id=1, source_target_pairs={{0,2},{2,0},{4,6},{6,4},{8,10},{10,8},{12,14},{14,12},{1,3},{3,1},... | collective-permute-start | bytes 393224 | tf_op jit(solution)/shard_map/ppermute | solution.py:204
  31.5 0.9 %shard_map.80 = (bf16[16,2048]{1,0:T(8,128)(2,1)S(1)}, f32[32,2048]{1,0:T(8,128)S(1)}, f32[32,2048]{1,0:T(8,128)S(1)}, f32[32,2048]{1,0:T(8,128)S(1)}, f32[32,2048]{1,0:T(8,128)S(1)}) custom-call(bf16[256,1024]{1,0:T(8,128)(2,1)S(1)} %get-tuple-element.39.low, bf16[1024,2048]{1,0:T(8,128)(2,1)S(1)} %shard_map.77.tile), custom_call_target="tpu_custom_call" | custom-call | bytes 16777216 | tf_op jit(solution)/shard_map/pallas_call | solution.py:282
  32.4 1.9 %collective-permute-start.9 = (bf16[16,2048]{1,0:T(8,128)(2,1)S(1)}, bf16[16,2048]{1,0:T(8,128)(2,1)S(1)}, u32[]{:S(2)}, u32[]{:S(2)}) collective-permute-start(bf16[16,2048]{1,0:T(8,128)(2,1)S(1)} %get-tuple-element.40), channel_id=1, source_target_pairs={{0,8},{2,10},{4,12},{6,14},{8,0},{10,2},{12,4},{14,6},{1,9},{3,11}... | collective-permute-start | bytes 196616 | tf_op jit(solution)/shard_map/ppermute | solution.py:204
  34.3 1.5 %collective-permute-start.14 = (bf16[64,2048]{1,0:T(8,128)(2,1)S(1)}, bf16[64,2048]{1,0:T(8,128)(2,1)S(1)}, u32[]{:S(2)}, u32[]{:S(2)}) collective-permute-start(bf16[64,2048]{1,0:T(8,128)(2,1)S(1)} %get-tuple-element.47), channel_id=1, source_target_pairs={{0,2},{2,0},{4,6},{6,4},{8,10},{10,8},{12,14},{14,12},{1,3},{3,1},... | collective-permute-start | bytes 786440 | tf_op jit(solution)/shard_map/ppermute | solution.py:204
  35.9 2.8 %collective-permute-done.11.arrived = bf16[32,2048]{1,0:T(8,128)(2,1)S(1)} collective-permute-done((bf16[32,2048]{1,0:T(8,128)(2,1)S(1)}, bf16[32,2048]{1,0:T(8,128)(2,1)S(1)}, u32[]{:S(2)}, u32[]{:S(2)}) %collective-permute-start.11) | collective-permute-done | bytes 131104 | tf_op jit(solution)/shard_map/ppermute | solution.py:204
  38.7 1.4 %collective-permute-start.12 = (bf16[16,2048]{1,0:T(8,128)(2,1)S(1)}, bf16[16,2048]{1,0:T(8,128)(2,1)S(1)}, u32[]{:S(2)}, u32[]{:S(2)}) collective-permute-start(bf16[16,2048]{1,0:T(8,128)(2,1)S(1)} %add_convert_fusion.1), channel_id=1, source_target_pairs={{0,4},{2,6},{4,0},{6,2},{8,12},{10,14},{12,8},{14,10},{1,5},{3,7},... | collective-permute-start | bytes 196616 | tf_op jit(solution)/shard_map/ppermute | solution.py:204
  40.1 2.0 %collective-permute-start.15 = (bf16[32,2048]{1,0:T(8,128)(2,1)S(1)}, bf16[32,2048]{1,0:T(8,128)(2,1)S(1)}, u32[]{:S(2)}, u32[]{:S(2)}) collective-permute-start(bf16[32,2048]{1,0:T(8,128)(2,1)S(1)} %shard_map.82), channel_id=1, source_target_pairs={{0,12},{2,14},{4,8},{6,10},{8,4},{10,6},{12,0},{14,2},{1,13},{3,15... | collective-permute-start | bytes 393224 | tf_op jit(solution)/shard_map/ppermute | solution.py:204
  42.1 0.4 collective-permute-start.16
  42.5 0.9 %collective-permute-done.14.arrived = bf16[64,2048]{1,0:T(8,128)(2,1)S(1)} collective-permute-done((bf16[64,2048]{1,0:T(8,128)(2,1)S(1)}, bf16[64,2048]{1,0:T(8,128)(2,1)S(1)}, u32[]{:S(2)}, u32[]{:S(2)}) %collective-permute-start.14) | collective-permute-done | bytes 262176 | tf_op jit(solution)/shard_map/ppermute | solution.py:204
  43.5 1.4 %collective-permute-start.17 = (bf16[32,2048]{1,0:T(8,128)(2,1)S(1)}, bf16[32,2048]{1,0:T(8,128)(2,1)S(1)}, u32[]{:S(2)}, u32[]{:S(2)}) collective-permute-start(bf16[32,2048]{1,0:T(8,128)(2,1)S(1)} %shard_map.83), channel_id=1, source_target_pairs={{0,4},{2,6},{4,0},{6,2},{8,12},{10,14},{12,8},{14,10},{1,5},{3,7},... | collective-permute-start | bytes 393224 | tf_op jit(solution)/shard_map/ppermute | solution.py:204
  44.9 1.6 %collective-permute-start.13 = (bf16[16,2048]{1,0:T(8,128)(2,1)S(1)}, bf16[16,2048]{1,0:T(8,128)(2,1)S(1)}, u32[]{:S(2)}, u32[]{:S(2)}) collective-permute-start(bf16[16,2048]{1,0:T(8,128)(2,1)S(1)} %add_convert_fusion), channel_id=1, source_target_pairs={{0,2},{2,0},{4,6},{6,4},{8,10},{10,8},{12,14},{14,12},{1,3},{3,1},... | collective-permute-start | bytes 196616 | tf_op jit(solution)/shard_map/ppermute | solution.py:204
  46.4 1.9 %collective-permute-done.15.third = bf16[32,2048]{1,0:T(8,128)(2,1)S(1)} collective-permute-done((bf16[32,2048]{1,0:T(8,128)(2,1)S(1)}, bf16[32,2048]{1,0:T(8,128)(2,1)S(1)}, u32[]{:S(2)}, u32[]{:S(2)}) %collective-permute-start.15) | collective-permute-done | bytes 131104 | tf_op jit(solution)/shard_map/ppermute | solution.py:204
  48.3 4.5 %collective-permute-done.16.second = bf16[32,2048]{1,0:T(8,128)(2,1)S(1)} collective-permute-done((bf16[32,2048]{1,0:T(8,128)(2,1)S(1)}, bf16[32,2048]{1,0:T(8,128)(2,1)S(1)}, u32[]{:S(2)}, u32[]{:S(2)}) %collective-permute-start.16) | collective-permute-done | bytes 131104 | tf_op jit(solution)/shard_map/ppermute | solution.py:204
  52.9 0.1 shard_map.84.data
  53.0 1.3 %collective-permute-done.18.other = f32[16,2048]{1,0:T(8,128)S(1)} collective-permute-done((f32[16,2048]{1,0:T(8,128)S(1)}, f32[16,2048]{1,0:T(8,128)S(1)}, u32[]{:S(2)}, u32[]{:S(2)}) %collective-permute-start.18) | collective-permute-done | bytes 131104 | tf_op jit(solution)/shard_map/ppermute | solution.py:207
  54.4 1.0 %shard_map.85 = f32[32,2048]{1,0:T(8,128)} custom-call(f32[16,2048]{1,0:T(8,128)S(1)} %convert_add_fusion.mine, f32[16,2048]{1,0:T(8,128)S(1)} %collective-permute-done.18.other, bf16[256,2048]{1,0:T(8,128)(2,1)S(1)} %get-tuple-element.52.panel, f32[32,2048]{1,0:T(8,128)S(1)} %copy-done, f32[32,2048]{1,0:T(8,128)S(1)} %shard_map.84.data), custom_call_target="tpu_custom_call" | custom-call | tf_op jit(solution)/shard_map/pallas_call | solution.py:303
  (23 shorter events, 0.3 us)
Async XLA Ops:
  1.6 10.5 %collective-permute-start.2 = (bf16[32,2048]{1,0:T(8,128)(2,1)S(1)}, bf16[32,2048]{1,0:T(8,128)(2,1)S(1)}, u32[]{:S(2)}, u32[]{:S(2)}) collective-permute-start(bf16[32,2048]{1,0:T(8,128)(2,1)S(1)} %convert_element_type.27.refs_0_), channel_id=1, source_target_pairs={{0,8},{2,10},{4,12},{6,14},{8,0},{10,2},{12,4},{14,6},{1,9},{3,11}... | collective-permute-start | bytes 393224 | tf_op jit(solution)/shard_map/ppermute | solution.py:204
  5.7 6.6 %collective-permute-start.1 = (bf16[32,2048]{1,0:T(8,128)(2,1)S(1)}, bf16[32,2048]{1,0:T(8,128)(2,1)S(1)}, u32[]{:S(2)}, u32[]{:S(2)}) collective-permute-start(bf16[32,2048]{1,0:T(8,128)(2,1)S(1)} %convert_element_type.27.refs_0_), channel_id=1, source_target_pairs={{0,4},{2,6},{4,0},{6,2},{8,12},{10,14},{12,8},{14,10},{1,5},{3,7},... | collective-permute-start | bytes 393224 | tf_op jit(solution)/shard_map/ppermute | solution.py:204
  7.3 5.0 %collective-permute-start = (bf16[32,2048]{1,0:T(8,128)(2,1)S(1)}, bf16[32,2048]{1,0:T(8,128)(2,1)S(1)}, u32[]{:S(2)}, u32[]{:S(2)}) collective-permute-start(bf16[32,2048]{1,0:T(8,128)(2,1)S(1)} %convert_element_type.27.refs_0_), channel_id=1, source_target_pairs={{0,2},{2,0},{4,6},{6,4},{8,10},{10,8},{12,14},{14,12},{1,3},{3,1},... | collective-permute-start | bytes 393224 | tf_op jit(solution)/shard_map/ppermute | solution.py:204
  12.3 11.4 %collective-permute-start.4 = (f32[128,1024]{1,0:T(8,128)}, f32[128,1024]{1,0:T(8,128)S(1)}, u32[]{:S(2)}, u32[]{:S(2)}) collective-permute-start(f32[128,1024]{1,0:T(8,128)} %factor_mine.1), channel_id=1, source_target_pairs={{0,1},{1,0},{2,3},{3,2},{4,5},{5,4},{6,7},{7,6},{8,9},{9,8},{10,11... | collective-permute-start | bytes 1572872 | tf_op jit(solution)/shard_map/ppermute | solution.py:207
  12.3 6.3 %collective-permute-start.6 = (bf16[32,2048]{1,0:T(8,128)(2,1)S(1)}, bf16[32,2048]{1,0:T(8,128)(2,1)S(1)}, u32[]{:S(2)}, u32[]{:S(2)}) collective-permute-start(bf16[32,2048]{1,0:T(8,128)(2,1)S(1)} %collective-permute-done.2.refs_4_), channel_id=1, source_target_pairs={{0,4},{2,6},{4,0},{6,2},{8,12},{10,14},{12,8},{14,10},{1,5},{3,7},... | collective-permute-start | bytes 393224 | tf_op jit(solution)/shard_map/ppermute | solution.py:204
  13.8 7.1 %collective-permute-start.3 = (bf16[32,2048]{1,0:T(8,128)(2,1)S(1)}, bf16[32,2048]{1,0:T(8,128)(2,1)S(1)}, u32[]{:S(2)}, u32[]{:S(2)}) collective-permute-start(bf16[32,2048]{1,0:T(8,128)(2,1)S(1)} %collective-permute-done.2.refs_4_), channel_id=1, source_target_pairs={{0,2},{2,0},{4,6},{6,4},{8,10},{10,8},{12,14},{14,12},{1,3},{3,1},... | collective-permute-start | bytes 393224 | tf_op jit(solution)/shard_map/ppermute | solution.py:204
  15.3 8.4 %collective-permute-start.5 = (bf16[32,2048]{1,0:T(8,128)(2,1)S(1)}, bf16[32,2048]{1,0:T(8,128)(2,1)S(1)}, u32[]{:S(2)}, u32[]{:S(2)}) collective-permute-start(bf16[32,2048]{1,0:T(8,128)(2,1)S(1)} %collective-permute-done.refs_1_), channel_id=1, source_target_pairs={{0,4},{2,6},{4,0},{6,2},{8,12},{10,14},{12,8},{14,10},{1,5},{3,7},... | collective-permute-start | bytes 393224 | tf_op jit(solution)/shard_map/ppermute | solution.py:204
  18.6 5.1 %collective-permute-start.7 = (bf16[32,2048]{1,0:T(8,128)(2,1)S(1)}, bf16[32,2048]{1,0:T(8,128)(2,1)S(1)}, u32[]{:S(2)}, u32[]{:S(2)}) collective-permute-start(bf16[32,2048]{1,0:T(8,128)(2,1)S(1)} %collective-permute-done.6.refs_6_), channel_id=1, source_target_pairs={{0,2},{2,0},{4,6},{6,4},{8,10},{10,8},{12,14},{14,12},{1,3},{3,1},... | collective-permute-start | bytes 393224 | tf_op jit(solution)/shard_map/ppermute | solution.py:204
  23.7 3.8 %copy-start.1 = (f32[128,1024]{1,0:T(8,128)S(1)}, f32[128,1024]{1,0:T(8,128)}, u32[]{:S(2)}) copy-start(f32[128,1024]{1,0:T(8,128)} %factor_mine.1) | copy-start | bytes 1572868
  25.3 2.2 %collective-permute-start.8 = (bf16[256,1280]{1,0:T(8,128)(2,1)S(1)}, bf16[256,1280]{1,0:T(8,128)(2,1)S(1)}, u32[]{:S(2)}, u32[]{:S(2)}) collective-permute-start(bf16[256,1280]{1,0:T(8,128)(2,1)S(1)} %get-tuple-element.36), channel_id=1, source_target_pairs={{0,1},{1,0},{2,3},{3,2},{4,5},{5,4},{6,7},{7,6},{8,9},{9,8},{10,11... | collective-permute-start | bytes 1966088 | tf_op jit(solution)/shard_map/ppermute | solution.py:207
  29.5 6.3 %collective-permute-start.10 = (bf16[32,2048]{1,0:T(8,128)(2,1)S(1)}, bf16[32,2048]{1,0:T(8,128)(2,1)S(1)}, u32[]{:S(2)}, u32[]{:S(2)}) collective-permute-start(bf16[32,2048]{1,0:T(8,128)(2,1)S(1)} %get-tuple-element.42), channel_id=1, source_target_pairs={{0,2},{2,0},{4,6},{6,4},{8,10},{10,8},{12,14},{14,12},{1,3},{3,1},... | collective-permute-start | bytes 393224 | tf_op jit(solution)/shard_map/ppermute | solution.py:204
  30.9 7.7 %collective-permute-start.11 = (bf16[32,2048]{1,0:T(8,128)(2,1)S(1)}, bf16[32,2048]{1,0:T(8,128)(2,1)S(1)}, u32[]{:S(2)}, u32[]{:S(2)}) collective-permute-start(bf16[32,2048]{1,0:T(8,128)(2,1)S(1)} %get-tuple-element.44), channel_id=1, source_target_pairs={{0,2},{2,0},{4,6},{6,4},{8,10},{10,8},{12,14},{14,12},{1,3},{3,1},... | collective-permute-start | bytes 393224 | tf_op jit(solution)/shard_map/ppermute | solution.py:204
  32.4 22.0 %copy-start = (f32[32,2048]{1,0:T(8,128)S(1)}, f32[32,2048]{1,0:T(8,128)}, u32[]{:S(2)}) copy-start(f32[32,2048]{1,0:T(8,128)} %factor.1) | copy-start | bytes 786436
  32.4 6.2 %collective-permute-start.9 = (bf16[16,2048]{1,0:T(8,128)(2,1)S(1)}, bf16[16,2048]{1,0:T(8,128)(2,1)S(1)}, u32[]{:S(2)}, u32[]{:S(2)}) collective-permute-start(bf16[16,2048]{1,0:T(8,128)(2,1)S(1)} %get-tuple-element.40), channel_id=1, source_target_pairs={{0,8},{2,10},{4,12},{6,14},{8,0},{10,2},{12,4},{14,6},{1,9},{3,11}... | collective-permute-start | bytes 196616 | tf_op jit(solution)/shard_map/ppermute | solution.py:204
  34.3 9.1 %collective-permute-start.14 = (bf16[64,2048]{1,0:T(8,128)(2,1)S(1)}, bf16[64,2048]{1,0:T(8,128)(2,1)S(1)}, u32[]{:S(2)}, u32[]{:S(2)}) collective-permute-start(bf16[64,2048]{1,0:T(8,128)(2,1)S(1)} %get-tuple-element.47), channel_id=1, source_target_pairs={{0,2},{2,0},{4,6},{6,4},{8,10},{10,8},{12,14},{14,12},{1,3},{3,1},... | collective-permute-start | bytes 786440 | tf_op jit(solution)/shard_map/ppermute | solution.py:204
  38.7 6.2 %collective-permute-start.12 = (bf16[16,2048]{1,0:T(8,128)(2,1)S(1)}, bf16[16,2048]{1,0:T(8,128)(2,1)S(1)}, u32[]{:S(2)}, u32[]{:S(2)}) collective-permute-start(bf16[16,2048]{1,0:T(8,128)(2,1)S(1)} %add_convert_fusion.1), channel_id=1, source_target_pairs={{0,4},{2,6},{4,0},{6,2},{8,12},{10,14},{12,8},{14,10},{1,5},{3,7},... | collective-permute-start | bytes 196616 | tf_op jit(solution)/shard_map/ppermute | solution.py:204
  40.1 8.2 %collective-permute-start.15 = (bf16[32,2048]{1,0:T(8,128)(2,1)S(1)}, bf16[32,2048]{1,0:T(8,128)(2,1)S(1)}, u32[]{:S(2)}, u32[]{:S(2)}) collective-permute-start(bf16[32,2048]{1,0:T(8,128)(2,1)S(1)} %shard_map.82), channel_id=1, source_target_pairs={{0,12},{2,14},{4,8},{6,10},{8,4},{10,6},{12,0},{14,2},{1,13},{3,15... | collective-permute-start | bytes 393224 | tf_op jit(solution)/shard_map/ppermute | solution.py:204
  42.1 10.8 %collective-permute-start.16 = (bf16[32,2048]{1,0:T(8,128)(2,1)S(1)}, bf16[32,2048]{1,0:T(8,128)(2,1)S(1)}, u32[]{:S(2)}, u32[]{:S(2)}) collective-permute-start(bf16[32,2048]{1,0:T(8,128)(2,1)S(1)} %shard_map.81), channel_id=1, source_target_pairs={{0,8},{2,10},{4,12},{6,14},{8,0},{10,2},{12,4},{14,6},{1,9},{3,11}... | collective-permute-start | bytes 393224 | tf_op jit(solution)/shard_map/ppermute | solution.py:204
  43.5 9.4 %collective-permute-start.17 = (bf16[32,2048]{1,0:T(8,128)(2,1)S(1)}, bf16[32,2048]{1,0:T(8,128)(2,1)S(1)}, u32[]{:S(2)}, u32[]{:S(2)}) collective-permute-start(bf16[32,2048]{1,0:T(8,128)(2,1)S(1)} %shard_map.83), channel_id=1, source_target_pairs={{0,4},{2,6},{4,0},{6,2},{8,12},{10,14},{12,8},{14,10},{1,5},{3,7},... | collective-permute-start | bytes 393224 | tf_op jit(solution)/shard_map/ppermute | solution.py:204
  44.9 8.0 %collective-permute-start.13 = (bf16[16,2048]{1,0:T(8,128)(2,1)S(1)}, bf16[16,2048]{1,0:T(8,128)(2,1)S(1)}, u32[]{:S(2)}, u32[]{:S(2)}) collective-permute-start(bf16[16,2048]{1,0:T(8,128)(2,1)S(1)} %add_convert_fusion), channel_id=1, source_target_pairs={{0,2},{2,0},{4,6},{6,4},{8,10},{10,8},{12,14},{14,12},{1,3},{3,1},... | collective-permute-start | bytes 196616 | tf_op jit(solution)/shard_map/ppermute | solution.py:204
  53.0 1.4 %collective-permute-start.18 = (f32[16,2048]{1,0:T(8,128)S(1)}, f32[16,2048]{1,0:T(8,128)S(1)}, u32[]{:S(2)}, u32[]{:S(2)}) collective-permute-start(f32[16,2048]{1,0:T(8,128)S(1)} %convert_add_fusion.mine), channel_id=1, source_target_pairs={{0,1},{1,0},{2,3},{3,2},{4,5},{5,4},{6,7},{7,6},{8,9},{9,8},{10,11... | collective-permute-start | bytes 393224 | tf_op jit(solution)/shard_map/ppermute | solution.py:207

commit v8 on v7

v8 whole, which is shorter than its diff:
```python
import functools

import jax
import jax.numpy as jnp
from jax import lax
from jax.experimental import pallas as pl
from jax.experimental.pallas import tpu as pltpu
from jax.sharding import PartitionSpec as P

BLK = 128
CELL_DEV = 1024
GENE_DEV = 2048
VMEM_BYTES = 24 * 2**20
AHEAD = 16 * 2**20

NT = (((1,), (1,)), ((), ()))
NN = (((1,), (0,)), ((), ()))
SMEM_SPEC = pl.BlockSpec(memory_space=pltpu.SMEM)
VMEM_SPEC = pl.BlockSpec(memory_space=pltpu.VMEM)


def dot(a, b, dims=NN):
    return lax.dot_general(a, b, dims, preferred_element_type=jnp.float32)


def split_dot(a, b):
    high = a.astype(jnp.bfloat16)
    low = (a - high.astype(jnp.float32)).astype(jnp.bfloat16)
    rows = a.shape[0]
    both = dot(jnp.concatenate([high, low], axis=0), b)
    return both[:rows] + both[rows:]


def call(body, outs, n_smem, n_vmem, flops, traffic, scratch=()):
    return pl.pallas_call(
        body,
        out_shape=outs,
        in_specs=[SMEM_SPEC] * n_smem + [VMEM_SPEC] * n_vmem,
        out_specs=jax.tree.map(lambda _: VMEM_SPEC, outs),
        scratch_shapes=list(scratch),
        compiler_params=pltpu.CompilerParams(vmem_limit_bytes=VMEM_BYTES),
        cost_estimate=pl.CostEstimate(flops=flops, bytes_accessed=traffic, transcendentals=0),
    )


def shape(dims, dtype):
    return jax.ShapeDtypeStruct(dims, dtype)


def dense_body(rows_in, cols_in, count, values, tile, rows, cols, sems, index_sems):
    copies = [
        pltpu.make_async_copy(rows_in, rows, index_sems.at[0]),
        pltpu.make_async_copy(cols_in, cols, index_sems.at[1]),
    ]
    for copy in copies:
        copy.start()
    tile[...] = jnp.zeros_like(tile)
    for copy in copies:
        copy.wait()

    def block(n):
        row = pl.multiple_of(rows[n] * BLK, BLK)
        col = pl.multiple_of(cols[n] * BLK, BLK)
        place = tile.at[pl.ds(row, BLK), pl.ds(col, BLK)]
        return pltpu.make_async_copy(values.at[n], place, sems.at[n])

    def start(n, carry):
        block(n).start()
        return carry

    def wait(n, carry):
        block(n).wait()
        return carry

    lax.fori_loop(0, count[0], start, 0)
    lax.fori_loop(0, count[0], wait, 0)


def pinned(array):
    return pltpu.with_memory_space_constraint(array, pltpu.HBM)


def dense_tile(values, rows, cols, count):
    anywhere = pl.BlockSpec(memory_space=pltpu.HBM)
    n_blocks = values.shape[0]
    return pl.pallas_call(
        dense_body,
        out_shape=shape((CELL_DEV, GENE_DEV), jnp.bfloat16),
        in_specs=[anywhere, anywhere, SMEM_SPEC, anywhere],
        out_specs=VMEM_SPEC,
        scratch_shapes=[
            pltpu.SMEM((n_blocks,), jnp.int32),
            pltpu.SMEM((n_blocks,), jnp.int32),
            pltpu.SemaphoreType.DMA((n_blocks,)),
            pltpu.SemaphoreType.DMA((2,)),
        ],
        compiler_params=pltpu.CompilerParams(vmem_limit_bytes=VMEM_BYTES),
        cost_estimate=pl.CostEstimate(flops=0, bytes_accessed=0, transcendentals=0),
    )(pinned(rows), pinned(cols), count, pinned(values))


def owned(bits, size):
    return pl.ds(pl.multiple_of((lax.axis_index("cell") ^ bits) * size, size), size)


STEP = 8
PARTS = 2


def coded(rows):
    above, parts = None, []
    for n in range(0, rows.shape[0], STEP):
        part = rows[n : n + STEP]
        part = (part if above is None else part - above).astype(jnp.bfloat16).astype(jnp.float32)
        above = part if above is None else above + part
        parts.append(part)
    return jnp.concatenate(parts, axis=0).astype(jnp.bfloat16)


def decoded(rows):
    rows, above, parts = rows.astype(jnp.float32), None, []
    for n in range(0, rows.shape[0], STEP):
        above = rows[n : n + STEP] if above is None else above + rows[n : n + STEP]
        parts.append(above)
    return jnp.concatenate(parts, axis=0)


def first_body(count, tile, *refs):
    shares, (panel, mine), messages = refs[: -2 - count], refs[-2 - count : -count], refs[-count:]
    row = 0
    for part in shares:
        panel[row : row + part.shape[0]] = part[...]
        row += part.shape[0]
    mine[...] = dot(panel[...], tile[...], NT)
    row = 0
    for out in messages:
        out[...] = mine[row : row + out.shape[0]].astype(out.dtype)
        row += out.shape[0]


def second_body(order, tile, first, share, panel, mine, message):
    size = share.shape[0]
    if order is None:
        panel[: first.shape[0]] = first[...]
        panel[first.shape[0] :] = share[...]
    else:
        for n, bits in enumerate(order[:-1]):
            panel[owned(bits, size)] = first[n * size : (n + 1) * size]
        panel[owned(order[-1], size)] = share[...]
    mine[:size] = dot(share[...], tile[...], NT)
    low = panel[...]
    gram = dot(low, low, NT)
    rows, width = mine.shape[0] - size, gram.shape[1]
    for n in range(gram.shape[0] // rows):
        mine[size:, n * width : (n + 1) * width] = gram[n * rows : (n + 1) * rows]
    message[...] = mine[...].astype(message.dtype)


def cell_body(
    order, picks, count, tile, mine_first, mine, other, factor_mine, factor_other, *refs
):
    others, (cell_next, low), sends = refs[:count], refs[count : count + 2], refs[count + 2 : -5]
    other_first, factor, data, updated, chosen = refs[-5:]
    for n, part in enumerate(others):
        other_first[n * part.shape[0] : (n + 1) * part.shape[0]] = part[...]
    share = factor_mine.shape[0]
    kdim = factor.shape[0]
    core = lax.axis_index("gene")
    own = pl.ds(pl.multiple_of(core * share, share), share)
    theirs = pl.ds(pl.multiple_of((1 - core) * share, share), share)
    factor[own] = factor_mine[...]
    factor[theirs] = factor_other[...]
    both = mine[...] + other[...].astype(jnp.float32)
    size = kdim - mine_first.shape[0]
    gram = jnp.concatenate([both[size:, n : n + kdim] for n in range(0, CELL_DEV, kdim)], axis=0)
    if order is None:
        data[:-size] = mine_first[...] + other_first[...].astype(jnp.float32)
        data[-size:] = both[:size]
    else:
        for n, bits in enumerate(order[:-1]):
            rows = slice(n * size, (n + 1) * size)
            data[owned(bits, size)] = mine_first[rows] + other_first[rows].astype(jnp.float32)
        data[owned(order[-1], size)] = both[:size]
    norm = jnp.sum(jnp.sum(gram * gram, axis=1, keepdims=True), axis=0, keepdims=True)
    rate = 1.0 / (jnp.sqrt(norm) + 1e-06)
    held = factor[...]
    stepped = split_dot(gram, held.astype(jnp.bfloat16))
    updated[...] = jnp.maximum(held - rate * (stepped - data[...]), 0.0)
    cell_next[...] = updated[own]
    low[...] = updated[...].astype(jnp.bfloat16)
    if sends:
        send, gram_out = sends
        send[...] = coded(picked_product(picks, low, tile, chosen)[0])
        half_gram(low, gram_out)


def half_gram(low, out):
    share = low.shape[0] // 2
    own = pl.ds(pl.multiple_of(lax.axis_index("gene") * share, share), share)
    half = dot(low[own], low[...], NT).astype(out.dtype)
    rows, width = out.shape[0], half.shape[1]
    for n in range(share // rows):
        out[:, n * width : (n + 1) * width] = half[n * rows : (n + 1) * rows]


def picked_product(picks, low, tile, chosen):
    size = chosen.shape[0] // len(picks)
    for n, bits in enumerate(picks):
        chosen[n * size : (n + 1) * size] = low[owned(bits, size)]
    product = dot(chosen[...], tile[...])
    return [product[n * size : (n + 1) * size] for n in range(len(picks))]


def keep_body(picks, low, tile, send, send_pair, *rest):
    first, second, third, *kept = picked_product(picks, low, tile, rest[-1])
    send[...] = coded(first)
    size = first.shape[0]
    send_pair[:size] = coded(second)
    send_pair[size:] = coded(third)
    for out, part in zip(rest[:-1], kept):
        out[...] = part


def pair_body(keep, other, arrived, out, total):
    size = keep.shape[0]
    out[...] = coded(keep[...] + decoded(arrived[:size]))
    total[...] = other[...] + decoded(arrived[size:])


def sum_body(keep, *refs):
    total = keep[...]
    for part in refs[:-1]:
        total = total + decoded(part[...])
    refs[-1][...] = coded(total)


def total_body(keep, *refs):
    total = keep[...]
    for part in refs[:-1]:
        total = total + decoded(part[...])
    refs[-1][...] = total


def last_body(mine, other, panel, factor, data, out, gram):
    rows, width = mine.shape[0], gram.shape[1]
    core = lax.axis_index("gene")
    for half, part in ((core, mine), (1 - core, other)):
        for n in range(part.shape[1] // width):
            row = pl.multiple_of(half * (gram.shape[0] // 2) + n * rows, rows)
            gram[pl.ds(row, rows)] = part[:, n * width : (n + 1) * width]
    whole = gram[...]
    norm = jnp.sum(jnp.sum(whole * whole, axis=1, keepdims=True), axis=0, keepdims=True)
    rate = 1.0 / (jnp.sqrt(norm) + 1e-06)
    stepped = split_dot(gram[owned(0, factor.shape[0])], panel[...])
    out[...] = jnp.maximum(factor[...] - rate * (stepped - data[...]), 0.0)


def gram_of(panel):
    return dot(panel, panel, NT)


def shards(block_values, block_rows, block_cols, block_count, cell_factor, gene_factor):
    n_cell = lax.axis_size("cell")
    kdim = cell_factor.shape[0] * lax.axis_size("gene")
    size = gene_factor.shape[0]
    gram_rows = kdim // 2 * kdim // GENE_DEV
    paired = n_cell == 8 and size % 16 == 0 and gram_rows % 16 == 0

    def swap(value, bits):
        return lax.ppermute(value, "cell", [(n, n ^ bits) for n in range(n_cell)])

    def swap_core(value):
        return lax.ppermute(value, "gene", [(0, 1), (1, 0)])

    def wide(rows, dtype):
        return shape((rows, GENE_DEV), dtype)

    low_share = gene_factor.astype(jnp.bfloat16)
    factor_other = swap_core(cell_factor)
    tile = dense_tile(block_values[0, 0], block_rows[0, 0], block_cols[0, 0], block_count[0])
    if paired:
        near = [swap(low_share, bits) for bits in (1, 2, 4)]
        beside, second, fourth, tile, factor_other = lax.optimization_barrier((*near, tile, factor_other))
        sixth, third, fifth = swap(fourth, 2), swap(beside, 2), swap(fourth, 1)
        seventh = swap(sixth, 1)
        shares = [low_share, beside, second, third, fourth, fifth, sixth]
        order = range(n_cell)
    else:
        whole = lax.all_gather(low_share, "cell", axis=0, tiled=True)
        shares, seventh, order = [whole[: -kdim // 8]], whole[-kdim // 8 :], None
    last_rows = seventh.shape[0]

    first_rows = kdim - last_rows
    part_rows = first_rows // PARTS if first_rows % (16 * PARTS) == 0 else first_rows
    n_parts = first_rows // part_rows
    panel_first, mine_first, *messages = call(
        functools.partial(first_body, n_parts),
        (
            wide(first_rows, jnp.bfloat16),
            shape((first_rows, CELL_DEV), jnp.float32),
            *[shape((part_rows, CELL_DEV), jnp.bfloat16) for _ in range(n_parts)],
        ),
        0,
        1 + len(shares),
        0,
        AHEAD,
    )(tile, *shares)
    others = [swap_core(part) for part in messages]
    rows = last_rows + kdim * kdim // CELL_DEV
    panel, mine, message = call(
        functools.partial(second_body, order),
        (
            wide(kdim, jnp.bfloat16),
            shape((rows, CELL_DEV), jnp.float32),
            shape((rows, CELL_DEV), jnp.bfloat16),
        ),
        0,
        3,
        0,
        0,
    )(tile, panel_first, seventh)
    other = swap_core(message)

    sent = [5, 3, 1]
    kept = [6, 4, 2, 0]
    cell_next, next_low, *sends = call(
        functools.partial(cell_body, order, [7], n_parts),
        (
            shape(cell_factor.shape, jnp.float32),
            shape((kdim, CELL_DEV), jnp.bfloat16),
            *([wide(size, jnp.bfloat16), wide(gram_rows, jnp.bfloat16)] if paired else []),
        ),
        0,
        6 + n_parts,
        0,
        0,
        [
            pltpu.VMEM((first_rows, CELL_DEV), jnp.bfloat16),
            pltpu.VMEM((kdim, CELL_DEV), jnp.float32),
            pltpu.VMEM((kdim, CELL_DEV), jnp.float32),
            pltpu.VMEM((kdim, CELL_DEV), jnp.float32),
            pltpu.VMEM((size, CELL_DEV), jnp.bfloat16),
        ],
    )(tile, mine_first, mine, other, cell_factor, factor_other, *others)

    if not paired:
        cell_gram = lax.psum(gram_of(next_low), "cell")
        own_cols = lax.psum_scatter(dot(next_low, tile), "cell", scatter_dimension=0, tiled=True)
        gram_part = lax.dynamic_slice_in_dim(cell_gram, lax.axis_index("cell") * size, size, 0)
        rate_gene = 1.0 / (jnp.sqrt(jnp.sum(cell_gram * cell_gram)) + 1e-06)
        stepped = jnp.dot(
            gram_part, panel.astype(jnp.float32), precision=lax.Precision.HIGHEST
        )
        return (cell_next, jnp.maximum(gene_factor - rate_gene * (stepped - own_cols), 0.0))

    arrived = [swap(sends[0], 1)]
    send, send_pair, *keeps = call(
        functools.partial(keep_body, sent + kept),
        (
            wide(size, jnp.bfloat16),
            wide(2 * size, jnp.bfloat16),
            *[wide(size, jnp.float32) for _ in kept],
        ),
        0,
        2,
        0,
        AHEAD,
        [pltpu.VMEM((kdim - size, CELL_DEV), jnp.bfloat16)],
    )(next_low, tile)
    gram = sends[1]
    arrived += [swap(send, 1), swap(send_pair, 1)]

    def add_up(cost, keep, *parts):
        body = call(sum_body, wide(size, jnp.bfloat16), 0, 1 + len(parts), 0, cost)
        return body(keep, *parts)

    through = add_up(AHEAD, keeps[0], arrived[0])
    gram_arrived = swap(gram, 4)
    through = swap(through, 2)
    beside, total = call(
        pair_body, (wide(size, jnp.bfloat16), wide(size, jnp.float32)), 0, 3, 0, AHEAD
    )(keeps[2], keeps[3], arrived[2])
    across = add_up(AHEAD, keeps[1], arrived[1], through)

    gram = (gram.astype(jnp.float32) + gram_arrived.astype(jnp.float32)).astype(jnp.bfloat16)
    gram_arrived = swap(gram, 2)
    gram_arrived, across = lax.optimization_barrier((gram_arrived, across))
    across = swap(across, 4)
    beside = swap(beside, 2)
    gram = (gram.astype(jnp.float32) + gram_arrived.astype(jnp.float32)).astype(jnp.bfloat16)

    partner = swap(gram, 1)
    total = call(total_body, wide(size, jnp.float32), 0, 3, 0, AHEAD)(total, beside, across)

    gram = gram.astype(jnp.float32) + partner.astype(jnp.float32)
    gene_next = call(
        last_body,
        wide(size, jnp.float32),
        0,
        5,
        0,
        0,
        [pltpu.VMEM((kdim, kdim), jnp.float32)],
    )(gram, swap_core(gram), panel, gene_factor, total)
    return (cell_next, gene_next)


def solution(mesh):
    return jax.shard_map(
        shards,
        mesh=mesh,
        in_specs=(
            P(("groups", "cell"), "gene", None, None, None),
            P(("groups", "cell"), "gene", None),
            P(("groups", "cell"), "gene", None),
            P(("groups", "cell"), "gene"),
            P(("groups", "gene"), "cell"),
            P(("groups", "cell"), "gene"),
        ),
        out_specs=(P(("groups", "gene"), "cell"), P(("groups", "cell"), "gene")),
        check_vma=False,
    )
```

time: 55.7 us -> 53 us (0.952)
  waiting for transfers between devices: 19.9 us -> 14.1 us
  Pallas kernels: 8.51 us -> 10.9 us
  starting transfers between devices: 24.6 us -> 25.3 us
    ppermute x16, waiting for transfers between devices: 16.4 us -> 12.6 us  [swap(): return lax.ppermute(value, 'cell', [(n, n ^ bits) for n in range(n_cell)])]
    pallas_call x7 -> x8, Pallas kernels: 4.65 us -> 7.06 us  [the longest x1 2.6 us: shards(): call(functools.partial(cell_body, order, [7], n_parts), (shape(cell_facto...]
    ppermute x3 -> x5, waiting for transfers between devices: 3.42 us -> 1.42 us  [swap_core(): return lax.ppermute(value, 'gene', [(0, 1), (1, 0)])]
    ppermute x3 -> x5, starting transfers between devices: 0.14 us -> 1.23 us  [swap_core(): return lax.ppermute(value, 'gene', [(0, 1), (1, 0)])]
  transfers between devices with their start and end apart: 19 -> 21, of which waited for: 9 -> 13; matrix products, arithmetic and copies ran while one was open for 0% -> 2% of each run, Pallas kernels for 7% -> 14%
where the time goes in v8:
time: 53 us; the launch traced here: 52.7 us
  starting transfers between devices  25.3 us (48%)
  waiting for transfers between devices  14.1 us (27%)
  Pallas kernels  10.9 us (21%)
  between operations  1.42 us (3%)
  other arithmetic  1.02 us (2%)
    ppermute x16, starting transfers between devices, swap(): return lax.ppermute(value, 'cell', [(n, n ^ bits) for n in range(n_cell)])  24 us
    ppermute x16, waiting for transfers between devices, swap(): return lax.ppermute(value, 'cell', [(n, n ^ bits) for n in range(n_cell)])  12.6 us
    pallas_call x1, Pallas kernels, dense_tile(): pl.pallas_call(dense_body, out_shape=shape((CELL_DEV, GENE_DEV), jnp.bflo...  2.84 us
    pallas_call x1, Pallas kernels, shards(): call(functools.partial(cell_body, order, [7], n_parts), (shape(cell_facto...  2.6 us
    pallas_call x1, Pallas kernels, shards(): call(functools.partial(second_body, order), (wide(kdim, jnp.bfloat16), sh...  1.65 us
    pallas_call x1, Pallas kernels, shards(): call(functools.partial(first_body, n_parts), (wide(first_rows, jnp.bfloat...  1.42 us
    ppermute x5, waiting for transfers between devices, swap_core(): return lax.ppermute(value, 'gene', [(0, 1), (1, 0)])  1.42 us
    ppermute x5, starting transfers between devices, swap_core(): return lax.ppermute(value, 'gene', [(0, 1), (1, 0)])  1.23 us
  transfers between devices with their start and end apart: 21, of which 13 were waited for; matrix products, arithmetic and copies ran while one was open for 2% of the time, Pallas kernels for 14%

profile of v8, /device:TPU:0, one launch (start us, length us, event | category | flops | bytes accessed | tf_op | source)
XLA Modules:
  0.0 52.7 jit_solution(1793537165168961016)
XLA Ops:
  0.6 0.5 collective-permute-start.3
  1.1 1.0 %convert_element_type.27.refs_0_ = bf16[32,2048]{1,0:T(8,128)(2,1)S(1)} convert(f32[32,2048]{1,0:T(8,128)} %factor.1) | non-fusion elementwise | flops 65536 | bytes 393216 | tf_op jit(solution)/shard_map/convert_element_type | solution.py:278
  2.1 3.7 %collective-permute-start.2 = (bf16[32,2048]{1,0:T(8,128)(2,1)S(1)}, bf16[32,2048]{1,0:T(8,128)(2,1)S(1)}, u32[]{:S(2)}, u32[]{:S(2)}) collective-permute-start(bf16[32,2048]{1,0:T(8,128)(2,1)S(1)} %convert_element_type.27.refs_0_), channel_id=1, source_target_pairs={{0,8},{2,10},{4,12},{6,14},{8,0},{10,2},{12,4},{14,6},{1,9},{3,11}... | collective-permute-start | bytes 393224 | tf_op jit(solution)/shard_map/ppermute | solution.py:270
  5.8 1.6 %collective-permute-start.1 = (bf16[32,2048]{1,0:T(8,128)(2,1)S(1)}, bf16[32,2048]{1,0:T(8,128)(2,1)S(1)}, u32[]{:S(2)}, u32[]{:S(2)}) collective-permute-start(bf16[32,2048]{1,0:T(8,128)(2,1)S(1)} %convert_element_type.27.refs_0_), channel_id=1, source_target_pairs={{0,4},{2,6},{4,0},{6,2},{8,12},{10,14},{12,8},{14,10},{1,5},{3,7},... | collective-permute-start | bytes 393224 | tf_op jit(solution)/shard_map/ppermute | solution.py:270
  7.4 1.5 %collective-permute-start = (bf16[32,2048]{1,0:T(8,128)(2,1)S(1)}, bf16[32,2048]{1,0:T(8,128)(2,1)S(1)}, u32[]{:S(2)}, u32[]{:S(2)}) collective-permute-start(bf16[32,2048]{1,0:T(8,128)(2,1)S(1)} %convert_element_type.27.refs_0_), channel_id=1, source_target_pairs={{0,2},{2,0},{4,6},{6,4},{8,10},{10,8},{12,14},{14,12},{1,3},{3,1},... | collective-permute-start | bytes 393224 | tf_op jit(solution)/shard_map/ppermute | solution.py:270
  9.5 2.8 %shard_map.77.tile = bf16[1024,2048]{1,0:T(8,128)(2,1)S(1)} custom-call(s32[64]{0:T(128)} %bitcast.6, s32[64]{0:T(128)} %bitcast.7, s32[1]{0:T(128)} %bitcast.4.count, bf16[64,128,128]{2,1,0:T(8,128)(2,1)} %bitcast.5), custom_call_target="tpu_custom_call" | custom-call | tf_op jit(solution)/shard_map/pallas_call | solution.py:86
  13.0 1.5 %collective-permute-start.6 = (bf16[32,2048]{1,0:T(8,128)(2,1)S(1)}, bf16[32,2048]{1,0:T(8,128)(2,1)S(1)}, u32[]{:S(2)}, u32[]{:S(2)}) collective-permute-start(bf16[32,2048]{1,0:T(8,128)(2,1)S(1)} %collective-permute-done.2.refs_4_), channel_id=1, source_target_pairs={{0,4},{2,6},{4,0},{6,2},{8,12},{10,14},{12,8},{14,10},{1,5},{3,7},... | collective-permute-start | bytes 393224 | tf_op jit(solution)/shard_map/ppermute | solution.py:270
  14.5 0.5 %collective-permute-start.4 = (bf16[32,2048]{1,0:T(8,128)(2,1)S(1)}, bf16[32,2048]{1,0:T(8,128)(2,1)S(1)}, u32[]{:S(2)}, u32[]{:S(2)}) collective-permute-start(bf16[32,2048]{1,0:T(8,128)(2,1)S(1)} %collective-permute-done.refs_1_), channel_id=1, source_target_pairs={{0,4},{2,6},{4,0},{6,2},{8,12},{10,14},{12,8},{14,10},{1,5},{3,7},... | collective-permute-start | bytes 393224 | tf_op jit(solution)/shard_map/ppermute | solution.py:270
  15.1 1.5 %collective-permute-start.5 = (bf16[32,2048]{1,0:T(8,128)(2,1)S(1)}, bf16[32,2048]{1,0:T(8,128)(2,1)S(1)}, u32[]{:S(2)}, u32[]{:S(2)}) collective-permute-start(bf16[32,2048]{1,0:T(8,128)(2,1)S(1)} %collective-permute-done.2.refs_4_), channel_id=1, source_target_pairs={{0,2},{2,0},{4,6},{6,4},{8,10},{10,8},{12,14},{14,12},{1,3},{3,1},... | collective-permute-start | bytes 393224 | tf_op jit(solution)/shard_map/ppermute | solution.py:270
  16.6 2.8 %collective-permute-done.6.refs_6_ = bf16[32,2048]{1,0:T(8,128)(2,1)S(1)} collective-permute-done((bf16[32,2048]{1,0:T(8,128)(2,1)S(1)}, bf16[32,2048]{1,0:T(8,128)(2,1)S(1)}, u32[]{:S(2)}, u32[]{:S(2)}) %collective-permute-start.6) | collective-permute-done | bytes 131104 | tf_op jit(solution)/shard_map/ppermute | solution.py:270
  19.5 1.4 %collective-permute-start.7 = (bf16[32,2048]{1,0:T(8,128)(2,1)S(1)}, bf16[32,2048]{1,0:T(8,128)(2,1)S(1)}, u32[]{:S(2)}, u32[]{:S(2)}) collective-permute-start(bf16[32,2048]{1,0:T(8,128)(2,1)S(1)} %collective-permute-done.6.refs_6_), channel_id=1, source_target_pairs={{0,2},{2,0},{4,6},{6,4},{8,10},{10,8},{12,14},{14,12},{1,3},{3,1},... | collective-permute-start | bytes 393224 | tf_op jit(solution)/shard_map/ppermute | solution.py:270
  21.0 1.4 %shard_map.78 = (bf16[224,2048]{1,0:T(8,128)(2,1)S(1)}, f32[224,1024]{1,0:T(8,128)S(1)}, bf16[112,1024]{1,0:T(8,128)(2,1)S(1)}, bf16[112,1024]{1,0:T(8,128)(2,1)S(1)}) custom-call(bf16[1024,2048]{1,0:T(8,128)(2,1)S(1)} %shard_map.77.tile, bf16[32,2048]{1,0:T(8,128)(2,1)S(1)} %convert_element_type.27.refs_0_, ...), custom_call_target="tpu_custom_call" | custom-call | bytes 16777216 | tf_op jit(solution)/shard_map/pallas_call | solution.py:296
  23.0 1.4 %collective-permute-done.7.share = bf16[32,2048]{1,0:T(8,128)(2,1)S(1)} collective-permute-done((bf16[32,2048]{1,0:T(8,128)(2,1)S(1)}, bf16[32,2048]{1,0:T(8,128)(2,1)S(1)}, u32[]{:S(2)}, u32[]{:S(2)}) %collective-permute-start.7) | collective-permute-done | bytes 131104 | tf_op jit(solution)/shard_map/ppermute | solution.py:270
  24.4 1.7 %shard_map.79 = (bf16[256,2048]{1,0:T(8,128)(2,1)S(1)}, f32[96,1024]{1,0:T(8,128)S(1)}, bf16[96,1024]{1,0:T(8,128)(2,1)S(1)}) custom-call(bf16[1024,2048]{1,0:T(8,128)(2,1)S(1)} %shard_map.77.tile, bf16[224,2048]{1,0:T(8,128)(2,1)S(1)} %get-tuple-element.33.first, bf16[32,2048]{1,0:T(8,128)(2,1)S(1)} %collective-permute-done.7.share), custom_call_target="tpu_custom_call" | custom-call | tf_op jit(solution)/shard_map/pallas_call | solution.py:310
  26.2 1.4 %collective-permute-done.8.other = bf16[96,1024]{1,0:T(8,128)(2,1)S(1)} collective-permute-done((bf16[96,1024]{1,0:T(8,128)(2,1)S(1)}, bf16[96,1024]{1,0:T(8,128)(2,1)S(1)}, u32[]{:S(2)}, u32[]{:S(2)}) %collective-permute-start.8) | collective-permute-done | bytes 196640 | tf_op jit(solution)/shard_map/ppermute | solution.py:273
  27.6 2.6 %shard_map.80 = (f32[128,1024]{1,0:T(8,128)}, bf16[256,1024]{1,0:T(8,128)(2,1)S(1)}, bf16[32,2048]{1,0:T(8,128)(2,1)S(1)}, bf16[16,2048]{1,0:T(8,128)(2,1)S(1)}) custom-call(bf16[1024,2048]{1,0:T(8,128)(2,1)S(1)} %shard_map.77.tile, f32[224,1024]{1,0:T(8,128)S(1)} %get-tuple-element.32.mine_first, f32[96,1024]{1,0:T(8,128)S(1)} %get-tuple-element.34.mine, ...), custom_call_target="tpu_custom_call" | custom-call | tf_op jit(solution)/shard_map/pallas_call | solution.py:326
  30.2 1.4 %collective-permute-start.14 = (bf16[32,2048]{1,0:T(8,128)(2,1)S(1)}, bf16[32,2048]{1,0:T(8,128)(2,1)S(1)}, u32[]{:S(2)}, u32[]{:S(2)}) collective-permute-start(bf16[32,2048]{1,0:T(8,128)(2,1)S(1)} %get-tuple-element.45), channel_id=1, source_target_pairs={{0,2},{2,0},{4,6},{6,4},{8,10},{10,8},{12,14},{14,12},{1,3},{3,1},... | collective-permute-start | bytes 393224 | tf_op jit(solution)/shard_map/ppermute | solution.py:270
  31.6 1.8 %collective-permute-start.11 = (bf16[16,2048]{1,0:T(8,128)(2,1)S(1)}, bf16[16,2048]{1,0:T(8,128)(2,1)S(1)}, u32[]{:S(2)}, u32[]{:S(2)}) collective-permute-start(bf16[16,2048]{1,0:T(8,128)(2,1)S(1)} %get-tuple-element.40), channel_id=1, source_target_pairs={{0,8},{2,10},{4,12},{6,14},{8,0},{10,2},{12,4},{14,6},{1,9},{3,11}... | collective-permute-start | bytes 196616 | tf_op jit(solution)/shard_map/ppermute | solution.py:270
  33.4 1.1 %shard_map.81 = (bf16[32,2048]{1,0:T(8,128)(2,1)S(1)}, bf16[64,2048]{1,0:T(8,128)(2,1)S(1)}, f32[32,2048]{1,0:T(8,128)S(1)}, f32[32,2048]{1,0:T(8,128)S(1)}, f32...) custom-call(bf16[256,1024]{1,0:T(8,128)(2,1)S(1)} %get-tuple-element.41.low, bf16[1024,2048]{1,0:T(8,128)(2,1)S(1)} %shard_map.77.tile), custom_call_target="tpu_custom_call" | custom-call | bytes 16777216 | tf_op jit(solution)/shard_map/pallas_call | solution.py:357
  34.6 0.6 %collective-permute-start.13 = (bf16[32,2048]{1,0:T(8,128)(2,1)S(1)}, bf16[32,2048]{1,0:T(8,128)(2,1)S(1)}, u32[]{:S(2)}, u32[]{:S(2)}) collective-permute-start(bf16[32,2048]{1,0:T(8,128)(2,1)S(1)} %get-tuple-element.43), channel_id=1, source_target_pairs={{0,2},{2,0},{4,6},{6,4},{8,10},{10,8},{12,14},{14,12},{1,3},{3,1},... | collective-permute-start | bytes 393224 | tf_op jit(solution)/shard_map/ppermute | solution.py:270
  35.2 0.6 %collective-permute-done.14.refs_0_ = bf16[32,2048]{1,0:T(8,128)(2,1)S(1)} collective-permute-done((bf16[32,2048]{1,0:T(8,128)(2,1)S(1)}, bf16[32,2048]{1,0:T(8,128)(2,1)S(1)}, u32[]{:S(2)}, u32[]{:S(2)}) %collective-permute-start.14) | collective-permute-done | bytes 131104 | tf_op jit(solution)/shard_map/ppermute | solution.py:270
  35.8 1.6 %collective-permute-start.15 = (bf16[32,2048]{1,0:T(8,128)(2,1)S(1)}, bf16[32,2048]{1,0:T(8,128)(2,1)S(1)}, u32[]{:S(2)}, u32[]{:S(2)}) collective-permute-start(bf16[32,2048]{1,0:T(8,128)(2,1)S(1)} %shard_map.82), channel_id=1, source_target_pairs={{0,4},{2,6},{4,0},{6,2},{8,12},{10,14},{12,8},{14,10},{1,5},{3,7},... | collective-permute-start | bytes 393224 | tf_op jit(solution)/shard_map/ppermute | solution.py:270
  37.4 0.7 %collective-permute-done.11 = bf16[16,2048]{1,0:T(8,128)(2,1)S(1)} collective-permute-done((bf16[16,2048]{1,0:T(8,128)(2,1)S(1)}, bf16[16,2048]{1,0:T(8,128)(2,1)S(1)}, u32[]{:S(2)}, u32[]{:S(2)}) %collective-permute-start.11) | collective-permute-done | bytes 65568 | tf_op jit(solution)/shard_map/ppermute | solution.py:270
  38.4 1.0 %collective-permute-start.18 = (bf16[64,2048]{1,0:T(8,128)(2,1)S(1)}, bf16[64,2048]{1,0:T(8,128)(2,1)S(1)}, u32[]{:S(2)}, u32[]{:S(2)}) collective-permute-start(bf16[64,2048]{1,0:T(8,128)(2,1)S(1)} %get-tuple-element.50), channel_id=1, source_target_pairs={{0,2},{2,0},{4,6},{6,4},{8,10},{10,8},{12,14},{14,12},{1,3},{3,1},... | collective-permute-start | bytes 786440 | tf_op jit(solution)/shard_map/ppermute | solution.py:270
  39.6 1.9 %collective-permute-done.15.refs_1_ = bf16[32,2048]{1,0:T(8,128)(2,1)S(1)} collective-permute-done((bf16[32,2048]{1,0:T(8,128)(2,1)S(1)}, bf16[32,2048]{1,0:T(8,128)(2,1)S(1)}, u32[]{:S(2)}, u32[]{:S(2)}) %collective-permute-start.15) | collective-permute-done | bytes 131104 | tf_op jit(solution)/shard_map/ppermute | solution.py:270
  41.7 0.8 %collective-permute-done.12 = bf16[16,2048]{1,0:T(8,128)(2,1)S(1)} collective-permute-done((bf16[16,2048]{1,0:T(8,128)(2,1)S(1)}, bf16[16,2048]{1,0:T(8,128)(2,1)S(1)}, u32[]{:S(2)}, u32[]{:S(2)}) %collective-permute-start.12) | collective-permute-done | bytes 65568 | tf_op jit(solution)/shard_map/ppermute | solution.py:270
  42.5 1.0 %collective-permute-start.16 = (bf16[16,2048]{1,0:T(8,128)(2,1)S(1)}, bf16[16,2048]{1,0:T(8,128)(2,1)S(1)}, u32[]{:S(2)}, u32[]{:S(2)}) collective-permute-start(bf16[16,2048]{1,0:T(8,128)(2,1)S(1)} %add_convert_fusion), channel_id=1, source_target_pairs={{0,2},{2,0},{4,6},{6,4},{8,10},{10,8},{12,14},{14,12},{1,3},{3,1},... | collective-permute-start | bytes 196616 | tf_op jit(solution)/shard_map/ppermute | solution.py:270
  43.5 2.9 %collective-permute-start.20 = (bf16[32,2048]{1,0:T(8,128)(2,1)S(1)}, bf16[32,2048]{1,0:T(8,128)(2,1)S(1)}, u32[]{:S(2)}, u32[]{:S(2)}) collective-permute-start(bf16[32,2048]{1,0:T(8,128)(2,1)S(1)} %shard_map.83), channel_id=1, source_target_pairs={{0,8},{2,10},{4,12},{6,14},{8,0},{10,2},{12,4},{14,6},{1,9},{3,11}... | collective-permute-start | bytes 393224 | tf_op jit(solution)/shard_map/ppermute | solution.py:270
  46.5 1.7 %collective-permute-start.19 = (bf16[32,2048]{1,0:T(8,128)(2,1)S(1)}, bf16[32,2048]{1,0:T(8,128)(2,1)S(1)}, u32[]{:S(2)}, u32[]{:S(2)}) collective-permute-start(bf16[32,2048]{1,0:T(8,128)(2,1)S(1)} %get-tuple-element.52), channel_id=1, source_target_pairs={{0,4},{2,6},{4,0},{6,2},{8,12},{10,14},{12,8},{14,10},{1,5},{3,7},... | collective-permute-start | bytes 393224 | tf_op jit(solution)/shard_map/ppermute | solution.py:270
  48.3 2.0 %collective-permute-done.20.refs_1_ = bf16[32,2048]{1,0:T(8,128)(2,1)S(1)} collective-permute-done((bf16[32,2048]{1,0:T(8,128)(2,1)S(1)}, bf16[32,2048]{1,0:T(8,128)(2,1)S(1)}, u32[]{:S(2)}, u32[]{:S(2)}) %collective-permute-start.20) | collective-permute-done | bytes 131104 | tf_op jit(solution)/shard_map/ppermute | solution.py:270
  50.2 1.3 %collective-permute-done.19.refs_0_ = bf16[32,2048]{1,0:T(8,128)(2,1)S(1)} collective-permute-done((bf16[32,2048]{1,0:T(8,128)(2,1)S(1)}, bf16[32,2048]{1,0:T(8,128)(2,1)S(1)}, u32[]{:S(2)}, u32[]{:S(2)}) %collective-permute-start.19) | collective-permute-done | bytes 131104 | tf_op jit(solution)/shard_map/ppermute | solution.py:270
  51.7 1.0 %shard_map.86 = f32[32,2048]{1,0:T(8,128)} custom-call(f32[16,2048]{1,0:T(8,128)S(1)} %convert_add_fusion.mine, f32[16,2048]{1,0:T(8,128)S(1)} %collective-permute-done.17.other, bf16[256,2048]{1,0:T(8,128)(2,1)S(1)} %get-tuple-element.47.panel, f32[32,2048]{1,0:T(8,128)S(1)} %copy-done, f32[32,2048]{1,0:T(8,128)S(1)} %shard_map.85.data), custom_call_target="tpu_custom_call" | custom-call | tf_op jit(solution)/shard_map/pallas_call | solution.py:396
  (28 shorter events, 2.4 us)
Async XLA Ops:
  0.6 12.4 %collective-permute-start.3 = (f32[128,1024]{1,0:T(8,128)}, f32[128,1024]{1,0:T(8,128)S(1)}, u32[]{:S(2)}, u32[]{:S(2)}) collective-permute-start(f32[128,1024]{1,0:T(8,128)} %factor_mine.1), channel_id=1, source_target_pairs={{0,1},{1,0},{2,3},{3,2},{4,5},{5,4},{6,7},{7,6},{8,9},{9,8},{10,11... | collective-permute-start | bytes 1572872 | tf_op jit(solution)/shard_map/ppermute | solution.py:273
  2.1 10.7 %collective-permute-start.2 = (bf16[32,2048]{1,0:T(8,128)(2,1)S(1)}, bf16[32,2048]{1,0:T(8,128)(2,1)S(1)}, u32[]{:S(2)}, u32[]{:S(2)}) collective-permute-start(bf16[32,2048]{1,0:T(8,128)(2,1)S(1)} %convert_element_type.27.refs_0_), channel_id=1, source_target_pairs={{0,8},{2,10},{4,12},{6,14},{8,0},{10,2},{12,4},{14,6},{1,9},{3,11}... | collective-permute-start | bytes 393224 | tf_op jit(solution)/shard_map/ppermute | solution.py:270
  5.8 7.3 %collective-permute-start.1 = (bf16[32,2048]{1,0:T(8,128)(2,1)S(1)}, bf16[32,2048]{1,0:T(8,128)(2,1)S(1)}, u32[]{:S(2)}, u32[]{:S(2)}) collective-permute-start(bf16[32,2048]{1,0:T(8,128)(2,1)S(1)} %convert_element_type.27.refs_0_), channel_id=1, source_target_pairs={{0,4},{2,6},{4,0},{6,2},{8,12},{10,14},{12,8},{14,10},{1,5},{3,7},... | collective-permute-start | bytes 393224 | tf_op jit(solution)/shard_map/ppermute | solution.py:270
  7.4 5.7 %collective-permute-start = (bf16[32,2048]{1,0:T(8,128)(2,1)S(1)}, bf16[32,2048]{1,0:T(8,128)(2,1)S(1)}, u32[]{:S(2)}, u32[]{:S(2)}) collective-permute-start(bf16[32,2048]{1,0:T(8,128)(2,1)S(1)} %convert_element_type.27.refs_0_), channel_id=1, source_target_pairs={{0,2},{2,0},{4,6},{6,4},{8,10},{10,8},{12,14},{14,12},{1,3},{3,1},... | collective-permute-start | bytes 393224 | tf_op jit(solution)/shard_map/ppermute | solution.py:270
  12.4 15.2 %copy-start.1 = (f32[128,1024]{1,0:T(8,128)S(1)}, f32[128,1024]{1,0:T(8,128)}, u32[]{:S(2)}) copy-start(f32[128,1024]{1,0:T(8,128)} %factor_mine.1) | copy-start | bytes 1572868
  13.0 6.4 %collective-permute-start.6 = (bf16[32,2048]{1,0:T(8,128)(2,1)S(1)}, bf16[32,2048]{1,0:T(8,128)(2,1)S(1)}, u32[]{:S(2)}, u32[]{:S(2)}) collective-permute-start(bf16[32,2048]{1,0:T(8,128)(2,1)S(1)} %collective-permute-done.2.refs_4_), channel_id=1, source_target_pairs={{0,4},{2,6},{4,0},{6,2},{8,12},{10,14},{12,8},{14,10},{1,5},{3,7},... | collective-permute-start | bytes 393224 | tf_op jit(solution)/shard_map/ppermute | solution.py:270
  14.5 6.5 %collective-permute-start.4 = (bf16[32,2048]{1,0:T(8,128)(2,1)S(1)}, bf16[32,2048]{1,0:T(8,128)(2,1)S(1)}, u32[]{:S(2)}, u32[]{:S(2)}) collective-permute-start(bf16[32,2048]{1,0:T(8,128)(2,1)S(1)} %collective-permute-done.refs_1_), channel_id=1, source_target_pairs={{0,4},{2,6},{4,0},{6,2},{8,12},{10,14},{12,8},{14,10},{1,5},{3,7},... | collective-permute-start | bytes 393224 | tf_op jit(solution)/shard_map/ppermute | solution.py:270
  15.1 5.9 %collective-permute-start.5 = (bf16[32,2048]{1,0:T(8,128)(2,1)S(1)}, bf16[32,2048]{1,0:T(8,128)(2,1)S(1)}, u32[]{:S(2)}, u32[]{:S(2)}) collective-permute-start(bf16[32,2048]{1,0:T(8,128)(2,1)S(1)} %collective-permute-done.2.refs_4_), channel_id=1, source_target_pairs={{0,2},{2,0},{4,6},{6,4},{8,10},{10,8},{12,14},{14,12},{1,3},{3,1},... | collective-permute-start | bytes 393224 | tf_op jit(solution)/shard_map/ppermute | solution.py:270
  19.5 5.0 %collective-permute-start.7 = (bf16[32,2048]{1,0:T(8,128)(2,1)S(1)}, bf16[32,2048]{1,0:T(8,128)(2,1)S(1)}, u32[]{:S(2)}, u32[]{:S(2)}) collective-permute-start(bf16[32,2048]{1,0:T(8,128)(2,1)S(1)} %collective-permute-done.6.refs_6_), channel_id=1, source_target_pairs={{0,2},{2,0},{4,6},{6,4},{8,10},{10,8},{12,14},{14,12},{1,3},{3,1},... | collective-permute-start | bytes 393224 | tf_op jit(solution)/shard_map/ppermute | solution.py:270
  22.4 3.7 %collective-permute-start.9 = (bf16[112,1024]{1,0:T(8,128)(2,1)S(1)}, bf16[112,1024]{1,0:T(8,128)(2,1)S(1)}, u32[]{:S(2)}, u32[]{:S(2)}) collective-permute-start(bf16[112,1024]{1,0:T(8,128)(2,1)S(1)} %get-tuple-element.37), channel_id=1, source_target_pairs={{0,1},{1,0},{2,3},{3,2},{4,5},{5,4},{6,7},{7,6},{8,9},{9,8},{10,11... | collective-permute-start | bytes 688136 | tf_op jit(solution)/shard_map/ppermute | solution.py:273
  22.5 3.7 %collective-permute-start.10 = (bf16[112,1024]{1,0:T(8,128)(2,1)S(1)}, bf16[112,1024]{1,0:T(8,128)(2,1)S(1)}, u32[]{:S(2)}, u32[]{:S(2)}) collective-permute-start(bf16[112,1024]{1,0:T(8,128)(2,1)S(1)} %get-tuple-element.38), channel_id=1, source_target_pairs={{0,1},{1,0},{2,3},{3,2},{4,5},{5,4},{6,7},{7,6},{8,9},{9,8},{10,11... | collective-permute-start | bytes 688136 | tf_op jit(solution)/shard_map/ppermute | solution.py:273
  26.1 1.5 %collective-permute-start.8 = (bf16[96,1024]{1,0:T(8,128)(2,1)S(1)}, bf16[96,1024]{1,0:T(8,128)(2,1)S(1)}, u32[]{:S(2)}, u32[]{:S(2)}) collective-permute-start(bf16[96,1024]{1,0:T(8,128)(2,1)S(1)} %get-tuple-element.35), channel_id=1, source_target_pairs={{0,1},{1,0},{2,3},{3,2},{4,5},{5,4},{6,7},{7,6},{8,9},{9,8},{10,11... | collective-permute-start | bytes 589832 | tf_op jit(solution)/shard_map/ppermute | solution.py:273
  30.2 21.5 %copy-start = (f32[32,2048]{1,0:T(8,128)S(1)}, f32[32,2048]{1,0:T(8,128)}, u32[]{:S(2)}) copy-start(f32[32,2048]{1,0:T(8,128)} %factor.1) | copy-start | bytes 786436
  30.2 5.5 %collective-permute-start.14 = (bf16[32,2048]{1,0:T(8,128)(2,1)S(1)}, bf16[32,2048]{1,0:T(8,128)(2,1)S(1)}, u32[]{:S(2)}, u32[]{:S(2)}) collective-permute-start(bf16[32,2048]{1,0:T(8,128)(2,1)S(1)} %get-tuple-element.45), channel_id=1, source_target_pairs={{0,2},{2,0},{4,6},{6,4},{8,10},{10,8},{12,14},{14,12},{1,3},{3,1},... | collective-permute-start | bytes 393224 | tf_op jit(solution)/shard_map/ppermute | solution.py:270
  31.6 6.5 %collective-permute-start.11 = (bf16[16,2048]{1,0:T(8,128)(2,1)S(1)}, bf16[16,2048]{1,0:T(8,128)(2,1)S(1)}, u32[]{:S(2)}, u32[]{:S(2)}) collective-permute-start(bf16[16,2048]{1,0:T(8,128)(2,1)S(1)} %get-tuple-element.40), channel_id=1, source_target_pairs={{0,8},{2,10},{4,12},{6,14},{8,0},{10,2},{12,4},{14,6},{1,9},{3,11}... | collective-permute-start | bytes 196616 | tf_op jit(solution)/shard_map/ppermute | solution.py:270
  34.6 5.1 %collective-permute-start.13 = (bf16[32,2048]{1,0:T(8,128)(2,1)S(1)}, bf16[32,2048]{1,0:T(8,128)(2,1)S(1)}, u32[]{:S(2)}, u32[]{:S(2)}) collective-permute-start(bf16[32,2048]{1,0:T(8,128)(2,1)S(1)} %get-tuple-element.43), channel_id=1, source_target_pairs={{0,2},{2,0},{4,6},{6,4},{8,10},{10,8},{12,14},{14,12},{1,3},{3,1},... | collective-permute-start | bytes 393224 | tf_op jit(solution)/shard_map/ppermute | solution.py:270
  35.8 5.8 %collective-permute-start.15 = (bf16[32,2048]{1,0:T(8,128)(2,1)S(1)}, bf16[32,2048]{1,0:T(8,128)(2,1)S(1)}, u32[]{:S(2)}, u32[]{:S(2)}) collective-permute-start(bf16[32,2048]{1,0:T(8,128)(2,1)S(1)} %shard_map.82), channel_id=1, source_target_pairs={{0,4},{2,6},{4,0},{6,2},{8,12},{10,14},{12,8},{14,10},{1,5},{3,7},... | collective-permute-start | bytes 393224 | tf_op jit(solution)/shard_map/ppermute | solution.py:270
  38.1 4.3 %collective-permute-start.12 = (bf16[16,2048]{1,0:T(8,128)(2,1)S(1)}, bf16[16,2048]{1,0:T(8,128)(2,1)S(1)}, u32[]{:S(2)}, u32[]{:S(2)}) collective-permute-start(bf16[16,2048]{1,0:T(8,128)(2,1)S(1)} %add_convert_fusion.1), channel_id=1, source_target_pairs={{0,4},{2,6},{4,0},{6,2},{8,12},{10,14},{12,8},{14,10},{1,5},{3,7},... | collective-permute-start | bytes 196616 | tf_op jit(solution)/shard_map/ppermute | solution.py:270
  38.4 8.0 %collective-permute-start.18 = (bf16[64,2048]{1,0:T(8,128)(2,1)S(1)}, bf16[64,2048]{1,0:T(8,128)(2,1)S(1)}, u32[]{:S(2)}, u32[]{:S(2)}) collective-permute-start(bf16[64,2048]{1,0:T(8,128)(2,1)S(1)} %get-tuple-element.50), channel_id=1, source_target_pairs={{0,2},{2,0},{4,6},{6,4},{8,10},{10,8},{12,14},{14,12},{1,3},{3,1},... | collective-permute-start | bytes 786440 | tf_op jit(solution)/shard_map/ppermute | solution.py:270
  42.5 5.7 %collective-permute-start.16 = (bf16[16,2048]{1,0:T(8,128)(2,1)S(1)}, bf16[16,2048]{1,0:T(8,128)(2,1)S(1)}, u32[]{:S(2)}, u32[]{:S(2)}) collective-permute-start(bf16[16,2048]{1,0:T(8,128)(2,1)S(1)} %add_convert_fusion), channel_id=1, source_target_pairs={{0,2},{2,0},{4,6},{6,4},{8,10},{10,8},{12,14},{14,12},{1,3},{3,1},... | collective-permute-start | bytes 196616 | tf_op jit(solution)/shard_map/ppermute | solution.py:270
  43.5 6.7 %collective-permute-start.20 = (bf16[32,2048]{1,0:T(8,128)(2,1)S(1)}, bf16[32,2048]{1,0:T(8,128)(2,1)S(1)}, u32[]{:S(2)}, u32[]{:S(2)}) collective-permute-start(bf16[32,2048]{1,0:T(8,128)(2,1)S(1)} %shard_map.83), channel_id=1, source_target_pairs={{0,8},{2,10},{4,12},{6,14},{8,0},{10,2},{12,4},{14,6},{1,9},{3,11}... | collective-permute-start | bytes 393224 | tf_op jit(solution)/shard_map/ppermute | solution.py:270
  46.5 5.1 %collective-permute-start.19 = (bf16[32,2048]{1,0:T(8,128)(2,1)S(1)}, bf16[32,2048]{1,0:T(8,128)(2,1)S(1)}, u32[]{:S(2)}, u32[]{:S(2)}) collective-permute-start(bf16[32,2048]{1,0:T(8,128)(2,1)S(1)} %get-tuple-element.52), channel_id=1, source_target_pairs={{0,4},{2,6},{4,0},{6,2},{8,12},{10,14},{12,8},{14,10},{1,5},{3,7},... | collective-permute-start | bytes 393224 | tf_op jit(solution)/shard_map/ppermute | solution.py:270
  48.2 3.5 %collective-permute-start.17 = (f32[16,2048]{1,0:T(8,128)S(1)}, f32[16,2048]{1,0:T(8,128)S(1)}, u32[]{:S(2)}, u32[]{:S(2)}) collective-permute-start(f32[16,2048]{1,0:T(8,128)S(1)} %convert_add_fusion.mine), channel_id=1, source_target_pairs={{0,1},{1,0},{2,3},{3,2},{4,5},{5,4},{6,7},{7,6},{8,9},{9,8},{10,11... | collective-permute-start | bytes 393224 | tf_op jit(solution)/shard_map/ppermute | solution.py:273

commit v9 on v8

--- a/solution.py
+++ b/solution.py
@@ -191,16 +191,16 @@
     if sends:
         send, gram_out = sends
         send[...] = coded(picked_product(picks, low, tile, chosen)[0])
-        half_gram(low, gram_out)
-
-
-def half_gram(low, out):
-    share = low.shape[0] // 2
-    own = pl.ds(pl.multiple_of(lax.axis_index("gene") * share, share), share)
-    half = dot(low[own], low[...], NT).astype(out.dtype)
-    rows, width = out.shape[0], half.shape[1]
-    for n in range(share // rows):
-        out[:, n * width : (n + 1) * width] = half[n * rows : (n + 1) * rows]
+        gram_blocks(low, gram_out)
+
+
+def gram_blocks(low, out):
+    half = low.shape[0] // 2
+    panel = low[...]
+    gram = dot(panel, panel, NT)
+    out[:half] = gram[:half, :half].astype(out.dtype)
+    out[half : 2 * half] = gram[:half, half:].astype(out.dtype)
+    out[2 * half :] = gram[half:, half:].astype(out.dtype)
 
 
 def picked_product(picks, low, tile, chosen):
@@ -211,20 +211,9 @@
     return [product[n * size : (n + 1) * size] for n in range(len(picks))]
 
 
-def keep_body(picks, low, tile, send, send_pair, *rest):
-    first, second, third, *kept = picked_product(picks, low, tile, rest[-1])
-    send[...] = coded(first)
-    size = first.shape[0]
-    send_pair[:size] = coded(second)
-    send_pair[size:] = coded(third)
-    for out, part in zip(rest[:-1], kept):
-        out[...] = part
-
-
-def pair_body(keep, other, arrived, out, total):
-    size = keep.shape[0]
-    out[...] = coded(keep[...] + decoded(arrived[:size]))
-    total[...] = other[...] + decoded(arrived[size:])
+def keep_body(picks, low, tile, *rest):
+    for out, part in zip(rest[:-1], picked_product(picks, low, tile, rest[-1])):
+        out[...] = coded(part) if out.dtype == jnp.bfloat16 else part
 
 
 def sum_body(keep, *refs):
@@ -242,14 +231,15 @@
 
 
 def last_body(mine, other, panel, factor, data, out, gram):
-    rows, width = mine.shape[0], gram.shape[1]
-    core = lax.axis_index("gene")
-    for half, part in ((core, mine), (1 - core, other)):
-        for n in range(part.shape[1] // width):
-            row = pl.multiple_of(half * (gram.shape[0] // 2) + n * rows, rows)
-            gram[pl.ds(row, rows)] = part[:, n * width : (n + 1) * width]
-    whole = gram[...]
-    norm = jnp.sum(jnp.sum(whole * whole, axis=1, keepdims=True), axis=0, keepdims=True)
+    half = mine.shape[0] // 3
+    quarters = mine[...].astype(jnp.float32) + other[...].astype(jnp.float32)
+    upper, side, lower = quarters[:half], quarters[half : 2 * half], quarters[2 * half :]
+    gram[:half, :half] = upper
+    gram[:half, half:] = side
+    gram[half:, :half] = side.T
+    gram[half:, half:] = lower
+    squares = upper * upper + 2.0 * (side * side) + lower * lower
+    norm = jnp.sum(jnp.sum(squares, axis=1, keepdims=True), axis=0, keepdims=True)
     rate = 1.0 / (jnp.sqrt(norm) + 1e-06)
     stepped = split_dot(gram[owned(0, factor.shape[0])], panel[...])
     out[...] = jnp.maximum(factor[...] - rate * (stepped - data[...]), 0.0)
@@ -263,8 +253,7 @@
     n_cell = lax.axis_size("cell")
     kdim = cell_factor.shape[0] * lax.axis_size("gene")
     size = gene_factor.shape[0]
-    gram_rows = kdim // 2 * kdim // GENE_DEV
-    paired = n_cell == 8 and size % 16 == 0 and gram_rows % 16 == 0
+    paired = n_cell == 8 and size % 16 == 0 and kdim % (2 * BLK) == 0
 
     def swap(value, bits):
         return lax.ppermute(value, "cell", [(n, n ^ bits) for n in range(n_cell)])
@@ -328,7 +317,7 @@
         (
             shape(cell_factor.shape, jnp.float32),
             shape((kdim, CELL_DEV), jnp.bfloat16),
-            *([wide(size, jnp.bfloat16), wide(gram_rows, jnp.bfloat16)] if paired else []),
+            *([wide(size, jnp.bfloat16), shape((3 * kdim // 2, kdim // 2), jnp.bfloat16)] if paired else []),
         ),
         0,
         6 + n_parts,
@@ -354,11 +343,10 @@
         return (cell_next, jnp.maximum(gene_factor - rate_gene * (stepped - own_cols), 0.0))
 
     arrived = [swap(sends[0], 1)]
-    send, send_pair, *keeps = call(
+    *parts, keep_third, keep_second, keep_near, own = call(
         functools.partial(keep_body, sent + kept),
         (
-            wide(size, jnp.bfloat16),
-            wide(2 * size, jnp.bfloat16),
+            *[wide(size, jnp.bfloat16) for _ in sent],
             *[wide(size, jnp.float32) for _ in kept],
         ),
         0,
@@ -368,31 +356,23 @@
         [pltpu.VMEM((kdim - size, CELL_DEV), jnp.bfloat16)],
     )(next_low, tile)
     gram = sends[1]
-    arrived += [swap(send, 1), swap(send_pair, 1)]
+    arrived += [swap(part, 1) for part in parts]
 
     def add_up(cost, keep, *parts):
         body = call(sum_body, wide(size, jnp.bfloat16), 0, 1 + len(parts), 0, cost)
         return body(keep, *parts)
 
-    through = add_up(AHEAD, keeps[0], arrived[0])
+    through = swap(add_up(AHEAD, keep_third, arrived[0]), 2)
     gram_arrived = swap(gram, 4)
-    through = swap(through, 2)
-    beside, total = call(
-        pair_body, (wide(size, jnp.bfloat16), wide(size, jnp.float32)), 0, 3, 0, AHEAD
-    )(keeps[2], keeps[3], arrived[2])
-    across = add_up(AHEAD, keeps[1], arrived[1], through)
-
+    beside = swap(add_up(AHEAD, keep_near, arrived[2]), 2)
+    across = add_up(AHEAD, keep_second, arrived[1], through)
     gram = (gram.astype(jnp.float32) + gram_arrived.astype(jnp.float32)).astype(jnp.bfloat16)
     gram_arrived = swap(gram, 2)
-    gram_arrived, across = lax.optimization_barrier((gram_arrived, across))
     across = swap(across, 4)
-    beside = swap(beside, 2)
     gram = (gram.astype(jnp.float32) + gram_arrived.astype(jnp.float32)).astype(jnp.bfloat16)
-
     partner = swap(gram, 1)
-    total = call(total_body, wide(size, jnp.float32), 0, 3, 0, AHEAD)(total, beside, across)
-
-    gram = gram.astype(jnp.float32) + partner.astype(jnp.float32)
+    total = call(total_body, wide(size, jnp.float32), 0, 4, 0, AHEAD)(own, arrived[3], beside, across)
+    partner, total = lax.optimization_barrier((partner, total))
     gene_next = call(
         last_body,
         wide(size, jnp.float32),
@@ -401,7 +381,7 @@
         0,
         0,
         [pltpu.VMEM((kdim, kdim), jnp.float32)],
-    )(gram, swap_core(gram), panel, gene_factor, total)
+    )(gram, partner, panel, gene_factor, total)
     return (cell_next, gene_next)
 
 

time: 53 us -> 52.9 us (level)
    ppermute x16 -> x17, starting transfers between devices: 24 us -> 23.6 us  [swap(): return lax.ppermute(value, 'cell', [(n, n ^ bits) for n in range(n_cell)])]
    ppermute x16 -> x17, waiting for transfers between devices: 12.6 us -> 13 us  [swap(): return lax.ppermute(value, 'cell', [(n, n ^ bits) for n in range(n_cell)])]
    ppermute x5 -> x4, starting transfers between devices: 1.23 us -> 1.16 us  [swap_core(): return lax.ppermute(value, 'gene', [(0, 1), (1, 0)])]
    pallas_call x3 -> x2, Pallas kernels: 1.25 us -> 1.2 us  [the longest x1 1.12 us: shards(): call(functools.partial(keep_body, sent + kept), (*[wide(size, jnp.bfloat1...]
    ppermute x5 -> x4, waiting for transfers between devices: 1.42 us -> 1.42 us  [swap_core(): return lax.ppermute(value, 'gene', [(0, 1), (1, 0)])]
  transfers between devices with their start and end apart: 21 -> 21, of which waited for: 13 -> 12; matrix products, arithmetic and copies ran while one was open for 2% -> 2% of each run, Pallas kernels for 14% -> 14%
where the time goes in v9:
time: 52.9 us; the launch traced here: 52.6 us
  starting transfers between devices  24.8 us (47%)
  waiting for transfers between devices  14.4 us (27%)
  Pallas kernels  11 us (21%)
  between operations  1.4 us (3%)
  other arithmetic  1.02 us (2%)
    ppermute x17, starting transfers between devices, swap(): return lax.ppermute(value, 'cell', [(n, n ^ bits) for n in range(n_cell)])  23.6 us
    ppermute x17, waiting for transfers between devices, swap(): return lax.ppermute(value, 'cell', [(n, n ^ bits) for n in range(n_cell)])  13 us
    pallas_call x1, Pallas kernels, dense_tile(): pl.pallas_call(dense_body, out_shape=shape((CELL_DEV, GENE_DEV), jnp.bflo...  2.84 us
    pallas_call x1, Pallas kernels, shards(): call(functools.partial(cell_body, order, [7], n_parts), (shape(cell_facto...  2.61 us
    pallas_call x1, Pallas kernels, shards(): call(functools.partial(second_body, order), (wide(kdim, jnp.bfloat16), sh...  1.65 us
    pallas_call x1, Pallas kernels, shards(): call(functools.partial(first_body, n_parts), (wide(first_rows, jnp.bfloat...  1.42 us
    ppermute x4, waiting for transfers between devices, swap_core(): return lax.ppermute(value, 'gene', [(0, 1), (1, 0)])  1.42 us
    ppermute x4, starting transfers between devices, swap_core(): return lax.ppermute(value, 'gene', [(0, 1), (1, 0)])  1.16 us
  transfers between devices with their start and end apart: 21, of which 12 were waited for; matrix products, arithmetic and copies ran while one was open for 2% of the time, Pallas kernels for 14%

profile of v9, /device:TPU:0, one launch (start us, length us, event | category | flops | bytes accessed | tf_op | source)
XLA Modules:
  0.0 52.6 jit_solution(3701377043576390400)
XLA Ops:
  0.6 0.5 collective-permute-start.3
  1.1 1.0 %convert_element_type.21.refs_0_ = bf16[32,2048]{1,0:T(8,128)(2,1)S(1)} convert(f32[32,2048]{1,0:T(8,128)} %factor.1) | non-fusion elementwise | flops 65536 | bytes 393216 | tf_op jit(solution)/shard_map/convert_element_type | solution.py:267
  2.1 3.7 %collective-permute-start.2 = (bf16[32,2048]{1,0:T(8,128)(2,1)S(1)}, bf16[32,2048]{1,0:T(8,128)(2,1)S(1)}, u32[]{:S(2)}, u32[]{:S(2)}) collective-permute-start(bf16[32,2048]{1,0:T(8,128)(2,1)S(1)} %convert_element_type.21.refs_0_), channel_id=1, source_target_pairs={{0,8},{2,10},{4,12},{6,14},{8,0},{10,2},{12,4},{14,6},{1,9},{3,11}... | collective-permute-start | bytes 393224 | tf_op jit(solution)/shard_map/ppermute | solution.py:259
  5.8 1.6 %collective-permute-start.1 = (bf16[32,2048]{1,0:T(8,128)(2,1)S(1)}, bf16[32,2048]{1,0:T(8,128)(2,1)S(1)}, u32[]{:S(2)}, u32[]{:S(2)}) collective-permute-start(bf16[32,2048]{1,0:T(8,128)(2,1)S(1)} %convert_element_type.21.refs_0_), channel_id=1, source_target_pairs={{0,4},{2,6},{4,0},{6,2},{8,12},{10,14},{12,8},{14,10},{1,5},{3,7},... | collective-permute-start | bytes 393224 | tf_op jit(solution)/shard_map/ppermute | solution.py:259
  7.4 1.5 %collective-permute-start = (bf16[32,2048]{1,0:T(8,128)(2,1)S(1)}, bf16[32,2048]{1,0:T(8,128)(2,1)S(1)}, u32[]{:S(2)}, u32[]{:S(2)}) collective-permute-start(bf16[32,2048]{1,0:T(8,128)(2,1)S(1)} %convert_element_type.21.refs_0_), channel_id=1, source_target_pairs={{0,2},{2,0},{4,6},{6,4},{8,10},{10,8},{12,14},{14,12},{1,3},{3,1},... | collective-permute-start | bytes 393224 | tf_op jit(solution)/shard_map/ppermute | solution.py:259
  9.5 2.8 %shard_map.77.tile = bf16[1024,2048]{1,0:T(8,128)(2,1)S(1)} custom-call(s32[64]{0:T(128)} %bitcast.6, s32[64]{0:T(128)} %bitcast.7, s32[1]{0:T(128)} %bitcast.4.count, bf16[64,128,128]{2,1,0:T(8,128)(2,1)} %bitcast.5), custom_call_target="tpu_custom_call" | custom-call | tf_op jit(solution)/shard_map/pallas_call | solution.py:86
  13.0 1.5 %collective-permute-start.6 = (bf16[32,2048]{1,0:T(8,128)(2,1)S(1)}, bf16[32,2048]{1,0:T(8,128)(2,1)S(1)}, u32[]{:S(2)}, u32[]{:S(2)}) collective-permute-start(bf16[32,2048]{1,0:T(8,128)(2,1)S(1)} %collective-permute-done.2.refs_4_), channel_id=1, source_target_pairs={{0,4},{2,6},{4,0},{6,2},{8,12},{10,14},{12,8},{14,10},{1,5},{3,7},... | collective-permute-start | bytes 393224 | tf_op jit(solution)/shard_map/ppermute | solution.py:259
  14.5 0.5 %collective-permute-start.4 = (bf16[32,2048]{1,0:T(8,128)(2,1)S(1)}, bf16[32,2048]{1,0:T(8,128)(2,1)S(1)}, u32[]{:S(2)}, u32[]{:S(2)}) collective-permute-start(bf16[32,2048]{1,0:T(8,128)(2,1)S(1)} %collective-permute-done.refs_1_), channel_id=1, source_target_pairs={{0,4},{2,6},{4,0},{6,2},{8,12},{10,14},{12,8},{14,10},{1,5},{3,7},... | collective-permute-start | bytes 393224 | tf_op jit(solution)/shard_map/ppermute | solution.py:259
  15.1 1.5 %collective-permute-start.5 = (bf16[32,2048]{1,0:T(8,128)(2,1)S(1)}, bf16[32,2048]{1,0:T(8,128)(2,1)S(1)}, u32[]{:S(2)}, u32[]{:S(2)}) collective-permute-start(bf16[32,2048]{1,0:T(8,128)(2,1)S(1)} %collective-permute-done.2.refs_4_), channel_id=1, source_target_pairs={{0,2},{2,0},{4,6},{6,4},{8,10},{10,8},{12,14},{14,12},{1,3},{3,1},... | collective-permute-start | bytes 393224 | tf_op jit(solution)/shard_map/ppermute | solution.py:259
  16.6 2.8 %collective-permute-done.6.refs_6_ = bf16[32,2048]{1,0:T(8,128)(2,1)S(1)} collective-permute-done((bf16[32,2048]{1,0:T(8,128)(2,1)S(1)}, bf16[32,2048]{1,0:T(8,128)(2,1)S(1)}, u32[]{:S(2)}, u32[]{:S(2)}) %collective-permute-start.6) | collective-permute-done | bytes 131104 | tf_op jit(solution)/shard_map/ppermute | solution.py:259
  19.5 1.4 %collective-permute-start.7 = (bf16[32,2048]{1,0:T(8,128)(2,1)S(1)}, bf16[32,2048]{1,0:T(8,128)(2,1)S(1)}, u32[]{:S(2)}, u32[]{:S(2)}) collective-permute-start(bf16[32,2048]{1,0:T(8,128)(2,1)S(1)} %collective-permute-done.6.refs_6_), channel_id=1, source_target_pairs={{0,2},{2,0},{4,6},{6,4},{8,10},{10,8},{12,14},{14,12},{1,3},{3,1},... | collective-permute-start | bytes 393224 | tf_op jit(solution)/shard_map/ppermute | solution.py:259
  21.0 1.4 %shard_map.78 = (bf16[224,2048]{1,0:T(8,128)(2,1)S(1)}, f32[224,1024]{1,0:T(8,128)S(1)}, bf16[112,1024]{1,0:T(8,128)(2,1)S(1)}, bf16[112,1024]{1,0:T(8,128)(2,1)S(1)}) custom-call(bf16[1024,2048]{1,0:T(8,128)(2,1)S(1)} %shard_map.77.tile, bf16[32,2048]{1,0:T(8,128)(2,1)S(1)} %convert_element_type.21.refs_0_, ...), custom_call_target="tpu_custom_call" | custom-call | bytes 16777216 | tf_op jit(solution)/shard_map/pallas_call | solution.py:285
  22.5 0.5 collective-permute-start.10
  23.0 1.4 %collective-permute-done.7.share = bf16[32,2048]{1,0:T(8,128)(2,1)S(1)} collective-permute-done((bf16[32,2048]{1,0:T(8,128)(2,1)S(1)}, bf16[32,2048]{1,0:T(8,128)(2,1)S(1)}, u32[]{:S(2)}, u32[]{:S(2)}) %collective-permute-start.7) | collective-permute-done | bytes 131104 | tf_op jit(solution)/shard_map/ppermute | solution.py:259
  24.4 1.7 %shard_map.79 = (bf16[256,2048]{1,0:T(8,128)(2,1)S(1)}, f32[96,1024]{1,0:T(8,128)S(1)}, bf16[96,1024]{1,0:T(8,128)(2,1)S(1)}) custom-call(bf16[1024,2048]{1,0:T(8,128)(2,1)S(1)} %shard_map.77.tile, bf16[224,2048]{1,0:T(8,128)(2,1)S(1)} %get-tuple-element.32.first, bf16[32,2048]{1,0:T(8,128)(2,1)S(1)} %collective-permute-done.7.share), custom_call_target="tpu_custom_call" | custom-call | tf_op jit(solution)/shard_map/pallas_call | solution.py:299
  26.2 1.4 %collective-permute-done.8.other = bf16[96,1024]{1,0:T(8,128)(2,1)S(1)} collective-permute-done((bf16[96,1024]{1,0:T(8,128)(2,1)S(1)}, bf16[96,1024]{1,0:T(8,128)(2,1)S(1)}, u32[]{:S(2)}, u32[]{:S(2)}) %collective-permute-start.8) | collective-permute-done | bytes 196640 | tf_op jit(solution)/shard_map/ppermute | solution.py:262
  27.6 2.6 %shard_map.80 = (f32[128,1024]{1,0:T(8,128)}, bf16[256,1024]{1,0:T(8,128)(2,1)S(1)}, bf16[32,2048]{1,0:T(8,128)(2,1)S(1)}, bf16[384,128]{1,0:T(8,128)(2,1)S(1)}) custom-call(bf16[1024,2048]{1,0:T(8,128)(2,1)S(1)} %shard_map.77.tile, f32[224,1024]{1,0:T(8,128)S(1)} %get-tuple-element.31.mine_first, f32[96,1024]{1,0:T(8,128)S(1)} %get-tuple-element.33.mine, ...), custom_call_target="tpu_custom_call" | custom-call | tf_op jit(solution)/shard_map/pallas_call | solution.py:315
  30.2 1.4 %collective-permute-start.18 = (bf16[32,2048]{1,0:T(8,128)(2,1)S(1)}, bf16[32,2048]{1,0:T(8,128)(2,1)S(1)}, u32[]{:S(2)}, u32[]{:S(2)}) collective-permute-start(bf16[32,2048]{1,0:T(8,128)(2,1)S(1)} %get-tuple-element.48), channel_id=1, source_target_pairs={{0,2},{2,0},{4,6},{6,4},{8,10},{10,8},{12,14},{14,12},{1,3},{3,1},... | collective-permute-start | bytes 393224 | tf_op jit(solution)/shard_map/ppermute | solution.py:259
  31.6 1.8 %collective-permute-start.11 = (bf16[384,128]{1,0:T(8,128)(2,1)S(1)}, bf16[384,128]{1,0:T(8,128)(2,1)S(1)}, u32[]{:S(2)}, u32[]{:S(2)}) collective-permute-start(bf16[384,128]{1,0:T(8,128)(2,1)S(1)} %get-tuple-element.39), channel_id=1, source_target_pairs={{0,8},{2,10},{4,12},{6,14},{8,0},{10,2},{12,4},{14,6},{1,9},{3,11}... | collective-permute-start | bytes 294920 | tf_op jit(solution)/shard_map/ppermute | solution.py:259
  33.5 1.1 %shard_map.81 = (bf16[32,2048]{1,0:T(8,128)(2,1)S(1)}, bf16[32,2048]{1,0:T(8,128)(2,1)S(1)}, bf16[32,2048]{1,0:T(8,128)(2,1)S(1)}, f32[32,2048]{1,0:T(8,128)S(1)...) custom-call(bf16[256,1024]{1,0:T(8,128)(2,1)S(1)} %get-tuple-element.40.low, ...), custom_call_target="tpu_custom_call" | custom-call | bytes 16777216 | tf_op jit(solution)/shard_map/pallas_call | solution.py:346
  34.6 0.6 %collective-permute-start.15 = (bf16[32,2048]{1,0:T(8,128)(2,1)S(1)}, bf16[32,2048]{1,0:T(8,128)(2,1)S(1)}, u32[]{:S(2)}, u32[]{:S(2)}) collective-permute-start(bf16[32,2048]{1,0:T(8,128)(2,1)S(1)} %get-tuple-element.44), channel_id=1, source_target_pairs={{0,2},{2,0},{4,6},{6,4},{8,10},{10,8},{12,14},{14,12},{1,3},{3,1},... | collective-permute-start | bytes 393224 | tf_op jit(solution)/shard_map/ppermute | solution.py:259
  35.2 1.5 %collective-permute-start.17 = (bf16[32,2048]{1,0:T(8,128)(2,1)S(1)}, bf16[32,2048]{1,0:T(8,128)(2,1)S(1)}, u32[]{:S(2)}, u32[]{:S(2)}) collective-permute-start(bf16[32,2048]{1,0:T(8,128)(2,1)S(1)} %get-tuple-element.46), channel_id=1, source_target_pairs={{0,2},{2,0},{4,6},{6,4},{8,10},{10,8},{12,14},{14,12},{1,3},{3,1},... | collective-permute-start | bytes 393224 | tf_op jit(solution)/shard_map/ppermute | solution.py:259
  36.7 2.1 %collective-permute-start.19 = (bf16[32,2048]{1,0:T(8,128)(2,1)S(1)}, bf16[32,2048]{1,0:T(8,128)(2,1)S(1)}, u32[]{:S(2)}, u32[]{:S(2)}) collective-permute-start(bf16[32,2048]{1,0:T(8,128)(2,1)S(1)} %shard_map.83), channel_id=1, source_target_pairs={{0,4},{2,6},{4,0},{6,2},{8,12},{10,14},{12,8},{14,10},{1,5},{3,7},... | collective-permute-start | bytes 393224 | tf_op jit(solution)/shard_map/ppermute | solution.py:259
  39.4 0.7 %collective-permute-start.14 = (bf16[32,2048]{1,0:T(8,128)(2,1)S(1)}, bf16[32,2048]{1,0:T(8,128)(2,1)S(1)}, u32[]{:S(2)}, u32[]{:S(2)}) collective-permute-start(bf16[32,2048]{1,0:T(8,128)(2,1)S(1)} %get-tuple-element.42), channel_id=1, source_target_pairs={{0,2},{2,0},{4,6},{6,4},{8,10},{10,8},{12,14},{14,12},{1,3},{3,1},... | collective-permute-start | bytes 393224 | tf_op jit(solution)/shard_map/ppermute | solution.py:259
  40.0 1.0 %collective-permute-done.15.refs_0_ = bf16[32,2048]{1,0:T(8,128)(2,1)S(1)} collective-permute-done((bf16[32,2048]{1,0:T(8,128)(2,1)S(1)}, bf16[32,2048]{1,0:T(8,128)(2,1)S(1)}, u32[]{:S(2)}, u32[]{:S(2)}) %collective-permute-start.15) | collective-permute-done | bytes 131104 | tf_op jit(solution)/shard_map/ppermute | solution.py:259
  41.1 2.1 %collective-permute-start.16 = (bf16[32,2048]{1,0:T(8,128)(2,1)S(1)}, bf16[32,2048]{1,0:T(8,128)(2,1)S(1)}, u32[]{:S(2)}, u32[]{:S(2)}) collective-permute-start(bf16[32,2048]{1,0:T(8,128)(2,1)S(1)} %shard_map.82), channel_id=1, source_target_pairs={{0,4},{2,6},{4,0},{6,2},{8,12},{10,14},{12,8},{14,10},{1,5},{3,7},... | collective-permute-start | bytes 393224 | tf_op jit(solution)/shard_map/ppermute | solution.py:259
  43.4 1.0 %collective-permute-start.20 = (bf16[32,2048]{1,0:T(8,128)(2,1)S(1)}, bf16[32,2048]{1,0:T(8,128)(2,1)S(1)}, u32[]{:S(2)}, u32[]{:S(2)}) collective-permute-start(bf16[32,2048]{1,0:T(8,128)(2,1)S(1)} %shard_map.84), channel_id=1, source_target_pairs={{0,8},{2,10},{4,12},{6,14},{8,0},{10,2},{12,4},{14,6},{1,9},{3,11}... | collective-permute-start | bytes 393224 | tf_op jit(solution)/shard_map/ppermute | solution.py:259
  44.4 2.4 %collective-permute-done.12 = bf16[384,128]{1,0:T(8,128)(2,1)S(1)} collective-permute-done((bf16[384,128]{1,0:T(8,128)(2,1)S(1)}, bf16[384,128]{1,0:T(8,128)(2,1)S(1)}, u32[]{:S(2)}, u32[]{:S(2)}) %collective-permute-start.12) | collective-permute-done | bytes 98336 | tf_op jit(solution)/shard_map/ppermute | solution.py:259
  47.3 1.4 %collective-permute-done.16.refs_1_ = bf16[32,2048]{1,0:T(8,128)(2,1)S(1)} collective-permute-done((bf16[32,2048]{1,0:T(8,128)(2,1)S(1)}, bf16[32,2048]{1,0:T(8,128)(2,1)S(1)}, u32[]{:S(2)}, u32[]{:S(2)}) %collective-permute-start.16) | collective-permute-done | bytes 131104 | tf_op jit(solution)/shard_map/ppermute | solution.py:259
  48.8 1.3 %collective-permute-done.20.refs_2_ = bf16[32,2048]{1,0:T(8,128)(2,1)S(1)} collective-permute-done((bf16[32,2048]{1,0:T(8,128)(2,1)S(1)}, bf16[32,2048]{1,0:T(8,128)(2,1)S(1)}, u32[]{:S(2)}, u32[]{:S(2)}) %collective-permute-start.20) | collective-permute-done | bytes 131104 | tf_op jit(solution)/shard_map/ppermute | solution.py:259
  50.1 1.4 %collective-permute-done.13.other = bf16[384,128]{1,0:T(8,128)(2,1)S(1)} collective-permute-done((bf16[384,128]{1,0:T(8,128)(2,1)S(1)}, bf16[384,128]{1,0:T(8,128)(2,1)S(1)}, u32[]{:S(2)}, u32[]{:S(2)}) %collective-permute-start.13) | collective-permute-done | bytes 98336 | tf_op jit(solution)/shard_map/ppermute | solution.py:259
  51.5 1.1 %shard_map.86 = f32[32,2048]{1,0:T(8,128)} custom-call(bf16[384,128]{1,0:T(8,128)(2,1)S(1)} %add_convert_fusion.mine, bf16[384,128]{1,0:T(8,128)(2,1)S(1)} %collective-permute-done.13.other, bf16[256,2048]{1,0:T(8,128)(2,1)S(1)} %get-tuple-element.50.panel, f32[32,2048]{1,0:T(8,128)S(1)} %copy-done, f32[32,2048]{1,0:T(8,128)S(1)} %shard_map.85.data), custom_call_target="tpu_custom_call" | custom-call | tf_op jit(solution)/shard_map/pallas_call | solution.py:376
  (27 shorter events, 2.2 us)
Async XLA Ops:
  0.6 12.4 %collective-permute-start.3 = (f32[128,1024]{1,0:T(8,128)}, f32[128,1024]{1,0:T(8,128)S(1)}, u32[]{:S(2)}, u32[]{:S(2)}) collective-permute-start(f32[128,1024]{1,0:T(8,128)} %factor_mine.1), channel_id=1, source_target_pairs={{0,1},{1,0},{2,3},{3,2},{4,5},{5,4},{6,7},{7,6},{8,9},{9,8},{10,11... | collective-permute-start | bytes 1572872 | tf_op jit(solution)/shard_map/ppermute | solution.py:262
  2.1 10.7 %collective-permute-start.2 = (bf16[32,2048]{1,0:T(8,128)(2,1)S(1)}, bf16[32,2048]{1,0:T(8,128)(2,1)S(1)}, u32[]{:S(2)}, u32[]{:S(2)}) collective-permute-start(bf16[32,2048]{1,0:T(8,128)(2,1)S(1)} %convert_element_type.21.refs_0_), channel_id=1, source_target_pairs={{0,8},{2,10},{4,12},{6,14},{8,0},{10,2},{12,4},{14,6},{1,9},{3,11}... | collective-permute-start | bytes 393224 | tf_op jit(solution)/shard_map/ppermute | solution.py:259
  5.8 7.3 %collective-permute-start.1 = (bf16[32,2048]{1,0:T(8,128)(2,1)S(1)}, bf16[32,2048]{1,0:T(8,128)(2,1)S(1)}, u32[]{:S(2)}, u32[]{:S(2)}) collective-permute-start(bf16[32,2048]{1,0:T(8,128)(2,1)S(1)} %convert_element_type.21.refs_0_), channel_id=1, source_target_pairs={{0,4},{2,6},{4,0},{6,2},{8,12},{10,14},{12,8},{14,10},{1,5},{3,7},... | collective-permute-start | bytes 393224 | tf_op jit(solution)/shard_map/ppermute | solution.py:259
  7.4 5.7 %collective-permute-start = (bf16[32,2048]{1,0:T(8,128)(2,1)S(1)}, bf16[32,2048]{1,0:T(8,128)(2,1)S(1)}, u32[]{:S(2)}, u32[]{:S(2)}) collective-permute-start(bf16[32,2048]{1,0:T(8,128)(2,1)S(1)} %convert_element_type.21.refs_0_), channel_id=1, source_target_pairs={{0,2},{2,0},{4,6},{6,4},{8,10},{10,8},{12,14},{14,12},{1,3},{3,1},... | collective-permute-start | bytes 393224 | tf_op jit(solution)/shard_map/ppermute | solution.py:259
  12.4 15.2 %copy-start.1 = (f32[128,1024]{1,0:T(8,128)S(1)}, f32[128,1024]{1,0:T(8,128)}, u32[]{:S(2)}) copy-start(f32[128,1024]{1,0:T(8,128)} %factor_mine.1) | copy-start | bytes 1572868
  13.0 6.4 %collective-permute-start.6 = (bf16[32,2048]{1,0:T(8,128)(2,1)S(1)}, bf16[32,2048]{1,0:T(8,128)(2,1)S(1)}, u32[]{:S(2)}, u32[]{:S(2)}) collective-permute-start(bf16[32,2048]{1,0:T(8,128)(2,1)S(1)} %collective-permute-done.2.refs_4_), channel_id=1, source_target_pairs={{0,4},{2,6},{4,0},{6,2},{8,12},{10,14},{12,8},{14,10},{1,5},{3,7},... | collective-permute-start | bytes 393224 | tf_op jit(solution)/shard_map/ppermute | solution.py:259
  14.5 6.5 %collective-permute-start.4 = (bf16[32,2048]{1,0:T(8,128)(2,1)S(1)}, bf16[32,2048]{1,0:T(8,128)(2,1)S(1)}, u32[]{:S(2)}, u32[]{:S(2)}) collective-permute-start(bf16[32,2048]{1,0:T(8,128)(2,1)S(1)} %collective-permute-done.refs_1_), channel_id=1, source_target_pairs={{0,4},{2,6},{4,0},{6,2},{8,12},{10,14},{12,8},{14,10},{1,5},{3,7},... | collective-permute-start | bytes 393224 | tf_op jit(solution)/shard_map/ppermute | solution.py:259
  15.1 5.9 %collective-permute-start.5 = (bf16[32,2048]{1,0:T(8,128)(2,1)S(1)}, bf16[32,2048]{1,0:T(8,128)(2,1)S(1)}, u32[]{:S(2)}, u32[]{:S(2)}) collective-permute-start(bf16[32,2048]{1,0:T(8,128)(2,1)S(1)} %collective-permute-done.2.refs_4_), channel_id=1, source_target_pairs={{0,2},{2,0},{4,6},{6,4},{8,10},{10,8},{12,14},{14,12},{1,3},{3,1},... | collective-permute-start | bytes 393224 | tf_op jit(solution)/shard_map/ppermute | solution.py:259
  19.5 5.0 %collective-permute-start.7 = (bf16[32,2048]{1,0:T(8,128)(2,1)S(1)}, bf16[32,2048]{1,0:T(8,128)(2,1)S(1)}, u32[]{:S(2)}, u32[]{:S(2)}) collective-permute-start(bf16[32,2048]{1,0:T(8,128)(2,1)S(1)} %collective-permute-done.6.refs_6_), channel_id=1, source_target_pairs={{0,2},{2,0},{4,6},{6,4},{8,10},{10,8},{12,14},{14,12},{1,3},{3,1},... | collective-permute-start | bytes 393224 | tf_op jit(solution)/shard_map/ppermute | solution.py:259
  22.4 3.7 %collective-permute-start.9 = (bf16[112,1024]{1,0:T(8,128)(2,1)S(1)}, bf16[112,1024]{1,0:T(8,128)(2,1)S(1)}, u32[]{:S(2)}, u32[]{:S(2)}) collective-permute-start(bf16[112,1024]{1,0:T(8,128)(2,1)S(1)} %get-tuple-element.36), channel_id=1, source_target_pairs={{0,1},{1,0},{2,3},{3,2},{4,5},{5,4},{6,7},{7,6},{8,9},{9,8},{10,11... | collective-permute-start | bytes 688136 | tf_op jit(solution)/shard_map/ppermute | solution.py:262
  22.5 3.7 %collective-permute-start.10 = (bf16[112,1024]{1,0:T(8,128)(2,1)S(1)}, bf16[112,1024]{1,0:T(8,128)(2,1)S(1)}, u32[]{:S(2)}, u32[]{:S(2)}) collective-permute-start(bf16[112,1024]{1,0:T(8,128)(2,1)S(1)} %get-tuple-element.37), channel_id=1, source_target_pairs={{0,1},{1,0},{2,3},{3,2},{4,5},{5,4},{6,7},{7,6},{8,9},{9,8},{10,11... | collective-permute-start | bytes 688136 | tf_op jit(solution)/shard_map/ppermute | solution.py:262
  26.1 1.5 %collective-permute-start.8 = (bf16[96,1024]{1,0:T(8,128)(2,1)S(1)}, bf16[96,1024]{1,0:T(8,128)(2,1)S(1)}, u32[]{:S(2)}, u32[]{:S(2)}) collective-permute-start(bf16[96,1024]{1,0:T(8,128)(2,1)S(1)} %get-tuple-element.34), channel_id=1, source_target_pairs={{0,1},{1,0},{2,3},{3,2},{4,5},{5,4},{6,7},{7,6},{8,9},{9,8},{10,11... | collective-permute-start | bytes 589832 | tf_op jit(solution)/shard_map/ppermute | solution.py:262
  30.2 21.3 %copy-start = (f32[32,2048]{1,0:T(8,128)S(1)}, f32[32,2048]{1,0:T(8,128)}, u32[]{:S(2)}) copy-start(f32[32,2048]{1,0:T(8,128)} %factor.1) | copy-start | bytes 786436
  30.2 6.5 %collective-permute-start.18 = (bf16[32,2048]{1,0:T(8,128)(2,1)S(1)}, bf16[32,2048]{1,0:T(8,128)(2,1)S(1)}, u32[]{:S(2)}, u32[]{:S(2)}) collective-permute-start(bf16[32,2048]{1,0:T(8,128)(2,1)S(1)} %get-tuple-element.48), channel_id=1, source_target_pairs={{0,2},{2,0},{4,6},{6,4},{8,10},{10,8},{12,14},{14,12},{1,3},{3,1},... | collective-permute-start | bytes 393224 | tf_op jit(solution)/shard_map/ppermute | solution.py:259
  31.6 7.6 %collective-permute-start.11 = (bf16[384,128]{1,0:T(8,128)(2,1)S(1)}, bf16[384,128]{1,0:T(8,128)(2,1)S(1)}, u32[]{:S(2)}, u32[]{:S(2)}) collective-permute-start(bf16[384,128]{1,0:T(8,128)(2,1)S(1)} %get-tuple-element.39), channel_id=1, source_target_pairs={{0,8},{2,10},{4,12},{6,14},{8,0},{10,2},{12,4},{14,6},{1,9},{3,11}... | collective-permute-start | bytes 294920 | tf_op jit(solution)/shard_map/ppermute | solution.py:259
  34.6 6.5 %collective-permute-start.15 = (bf16[32,2048]{1,0:T(8,128)(2,1)S(1)}, bf16[32,2048]{1,0:T(8,128)(2,1)S(1)}, u32[]{:S(2)}, u32[]{:S(2)}) collective-permute-start(bf16[32,2048]{1,0:T(8,128)(2,1)S(1)} %get-tuple-element.44), channel_id=1, source_target_pairs={{0,2},{2,0},{4,6},{6,4},{8,10},{10,8},{12,14},{14,12},{1,3},{3,1},... | collective-permute-start | bytes 393224 | tf_op jit(solution)/shard_map/ppermute | solution.py:259
  35.2 8.1 %collective-permute-start.17 = (bf16[32,2048]{1,0:T(8,128)(2,1)S(1)}, bf16[32,2048]{1,0:T(8,128)(2,1)S(1)}, u32[]{:S(2)}, u32[]{:S(2)}) collective-permute-start(bf16[32,2048]{1,0:T(8,128)(2,1)S(1)} %get-tuple-element.46), channel_id=1, source_target_pairs={{0,2},{2,0},{4,6},{6,4},{8,10},{10,8},{12,14},{14,12},{1,3},{3,1},... | collective-permute-start | bytes 393224 | tf_op jit(solution)/shard_map/ppermute | solution.py:259
  36.7 6.6 %collective-permute-start.19 = (bf16[32,2048]{1,0:T(8,128)(2,1)S(1)}, bf16[32,2048]{1,0:T(8,128)(2,1)S(1)}, u32[]{:S(2)}, u32[]{:S(2)}) collective-permute-start(bf16[32,2048]{1,0:T(8,128)(2,1)S(1)} %shard_map.83), channel_id=1, source_target_pairs={{0,4},{2,6},{4,0},{6,2},{8,12},{10,14},{12,8},{14,10},{1,5},{3,7},... | collective-permute-start | bytes 393224 | tf_op jit(solution)/shard_map/ppermute | solution.py:259
  39.3 7.5 %collective-permute-start.12 = (bf16[384,128]{1,0:T(8,128)(2,1)S(1)}, bf16[384,128]{1,0:T(8,128)(2,1)S(1)}, u32[]{:S(2)}, u32[]{:S(2)}) collective-permute-start(bf16[384,128]{1,0:T(8,128)(2,1)S(1)} %add_convert_fusion.1), channel_id=1, source_target_pairs={{0,4},{2,6},{4,0},{6,2},{8,12},{10,14},{12,8},{14,10},{1,5},{3,7},... | collective-permute-start | bytes 294920 | tf_op jit(solution)/shard_map/ppermute | solution.py:259
  39.4 8.0 %collective-permute-start.14 = (bf16[32,2048]{1,0:T(8,128)(2,1)S(1)}, bf16[32,2048]{1,0:T(8,128)(2,1)S(1)}, u32[]{:S(2)}, u32[]{:S(2)}) collective-permute-start(bf16[32,2048]{1,0:T(8,128)(2,1)S(1)} %get-tuple-element.42), channel_id=1, source_target_pairs={{0,2},{2,0},{4,6},{6,4},{8,10},{10,8},{12,14},{14,12},{1,3},{3,1},... | collective-permute-start | bytes 393224 | tf_op jit(solution)/shard_map/ppermute | solution.py:259
  41.1 7.6 %collective-permute-start.16 = (bf16[32,2048]{1,0:T(8,128)(2,1)S(1)}, bf16[32,2048]{1,0:T(8,128)(2,1)S(1)}, u32[]{:S(2)}, u32[]{:S(2)}) collective-permute-start(bf16[32,2048]{1,0:T(8,128)(2,1)S(1)} %shard_map.82), channel_id=1, source_target_pairs={{0,4},{2,6},{4,0},{6,2},{8,12},{10,14},{12,8},{14,10},{1,5},{3,7},... | collective-permute-start | bytes 393224 | tf_op jit(solution)/shard_map/ppermute | solution.py:259
  43.4 6.6 %collective-permute-start.20 = (bf16[32,2048]{1,0:T(8,128)(2,1)S(1)}, bf16[32,2048]{1,0:T(8,128)(2,1)S(1)}, u32[]{:S(2)}, u32[]{:S(2)}) collective-permute-start(bf16[32,2048]{1,0:T(8,128)(2,1)S(1)} %shard_map.84), channel_id=1, source_target_pairs={{0,8},{2,10},{4,12},{6,14},{8,0},{10,2},{12,4},{14,6},{1,9},{3,11}... | collective-permute-start | bytes 393224 | tf_op jit(solution)/shard_map/ppermute | solution.py:259
  46.8 4.7 %collective-permute-start.13 = (bf16[384,128]{1,0:T(8,128)(2,1)S(1)}, bf16[384,128]{1,0:T(8,128)(2,1)S(1)}, u32[]{:S(2)}, u32[]{:S(2)}) collective-permute-start(bf16[384,128]{1,0:T(8,128)(2,1)S(1)} %add_convert_fusion.mine), channel_id=1, source_target_pairs={{0,2},{2,0},{4,6},{6,4},{8,10},{10,8},{12,14},{14,12},{1,3},{3,1},... | collective-permute-start | bytes 294920 | tf_op jit(solution)/shard_map/ppermute | solution.py:259

commit v10 on v9

--- a/solution.py
+++ b/solution.py
@@ -47,7 +47,7 @@
     return jax.ShapeDtypeStruct(dims, dtype)
 
 
-def dense_body(rows_in, cols_in, count, values, tile, rows, cols, sems, index_sems):
+def dense_body(rows_in, cols_in, count, values, tile, turned, rows, cols, sems, index_sems):
     copies = [
         pltpu.make_async_copy(rows_in, rows, index_sems.at[0]),
         pltpu.make_async_copy(cols_in, cols, index_sems.at[1]),
@@ -74,6 +74,8 @@
 
     lax.fori_loop(0, count[0], start, 0)
     lax.fori_loop(0, count[0], wait, 0)
+    for row in range(0, tile.shape[0], TURN):
+        turned[:, row : row + TURN] = tile[row : row + TURN].T
 
 
 def pinned(array):
@@ -85,9 +87,9 @@
     n_blocks = values.shape[0]
     return pl.pallas_call(
         dense_body,
-        out_shape=shape((CELL_DEV, GENE_DEV), jnp.bfloat16),
+        out_shape=(shape((CELL_DEV, GENE_DEV), jnp.bfloat16), shape((GENE_DEV, CELL_DEV), jnp.bfloat16)),
         in_specs=[anywhere, anywhere, SMEM_SPEC, anywhere],
-        out_specs=VMEM_SPEC,
+        out_specs=(VMEM_SPEC, VMEM_SPEC),
         scratch_shapes=[
             pltpu.SMEM((n_blocks,), jnp.int32),
             pltpu.SMEM((n_blocks,), jnp.int32),
@@ -104,6 +106,7 @@
 
 
 STEP = 8
+TURN = 256
 PARTS = 2
 
 
@@ -125,20 +128,20 @@
     return jnp.concatenate(parts, axis=0)
 
 
-def first_body(count, tile, *refs):
+def first_body(count, turned, *refs):
     shares, (panel, mine), messages = refs[: -2 - count], refs[-2 - count : -count], refs[-count:]
     row = 0
     for part in shares:
         panel[row : row + part.shape[0]] = part[...]
         row += part.shape[0]
-    mine[...] = dot(panel[...], tile[...], NT)
+    mine[...] = dot(panel[...], turned[...])
     row = 0
     for out in messages:
         out[...] = mine[row : row + out.shape[0]].astype(out.dtype)
         row += out.shape[0]
 
 
-def second_body(order, tile, first, share, panel, mine, message):
+def second_body(order, turned, first, share, panel, mine, message):
     size = share.shape[0]
     if order is None:
         panel[: first.shape[0]] = first[...]
@@ -147,7 +150,7 @@
         for n, bits in enumerate(order[:-1]):
             panel[owned(bits, size)] = first[n * size : (n + 1) * size]
         panel[owned(order[-1], size)] = share[...]
-    mine[:size] = dot(share[...], tile[...], NT)
+    mine[:size] = dot(share[...], turned[...])
     low = panel[...]
     gram = dot(low, low, NT)
     rows, width = mine.shape[0] - size, gram.shape[1]
@@ -266,10 +269,12 @@
 
     low_share = gene_factor.astype(jnp.bfloat16)
     factor_other = swap_core(cell_factor)
-    tile = dense_tile(block_values[0, 0], block_rows[0, 0], block_cols[0, 0], block_count[0])
+    tile, turned = dense_tile(block_values[0, 0], block_rows[0, 0], block_cols[0, 0], block_count[0])
     if paired:
         near = [swap(low_share, bits) for bits in (1, 2, 4)]
-        beside, second, fourth, tile, factor_other = lax.optimization_barrier((*near, tile, factor_other))
+        beside, second, fourth, tile, turned, factor_other = lax.optimization_barrier(
+            (*near, tile, turned, factor_other)
+        )
         sixth, third, fifth = swap(fourth, 2), swap(beside, 2), swap(fourth, 1)
         seventh = swap(sixth, 1)
         shares = [low_share, beside, second, third, fourth, fifth, sixth]
@@ -293,7 +298,7 @@
         1 + len(shares),
         0,
         AHEAD,
-    )(tile, *shares)
+    )(turned, *shares)
     others = [swap_core(part) for part in messages]
     rows = last_rows + kdim * kdim // CELL_DEV
     panel, mine, message = call(
@@ -307,7 +312,7 @@
         3,
         0,
         0,
-    )(tile, panel_first, seventh)
+    )(turned, panel_first, seventh)
     other = swap_core(message)
 
     sent = [5, 3, 1]

time: 52.9 us -> 52.4 us (level)
  starting transfers between devices: 24.8 us -> 23.2 us
    ppermute x17, starting transfers between devices: 23.6 us -> 22.1 us  [swap(): return lax.ppermute(value, 'cell', [(n, n ^ bits) for n in range(n_cell)])]
    pallas_call x1, Pallas kernels: 2.84 us -> 4.09 us  [dense_tile(): pl.pallas_call(dense_body, out_shape=(shape((CELL_DEV, GENE_DEV), jnp.bfl...]
    ppermute x17, waiting for transfers between devices: 13 us -> 13.5 us  [swap(): return lax.ppermute(value, 'cell', [(n, n ^ bits) for n in range(n_cell)])]
  transfers between devices with their start and end apart: 21 -> 21, of which waited for: 12 -> 11; matrix products, arithmetic and copies ran while one was open for 2% -> 2% of each run, Pallas kernels for 14% -> 15%
where the time goes in v10:
time: 52.4 us; the launch traced here: 52.2 us
  starting transfers between devices  23.2 us (44%)
  waiting for transfers between devices  14.9 us (28%)
  Pallas kernels  11.5 us (22%)
  between operations  1.45 us (3%)
  other arithmetic  1.02 us (2%)
    ppermute x17, starting transfers between devices, swap(): return lax.ppermute(value, 'cell', [(n, n ^ bits) for n in range(n_cell)])  22.1 us
    ppermute x17, waiting for transfers between devices, swap(): return lax.ppermute(value, 'cell', [(n, n ^ bits) for n in range(n_cell)])  13.5 us
    pallas_call x1, Pallas kernels, dense_tile(): pl.pallas_call(dense_body, out_shape=(shape((CELL_DEV, GENE_DEV), jnp.bfl...  4.09 us
    pallas_call x1, Pallas kernels, shards(): call(functools.partial(cell_body, order, [7], n_parts), (shape(cell_facto...  2.61 us
    ppermute x4, waiting for transfers between devices, swap_core(): return lax.ppermute(value, 'gene', [(0, 1), (1, 0)])  1.42 us
    pallas_call x1, Pallas kernels, shards(): call(functools.partial(second_body, order), (wide(kdim, jnp.bfloat16), sh...  1.21 us
    ppermute x4, starting transfers between devices, swap_core(): return lax.ppermute(value, 'gene', [(0, 1), (1, 0)])  1.16 us
    pallas_call x1, Pallas kernels, shards(): call(functools.partial(first_body, n_parts), (wide(first_rows, jnp.bfloat...  1.13 us
  transfers between devices with their start and end apart: 21, of which 11 were waited for; matrix products, arithmetic and copies ran while one was open for 2% of the time, Pallas kernels for 15%

profile of v10, /device:TPU:0, one launch (start us, length us, event | category | flops | bytes accessed | tf_op | source)
XLA Modules:
  0.0 52.2 jit_solution(6612939866539841125)
XLA Ops:
  0.6 0.5 collective-permute-start.3
  1.1 1.0 %convert_element_type.21.refs_0_ = bf16[32,2048]{1,0:T(8,128)(2,1)S(1)} convert(f32[32,2048]{1,0:T(8,128)} %factor.1) | non-fusion elementwise | flops 65536 | bytes 393216 | tf_op jit(solution)/shard_map/convert_element_type | solution.py:270
  2.1 3.7 %collective-permute-start.2 = (bf16[32,2048]{1,0:T(8,128)(2,1)S(1)}, bf16[32,2048]{1,0:T(8,128)(2,1)S(1)}, u32[]{:S(2)}, u32[]{:S(2)}) collective-permute-start(bf16[32,2048]{1,0:T(8,128)(2,1)S(1)} %convert_element_type.21.refs_0_), channel_id=1, source_target_pairs={{0,8},{2,10},{4,12},{6,14},{8,0},{10,2},{12,4},{14,6},{1,9},{3,11}... | collective-permute-start | bytes 393224 | tf_op jit(solution)/shard_map/ppermute | solution.py:262
  5.8 1.6 %collective-permute-start.1 = (bf16[32,2048]{1,0:T(8,128)(2,1)S(1)}, bf16[32,2048]{1,0:T(8,128)(2,1)S(1)}, u32[]{:S(2)}, u32[]{:S(2)}) collective-permute-start(bf16[32,2048]{1,0:T(8,128)(2,1)S(1)} %convert_element_type.21.refs_0_), channel_id=1, source_target_pairs={{0,4},{2,6},{4,0},{6,2},{8,12},{10,14},{12,8},{14,10},{1,5},{3,7},... | collective-permute-start | bytes 393224 | tf_op jit(solution)/shard_map/ppermute | solution.py:262
  7.4 1.5 %collective-permute-start = (bf16[32,2048]{1,0:T(8,128)(2,1)S(1)}, bf16[32,2048]{1,0:T(8,128)(2,1)S(1)}, u32[]{:S(2)}, u32[]{:S(2)}) collective-permute-start(bf16[32,2048]{1,0:T(8,128)(2,1)S(1)} %convert_element_type.21.refs_0_), channel_id=1, source_target_pairs={{0,2},{2,0},{4,6},{6,4},{8,10},{10,8},{12,14},{14,12},{1,3},{3,1},... | collective-permute-start | bytes 393224 | tf_op jit(solution)/shard_map/ppermute | solution.py:262
  9.5 4.1 %shard_map.77 = (bf16[1024,2048]{1,0:T(8,128)(2,1)S(1)}, bf16[2048,1024]{1,0:T(8,128)(2,1)S(1)}) custom-call(s32[64]{0:T(128)} %bitcast.6, s32[64]{0:T(128)} %bitcast.7, s32[1]{0:T(128)} %bitcast.4.count, bf16[64,128,128]{2,1,0:T(8,128)(2,1)} %bitcast.5), custom_call_target="tpu_custom_call" | custom-call | tf_op jit(solution)/shard_map/pallas_call | solution.py:88
  13.7 1.0 %collective-permute-start.6 = (bf16[32,2048]{1,0:T(8,128)(2,1)S(1)}, bf16[32,2048]{1,0:T(8,128)(2,1)S(1)}, u32[]{:S(2)}, u32[]{:S(2)}) collective-permute-start(bf16[32,2048]{1,0:T(8,128)(2,1)S(1)} %collective-permute-done.2.refs_4_), channel_id=1, source_target_pairs={{0,4},{2,6},{4,0},{6,2},{8,12},{10,14},{12,8},{14,10},{1,5},{3,7},... | collective-permute-start | bytes 393224 | tf_op jit(solution)/shard_map/ppermute | solution.py:262
  14.6 1.1 %collective-permute-start.4 = (bf16[32,2048]{1,0:T(8,128)(2,1)S(1)}, bf16[32,2048]{1,0:T(8,128)(2,1)S(1)}, u32[]{:S(2)}, u32[]{:S(2)}) collective-permute-start(bf16[32,2048]{1,0:T(8,128)(2,1)S(1)} %collective-permute-done.refs_1_), channel_id=1, source_target_pairs={{0,4},{2,6},{4,0},{6,2},{8,12},{10,14},{12,8},{14,10},{1,5},{3,7},... | collective-permute-start | bytes 393224 | tf_op jit(solution)/shard_map/ppermute | solution.py:262
  15.7 0.9 %collective-permute-start.5 = (bf16[32,2048]{1,0:T(8,128)(2,1)S(1)}, bf16[32,2048]{1,0:T(8,128)(2,1)S(1)}, u32[]{:S(2)}, u32[]{:S(2)}) collective-permute-start(bf16[32,2048]{1,0:T(8,128)(2,1)S(1)} %collective-permute-done.2.refs_4_), channel_id=1, source_target_pairs={{0,2},{2,0},{4,6},{6,4},{8,10},{10,8},{12,14},{14,12},{1,3},{3,1},... | collective-permute-start | bytes 393224 | tf_op jit(solution)/shard_map/ppermute | solution.py:262
  16.7 3.4 %collective-permute-done.6.refs_6_ = bf16[32,2048]{1,0:T(8,128)(2,1)S(1)} collective-permute-done((bf16[32,2048]{1,0:T(8,128)(2,1)S(1)}, bf16[32,2048]{1,0:T(8,128)(2,1)S(1)}, u32[]{:S(2)}, u32[]{:S(2)}) %collective-permute-start.6) | collective-permute-done | bytes 131104 | tf_op jit(solution)/shard_map/ppermute | solution.py:262
  20.1 0.8 %collective-permute-start.7 = (bf16[32,2048]{1,0:T(8,128)(2,1)S(1)}, bf16[32,2048]{1,0:T(8,128)(2,1)S(1)}, u32[]{:S(2)}, u32[]{:S(2)}) collective-permute-start(bf16[32,2048]{1,0:T(8,128)(2,1)S(1)} %collective-permute-done.6.refs_6_), channel_id=1, source_target_pairs={{0,2},{2,0},{4,6},{6,4},{8,10},{10,8},{12,14},{14,12},{1,3},{3,1},... | collective-permute-start | bytes 393224 | tf_op jit(solution)/shard_map/ppermute | solution.py:262
  20.9 0.6 %collective-permute-done.4.refs_3_ = bf16[32,2048]{1,0:T(8,128)(2,1)S(1)} collective-permute-done((bf16[32,2048]{1,0:T(8,128)(2,1)S(1)}, bf16[32,2048]{1,0:T(8,128)(2,1)S(1)}, u32[]{:S(2)}, u32[]{:S(2)}) %collective-permute-start.4) | collective-permute-done | bytes 131104 | tf_op jit(solution)/shard_map/ppermute | solution.py:262
  21.8 1.1 %shard_map.78 = (bf16[224,2048]{1,0:T(8,128)(2,1)S(1)}, f32[224,1024]{1,0:T(8,128)S(1)}, bf16[112,1024]{1,0:T(8,128)(2,1)S(1)}, bf16[112,1024]{1,0:T(8,128)(2,1)S(1)}) custom-call(bf16[2048,1024]{1,0:T(8,128)(2,1)S(1)} %get-tuple-element.33.turned, bf16[32,2048]{1,0:T(8,128)(2,1)S(1)} %convert_element_type.21.refs_0_, ...), custom_call_target="tpu_custom_call" | custom-call | bytes 16777216 | tf_op jit(solution)/shard_map/pallas_call | solution.py:290
  23.0 0.5 collective-permute-start.10
  23.5 1.5 %collective-permute-done.7.share = bf16[32,2048]{1,0:T(8,128)(2,1)S(1)} collective-permute-done((bf16[32,2048]{1,0:T(8,128)(2,1)S(1)}, bf16[32,2048]{1,0:T(8,128)(2,1)S(1)}, u32[]{:S(2)}, u32[]{:S(2)}) %collective-permute-start.7) | collective-permute-done | bytes 131104 | tf_op jit(solution)/shard_map/ppermute | solution.py:262
  25.1 1.2 %shard_map.79 = (bf16[256,2048]{1,0:T(8,128)(2,1)S(1)}, f32[96,1024]{1,0:T(8,128)S(1)}, bf16[96,1024]{1,0:T(8,128)(2,1)S(1)}) custom-call(bf16[2048,1024]{1,0:T(8,128)(2,1)S(1)} %get-tuple-element.33.turned, bf16[224,2048]{1,0:T(8,128)(2,1)S(1)} %get-tuple-element.38.first, bf16[32,2048]{1,0:T(8,128)(2,1)S(1)} %collective-permute-done.7.share), custom_call_target="tpu_custom_call" | custom-call | tf_op jit(solution)/shard_map/pallas_call | solution.py:304
  26.4 1.4 %collective-permute-done.8.other = bf16[96,1024]{1,0:T(8,128)(2,1)S(1)} collective-permute-done((bf16[96,1024]{1,0:T(8,128)(2,1)S(1)}, bf16[96,1024]{1,0:T(8,128)(2,1)S(1)}, u32[]{:S(2)}, u32[]{:S(2)}) %collective-permute-start.8) | collective-permute-done | bytes 196640 | tf_op jit(solution)/shard_map/ppermute | solution.py:265
  27.8 2.6 %shard_map.80 = (f32[128,1024]{1,0:T(8,128)}, bf16[256,1024]{1,0:T(8,128)(2,1)S(1)}, bf16[32,2048]{1,0:T(8,128)(2,1)S(1)}, bf16[384,128]{1,0:T(8,128)(2,1)S(1)}) custom-call(bf16[1024,2048]{1,0:T(8,128)(2,1)S(1)} %get-tuple-element.32.tile, f32[224,1024]{1,0:T(8,128)S(1)} %get-tuple-element.37.mine_first, f32[96,1024]{1,0:T(8,128)S(1)} %get-tuple-element.39.mine, ...), custom_call_target="tpu_custom_call" | custom-call | tf_op jit(solution)/shard_map/pallas_call | solution.py:320
  30.4 0.8 %collective-permute-start.18 = (bf16[32,2048]{1,0:T(8,128)(2,1)S(1)}, bf16[32,2048]{1,0:T(8,128)(2,1)S(1)}, u32[]{:S(2)}, u32[]{:S(2)}) collective-permute-start(bf16[32,2048]{1,0:T(8,128)(2,1)S(1)} %get-tuple-element.54), channel_id=1, source_target_pairs={{0,2},{2,0},{4,6},{6,4},{8,10},{10,8},{12,14},{14,12},{1,3},{3,1},... | collective-permute-start | bytes 393224 | tf_op jit(solution)/shard_map/ppermute | solution.py:262
  31.2 1.8 %collective-permute-start.11 = (bf16[384,128]{1,0:T(8,128)(2,1)S(1)}, bf16[384,128]{1,0:T(8,128)(2,1)S(1)}, u32[]{:S(2)}, u32[]{:S(2)}) collective-permute-start(bf16[384,128]{1,0:T(8,128)(2,1)S(1)} %get-tuple-element.45), channel_id=1, source_target_pairs={{0,8},{2,10},{4,12},{6,14},{8,0},{10,2},{12,4},{14,6},{1,9},{3,11}... | collective-permute-start | bytes 294920 | tf_op jit(solution)/shard_map/ppermute | solution.py:262
  33.0 1.1 %shard_map.81 = (bf16[32,2048]{1,0:T(8,128)(2,1)S(1)}, bf16[32,2048]{1,0:T(8,128)(2,1)S(1)}, bf16[32,2048]{1,0:T(8,128)(2,1)S(1)}, f32[32,2048]{1,0:T(8,128)S(1)...) custom-call(bf16[256,1024]{1,0:T(8,128)(2,1)S(1)} %get-tuple-element.46.low, ...), custom_call_target="tpu_custom_call" | custom-call | bytes 16777216 | tf_op jit(solution)/shard_map/pallas_call | solution.py:351
  34.2 0.6 %collective-permute-start.15 = (bf16[32,2048]{1,0:T(8,128)(2,1)S(1)}, bf16[32,2048]{1,0:T(8,128)(2,1)S(1)}, u32[]{:S(2)}, u32[]{:S(2)}) collective-permute-start(bf16[32,2048]{1,0:T(8,128)(2,1)S(1)} %get-tuple-element.50), channel_id=1, source_target_pairs={{0,2},{2,0},{4,6},{6,4},{8,10},{10,8},{12,14},{14,12},{1,3},{3,1},... | collective-permute-start | bytes 393224 | tf_op jit(solution)/shard_map/ppermute | solution.py:262
  34.8 1.5 %collective-permute-start.17 = (bf16[32,2048]{1,0:T(8,128)(2,1)S(1)}, bf16[32,2048]{1,0:T(8,128)(2,1)S(1)}, u32[]{:S(2)}, u32[]{:S(2)}) collective-permute-start(bf16[32,2048]{1,0:T(8,128)(2,1)S(1)} %get-tuple-element.52), channel_id=1, source_target_pairs={{0,2},{2,0},{4,6},{6,4},{8,10},{10,8},{12,14},{14,12},{1,3},{3,1},... | collective-permute-start | bytes 393224 | tf_op jit(solution)/shard_map/ppermute | solution.py:262
  36.3 2.1 %collective-permute-start.19 = (bf16[32,2048]{1,0:T(8,128)(2,1)S(1)}, bf16[32,2048]{1,0:T(8,128)(2,1)S(1)}, u32[]{:S(2)}, u32[]{:S(2)}) collective-permute-start(bf16[32,2048]{1,0:T(8,128)(2,1)S(1)} %shard_map.83), channel_id=1, source_target_pairs={{0,4},{2,6},{4,0},{6,2},{8,12},{10,14},{12,8},{14,10},{1,5},{3,7},... | collective-permute-start | bytes 393224 | tf_op jit(solution)/shard_map/ppermute | solution.py:262
  39.0 1.3 %collective-permute-start.14 = (bf16[32,2048]{1,0:T(8,128)(2,1)S(1)}, bf16[32,2048]{1,0:T(8,128)(2,1)S(1)}, u32[]{:S(2)}, u32[]{:S(2)}) collective-permute-start(bf16[32,2048]{1,0:T(8,128)(2,1)S(1)} %get-tuple-element.48), channel_id=1, source_target_pairs={{0,2},{2,0},{4,6},{6,4},{8,10},{10,8},{12,14},{14,12},{1,3},{3,1},... | collective-permute-start | bytes 393224 | tf_op jit(solution)/shard_map/ppermute | solution.py:262
  40.7 2.1 %collective-permute-start.16 = (bf16[32,2048]{1,0:T(8,128)(2,1)S(1)}, bf16[32,2048]{1,0:T(8,128)(2,1)S(1)}, u32[]{:S(2)}, u32[]{:S(2)}) collective-permute-start(bf16[32,2048]{1,0:T(8,128)(2,1)S(1)} %shard_map.82), channel_id=1, source_target_pairs={{0,4},{2,6},{4,0},{6,2},{8,12},{10,14},{12,8},{14,10},{1,5},{3,7},... | collective-permute-start | bytes 393224 | tf_op jit(solution)/shard_map/ppermute | solution.py:262
  43.0 1.0 %collective-permute-start.20 = (bf16[32,2048]{1,0:T(8,128)(2,1)S(1)}, bf16[32,2048]{1,0:T(8,128)(2,1)S(1)}, u32[]{:S(2)}, u32[]{:S(2)}) collective-permute-start(bf16[32,2048]{1,0:T(8,128)(2,1)S(1)} %shard_map.84), channel_id=1, source_target_pairs={{0,8},{2,10},{4,12},{6,14},{8,0},{10,2},{12,4},{14,6},{1,9},{3,11}... | collective-permute-start | bytes 393224 | tf_op jit(solution)/shard_map/ppermute | solution.py:262
  44.0 2.4 %collective-permute-done.12 = bf16[384,128]{1,0:T(8,128)(2,1)S(1)} collective-permute-done((bf16[384,128]{1,0:T(8,128)(2,1)S(1)}, bf16[384,128]{1,0:T(8,128)(2,1)S(1)}, u32[]{:S(2)}, u32[]{:S(2)}) %collective-permute-start.12) | collective-permute-done | bytes 98336 | tf_op jit(solution)/shard_map/ppermute | solution.py:262
  46.5 1.9 %collective-permute-done.16.refs_1_ = bf16[32,2048]{1,0:T(8,128)(2,1)S(1)} collective-permute-done((bf16[32,2048]{1,0:T(8,128)(2,1)S(1)}, bf16[32,2048]{1,0:T(8,128)(2,1)S(1)}, u32[]{:S(2)}, u32[]{:S(2)}) %collective-permute-start.16) | collective-permute-done | bytes 131104 | tf_op jit(solution)/shard_map/ppermute | solution.py:262
  48.4 1.2 %collective-permute-done.20.refs_2_ = bf16[32,2048]{1,0:T(8,128)(2,1)S(1)} collective-permute-done((bf16[32,2048]{1,0:T(8,128)(2,1)S(1)}, bf16[32,2048]{1,0:T(8,128)(2,1)S(1)}, u32[]{:S(2)}, u32[]{:S(2)}) %collective-permute-start.20) | collective-permute-done | bytes 131104 | tf_op jit(solution)/shard_map/ppermute | solution.py:262
  49.7 1.4 %collective-permute-done.13.other = bf16[384,128]{1,0:T(8,128)(2,1)S(1)} collective-permute-done((bf16[384,128]{1,0:T(8,128)(2,1)S(1)}, bf16[384,128]{1,0:T(8,128)(2,1)S(1)}, u32[]{:S(2)}, u32[]{:S(2)}) %collective-permute-start.13) | collective-permute-done | bytes 98336 | tf_op jit(solution)/shard_map/ppermute | solution.py:262
  51.1 1.1 %shard_map.86 = f32[32,2048]{1,0:T(8,128)} custom-call(bf16[384,128]{1,0:T(8,128)(2,1)S(1)} %add_convert_fusion.mine, bf16[384,128]{1,0:T(8,128)(2,1)S(1)} %collective-permute-done.13.other, bf16[256,2048]{1,0:T(8,128)(2,1)S(1)} %get-tuple-element.56.panel, f32[32,2048]{1,0:T(8,128)S(1)} %copy-done, f32[32,2048]{1,0:T(8,128)S(1)} %shard_map.85.data), custom_call_target="tpu_custom_call" | custom-call | tf_op jit(solution)/shard_map/pallas_call | solution.py:381
  (27 shorter events, 1.7 us)
Async XLA Ops:
  0.6 13.0 %collective-permute-start.3 = (f32[128,1024]{1,0:T(8,128)}, f32[128,1024]{1,0:T(8,128)S(1)}, u32[]{:S(2)}, u32[]{:S(2)}) collective-permute-start(f32[128,1024]{1,0:T(8,128)} %factor_mine.1), channel_id=1, source_target_pairs={{0,1},{1,0},{2,3},{3,2},{4,5},{5,4},{6,7},{7,6},{8,9},{9,8},{10,11... | collective-permute-start | bytes 1572872 | tf_op jit(solution)/shard_map/ppermute | solution.py:265
  2.1 11.5 %collective-permute-start.2 = (bf16[32,2048]{1,0:T(8,128)(2,1)S(1)}, bf16[32,2048]{1,0:T(8,128)(2,1)S(1)}, u32[]{:S(2)}, u32[]{:S(2)}) collective-permute-start(bf16[32,2048]{1,0:T(8,128)(2,1)S(1)} %convert_element_type.21.refs_0_), channel_id=1, source_target_pairs={{0,8},{2,10},{4,12},{6,14},{8,0},{10,2},{12,4},{14,6},{1,9},{3,11}... | collective-permute-start | bytes 393224 | tf_op jit(solution)/shard_map/ppermute | solution.py:262
  5.8 7.8 %collective-permute-start.1 = (bf16[32,2048]{1,0:T(8,128)(2,1)S(1)}, bf16[32,2048]{1,0:T(8,128)(2,1)S(1)}, u32[]{:S(2)}, u32[]{:S(2)}) collective-permute-start(bf16[32,2048]{1,0:T(8,128)(2,1)S(1)} %convert_element_type.21.refs_0_), channel_id=1, source_target_pairs={{0,4},{2,6},{4,0},{6,2},{8,12},{10,14},{12,8},{14,10},{1,5},{3,7},... | collective-permute-start | bytes 393224 | tf_op jit(solution)/shard_map/ppermute | solution.py:262
  7.4 6.3 %collective-permute-start = (bf16[32,2048]{1,0:T(8,128)(2,1)S(1)}, bf16[32,2048]{1,0:T(8,128)(2,1)S(1)}, u32[]{:S(2)}, u32[]{:S(2)}) collective-permute-start(bf16[32,2048]{1,0:T(8,128)(2,1)S(1)} %convert_element_type.21.refs_0_), channel_id=1, source_target_pairs={{0,2},{2,0},{4,6},{6,4},{8,10},{10,8},{12,14},{14,12},{1,3},{3,1},... | collective-permute-start | bytes 393224 | tf_op jit(solution)/shard_map/ppermute | solution.py:262
  13.6 14.2 %copy-start.1 = (f32[128,1024]{1,0:T(8,128)S(1)}, f32[128,1024]{1,0:T(8,128)}, u32[]{:S(2)}) copy-start(f32[128,1024]{1,0:T(8,128)} %factor_mine.1) | copy-start | bytes 1572868
  13.7 6.4 %collective-permute-start.6 = (bf16[32,2048]{1,0:T(8,128)(2,1)S(1)}, bf16[32,2048]{1,0:T(8,128)(2,1)S(1)}, u32[]{:S(2)}, u32[]{:S(2)}) collective-permute-start(bf16[32,2048]{1,0:T(8,128)(2,1)S(1)} %collective-permute-done.2.refs_4_), channel_id=1, source_target_pairs={{0,4},{2,6},{4,0},{6,2},{8,12},{10,14},{12,8},{14,10},{1,5},{3,7},... | collective-permute-start | bytes 393224 | tf_op jit(solution)/shard_map/ppermute | solution.py:262
  14.6 6.9 %collective-permute-start.4 = (bf16[32,2048]{1,0:T(8,128)(2,1)S(1)}, bf16[32,2048]{1,0:T(8,128)(2,1)S(1)}, u32[]{:S(2)}, u32[]{:S(2)}) collective-permute-start(bf16[32,2048]{1,0:T(8,128)(2,1)S(1)} %collective-permute-done.refs_1_), channel_id=1, source_target_pairs={{0,4},{2,6},{4,0},{6,2},{8,12},{10,14},{12,8},{14,10},{1,5},{3,7},... | collective-permute-start | bytes 393224 | tf_op jit(solution)/shard_map/ppermute | solution.py:262
  15.7 6.1 %collective-permute-start.5 = (bf16[32,2048]{1,0:T(8,128)(2,1)S(1)}, bf16[32,2048]{1,0:T(8,128)(2,1)S(1)}, u32[]{:S(2)}, u32[]{:S(2)}) collective-permute-start(bf16[32,2048]{1,0:T(8,128)(2,1)S(1)} %collective-permute-done.2.refs_4_), channel_id=1, source_target_pairs={{0,2},{2,0},{4,6},{6,4},{8,10},{10,8},{12,14},{14,12},{1,3},{3,1},... | collective-permute-start | bytes 393224 | tf_op jit(solution)/shard_map/ppermute | solution.py:262
  20.1 5.0 %collective-permute-start.7 = (bf16[32,2048]{1,0:T(8,128)(2,1)S(1)}, bf16[32,2048]{1,0:T(8,128)(2,1)S(1)}, u32[]{:S(2)}, u32[]{:S(2)}) collective-permute-start(bf16[32,2048]{1,0:T(8,128)(2,1)S(1)} %collective-permute-done.6.refs_6_), channel_id=1, source_target_pairs={{0,2},{2,0},{4,6},{6,4},{8,10},{10,8},{12,14},{14,12},{1,3},{3,1},... | collective-permute-start | bytes 393224 | tf_op jit(solution)/shard_map/ppermute | solution.py:262
  23.0 3.4 %collective-permute-start.9 = (bf16[112,1024]{1,0:T(8,128)(2,1)S(1)}, bf16[112,1024]{1,0:T(8,128)(2,1)S(1)}, u32[]{:S(2)}, u32[]{:S(2)}) collective-permute-start(bf16[112,1024]{1,0:T(8,128)(2,1)S(1)} %get-tuple-element.42), channel_id=1, source_target_pairs={{0,1},{1,0},{2,3},{3,2},{4,5},{5,4},{6,7},{7,6},{8,9},{9,8},{10,11... | collective-permute-start | bytes 688136 | tf_op jit(solution)/shard_map/ppermute | solution.py:265
  23.0 3.3 %collective-permute-start.10 = (bf16[112,1024]{1,0:T(8,128)(2,1)S(1)}, bf16[112,1024]{1,0:T(8,128)(2,1)S(1)}, u32[]{:S(2)}, u32[]{:S(2)}) collective-permute-start(bf16[112,1024]{1,0:T(8,128)(2,1)S(1)} %get-tuple-element.43), channel_id=1, source_target_pairs={{0,1},{1,0},{2,3},{3,2},{4,5},{5,4},{6,7},{7,6},{8,9},{9,8},{10,11... | collective-permute-start | bytes 688136 | tf_op jit(solution)/shard_map/ppermute | solution.py:265
  26.3 1.5 %collective-permute-start.8 = (bf16[96,1024]{1,0:T(8,128)(2,1)S(1)}, bf16[96,1024]{1,0:T(8,128)(2,1)S(1)}, u32[]{:S(2)}, u32[]{:S(2)}) collective-permute-start(bf16[96,1024]{1,0:T(8,128)(2,1)S(1)} %get-tuple-element.40), channel_id=1, source_target_pairs={{0,1},{1,0},{2,3},{3,2},{4,5},{5,4},{6,7},{7,6},{8,9},{9,8},{10,11... | collective-permute-start | bytes 589832 | tf_op jit(solution)/shard_map/ppermute | solution.py:265
  30.4 20.7 %copy-start = (f32[32,2048]{1,0:T(8,128)S(1)}, f32[32,2048]{1,0:T(8,128)}, u32[]{:S(2)}) copy-start(f32[32,2048]{1,0:T(8,128)} %factor.1) | copy-start | bytes 786436
  30.4 5.8 %collective-permute-start.18 = (bf16[32,2048]{1,0:T(8,128)(2,1)S(1)}, bf16[32,2048]{1,0:T(8,128)(2,1)S(1)}, u32[]{:S(2)}, u32[]{:S(2)}) collective-permute-start(bf16[32,2048]{1,0:T(8,128)(2,1)S(1)} %get-tuple-element.54), channel_id=1, source_target_pairs={{0,2},{2,0},{4,6},{6,4},{8,10},{10,8},{12,14},{14,12},{1,3},{3,1},... | collective-permute-start | bytes 393224 | tf_op jit(solution)/shard_map/ppermute | solution.py:262
  31.2 7.6 %collective-permute-start.11 = (bf16[384,128]{1,0:T(8,128)(2,1)S(1)}, bf16[384,128]{1,0:T(8,128)(2,1)S(1)}, u32[]{:S(2)}, u32[]{:S(2)}) collective-permute-start(bf16[384,128]{1,0:T(8,128)(2,1)S(1)} %get-tuple-element.45), channel_id=1, source_target_pairs={{0,8},{2,10},{4,12},{6,14},{8,0},{10,2},{12,4},{14,6},{1,9},{3,11}... | collective-permute-start | bytes 294920 | tf_op jit(solution)/shard_map/ppermute | solution.py:262
  34.2 6.5 %collective-permute-start.15 = (bf16[32,2048]{1,0:T(8,128)(2,1)S(1)}, bf16[32,2048]{1,0:T(8,128)(2,1)S(1)}, u32[]{:S(2)}, u32[]{:S(2)}) collective-permute-start(bf16[32,2048]{1,0:T(8,128)(2,1)S(1)} %get-tuple-element.50), channel_id=1, source_target_pairs={{0,2},{2,0},{4,6},{6,4},{8,10},{10,8},{12,14},{14,12},{1,3},{3,1},... | collective-permute-start | bytes 393224 | tf_op jit(solution)/shard_map/ppermute | solution.py:262
  34.8 8.1 %collective-permute-start.17 = (bf16[32,2048]{1,0:T(8,128)(2,1)S(1)}, bf16[32,2048]{1,0:T(8,128)(2,1)S(1)}, u32[]{:S(2)}, u32[]{:S(2)}) collective-permute-start(bf16[32,2048]{1,0:T(8,128)(2,1)S(1)} %get-tuple-element.52), channel_id=1, source_target_pairs={{0,2},{2,0},{4,6},{6,4},{8,10},{10,8},{12,14},{14,12},{1,3},{3,1},... | collective-permute-start | bytes 393224 | tf_op jit(solution)/shard_map/ppermute | solution.py:262
  36.3 6.6 %collective-permute-start.19 = (bf16[32,2048]{1,0:T(8,128)(2,1)S(1)}, bf16[32,2048]{1,0:T(8,128)(2,1)S(1)}, u32[]{:S(2)}, u32[]{:S(2)}) collective-permute-start(bf16[32,2048]{1,0:T(8,128)(2,1)S(1)} %shard_map.83), channel_id=1, source_target_pairs={{0,4},{2,6},{4,0},{6,2},{8,12},{10,14},{12,8},{14,10},{1,5},{3,7},... | collective-permute-start | bytes 393224 | tf_op jit(solution)/shard_map/ppermute | solution.py:262
  38.9 7.5 %collective-permute-start.12 = (bf16[384,128]{1,0:T(8,128)(2,1)S(1)}, bf16[384,128]{1,0:T(8,128)(2,1)S(1)}, u32[]{:S(2)}, u32[]{:S(2)}) collective-permute-start(bf16[384,128]{1,0:T(8,128)(2,1)S(1)} %add_convert_fusion.1), channel_id=1, source_target_pairs={{0,4},{2,6},{4,0},{6,2},{8,12},{10,14},{12,8},{14,10},{1,5},{3,7},... | collective-permute-start | bytes 294920 | tf_op jit(solution)/shard_map/ppermute | solution.py:262
  39.0 7.5 %collective-permute-start.14 = (bf16[32,2048]{1,0:T(8,128)(2,1)S(1)}, bf16[32,2048]{1,0:T(8,128)(2,1)S(1)}, u32[]{:S(2)}, u32[]{:S(2)}) collective-permute-start(bf16[32,2048]{1,0:T(8,128)(2,1)S(1)} %get-tuple-element.48), channel_id=1, source_target_pairs={{0,2},{2,0},{4,6},{6,4},{8,10},{10,8},{12,14},{14,12},{1,3},{3,1},... | collective-permute-start | bytes 393224 | tf_op jit(solution)/shard_map/ppermute | solution.py:262
  40.7 7.7 %collective-permute-start.16 = (bf16[32,2048]{1,0:T(8,128)(2,1)S(1)}, bf16[32,2048]{1,0:T(8,128)(2,1)S(1)}, u32[]{:S(2)}, u32[]{:S(2)}) collective-permute-start(bf16[32,2048]{1,0:T(8,128)(2,1)S(1)} %shard_map.82), channel_id=1, source_target_pairs={{0,4},{2,6},{4,0},{6,2},{8,12},{10,14},{12,8},{14,10},{1,5},{3,7},... | collective-permute-start | bytes 393224 | tf_op jit(solution)/shard_map/ppermute | solution.py:262
  43.0 6.6 %collective-permute-start.20 = (bf16[32,2048]{1,0:T(8,128)(2,1)S(1)}, bf16[32,2048]{1,0:T(8,128)(2,1)S(1)}, u32[]{:S(2)}, u32[]{:S(2)}) collective-permute-start(bf16[32,2048]{1,0:T(8,128)(2,1)S(1)} %shard_map.84), channel_id=1, source_target_pairs={{0,8},{2,10},{4,12},{6,14},{8,0},{10,2},{12,4},{14,6},{1,9},{3,11}... | collective-permute-start | bytes 393224 | tf_op jit(solution)/shard_map/ppermute | solution.py:262
  46.4 4.7 %collective-permute-start.13 = (bf16[384,128]{1,0:T(8,128)(2,1)S(1)}, bf16[384,128]{1,0:T(8,128)(2,1)S(1)}, u32[]{:S(2)}, u32[]{:S(2)}) collective-permute-start(bf16[384,128]{1,0:T(8,128)(2,1)S(1)} %add_convert_fusion.mine), channel_id=1, source_target_pairs={{0,2},{2,0},{4,6},{6,4},{8,10},{10,8},{12,14},{14,12},{1,3},{3,1},... | collective-permute-start | bytes 294920 | tf_op jit(solution)/shard_map/ppermute | solution.py:262

commit v11 on v10

--- a/solution.py
+++ b/solution.py
@@ -219,6 +219,10 @@
         out[...] = coded(part) if out.dtype == jnp.bfloat16 else part
 
 
+def copy_body(source, out):
+    out[...] = source[...]
+
+
 def sum_body(keep, *refs):
     total = keep[...]
     for part in refs[:-1]:
@@ -226,14 +230,7 @@
     refs[-1][...] = coded(total)
 
 
-def total_body(keep, *refs):
-    total = keep[...]
-    for part in refs[:-1]:
-        total = total + decoded(part[...])
-    refs[-1][...] = total
-
-
-def last_body(mine, other, panel, factor, data, out, gram):
+def base_body(mine, other, panel, factor, base, rate_out, gram):
     half = mine.shape[0] // 3
     quarters = mine[...].astype(jnp.float32) + other[...].astype(jnp.float32)
     upper, side, lower = quarters[:half], quarters[half : 2 * half], quarters[2 * half :]
@@ -244,8 +241,15 @@
     squares = upper * upper + 2.0 * (side * side) + lower * lower
     norm = jnp.sum(jnp.sum(squares, axis=1, keepdims=True), axis=0, keepdims=True)
     rate = 1.0 / (jnp.sqrt(norm) + 1e-06)
-    stepped = split_dot(gram[owned(0, factor.shape[0])], panel[...])
-    out[...] = jnp.maximum(factor[...] - rate * (stepped - data[...]), 0.0)
+    base[...] = factor[...] - rate * split_dot(gram[owned(0, factor.shape[0])], panel[...])
+    rate_out[...] = jnp.broadcast_to(rate, rate_out.shape)
+
+
+def last_body(rate, base, own, *refs):
+    total = own[...]
+    for part in refs[:-1]:
+        total = total + decoded(part[...])
+    refs[-1][...] = jnp.maximum(base[...] + rate[0:1, 0:1] * total, 0.0)
 
 
 def gram_of(panel):
@@ -272,10 +276,11 @@
     tile, turned = dense_tile(block_values[0, 0], block_rows[0, 0], block_cols[0, 0], block_count[0])
     if paired:
         near = [swap(low_share, bits) for bits in (1, 2, 4)]
+        sixth = swap(low_share, 6)
         beside, second, fourth, tile, turned, factor_other = lax.optimization_barrier(
             (*near, tile, turned, factor_other)
         )
-        sixth, third, fifth = swap(fourth, 2), swap(beside, 2), swap(fourth, 1)
+        third, fifth = swap(beside, 2), swap(fourth, 1)
         seventh = swap(sixth, 1)
         shares = [low_share, beside, second, third, fourth, fifth, sixth]
         order = range(n_cell)
@@ -317,7 +322,7 @@
 
     sent = [5, 3, 1]
     kept = [6, 4, 2, 0]
-    cell_next, next_low, *sends = call(
+    updated, next_low, *sends = call(
         functools.partial(cell_body, order, [7], n_parts),
         (
             shape(cell_factor.shape, jnp.float32),
@@ -345,7 +350,7 @@
         stepped = jnp.dot(
             gram_part, panel.astype(jnp.float32), precision=lax.Precision.HIGHEST
         )
-        return (cell_next, jnp.maximum(gene_factor - rate_gene * (stepped - own_cols), 0.0))
+        return (updated, jnp.maximum(gene_factor - rate_gene * (stepped - own_cols), 0.0))
 
     arrived = [swap(sends[0], 1)]
     *parts, keep_third, keep_second, keep_near, own = call(
@@ -376,17 +381,21 @@
     across = swap(across, 4)
     gram = (gram.astype(jnp.float32) + gram_arrived.astype(jnp.float32)).astype(jnp.bfloat16)
     partner = swap(gram, 1)
-    total = call(total_body, wide(size, jnp.float32), 0, 4, 0, AHEAD)(own, arrived[3], beside, across)
-    partner, total = lax.optimization_barrier((partner, total))
-    gene_next = call(
-        last_body,
-        wide(size, jnp.float32),
-        0,
-        5,
+    gram, updated = lax.optimization_barrier((gram, updated))
+    cell_next = call(copy_body, shape(cell_factor.shape, jnp.float32), 0, 1, 0, 0)(updated)
+    own, cell_next = lax.optimization_barrier((own, cell_next))
+    base, rate = call(
+        base_body,
+        (wide(size, jnp.float32), shape((8, 128), jnp.float32)),
+        0,
+        4,
         0,
         0,
         [pltpu.VMEM((kdim, kdim), jnp.float32)],
-    )(gram, partner, panel, gene_factor, total)
+    )(gram, partner, panel, gene_factor)
+    gene_next = call(last_body, wide(size, jnp.float32), 0, 6, 0, AHEAD)(
+        rate, base, own, arrived[3], beside, across
+    )
     return (cell_next, gene_next)
 
 

time: 52.4 us -> 51.4 us (0.981)
  waiting for transfers between devices: 14.9 us -> 14 us
    ppermute x17, waiting for transfers between devices: 13.5 us -> 12.6 us  [swap(): return lax.ppermute(value, 'cell', [(n, n ^ bits) for n in range(n_cell)])]
    pallas_call x2 -> x3, Pallas kernels: 1.16 us -> 2.06 us  [the longest x1 0.86 us: shards(): call(last_body, wide(size, jnp.float32), 0, 6, 0, AHEAD)]
    pallas_call x1, Pallas kernels: 2.61 us -> 2.03 us  [shards(): call(functools.partial(cell_body, order, [7], n_parts), (shape(cell_facto...]
  transfers between devices with their start and end apart: 21 -> 21, of which waited for: 11 -> 10; matrix products, arithmetic and copies ran while one was open for 2% -> 2% of each run, Pallas kernels for 15% -> 18%
where the time goes in v11:
time: 51.4 us; the launch traced here: 51.1 us
  starting transfers between devices  22.8 us (44%)
  waiting for transfers between devices  14 us (27%)
  Pallas kernels  11.9 us (23%)
  between operations  1.45 us (3%)
  other arithmetic  1.02 us (2%)
    ppermute x17, starting transfers between devices, swap(): return lax.ppermute(value, 'cell', [(n, n ^ bits) for n in range(n_cell)])  21.6 us
    ppermute x17, waiting for transfers between devices, swap(): return lax.ppermute(value, 'cell', [(n, n ^ bits) for n in range(n_cell)])  12.6 us
    pallas_call x1, Pallas kernels, dense_tile(): pl.pallas_call(dense_body, out_shape=(shape((CELL_DEV, GENE_DEV), jnp.bfl...  4.09 us
    pallas_call x1, Pallas kernels, shards(): call(functools.partial(cell_body, order, [7], n_parts), (shape(cell_facto...  2.03 us
    ppermute x4, waiting for transfers between devices, swap_core(): return lax.ppermute(value, 'gene', [(0, 1), (1, 0)])  1.41 us
    pallas_call x1, Pallas kernels, shards(): call(functools.partial(second_body, order), (wide(kdim, jnp.bfloat16), sh...  1.21 us
    ppermute x4, starting transfers between devices, swap_core(): return lax.ppermute(value, 'gene', [(0, 1), (1, 0)])  1.19 us
    pallas_call x1, Pallas kernels, shards(): call(functools.partial(first_body, n_parts), (wide(first_rows, jnp.bfloat...  1.14 us
  transfers between devices with their start and end apart: 21, of which 10 were waited for; matrix products, arithmetic and copies ran while one was open for 2% of the time, Pallas kernels for 18%

profile of v11, /device:TPU:0, one launch (start us, length us, event | category | flops | bytes accessed | tf_op | source)
XLA Modules:
  0.0 51.1 jit_solution(10560231256927190990)
XLA Ops:
  0.6 0.5 %collective-permute-start.3 = (f32[128,1024]{1,0:T(8,128)}, f32[128,1024]{1,0:T(8,128)S(1)}, u32[]{:S(2)}, u32[]{:S(2)}) collective-permute-start(f32[128,1024]{1,0:T(8,128)} %factor_mine.1), channel_id=1, source_target_pairs={{0,1},{1,0},{2,3},{3,2},{4,5},{5,4},{6,7},{7,6},{8,9},{9,8},{10,11... | collective-permute-start | bytes 1572872 | tf_op jit(solution)/shard_map/ppermute | solution.py:269
  1.1 1.0 %convert_element_type.21.refs_0_ = bf16[32,2048]{1,0:T(8,128)(2,1)S(1)} convert(f32[32,2048]{1,0:T(8,128)} %factor.1) | non-fusion elementwise | flops 65536 | bytes 393216 | tf_op jit(solution)/shard_map/convert_element_type | solution.py:274
  2.1 3.7 %collective-permute-start.2 = (bf16[32,2048]{1,0:T(8,128)(2,1)S(1)}, bf16[32,2048]{1,0:T(8,128)(2,1)S(1)}, u32[]{:S(2)}, u32[]{:S(2)}) collective-permute-start(bf16[32,2048]{1,0:T(8,128)(2,1)S(1)} %convert_element_type.21.refs_0_), channel_id=1, source_target_pairs={{0,8},{2,10},{4,12},{6,14},{8,0},{10,2},{12,4},{14,6},{1,9},{3,11}... | collective-permute-start | bytes 393224 | tf_op jit(solution)/shard_map/ppermute | solution.py:266
  5.8 1.6 %collective-permute-start.1 = (bf16[32,2048]{1,0:T(8,128)(2,1)S(1)}, bf16[32,2048]{1,0:T(8,128)(2,1)S(1)}, u32[]{:S(2)}, u32[]{:S(2)}) collective-permute-start(bf16[32,2048]{1,0:T(8,128)(2,1)S(1)} %convert_element_type.21.refs_0_), channel_id=1, source_target_pairs={{0,4},{2,6},{4,0},{6,2},{8,12},{10,14},{12,8},{14,10},{1,5},{3,7},... | collective-permute-start | bytes 393224 | tf_op jit(solution)/shard_map/ppermute | solution.py:266
  7.4 1.5 %collective-permute-start = (bf16[32,2048]{1,0:T(8,128)(2,1)S(1)}, bf16[32,2048]{1,0:T(8,128)(2,1)S(1)}, u32[]{:S(2)}, u32[]{:S(2)}) collective-permute-start(bf16[32,2048]{1,0:T(8,128)(2,1)S(1)} %convert_element_type.21.refs_0_), channel_id=1, source_target_pairs={{0,2},{2,0},{4,6},{6,4},{8,10},{10,8},{12,14},{14,12},{1,3},{3,1},... | collective-permute-start | bytes 393224 | tf_op jit(solution)/shard_map/ppermute | solution.py:266
  9.7 4.1 %shard_map.77 = (bf16[1024,2048]{1,0:T(8,128)(2,1)S(1)}, bf16[2048,1024]{1,0:T(8,128)(2,1)S(1)}) custom-call(s32[64]{0:T(128)} %bitcast.6, s32[64]{0:T(128)} %bitcast.7, s32[1]{0:T(128)} %bitcast.4.count, bf16[64,128,128]{2,1,0:T(8,128)(2,1)} %bitcast.5), custom_call_target="tpu_custom_call" | custom-call | tf_op jit(solution)/shard_map/pallas_call | solution.py:88
  13.9 1.1 %collective-permute-start.4 = (bf16[32,2048]{1,0:T(8,128)(2,1)S(1)}, bf16[32,2048]{1,0:T(8,128)(2,1)S(1)}, u32[]{:S(2)}, u32[]{:S(2)}) collective-permute-start(bf16[32,2048]{1,0:T(8,128)(2,1)S(1)} %collective-permute-done.refs_1_), channel_id=1, source_target_pairs={{0,4},{2,6},{4,0},{6,2},{8,12},{10,14},{12,8},{14,10},{1,5},{3,7},... | collective-permute-start | bytes 393224 | tf_op jit(solution)/shard_map/ppermute | solution.py:266
  15.0 1.5 %collective-permute-start.5 = (bf16[32,2048]{1,0:T(8,128)(2,1)S(1)}, bf16[32,2048]{1,0:T(8,128)(2,1)S(1)}, u32[]{:S(2)}, u32[]{:S(2)}) collective-permute-start(bf16[32,2048]{1,0:T(8,128)(2,1)S(1)} %collective-permute-done.2.refs_4_), channel_id=1, source_target_pairs={{0,2},{2,0},{4,6},{6,4},{8,10},{10,8},{12,14},{14,12},{1,3},{3,1},... | collective-permute-start | bytes 393224 | tf_op jit(solution)/shard_map/ppermute | solution.py:266
  16.9 1.4 %collective-permute-start.7 = (bf16[32,2048]{1,0:T(8,128)(2,1)S(1)}, bf16[32,2048]{1,0:T(8,128)(2,1)S(1)}, u32[]{:S(2)}, u32[]{:S(2)}) collective-permute-start(bf16[32,2048]{1,0:T(8,128)(2,1)S(1)} %collective-permute-done.6.refs_6_), channel_id=1, source_target_pairs={{0,2},{2,0},{4,6},{6,4},{8,10},{10,8},{12,14},{14,12},{1,3},{3,1},... | collective-permute-start | bytes 393224 | tf_op jit(solution)/shard_map/ppermute | solution.py:266
  18.3 1.3 %collective-permute-done.4.refs_3_ = bf16[32,2048]{1,0:T(8,128)(2,1)S(1)} collective-permute-done((bf16[32,2048]{1,0:T(8,128)(2,1)S(1)}, bf16[32,2048]{1,0:T(8,128)(2,1)S(1)}, u32[]{:S(2)}, u32[]{:S(2)}) %collective-permute-start.4) | collective-permute-done | bytes 131104 | tf_op jit(solution)/shard_map/ppermute | solution.py:266
  19.6 1.4 %collective-permute-done.5.refs_5_ = bf16[32,2048]{1,0:T(8,128)(2,1)S(1)} collective-permute-done((bf16[32,2048]{1,0:T(8,128)(2,1)S(1)}, bf16[32,2048]{1,0:T(8,128)(2,1)S(1)}, u32[]{:S(2)}, u32[]{:S(2)}) %collective-permute-start.5) | collective-permute-done | bytes 131104 | tf_op jit(solution)/shard_map/ppermute | solution.py:266
  21.0 1.1 %shard_map.78 = (bf16[224,2048]{1,0:T(8,128)(2,1)S(1)}, f32[224,1024]{1,0:T(8,128)S(1)}, bf16[112,1024]{1,0:T(8,128)(2,1)S(1)}, bf16[112,1024]{1,0:T(8,128)(2,1)S(1)}) custom-call(bf16[2048,1024]{1,0:T(8,128)(2,1)S(1)} %get-tuple-element.37.turned, bf16[32,2048]{1,0:T(8,128)(2,1)S(1)} %convert_element_type.21.refs_0_, ...), custom_call_target="tpu_custom_call" | custom-call | bytes 16777216 | tf_op jit(solution)/shard_map/pallas_call | solution.py:295
  22.2 0.5 collective-permute-start.10
  22.8 1.2 %shard_map.79 = (bf16[256,2048]{1,0:T(8,128)(2,1)S(1)}, f32[96,1024]{1,0:T(8,128)S(1)}, bf16[96,1024]{1,0:T(8,128)(2,1)S(1)}) custom-call(bf16[2048,1024]{1,0:T(8,128)(2,1)S(1)} %get-tuple-element.37.turned, bf16[224,2048]{1,0:T(8,128)(2,1)S(1)} %get-tuple-element.42.first, bf16[32,2048]{1,0:T(8,128)(2,1)S(1)} %collective-permute-done.7.share), custom_call_target="tpu_custom_call" | custom-call | tf_op jit(solution)/shard_map/pallas_call | solution.py:309
  24.1 1.4 %collective-permute-done.8.other = bf16[96,1024]{1,0:T(8,128)(2,1)S(1)} collective-permute-done((bf16[96,1024]{1,0:T(8,128)(2,1)S(1)}, bf16[96,1024]{1,0:T(8,128)(2,1)S(1)}, u32[]{:S(2)}, u32[]{:S(2)}) %collective-permute-start.8) | collective-permute-done | bytes 196640 | tf_op jit(solution)/shard_map/ppermute | solution.py:269
  25.5 2.0 %shard_map.80 = (f32[128,1024]{1,0:T(8,128)S(1)}, bf16[256,1024]{1,0:T(8,128)(2,1)S(1)}, bf16[32,2048]{1,0:T(8,128)(2,1)S(1)}, bf16[384,128]{1,0:T(8,128)(2,1)S(1)}) custom-call(bf16[1024,2048]{1,0:T(8,128)(2,1)S(1)} %get-tuple-element.36.tile, f32[224,1024]{1,0:T(8,128)S(1)} %get-tuple-element.41.mine_first, f32[96,1024]{1,0:T(8,128)S(1)} %get-tuple-element.43.mine, ...), custom_call_target="tpu_custom_call" | custom-call | tf_op jit(solution)/shard_map/pallas_call | solution.py:325
  27.6 1.6 %collective-permute-start.18 = (bf16[32,2048]{1,0:T(8,128)(2,1)S(1)}, bf16[32,2048]{1,0:T(8,128)(2,1)S(1)}, u32[]{:S(2)}, u32[]{:S(2)}) collective-permute-start(bf16[32,2048]{1,0:T(8,128)(2,1)S(1)} %get-tuple-element.65), channel_id=1, source_target_pairs={{0,2},{2,0},{4,6},{6,4},{8,10},{10,8},{12,14},{14,12},{1,3},{3,1},... | collective-permute-start | bytes 393224 | tf_op jit(solution)/shard_map/ppermute | solution.py:266
  29.1 3.7 %collective-permute-start.11 = (bf16[384,128]{1,0:T(8,128)(2,1)S(1)}, bf16[384,128]{1,0:T(8,128)(2,1)S(1)}, u32[]{:S(2)}, u32[]{:S(2)}) collective-permute-start(bf16[384,128]{1,0:T(8,128)(2,1)S(1)} %get-tuple-element.50), channel_id=1, source_target_pairs={{0,8},{2,10},{4,12},{6,14},{8,0},{10,2},{12,4},{14,6},{1,9},{3,11}... | collective-permute-start | bytes 294920 | tf_op jit(solution)/shard_map/ppermute | solution.py:266
  32.8 1.1 %shard_map.81 = (bf16[32,2048]{1,0:T(8,128)(2,1)S(1)}, bf16[32,2048]{1,0:T(8,128)(2,1)S(1)}, bf16[32,2048]{1,0:T(8,128)(2,1)S(1)}, f32[32,2048]{1,0:T(8,128)S(1)...) custom-call(bf16[256,1024]{1,0:T(8,128)(2,1)S(1)} %get-tuple-element.48.low, ...), custom_call_target="tpu_custom_call" | custom-call | bytes 16777216 | tf_op jit(solution)/shard_map/pallas_call | solution.py:356
  34.0 0.6 %collective-permute-start.15 = (bf16[32,2048]{1,0:T(8,128)(2,1)S(1)}, bf16[32,2048]{1,0:T(8,128)(2,1)S(1)}, u32[]{:S(2)}, u32[]{:S(2)}) collective-permute-start(bf16[32,2048]{1,0:T(8,128)(2,1)S(1)} %get-tuple-element.61), channel_id=1, source_target_pairs={{0,2},{2,0},{4,6},{6,4},{8,10},{10,8},{12,14},{14,12},{1,3},{3,1},... | collective-permute-start | bytes 393224 | tf_op jit(solution)/shard_map/ppermute | solution.py:266
  34.6 1.5 %collective-permute-start.17 = (bf16[32,2048]{1,0:T(8,128)(2,1)S(1)}, bf16[32,2048]{1,0:T(8,128)(2,1)S(1)}, u32[]{:S(2)}, u32[]{:S(2)}) collective-permute-start(bf16[32,2048]{1,0:T(8,128)(2,1)S(1)} %get-tuple-element.63), channel_id=1, source_target_pairs={{0,2},{2,0},{4,6},{6,4},{8,10},{10,8},{12,14},{14,12},{1,3},{3,1},... | collective-permute-start | bytes 393224 | tf_op jit(solution)/shard_map/ppermute | solution.py:266
  36.2 1.6 %collective-permute-done.11 = bf16[384,128]{1,0:T(8,128)(2,1)S(1)} collective-permute-done((bf16[384,128]{1,0:T(8,128)(2,1)S(1)}, bf16[384,128]{1,0:T(8,128)(2,1)S(1)}, u32[]{:S(2)}, u32[]{:S(2)}) %collective-permute-start.11) | collective-permute-done | bytes 98336 | tf_op jit(solution)/shard_map/ppermute | solution.py:266
  37.8 0.5 %collective-permute-start.12 = (bf16[384,128]{1,0:T(8,128)(2,1)S(1)}, bf16[384,128]{1,0:T(8,128)(2,1)S(1)}, u32[]{:S(2)}, u32[]{:S(2)}) collective-permute-start(bf16[384,128]{1,0:T(8,128)(2,1)S(1)} %add_convert_fusion.1), channel_id=1, source_target_pairs={{0,4},{2,6},{4,0},{6,2},{8,12},{10,14},{12,8},{14,10},{1,5},{3,7},... | collective-permute-start | bytes 294920 | tf_op jit(solution)/shard_map/ppermute | solution.py:266
  38.3 0.5 %collective-permute-start.14 = (bf16[32,2048]{1,0:T(8,128)(2,1)S(1)}, bf16[32,2048]{1,0:T(8,128)(2,1)S(1)}, u32[]{:S(2)}, u32[]{:S(2)}) collective-permute-start(bf16[32,2048]{1,0:T(8,128)(2,1)S(1)} %get-tuple-element.59), channel_id=1, source_target_pairs={{0,2},{2,0},{4,6},{6,4},{8,10},{10,8},{12,14},{14,12},{1,3},{3,1},... | collective-permute-start | bytes 393224 | tf_op jit(solution)/shard_map/ppermute | solution.py:266
  38.8 1.6 %collective-permute-done.15.refs_0_ = bf16[32,2048]{1,0:T(8,128)(2,1)S(1)} collective-permute-done((bf16[32,2048]{1,0:T(8,128)(2,1)S(1)}, bf16[32,2048]{1,0:T(8,128)(2,1)S(1)}, u32[]{:S(2)}, u32[]{:S(2)}) %collective-permute-start.15) | collective-permute-done | bytes 131104 | tf_op jit(solution)/shard_map/ppermute | solution.py:266
  40.6 2.6 %collective-permute-done.17.refs_0_ = bf16[32,2048]{1,0:T(8,128)(2,1)S(1)} collective-permute-done((bf16[32,2048]{1,0:T(8,128)(2,1)S(1)}, bf16[32,2048]{1,0:T(8,128)(2,1)S(1)}, u32[]{:S(2)}, u32[]{:S(2)}) %collective-permute-start.17) | collective-permute-done | bytes 131104 | tf_op jit(solution)/shard_map/ppermute | solution.py:266
  43.3 0.6 %collective-permute-start.20 = (bf16[32,2048]{1,0:T(8,128)(2,1)S(1)}, bf16[32,2048]{1,0:T(8,128)(2,1)S(1)}, u32[]{:S(2)}, u32[]{:S(2)}) collective-permute-start(bf16[32,2048]{1,0:T(8,128)(2,1)S(1)} %shard_map.86), channel_id=1, source_target_pairs={{0,8},{2,10},{4,12},{6,14},{8,0},{10,2},{12,4},{14,6},{1,9},{3,11}... | collective-permute-start | bytes 393224 | tf_op jit(solution)/shard_map/ppermute | solution.py:266
  44.2 1.5 %collective-permute-start.13 = (bf16[384,128]{1,0:T(8,128)(2,1)S(1)}, bf16[384,128]{1,0:T(8,128)(2,1)S(1)}, u32[]{:S(2)}, u32[]{:S(2)}) collective-permute-start(bf16[384,128]{1,0:T(8,128)(2,1)S(1)} %add_convert_fusion.mine), channel_id=1, source_target_pairs={{0,2},{2,0},{4,6},{6,4},{8,10},{10,8},{12,14},{14,12},{1,3},{3,1},... | collective-permute-start | bytes 294920 | tf_op jit(solution)/shard_map/ppermute | solution.py:266
  45.7 0.8 %shard_map.82 = f32[128,1024]{1,0:T(8,128)} custom-call(f32[128,1024]{1,0:T(8,128)S(1)} %get-tuple-element.52.source), custom_call_target="tpu_custom_call" | custom-call | tf_op jit(solution)/shard_map/pallas_call | solution.py:385
  46.5 2.4 %collective-permute-done.13.other = bf16[384,128]{1,0:T(8,128)(2,1)S(1)} collective-permute-done((bf16[384,128]{1,0:T(8,128)(2,1)S(1)}, bf16[384,128]{1,0:T(8,128)(2,1)S(1)}, u32[]{:S(2)}, u32[]{:S(2)}) %collective-permute-start.13) | collective-permute-done | bytes 98336 | tf_op jit(solution)/shard_map/ppermute | solution.py:266
  49.3 1.0 %collective-permute-done.20.refs_2_ = bf16[32,2048]{1,0:T(8,128)(2,1)S(1)} collective-permute-done((bf16[32,2048]{1,0:T(8,128)(2,1)S(1)}, bf16[32,2048]{1,0:T(8,128)(2,1)S(1)}, u32[]{:S(2)}, u32[]{:S(2)}) %collective-permute-start.20) | collective-permute-done | bytes 131104 | tf_op jit(solution)/shard_map/ppermute | solution.py:266
  50.3 0.9 %shard_map.87 = f32[32,2048]{1,0:T(8,128)} custom-call(f32[8,128]{1,0:T(8,128)S(1)} %get-tuple-element.56.rate, f32[32,2048]{1,0:T(8,128)S(1)} %get-tuple-element.57.base, f32[32,2048]{1,0:T(8,128)S(1)} %get-tuple-element.58.own, bf16[32,2048]{1,0:T(8,128)(2,1)S(1)} %collective-permute-done.14.refs_0_, bf16[32,2048]{1,0:T(8,128)(2,1)S(1)} %collective-permute-done.16.refs_1_, ...), custom_call_target="tpu_custom_call" | custom-call | bytes 16777216 | tf_op jit(solution)/shard_map/pallas_call | solution.py:396
  (28 shorter events, 1.9 us)
Async XLA Ops:
  0.6 13.2 %collective-permute-start.3 = (f32[128,1024]{1,0:T(8,128)}, f32[128,1024]{1,0:T(8,128)S(1)}, u32[]{:S(2)}, u32[]{:S(2)}) collective-permute-start(f32[128,1024]{1,0:T(8,128)} %factor_mine.1), channel_id=1, source_target_pairs={{0,1},{1,0},{2,3},{3,2},{4,5},{5,4},{6,7},{7,6},{8,9},{9,8},{10,11... | collective-permute-start | bytes 1572872 | tf_op jit(solution)/shard_map/ppermute | solution.py:269
  2.1 11.7 %collective-permute-start.2 = (bf16[32,2048]{1,0:T(8,128)(2,1)S(1)}, bf16[32,2048]{1,0:T(8,128)(2,1)S(1)}, u32[]{:S(2)}, u32[]{:S(2)}) collective-permute-start(bf16[32,2048]{1,0:T(8,128)(2,1)S(1)} %convert_element_type.21.refs_0_), channel_id=1, source_target_pairs={{0,8},{2,10},{4,12},{6,14},{8,0},{10,2},{12,4},{14,6},{1,9},{3,11}... | collective-permute-start | bytes 393224 | tf_op jit(solution)/shard_map/ppermute | solution.py:266
  5.8 8.1 %collective-permute-start.1 = (bf16[32,2048]{1,0:T(8,128)(2,1)S(1)}, bf16[32,2048]{1,0:T(8,128)(2,1)S(1)}, u32[]{:S(2)}, u32[]{:S(2)}) collective-permute-start(bf16[32,2048]{1,0:T(8,128)(2,1)S(1)} %convert_element_type.21.refs_0_), channel_id=1, source_target_pairs={{0,4},{2,6},{4,0},{6,2},{8,12},{10,14},{12,8},{14,10},{1,5},{3,7},... | collective-permute-start | bytes 393224 | tf_op jit(solution)/shard_map/ppermute | solution.py:266
  7.4 6.5 %collective-permute-start = (bf16[32,2048]{1,0:T(8,128)(2,1)S(1)}, bf16[32,2048]{1,0:T(8,128)(2,1)S(1)}, u32[]{:S(2)}, u32[]{:S(2)}) collective-permute-start(bf16[32,2048]{1,0:T(8,128)(2,1)S(1)} %convert_element_type.21.refs_0_), channel_id=1, source_target_pairs={{0,2},{2,0},{4,6},{6,4},{8,10},{10,8},{12,14},{14,12},{1,3},{3,1},... | collective-permute-start | bytes 393224 | tf_op jit(solution)/shard_map/ppermute | solution.py:266
  8.9 8.0 %collective-permute-start.6 = (bf16[32,2048]{1,0:T(8,128)(2,1)S(1)}, bf16[32,2048]{1,0:T(8,128)(2,1)S(1)}, u32[]{:S(2)}, u32[]{:S(2)}) collective-permute-start(bf16[32,2048]{1,0:T(8,128)(2,1)S(1)} %convert_element_type.21.refs_0_), channel_id=1, source_target_pairs={{0,12},{2,14},{4,8},{6,10},{8,4},{10,6},{12,0},{14,2},{1,13},{3,15... | collective-permute-start | bytes 393224 | tf_op jit(solution)/shard_map/ppermute | solution.py:266
  13.9 11.7 %copy-start.1 = (f32[128,1024]{1,0:T(8,128)S(1)}, f32[128,1024]{1,0:T(8,128)}, u32[]{:S(2)}) copy-start(f32[128,1024]{1,0:T(8,128)} %factor_mine.1) | copy-start | bytes 1572868
  13.9 5.7 %collective-permute-start.4 = (bf16[32,2048]{1,0:T(8,128)(2,1)S(1)}, bf16[32,2048]{1,0:T(8,128)(2,1)S(1)}, u32[]{:S(2)}, u32[]{:S(2)}) collective-permute-start(bf16[32,2048]{1,0:T(8,128)(2,1)S(1)} %collective-permute-done.refs_1_), channel_id=1, source_target_pairs={{0,4},{2,6},{4,0},{6,2},{8,12},{10,14},{12,8},{14,10},{1,5},{3,7},... | collective-permute-start | bytes 393224 | tf_op jit(solution)/shard_map/ppermute | solution.py:266
  15.0 6.0 %collective-permute-start.5 = (bf16[32,2048]{1,0:T(8,128)(2,1)S(1)}, bf16[32,2048]{1,0:T(8,128)(2,1)S(1)}, u32[]{:S(2)}, u32[]{:S(2)}) collective-permute-start(bf16[32,2048]{1,0:T(8,128)(2,1)S(1)} %collective-permute-done.2.refs_4_), channel_id=1, source_target_pairs={{0,2},{2,0},{4,6},{6,4},{8,10},{10,8},{12,14},{14,12},{1,3},{3,1},... | collective-permute-start | bytes 393224 | tf_op jit(solution)/shard_map/ppermute | solution.py:266
  16.9 5.9 %collective-permute-start.7 = (bf16[32,2048]{1,0:T(8,128)(2,1)S(1)}, bf16[32,2048]{1,0:T(8,128)(2,1)S(1)}, u32[]{:S(2)}, u32[]{:S(2)}) collective-permute-start(bf16[32,2048]{1,0:T(8,128)(2,1)S(1)} %collective-permute-done.6.refs_6_), channel_id=1, source_target_pairs={{0,2},{2,0},{4,6},{6,4},{8,10},{10,8},{12,14},{14,12},{1,3},{3,1},... | collective-permute-start | bytes 393224 | tf_op jit(solution)/shard_map/ppermute | solution.py:266
  22.2 3.4 %collective-permute-start.9 = (bf16[112,1024]{1,0:T(8,128)(2,1)S(1)}, bf16[112,1024]{1,0:T(8,128)(2,1)S(1)}, u32[]{:S(2)}, u32[]{:S(2)}) collective-permute-start(bf16[112,1024]{1,0:T(8,128)(2,1)S(1)} %get-tuple-element.46), channel_id=1, source_target_pairs={{0,1},{1,0},{2,3},{3,2},{4,5},{5,4},{6,7},{7,6},{8,9},{9,8},{10,11... | collective-permute-start | bytes 688136 | tf_op jit(solution)/shard_map/ppermute | solution.py:269
  22.2 3.3 %collective-permute-start.10 = (bf16[112,1024]{1,0:T(8,128)(2,1)S(1)}, bf16[112,1024]{1,0:T(8,128)(2,1)S(1)}, u32[]{:S(2)}, u32[]{:S(2)}) collective-permute-start(bf16[112,1024]{1,0:T(8,128)(2,1)S(1)} %get-tuple-element.47), channel_id=1, source_target_pairs={{0,1},{1,0},{2,3},{3,2},{4,5},{5,4},{6,7},{7,6},{8,9},{9,8},{10,11... | collective-permute-start | bytes 688136 | tf_op jit(solution)/shard_map/ppermute | solution.py:269
  24.0 1.5 %collective-permute-start.8 = (bf16[96,1024]{1,0:T(8,128)(2,1)S(1)}, bf16[96,1024]{1,0:T(8,128)(2,1)S(1)}, u32[]{:S(2)}, u32[]{:S(2)}) collective-permute-start(bf16[96,1024]{1,0:T(8,128)(2,1)S(1)} %get-tuple-element.44), channel_id=1, source_target_pairs={{0,1},{1,0},{2,3},{3,2},{4,5},{5,4},{6,7},{7,6},{8,9},{9,8},{10,11... | collective-permute-start | bytes 589832 | tf_op jit(solution)/shard_map/ppermute | solution.py:269
  27.6 21.3 %copy-start = (f32[32,2048]{1,0:T(8,128)S(1)}, f32[32,2048]{1,0:T(8,128)}, u32[]{:S(2)}) copy-start(f32[32,2048]{1,0:T(8,128)} %factor.1) | copy-start | bytes 786436
  27.6 8.5 %collective-permute-start.18 = (bf16[32,2048]{1,0:T(8,128)(2,1)S(1)}, bf16[32,2048]{1,0:T(8,128)(2,1)S(1)}, u32[]{:S(2)}, u32[]{:S(2)}) collective-permute-start(bf16[32,2048]{1,0:T(8,128)(2,1)S(1)} %get-tuple-element.65), channel_id=1, source_target_pairs={{0,2},{2,0},{4,6},{6,4},{8,10},{10,8},{12,14},{14,12},{1,3},{3,1},... | collective-permute-start | bytes 393224 | tf_op jit(solution)/shard_map/ppermute | solution.py:266
  29.1 8.6 %collective-permute-start.11 = (bf16[384,128]{1,0:T(8,128)(2,1)S(1)}, bf16[384,128]{1,0:T(8,128)(2,1)S(1)}, u32[]{:S(2)}, u32[]{:S(2)}) collective-permute-start(bf16[384,128]{1,0:T(8,128)(2,1)S(1)} %get-tuple-element.50), channel_id=1, source_target_pairs={{0,8},{2,10},{4,12},{6,14},{8,0},{10,2},{12,4},{14,6},{1,9},{3,11}... | collective-permute-start | bytes 294920 | tf_op jit(solution)/shard_map/ppermute | solution.py:266
  34.0 6.5 %collective-permute-start.15 = (bf16[32,2048]{1,0:T(8,128)(2,1)S(1)}, bf16[32,2048]{1,0:T(8,128)(2,1)S(1)}, u32[]{:S(2)}, u32[]{:S(2)}) collective-permute-start(bf16[32,2048]{1,0:T(8,128)(2,1)S(1)} %get-tuple-element.61), channel_id=1, source_target_pairs={{0,2},{2,0},{4,6},{6,4},{8,10},{10,8},{12,14},{14,12},{1,3},{3,1},... | collective-permute-start | bytes 393224 | tf_op jit(solution)/shard_map/ppermute | solution.py:266
  34.6 8.7 %collective-permute-start.17 = (bf16[32,2048]{1,0:T(8,128)(2,1)S(1)}, bf16[32,2048]{1,0:T(8,128)(2,1)S(1)}, u32[]{:S(2)}, u32[]{:S(2)}) collective-permute-start(bf16[32,2048]{1,0:T(8,128)(2,1)S(1)} %get-tuple-element.63), channel_id=1, source_target_pairs={{0,2},{2,0},{4,6},{6,4},{8,10},{10,8},{12,14},{14,12},{1,3},{3,1},... | collective-permute-start | bytes 393224 | tf_op jit(solution)/shard_map/ppermute | solution.py:266
  36.1 7.1 %collective-permute-start.19 = (bf16[32,2048]{1,0:T(8,128)(2,1)S(1)}, bf16[32,2048]{1,0:T(8,128)(2,1)S(1)}, u32[]{:S(2)}, u32[]{:S(2)}) collective-permute-start(bf16[32,2048]{1,0:T(8,128)(2,1)S(1)} %shard_map.85), channel_id=1, source_target_pairs={{0,4},{2,6},{4,0},{6,2},{8,12},{10,14},{12,8},{14,10},{1,5},{3,7},... | collective-permute-start | bytes 393224 | tf_op jit(solution)/shard_map/ppermute | solution.py:266
  37.8 6.4 %collective-permute-start.12 = (bf16[384,128]{1,0:T(8,128)(2,1)S(1)}, bf16[384,128]{1,0:T(8,128)(2,1)S(1)}, u32[]{:S(2)}, u32[]{:S(2)}) collective-permute-start(bf16[384,128]{1,0:T(8,128)(2,1)S(1)} %add_convert_fusion.1), channel_id=1, source_target_pairs={{0,4},{2,6},{4,0},{6,2},{8,12},{10,14},{12,8},{14,10},{1,5},{3,7},... | collective-permute-start | bytes 294920 | tf_op jit(solution)/shard_map/ppermute | solution.py:266
  38.3 11.0 %collective-permute-start.14 = (bf16[32,2048]{1,0:T(8,128)(2,1)S(1)}, bf16[32,2048]{1,0:T(8,128)(2,1)S(1)}, u32[]{:S(2)}, u32[]{:S(2)}) collective-permute-start(bf16[32,2048]{1,0:T(8,128)(2,1)S(1)} %get-tuple-element.59), channel_id=1, source_target_pairs={{0,2},{2,0},{4,6},{6,4},{8,10},{10,8},{12,14},{14,12},{1,3},{3,1},... | collective-permute-start | bytes 393224 | tf_op jit(solution)/shard_map/ppermute | solution.py:266
  40.5 8.8 %collective-permute-start.16 = (bf16[32,2048]{1,0:T(8,128)(2,1)S(1)}, bf16[32,2048]{1,0:T(8,128)(2,1)S(1)}, u32[]{:S(2)}, u32[]{:S(2)}) collective-permute-start(bf16[32,2048]{1,0:T(8,128)(2,1)S(1)} %shard_map.84), channel_id=1, source_target_pairs={{0,4},{2,6},{4,0},{6,2},{8,12},{10,14},{12,8},{14,10},{1,5},{3,7},... | collective-permute-start | bytes 393224 | tf_op jit(solution)/shard_map/ppermute | solution.py:266
  43.3 7.0 %collective-permute-start.20 = (bf16[32,2048]{1,0:T(8,128)(2,1)S(1)}, bf16[32,2048]{1,0:T(8,128)(2,1)S(1)}, u32[]{:S(2)}, u32[]{:S(2)}) collective-permute-start(bf16[32,2048]{1,0:T(8,128)(2,1)S(1)} %shard_map.86), channel_id=1, source_target_pairs={{0,8},{2,10},{4,12},{6,14},{8,0},{10,2},{12,4},{14,6},{1,9},{3,11}... | collective-permute-start | bytes 393224 | tf_op jit(solution)/shard_map/ppermute | solution.py:266
  44.2 4.7 %collective-permute-start.13 = (bf16[384,128]{1,0:T(8,128)(2,1)S(1)}, bf16[384,128]{1,0:T(8,128)(2,1)S(1)}, u32[]{:S(2)}, u32[]{:S(2)}) collective-permute-start(bf16[384,128]{1,0:T(8,128)(2,1)S(1)} %add_convert_fusion.mine), channel_id=1, source_target_pairs={{0,2},{2,0},{4,6},{6,4},{8,10},{10,8},{12,14},{14,12},{1,3},{3,1},... | collective-permute-start | bytes 294920 | tf_op jit(solution)/shard_map/ppermute | solution.py:266

commit v12 on v11

--- a/solution.py
+++ b/solution.py
@@ -199,11 +199,18 @@
 
 def gram_blocks(low, out):
     half = low.shape[0] // 2
-    panel = low[...]
-    gram = dot(panel, panel, NT)
-    out[:half] = gram[:half, :half].astype(out.dtype)
-    out[half : 2 * half] = gram[:half, half:].astype(out.dtype)
-    out[2 * half :] = gram[half:, half:].astype(out.dtype)
+
+    @pl.when(lax.axis_index("gene") == 1)
+    def _():
+        panel = low[...]
+        gram = dot(panel, panel, NT)
+        out[:half] = gram[:half, :half].astype(out.dtype)
+        out[half : 2 * half] = gram[:half, half:].astype(out.dtype)
+        out[2 * half :] = gram[half:, half:].astype(out.dtype)
+
+    @pl.when(lax.axis_index("gene") == 0)
+    def _():
+        out[...] = jnp.zeros_like(out)
 
 
 def picked_product(picks, low, tile, chosen):
@@ -230,9 +237,11 @@
     refs[-1][...] = coded(total)
 
 
-def base_body(mine, other, panel, factor, base, rate_out, gram):
+def base_body(mine, other_1, other_0, given, panel, factor, base, rate_out, gram):
     half = mine.shape[0] // 3
-    quarters = mine[...].astype(jnp.float32) + other[...].astype(jnp.float32)
+    first = jnp.where(lax.axis_index("gene") == 1, mine[...].astype(jnp.float32), given[...].astype(jnp.float32))
+    last = jnp.where(lax.axis_index("gene") == 1, other_1[...].astype(jnp.float32), other_0[...].astype(jnp.float32))
+    quarters = first + last
     upper, side, lower = quarters[:half], quarters[half : 2 * half], quarters[2 * half :]
     gram[:half, :half] = upper
     gram[:half, half:] = side
@@ -264,6 +273,11 @@
 
     def swap(value, bits):
         return lax.ppermute(value, "cell", [(n, n ^ bits) for n in range(n_cell)])
+
+    def from_core_1(value, bits, core):
+        n_gene = lax.axis_size("gene")
+        pairs = [(n * n_gene + 1, (n ^ bits) * n_gene + core) for n in range(n_cell)]
+        return lax.ppermute(value, ("cell", "gene"), pairs)
 
     def swap_core(value):
         return lax.ppermute(value, "gene", [(0, 1), (1, 0)])
@@ -373,26 +387,27 @@
         return body(keep, *parts)
 
     through = swap(add_up(AHEAD, keep_third, arrived[0]), 2)
-    gram_arrived = swap(gram, 4)
+    gram_arrived = from_core_1(gram, 4, 1)
     beside = swap(add_up(AHEAD, keep_near, arrived[2]), 2)
     across = add_up(AHEAD, keep_second, arrived[1], through)
     gram = (gram.astype(jnp.float32) + gram_arrived.astype(jnp.float32)).astype(jnp.bfloat16)
-    gram_arrived = swap(gram, 2)
+    gram_arrived = from_core_1(gram, 2, 1)
     across = swap(across, 4)
     gram = (gram.astype(jnp.float32) + gram_arrived.astype(jnp.float32)).astype(jnp.bfloat16)
-    partner = swap(gram, 1)
+    partner = (from_core_1(gram, 1, 1), from_core_1(gram, 1, 0), from_core_1(gram, 0, 0))
     gram, updated = lax.optimization_barrier((gram, updated))
     cell_next = call(copy_body, shape(cell_factor.shape, jnp.float32), 0, 1, 0, 0)(updated)
     own, cell_next = lax.optimization_barrier((own, cell_next))
+    *partner, beside = lax.optimization_barrier((*partner, beside))
     base, rate = call(
         base_body,
         (wide(size, jnp.float32), shape((8, 128), jnp.float32)),
         0,
-        4,
+        6,
         0,
         0,
         [pltpu.VMEM((kdim, kdim), jnp.float32)],
-    )(gram, partner, panel, gene_factor)
+    )(gram, *partner, panel, gene_factor)
     gene_next = call(last_body, wide(size, jnp.float32), 0, 6, 0, AHEAD)(
         rate, base, own, arrived[3], beside, across
     )

time: 51.4 us -> 53.6 us (1.043)
  the two profiles are of different devices: /device:TPU:0 before, /device:TPU:1 now
where the time goes in v12:
time: 53.6 us; the launch traced here: 53.3 us
  starting transfers between devices  32.7 us (61%)
  Pallas kernels  11.6 us (22%)
  waiting for transfers between devices  6.45 us (12%)
  between operations  1.48 us (3%)
  other arithmetic  1.02 us (2%)
    ppermute x5, starting transfers between devices, from_core_1(): return lax.ppermute(value, ('cell', 'gene'), pairs)  14.7 us
    ppermute x14, starting transfers between devices, swap(): return lax.ppermute(value, 'cell', [(n, n ^ bits) for n in range(n_cell)])  14.6 us
    pallas_call x1, Pallas kernels, dense_tile(): pl.pallas_call(dense_body, out_shape=(shape((CELL_DEV, GENE_DEV), jnp.bfl...  3.9 us
    ppermute x14, waiting for transfers between devices, swap(): return lax.ppermute(value, 'cell', [(n, n ^ bits) for n in range(n_cell)])  3.65 us
    ppermute x4, starting transfers between devices, swap_core(): return lax.ppermute(value, 'gene', [(0, 1), (1, 0)])  3.46 us
    pallas_call x1, Pallas kernels, shards(): call(functools.partial(cell_body, order, [7], n_parts), (shape(cell_facto...  1.92 us
    ppermute x5, waiting for transfers between devices, from_core_1(): return lax.ppermute(value, ('cell', 'gene'), pairs)  1.72 us
    pallas_call x1, Pallas kernels, shards(): call(functools.partial(second_body, order), (wide(kdim, jnp.bfloat16), sh...  1.21 us
  transfers between devices with their start and end apart: 23, of which 6 were waited for; matrix products, arithmetic and copies ran while one was open for 2% of the time, Pallas kernels for 16%

profile of v12, /device:TPU:1, one launch (start us, length us, event | category | flops | bytes accessed | tf_op | source)
XLA Modules:
  0.0 53.3 jit_solution(10458200677808226088)
XLA Ops:
  0.8 1.0 %convert_element_type.21.refs_0_ = bf16[32,2048]{1,0:T(8,128)(2,1)S(1)} convert(f32[32,2048]{1,0:T(8,128)} %factor.1) | non-fusion elementwise | flops 65536 | bytes 393216 | tf_op jit(solution)/shard_map/convert_element_type | solution.py:288
  1.7 3.8 %collective-permute-start.2 = (bf16[32,2048]{1,0:T(8,128)(2,1)S(1)}, bf16[32,2048]{1,0:T(8,128)(2,1)S(1)}, u32[]{:S(2)}, u32[]{:S(2)}) collective-permute-start(bf16[32,2048]{1,0:T(8,128)(2,1)S(1)} %convert_element_type.21.refs_0_), channel_id=1, source_target_pairs={{0,8},{2,10},{4,12},{6,14},{8,0},{10,2},{12,4},{14,6},{1,9},{3,11}... | collective-permute-start | bytes 393224 | tf_op jit(solution)/shard_map/ppermute | solution.py:275
  5.5 1.3 %collective-permute-start.1 = (bf16[32,2048]{1,0:T(8,128)(2,1)S(1)}, bf16[32,2048]{1,0:T(8,128)(2,1)S(1)}, u32[]{:S(2)}, u32[]{:S(2)}) collective-permute-start(bf16[32,2048]{1,0:T(8,128)(2,1)S(1)} %convert_element_type.21.refs_0_), channel_id=1, source_target_pairs={{0,4},{2,6},{4,0},{6,2},{8,12},{10,14},{12,8},{14,10},{1,5},{3,7},... | collective-permute-start | bytes 393224 | tf_op jit(solution)/shard_map/ppermute | solution.py:275
  6.8 1.2 %collective-permute-start = (bf16[32,2048]{1,0:T(8,128)(2,1)S(1)}, bf16[32,2048]{1,0:T(8,128)(2,1)S(1)}, u32[]{:S(2)}, u32[]{:S(2)}) collective-permute-start(bf16[32,2048]{1,0:T(8,128)(2,1)S(1)} %convert_element_type.21.refs_0_), channel_id=1, source_target_pairs={{0,2},{2,0},{4,6},{6,4},{8,10},{10,8},{12,14},{14,12},{1,3},{3,1},... | collective-permute-start | bytes 393224 | tf_op jit(solution)/shard_map/ppermute | solution.py:275
  8.7 3.9 %shard_map.77 = (bf16[1024,2048]{1,0:T(8,128)(2,1)S(1)}, bf16[2048,1024]{1,0:T(8,128)(2,1)S(1)}) custom-call(s32[64]{0:T(128)} %bitcast.6, s32[64]{0:T(128)} %bitcast.7, s32[1]{0:T(128)} %bitcast.4.count, bf16[64,128,128]{2,1,0:T(8,128)(2,1)} %bitcast.5), custom_call_target="tpu_custom_call" | custom-call | tf_op jit(solution)/shard_map/pallas_call | solution.py:88
  12.7 0.9 %collective-permute-start.4 = (bf16[32,2048]{1,0:T(8,128)(2,1)S(1)}, bf16[32,2048]{1,0:T(8,128)(2,1)S(1)}, u32[]{:S(2)}, u32[]{:S(2)}) collective-permute-start(bf16[32,2048]{1,0:T(8,128)(2,1)S(1)} %collective-permute-done.refs_1_), channel_id=1, source_target_pairs={{0,4},{2,6},{4,0},{6,2},{8,12},{10,14},{12,8},{14,10},{1,5},{3,7},... | collective-permute-start | bytes 393224 | tf_op jit(solution)/shard_map/ppermute | solution.py:275
  13.6 1.2 %collective-permute-start.5 = (bf16[32,2048]{1,0:T(8,128)(2,1)S(1)}, bf16[32,2048]{1,0:T(8,128)(2,1)S(1)}, u32[]{:S(2)}, u32[]{:S(2)}) collective-permute-start(bf16[32,2048]{1,0:T(8,128)(2,1)S(1)} %collective-permute-done.2.refs_4_), channel_id=1, source_target_pairs={{0,2},{2,0},{4,6},{6,4},{8,10},{10,8},{12,14},{14,12},{1,3},{3,1},... | collective-permute-start | bytes 393224 | tf_op jit(solution)/shard_map/ppermute | solution.py:275
  14.8 1.2 %collective-permute-done.6.refs_6_ = bf16[32,2048]{1,0:T(8,128)(2,1)S(1)} collective-permute-done((bf16[32,2048]{1,0:T(8,128)(2,1)S(1)}, bf16[32,2048]{1,0:T(8,128)(2,1)S(1)}, u32[]{:S(2)}, u32[]{:S(2)}) %collective-permute-start.6) | collective-permute-done | bytes 131104 | tf_op jit(solution)/shard_map/ppermute | solution.py:275
  16.0 1.2 %collective-permute-start.7 = (bf16[32,2048]{1,0:T(8,128)(2,1)S(1)}, bf16[32,2048]{1,0:T(8,128)(2,1)S(1)}, u32[]{:S(2)}, u32[]{:S(2)}) collective-permute-start(bf16[32,2048]{1,0:T(8,128)(2,1)S(1)} %collective-permute-done.6.refs_6_), channel_id=1, source_target_pairs={{0,2},{2,0},{4,6},{6,4},{8,10},{10,8},{12,14},{14,12},{1,3},{3,1},... | collective-permute-start | bytes 393224 | tf_op jit(solution)/shard_map/ppermute | solution.py:275
  17.2 1.2 %collective-permute-done.4.refs_3_ = bf16[32,2048]{1,0:T(8,128)(2,1)S(1)} collective-permute-done((bf16[32,2048]{1,0:T(8,128)(2,1)S(1)}, bf16[32,2048]{1,0:T(8,128)(2,1)S(1)}, u32[]{:S(2)}, u32[]{:S(2)}) %collective-permute-start.4) | collective-permute-done | bytes 131104 | tf_op jit(solution)/shard_map/ppermute | solution.py:275
  18.4 1.1 %shard_map.78 = (bf16[224,2048]{1,0:T(8,128)(2,1)S(1)}, f32[224,1024]{1,0:T(8,128)S(1)}, bf16[112,1024]{1,0:T(8,128)(2,1)S(1)}, bf16[112,1024]{1,0:T(8,128)(2,1)S(1)}) custom-call(bf16[2048,1024]{1,0:T(8,128)(2,1)S(1)} %get-tuple-element.41.turned, bf16[32,2048]{1,0:T(8,128)(2,1)S(1)} %convert_element_type.21.refs_0_, ...), custom_call_target="tpu_custom_call" | custom-call | bytes 16777216 | tf_op jit(solution)/shard_map/pallas_call | solution.py:309
  19.6 2.7 %collective-permute-start.9 = (bf16[112,1024]{1,0:T(8,128)(2,1)S(1)}, bf16[112,1024]{1,0:T(8,128)(2,1)S(1)}, u32[]{:S(2)}, u32[]{:S(2)}) collective-permute-start(bf16[112,1024]{1,0:T(8,128)(2,1)S(1)} %get-tuple-element.50), channel_id=1, source_target_pairs={{0,1},{1,0},{2,3},{3,2},{4,5},{5,4},{6,7},{7,6},{8,9},{9,8},{10,11... | collective-permute-start | bytes 688136 | tf_op jit(solution)/shard_map/ppermute | solution.py:283
  22.4 1.2 %shard_map.79 = (bf16[256,2048]{1,0:T(8,128)(2,1)S(1)}, f32[96,1024]{1,0:T(8,128)S(1)}, bf16[96,1024]{1,0:T(8,128)(2,1)S(1)}) custom-call(bf16[2048,1024]{1,0:T(8,128)(2,1)S(1)} %get-tuple-element.41.turned, bf16[224,2048]{1,0:T(8,128)(2,1)S(1)} %get-tuple-element.46.first, bf16[32,2048]{1,0:T(8,128)(2,1)S(1)} %collective-permute-done.7.share), custom_call_target="tpu_custom_call" | custom-call | tf_op jit(solution)/shard_map/pallas_call | solution.py:323
  23.6 0.5 %collective-permute-start.8 = (bf16[96,1024]{1,0:T(8,128)(2,1)S(1)}, bf16[96,1024]{1,0:T(8,128)(2,1)S(1)}, u32[]{:S(2)}, u32[]{:S(2)}) collective-permute-start(bf16[96,1024]{1,0:T(8,128)(2,1)S(1)} %get-tuple-element.48), channel_id=1, source_target_pairs={{0,1},{1,0},{2,3},{3,2},{4,5},{5,4},{6,7},{7,6},{8,9},{9,8},{10,11... | collective-permute-start | bytes 589832 | tf_op jit(solution)/shard_map/ppermute | solution.py:283
  24.1 1.1 %collective-permute-done.8.other = bf16[96,1024]{1,0:T(8,128)(2,1)S(1)} collective-permute-done((bf16[96,1024]{1,0:T(8,128)(2,1)S(1)}, bf16[96,1024]{1,0:T(8,128)(2,1)S(1)}, u32[]{:S(2)}, u32[]{:S(2)}) %collective-permute-start.8) | collective-permute-done | bytes 196640 | tf_op jit(solution)/shard_map/ppermute | solution.py:283
  25.2 1.9 %shard_map.80 = (f32[128,1024]{1,0:T(8,128)S(1)}, bf16[256,1024]{1,0:T(8,128)(2,1)S(1)}, bf16[32,2048]{1,0:T(8,128)(2,1)S(1)}, bf16[384,128]{1,0:T(8,128)(2,1)S(1)}) custom-call(bf16[1024,2048]{1,0:T(8,128)(2,1)S(1)} %get-tuple-element.40.tile, f32[224,1024]{1,0:T(8,128)S(1)} %get-tuple-element.45.mine_first, f32[96,1024]{1,0:T(8,128)S(1)} %get-tuple-element.47.mine, ...), custom_call_target="tpu_custom_call" | custom-call | tf_op jit(solution)/shard_map/pallas_call | solution.py:339
  27.1 1.3 %collective-permute-start.20 = (bf16[32,2048]{1,0:T(8,128)(2,1)S(1)}, bf16[32,2048]{1,0:T(8,128)(2,1)S(1)}, u32[]{:S(2)}, u32[]{:S(2)}) collective-permute-start(bf16[32,2048]{1,0:T(8,128)(2,1)S(1)} %get-tuple-element.73), channel_id=1, source_target_pairs={{0,2},{2,0},{4,6},{6,4},{8,10},{10,8},{12,14},{14,12},{1,3},{3,1},... | collective-permute-start | bytes 393224 | tf_op jit(solution)/shard_map/ppermute | solution.py:275
  28.4 5.3 %collective-permute-start.11 = (bf16[384,128]{1,0:T(8,128)(2,1)S(1)}, bf16[384,128]{1,0:T(8,128)(2,1)S(1)}, u32[]{:S(2)}, u32[]{:S(2)}) collective-permute-start(bf16[384,128]{1,0:T(8,128)(2,1)S(1)} %get-tuple-element.54), channel_id=1, source_target_pairs={{1,9},{3,11},{5,13},{7,15},{9,1},{11,3},{13,5},{15,7},{17,25},{19,... | collective-permute-start | bytes 294920 | tf_op jit(solution)/shard_map/ppermute | solution.py:280
  33.7 1.1 %shard_map.81 = (bf16[32,2048]{1,0:T(8,128)(2,1)S(1)}, bf16[32,2048]{1,0:T(8,128)(2,1)S(1)}, bf16[32,2048]{1,0:T(8,128)(2,1)S(1)}, f32[32,2048]{1,0:T(8,128)S(1)...) custom-call(bf16[256,1024]{1,0:T(8,128)(2,1)S(1)} %get-tuple-element.52.low, ...), custom_call_target="tpu_custom_call" | custom-call | bytes 16777216 | tf_op jit(solution)/shard_map/pallas_call | solution.py:370
  34.9 0.3 collective-permute-start.16
  35.2 1.2 %collective-permute-start.19 = (bf16[32,2048]{1,0:T(8,128)(2,1)S(1)}, bf16[32,2048]{1,0:T(8,128)(2,1)S(1)}, u32[]{:S(2)}, u32[]{:S(2)}) collective-permute-start(bf16[32,2048]{1,0:T(8,128)(2,1)S(1)} %get-tuple-element.71), channel_id=1, source_target_pairs={{0,2},{2,0},{4,6},{6,4},{8,10},{10,8},{12,14},{14,12},{1,3},{3,1},... | collective-permute-start | bytes 393224 | tf_op jit(solution)/shard_map/ppermute | solution.py:275
  36.9 3.1 %collective-permute-start.12 = (bf16[384,128]{1,0:T(8,128)(2,1)S(1)}, bf16[384,128]{1,0:T(8,128)(2,1)S(1)}, u32[]{:S(2)}, u32[]{:S(2)}) collective-permute-start(bf16[384,128]{1,0:T(8,128)(2,1)S(1)} %add_convert_fusion.1), channel_id=1, source_target_pairs={{1,5},{3,7},{5,1},{7,3},{9,13},{11,15},{13,9},{15,11},{17,21},{19,... | collective-permute-start | bytes 294920 | tf_op jit(solution)/shard_map/ppermute | solution.py:280
  40.0 0.3 collective-permute-start.18
  40.7 1.2 %collective-permute-done.19.refs_0_ = bf16[32,2048]{1,0:T(8,128)(2,1)S(1)} collective-permute-done((bf16[32,2048]{1,0:T(8,128)(2,1)S(1)}, bf16[32,2048]{1,0:T(8,128)(2,1)S(1)}, u32[]{:S(2)}, u32[]{:S(2)}) %collective-permute-start.19) | collective-permute-done | bytes 131104 | tf_op jit(solution)/shard_map/ppermute | solution.py:275
  42.0 1.4 %collective-permute-start.22 = (bf16[32,2048]{1,0:T(8,128)(2,1)S(1)}, bf16[32,2048]{1,0:T(8,128)(2,1)S(1)}, u32[]{:S(2)}, u32[]{:S(2)}) collective-permute-start(bf16[32,2048]{1,0:T(8,128)(2,1)S(1)} %shard_map.86), channel_id=1, source_target_pairs={{0,8},{2,10},{4,12},{6,14},{8,0},{10,2},{12,4},{14,6},{1,9},{3,11}... | collective-permute-start | bytes 393224 | tf_op jit(solution)/shard_map/ppermute | solution.py:275
  43.4 1.8 %collective-permute-start.15 = (bf16[384,128]{1,0:T(8,128)(2,1)S(1)}, bf16[384,128]{1,0:T(8,128)(2,1)S(1)}, u32[]{:S(2)}, u32[]{:S(2)}) collective-permute-start(bf16[384,128]{1,0:T(8,128)(2,1)S(1)} %add_convert_fusion.mine), channel_id=1, source_target_pairs={{1,0},{3,2},{5,4},{7,6},{9,8},{11,10},{13,12},{15,14},{17,16},{19,... | collective-permute-start | bytes 294920 | tf_op jit(solution)/shard_map/ppermute | solution.py:280
  45.2 1.4 %collective-permute-start.14 = (bf16[384,128]{1,0:T(8,128)(2,1)S(1)}, bf16[384,128]{1,0:T(8,128)(2,1)S(1)}, u32[]{:S(2)}, u32[]{:S(2)}) collective-permute-start(bf16[384,128]{1,0:T(8,128)(2,1)S(1)} %add_convert_fusion.mine), channel_id=1, source_target_pairs={{1,2},{3,0},{5,6},{7,4},{9,10},{11,8},{13,14},{15,12},{17,18},{19,... | collective-permute-start | bytes 294920 | tf_op jit(solution)/shard_map/ppermute | solution.py:280
  46.6 3.1 %collective-permute-start.13 = (bf16[384,128]{1,0:T(8,128)(2,1)S(1)}, bf16[384,128]{1,0:T(8,128)(2,1)S(1)}, u32[]{:S(2)}, u32[]{:S(2)}) collective-permute-start(bf16[384,128]{1,0:T(8,128)(2,1)S(1)} %add_convert_fusion.mine), channel_id=1, source_target_pairs={{1,3},{3,1},{5,7},{7,5},{9,11},{11,9},{13,15},{15,13},{17,19},{19,... | collective-permute-start | bytes 294920 | tf_op jit(solution)/shard_map/ppermute | solution.py:280
  49.8 0.8 %shard_map.82 = f32[128,1024]{1,0:T(8,128)} custom-call(f32[128,1024]{1,0:T(8,128)S(1)} %get-tuple-element.56.source), custom_call_target="tpu_custom_call" | custom-call | tf_op jit(solution)/shard_map/pallas_call | solution.py:399
  50.6 1.4 %collective-permute-done.13.other_1 = bf16[384,128]{1,0:T(8,128)(2,1)S(1)} collective-permute-done((bf16[384,128]{1,0:T(8,128)(2,1)S(1)}, bf16[384,128]{1,0:T(8,128)(2,1)S(1)}, u32[]{:S(2)}, u32[]{:S(2)}) %collective-permute-start.13) | collective-permute-done | bytes 98336 | tf_op jit(solution)/shard_map/ppermute | solution.py:280
  52.0 0.4 shard_map.84
  52.4 0.9 %shard_map.87 = f32[32,2048]{1,0:T(8,128)} custom-call(f32[8,128]{1,0:T(8,128)S(1)} %get-tuple-element.65.rate, f32[32,2048]{1,0:T(8,128)S(1)} %get-tuple-element.66.base, f32[32,2048]{1,0:T(8,128)S(1)} %get-tuple-element.67.own, bf16[32,2048]{1,0:T(8,128)(2,1)S(1)} %collective-permute-done.18.refs_0_, bf16[32,2048]{1,0:T(8,128)(2,1)S(1)} %collective-permute-done.17.refs_1_, ...), custom_call_target="tpu_custom_call" | custom-call | bytes 16777216 | tf_op jit(solution)/shard_map/pallas_call | solution.py:411
  (32 shorter events, 1.2 us)
Async XLA Ops:
  0.6 12.0 %collective-permute-start.3 = (f32[128,1024]{1,0:T(8,128)}, f32[128,1024]{1,0:T(8,128)S(1)}, u32[]{:S(2)}, u32[]{:S(2)}) collective-permute-start(f32[128,1024]{1,0:T(8,128)} %factor_mine.1), channel_id=1, source_target_pairs={{0,1},{1,0},{2,3},{3,2},{4,5},{5,4},{6,7},{7,6},{8,9},{9,8},{10,11... | collective-permute-start | bytes 1572872 | tf_op jit(solution)/shard_map/ppermute | solution.py:283
  1.7 10.9 %collective-permute-start.2 = (bf16[32,2048]{1,0:T(8,128)(2,1)S(1)}, bf16[32,2048]{1,0:T(8,128)(2,1)S(1)}, u32[]{:S(2)}, u32[]{:S(2)}) collective-permute-start(bf16[32,2048]{1,0:T(8,128)(2,1)S(1)} %convert_element_type.21.refs_0_), channel_id=1, source_target_pairs={{0,8},{2,10},{4,12},{6,14},{8,0},{10,2},{12,4},{14,6},{1,9},{3,11}... | collective-permute-start | bytes 393224 | tf_op jit(solution)/shard_map/ppermute | solution.py:275
  5.5 7.1 %collective-permute-start.1 = (bf16[32,2048]{1,0:T(8,128)(2,1)S(1)}, bf16[32,2048]{1,0:T(8,128)(2,1)S(1)}, u32[]{:S(2)}, u32[]{:S(2)}) collective-permute-start(bf16[32,2048]{1,0:T(8,128)(2,1)S(1)} %convert_element_type.21.refs_0_), channel_id=1, source_target_pairs={{0,4},{2,6},{4,0},{6,2},{8,12},{10,14},{12,8},{14,10},{1,5},{3,7},... | collective-permute-start | bytes 393224 | tf_op jit(solution)/shard_map/ppermute | solution.py:275
  6.8 5.8 %collective-permute-start = (bf16[32,2048]{1,0:T(8,128)(2,1)S(1)}, bf16[32,2048]{1,0:T(8,128)(2,1)S(1)}, u32[]{:S(2)}, u32[]{:S(2)}) collective-permute-start(bf16[32,2048]{1,0:T(8,128)(2,1)S(1)} %convert_element_type.21.refs_0_), channel_id=1, source_target_pairs={{0,2},{2,0},{4,6},{6,4},{8,10},{10,8},{12,14},{14,12},{1,3},{3,1},... | collective-permute-start | bytes 393224 | tf_op jit(solution)/shard_map/ppermute | solution.py:275
  8.1 7.9 %collective-permute-start.6 = (bf16[32,2048]{1,0:T(8,128)(2,1)S(1)}, bf16[32,2048]{1,0:T(8,128)(2,1)S(1)}, u32[]{:S(2)}, u32[]{:S(2)}) collective-permute-start(bf16[32,2048]{1,0:T(8,128)(2,1)S(1)} %convert_element_type.21.refs_0_), channel_id=1, source_target_pairs={{0,12},{2,14},{4,8},{6,10},{8,4},{10,6},{12,0},{14,2},{1,13},{3,15... | collective-permute-start | bytes 393224 | tf_op jit(solution)/shard_map/ppermute | solution.py:275
  12.7 12.6 %copy-start.1 = (f32[128,1024]{1,0:T(8,128)S(1)}, f32[128,1024]{1,0:T(8,128)}, u32[]{:S(2)}) copy-start(f32[128,1024]{1,0:T(8,128)} %factor_mine.1) | copy-start | bytes 1572868
  12.7 5.8 %collective-permute-start.4 = (bf16[32,2048]{1,0:T(8,128)(2,1)S(1)}, bf16[32,2048]{1,0:T(8,128)(2,1)S(1)}, u32[]{:S(2)}, u32[]{:S(2)}) collective-permute-start(bf16[32,2048]{1,0:T(8,128)(2,1)S(1)} %collective-permute-done.refs_1_), channel_id=1, source_target_pairs={{0,4},{2,6},{4,0},{6,2},{8,12},{10,14},{12,8},{14,10},{1,5},{3,7},... | collective-permute-start | bytes 393224 | tf_op jit(solution)/shard_map/ppermute | solution.py:275
  13.6 4.8 %collective-permute-start.5 = (bf16[32,2048]{1,0:T(8,128)(2,1)S(1)}, bf16[32,2048]{1,0:T(8,128)(2,1)S(1)}, u32[]{:S(2)}, u32[]{:S(2)}) collective-permute-start(bf16[32,2048]{1,0:T(8,128)(2,1)S(1)} %collective-permute-done.2.refs_4_), channel_id=1, source_target_pairs={{0,2},{2,0},{4,6},{6,4},{8,10},{10,8},{12,14},{14,12},{1,3},{3,1},... | collective-permute-start | bytes 393224 | tf_op jit(solution)/shard_map/ppermute | solution.py:275
  16.0 6.4 %collective-permute-start.7 = (bf16[32,2048]{1,0:T(8,128)(2,1)S(1)}, bf16[32,2048]{1,0:T(8,128)(2,1)S(1)}, u32[]{:S(2)}, u32[]{:S(2)}) collective-permute-start(bf16[32,2048]{1,0:T(8,128)(2,1)S(1)} %collective-permute-done.6.refs_6_), channel_id=1, source_target_pairs={{0,2},{2,0},{4,6},{6,4},{8,10},{10,8},{12,14},{14,12},{1,3},{3,1},... | collective-permute-start | bytes 393224 | tf_op jit(solution)/shard_map/ppermute | solution.py:275
  19.6 5.6 %collective-permute-start.9 = (bf16[112,1024]{1,0:T(8,128)(2,1)S(1)}, bf16[112,1024]{1,0:T(8,128)(2,1)S(1)}, u32[]{:S(2)}, u32[]{:S(2)}) collective-permute-start(bf16[112,1024]{1,0:T(8,128)(2,1)S(1)} %get-tuple-element.50), channel_id=1, source_target_pairs={{0,1},{1,0},{2,3},{3,2},{4,5},{5,4},{6,7},{7,6},{8,9},{9,8},{10,11... | collective-permute-start | bytes 688136 | tf_op jit(solution)/shard_map/ppermute | solution.py:283
  22.3 2.9 %collective-permute-start.10 = (bf16[112,1024]{1,0:T(8,128)(2,1)S(1)}, bf16[112,1024]{1,0:T(8,128)(2,1)S(1)}, u32[]{:S(2)}, u32[]{:S(2)}) collective-permute-start(bf16[112,1024]{1,0:T(8,128)(2,1)S(1)} %get-tuple-element.51), channel_id=1, source_target_pairs={{0,1},{1,0},{2,3},{3,2},{4,5},{5,4},{6,7},{7,6},{8,9},{9,8},{10,11... | collective-permute-start | bytes 688136 | tf_op jit(solution)/shard_map/ppermute | solution.py:283
  23.6 1.6 %collective-permute-start.8 = (bf16[96,1024]{1,0:T(8,128)(2,1)S(1)}, bf16[96,1024]{1,0:T(8,128)(2,1)S(1)}, u32[]{:S(2)}, u32[]{:S(2)}) collective-permute-start(bf16[96,1024]{1,0:T(8,128)(2,1)S(1)} %get-tuple-element.48), channel_id=1, source_target_pairs={{0,1},{1,0},{2,3},{3,2},{4,5},{5,4},{6,7},{7,6},{8,9},{9,8},{10,11... | collective-permute-start | bytes 589832 | tf_op jit(solution)/shard_map/ppermute | solution.py:283
  27.1 24.9 %copy-start = (f32[32,2048]{1,0:T(8,128)S(1)}, f32[32,2048]{1,0:T(8,128)}, u32[]{:S(2)}) copy-start(f32[32,2048]{1,0:T(8,128)} %factor.1) | copy-start | bytes 786436
  27.1 9.3 %collective-permute-start.20 = (bf16[32,2048]{1,0:T(8,128)(2,1)S(1)}, bf16[32,2048]{1,0:T(8,128)(2,1)S(1)}, u32[]{:S(2)}, u32[]{:S(2)}) collective-permute-start(bf16[32,2048]{1,0:T(8,128)(2,1)S(1)} %get-tuple-element.73), channel_id=1, source_target_pairs={{0,2},{2,0},{4,6},{6,4},{8,10},{10,8},{12,14},{14,12},{1,3},{3,1},... | collective-permute-start | bytes 393224 | tf_op jit(solution)/shard_map/ppermute | solution.py:275
  28.4 8.4 %collective-permute-start.11 = (bf16[384,128]{1,0:T(8,128)(2,1)S(1)}, bf16[384,128]{1,0:T(8,128)(2,1)S(1)}, u32[]{:S(2)}, u32[]{:S(2)}) collective-permute-start(bf16[384,128]{1,0:T(8,128)(2,1)S(1)} %get-tuple-element.54), channel_id=1, source_target_pairs={{1,9},{3,11},{5,13},{7,15},{9,1},{11,3},{13,5},{15,7},{17,25},{19,... | collective-permute-start | bytes 294920 | tf_op jit(solution)/shard_map/ppermute | solution.py:280
  34.9 5.4 %collective-permute-start.16 = (bf16[32,2048]{1,0:T(8,128)(2,1)S(1)}, bf16[32,2048]{1,0:T(8,128)(2,1)S(1)}, u32[]{:S(2)}, u32[]{:S(2)}) collective-permute-start(bf16[32,2048]{1,0:T(8,128)(2,1)S(1)} %get-tuple-element.60), channel_id=1, source_target_pairs={{0,2},{2,0},{4,6},{6,4},{8,10},{10,8},{12,14},{14,12},{1,3},{3,1},... | collective-permute-start | bytes 393224 | tf_op jit(solution)/shard_map/ppermute | solution.py:275
  35.2 6.7 %collective-permute-start.19 = (bf16[32,2048]{1,0:T(8,128)(2,1)S(1)}, bf16[32,2048]{1,0:T(8,128)(2,1)S(1)}, u32[]{:S(2)}, u32[]{:S(2)}) collective-permute-start(bf16[32,2048]{1,0:T(8,128)(2,1)S(1)} %get-tuple-element.71), channel_id=1, source_target_pairs={{0,2},{2,0},{4,6},{6,4},{8,10},{10,8},{12,14},{14,12},{1,3},{3,1},... | collective-permute-start | bytes 393224 | tf_op jit(solution)/shard_map/ppermute | solution.py:275
  36.5 5.4 %collective-permute-start.21 = (bf16[32,2048]{1,0:T(8,128)(2,1)S(1)}, bf16[32,2048]{1,0:T(8,128)(2,1)S(1)}, u32[]{:S(2)}, u32[]{:S(2)}) collective-permute-start(bf16[32,2048]{1,0:T(8,128)(2,1)S(1)} %shard_map.85), channel_id=1, source_target_pairs={{0,4},{2,6},{4,0},{6,2},{8,12},{10,14},{12,8},{14,10},{1,5},{3,7},... | collective-permute-start | bytes 393224 | tf_op jit(solution)/shard_map/ppermute | solution.py:275
  36.9 6.5 %collective-permute-start.12 = (bf16[384,128]{1,0:T(8,128)(2,1)S(1)}, bf16[384,128]{1,0:T(8,128)(2,1)S(1)}, u32[]{:S(2)}, u32[]{:S(2)}) collective-permute-start(bf16[384,128]{1,0:T(8,128)(2,1)S(1)} %add_convert_fusion.1), channel_id=1, source_target_pairs={{1,5},{3,7},{5,1},{7,3},{9,13},{11,15},{13,9},{15,11},{17,21},{19,... | collective-permute-start | bytes 294920 | tf_op jit(solution)/shard_map/ppermute | solution.py:280
  40.0 12.4 %collective-permute-start.18 = (bf16[32,2048]{1,0:T(8,128)(2,1)S(1)}, bf16[32,2048]{1,0:T(8,128)(2,1)S(1)}, u32[]{:S(2)}, u32[]{:S(2)}) collective-permute-start(bf16[32,2048]{1,0:T(8,128)(2,1)S(1)} %get-tuple-element.68), channel_id=1, source_target_pairs={{0,2},{2,0},{4,6},{6,4},{8,10},{10,8},{12,14},{14,12},{1,3},{3,1},... | collective-permute-start | bytes 393224 | tf_op jit(solution)/shard_map/ppermute | solution.py:275
  40.3 6.3 %collective-permute-start.17 = (bf16[32,2048]{1,0:T(8,128)(2,1)S(1)}, bf16[32,2048]{1,0:T(8,128)(2,1)S(1)}, u32[]{:S(2)}, u32[]{:S(2)}) collective-permute-start(bf16[32,2048]{1,0:T(8,128)(2,1)S(1)} %shard_map.83), channel_id=1, source_target_pairs={{0,4},{2,6},{4,0},{6,2},{8,12},{10,14},{12,8},{14,10},{1,5},{3,7},... | collective-permute-start | bytes 393224 | tf_op jit(solution)/shard_map/ppermute | solution.py:275
  42.0 10.4 %collective-permute-start.22 = (bf16[32,2048]{1,0:T(8,128)(2,1)S(1)}, bf16[32,2048]{1,0:T(8,128)(2,1)S(1)}, u32[]{:S(2)}, u32[]{:S(2)}) collective-permute-start(bf16[32,2048]{1,0:T(8,128)(2,1)S(1)} %shard_map.86), channel_id=1, source_target_pairs={{0,8},{2,10},{4,12},{6,14},{8,0},{10,2},{12,4},{14,6},{1,9},{3,11}... | collective-permute-start | bytes 393224 | tf_op jit(solution)/shard_map/ppermute | solution.py:275
  43.4 7.2 %collective-permute-start.15 = (bf16[384,128]{1,0:T(8,128)(2,1)S(1)}, bf16[384,128]{1,0:T(8,128)(2,1)S(1)}, u32[]{:S(2)}, u32[]{:S(2)}) collective-permute-start(bf16[384,128]{1,0:T(8,128)(2,1)S(1)} %add_convert_fusion.mine), channel_id=1, source_target_pairs={{1,0},{3,2},{5,4},{7,6},{9,8},{11,10},{13,12},{15,14},{17,16},{19,... | collective-permute-start | bytes 294920 | tf_op jit(solution)/shard_map/ppermute | solution.py:280
  45.2 5.4 %collective-permute-start.14 = (bf16[384,128]{1,0:T(8,128)(2,1)S(1)}, bf16[384,128]{1,0:T(8,128)(2,1)S(1)}, u32[]{:S(2)}, u32[]{:S(2)}) collective-permute-start(bf16[384,128]{1,0:T(8,128)(2,1)S(1)} %add_convert_fusion.mine), channel_id=1, source_target_pairs={{1,2},{3,0},{5,6},{7,4},{9,10},{11,8},{13,14},{15,12},{17,18},{19,... | collective-permute-start | bytes 294920 | tf_op jit(solution)/shard_map/ppermute | solution.py:280
  46.6 5.4 %collective-permute-start.13 = (bf16[384,128]{1,0:T(8,128)(2,1)S(1)}, bf16[384,128]{1,0:T(8,128)(2,1)S(1)}, u32[]{:S(2)}, u32[]{:S(2)}) collective-permute-start(bf16[384,128]{1,0:T(8,128)(2,1)S(1)} %add_convert_fusion.mine), channel_id=1, source_target_pairs={{1,3},{3,1},{5,7},{7,5},{9,11},{11,9},{13,15},{15,13},{17,19},{19,... | collective-permute-start | bytes 294920 | tf_op jit(solution)/shard_map/ppermute | solution.py:280

commit v13 on v11

--- a/solution.py
+++ b/solution.py
@@ -214,18 +214,24 @@
     return [product[n * size : (n + 1) * size] for n in range(len(picks))]
 
 
-def keep_body(picks, low, tile, *rest):
-    for out, part in zip(rest[:-1], picked_product(picks, low, tile, rest[-1])):
-        out[...] = coded(part) if out.dtype == jnp.bfloat16 else part
+def keep_body(picks, low, tile, send_pair, send, *rest):
+    first, second, third, *kept = picked_product(picks, low, tile, rest[-1])
+    size = first.shape[0]
+    send_pair[:size] = coded(first)
+    send_pair[size:] = coded(second)
+    send[...] = coded(third)
+    for out, part in zip(rest[:-1], kept):
+        out[...] = part
 
 
 def copy_body(source, out):
     out[...] = source[...]
 
 
-def sum_body(keep, *refs):
-    total = keep[...]
-    for part in refs[:-1]:
+def sum_body(which, keep, *refs):
+    size = keep.shape[0]
+    total = keep[...] + decoded(refs[0][which * size : (which + 1) * size])
+    for part in refs[1:-1]:
         total = total + decoded(part[...])
     refs[-1][...] = coded(total)
 
@@ -356,7 +362,8 @@
     *parts, keep_third, keep_second, keep_near, own = call(
         functools.partial(keep_body, sent + kept),
         (
-            *[wide(size, jnp.bfloat16) for _ in sent],
+            wide(2 * size, jnp.bfloat16),
+            wide(size, jnp.bfloat16),
             *[wide(size, jnp.float32) for _ in kept],
         ),
         0,
@@ -368,14 +375,14 @@
     gram = sends[1]
     arrived += [swap(part, 1) for part in parts]
 
-    def add_up(cost, keep, *parts):
-        body = call(sum_body, wide(size, jnp.bfloat16), 0, 1 + len(parts), 0, cost)
-        return body(keep, *parts)
-
-    through = swap(add_up(AHEAD, keep_third, arrived[0]), 2)
+    def add_up(which, keep, *parts):
+        body = functools.partial(sum_body, which)
+        return call(body, wide(size, jnp.bfloat16), 0, 1 + len(parts), 0, AHEAD)(keep, *parts)
+
+    through = swap(add_up(0, keep_third, arrived[0]), 2)
     gram_arrived = swap(gram, 4)
-    beside = swap(add_up(AHEAD, keep_near, arrived[2]), 2)
-    across = add_up(AHEAD, keep_second, arrived[1], through)
+    beside = swap(add_up(1, keep_near, arrived[1]), 2)
+    across = add_up(0, keep_second, arrived[1], through)
     gram = (gram.astype(jnp.float32) + gram_arrived.astype(jnp.float32)).astype(jnp.bfloat16)
     gram_arrived = swap(gram, 2)
     across = swap(across, 4)
@@ -394,7 +401,7 @@
         [pltpu.VMEM((kdim, kdim), jnp.float32)],
     )(gram, partner, panel, gene_factor)
     gene_next = call(last_body, wide(size, jnp.float32), 0, 6, 0, AHEAD)(
-        rate, base, own, arrived[3], beside, across
+        rate, base, own, arrived[2], beside, across
     )
     return (cell_next, gene_next)
 

time: 51.4 us -> 50.9 us (level)
  starting transfers between devices: 22.8 us -> 20.9 us
  waiting for transfers between devices: 14 us -> 15.4 us
    ppermute x17 -> x16, starting transfers between devices: 21.6 us -> 19.7 us  [swap(): return lax.ppermute(value, 'cell', [(n, n ^ bits) for n in range(n_cell)])]
    ppermute x17 -> x16, waiting for transfers between devices: 12.6 us -> 14 us  [swap(): return lax.ppermute(value, 'cell', [(n, n ^ bits) for n in range(n_cell)])]
  transfers between devices with their start and end apart: 21 -> 20, of which waited for: 10 -> 8; matrix products, arithmetic and copies ran while one was open for 2% -> 2% of each run, Pallas kernels for 18% -> 18%
where the time goes in v13:
time: 50.9 us; the launch traced here: 50.6 us
  starting transfers between devices  20.9 us (41%)
  waiting for transfers between devices  15.4 us (30%)
  Pallas kernels  11.8 us (23%)
  between operations  1.45 us (3%)
  other arithmetic  1.02 us (2%)
    ppermute x16, starting transfers between devices, swap(): return lax.ppermute(value, 'cell', [(n, n ^ bits) for n in range(n_cell)])  19.7 us
    ppermute x16, waiting for transfers between devices, swap(): return lax.ppermute(value, 'cell', [(n, n ^ bits) for n in range(n_cell)])  14 us
    pallas_call x1, Pallas kernels, dense_tile(): pl.pallas_call(dense_body, out_shape=(shape((CELL_DEV, GENE_DEV), jnp.bfl...  4.09 us
    pallas_call x1, Pallas kernels, shards(): call(functools.partial(cell_body, order, [7], n_parts), (shape(cell_facto...  2.03 us
    ppermute x4, waiting for transfers between devices, swap_core(): return lax.ppermute(value, 'gene', [(0, 1), (1, 0)])  1.41 us
    pallas_call x1, Pallas kernels, shards(): call(functools.partial(second_body, order), (wide(kdim, jnp.bfloat16), sh...  1.21 us
    ppermute x4, starting transfers between devices, swap_core(): return lax.ppermute(value, 'gene', [(0, 1), (1, 0)])  1.19 us
    pallas_call x1, Pallas kernels, shards(): call(functools.partial(first_body, n_parts), (wide(first_rows, jnp.bfloat...  1.14 us
  transfers between devices with their start and end apart: 20, of which 8 were waited for; matrix products, arithmetic and copies ran while one was open for 2% of the time, Pallas kernels for 18%

profile of v13, /device:TPU:0, one launch (start us, length us, event | category | flops | bytes accessed | tf_op | source)
XLA Modules:
  0.0 50.6 jit_solution(1107245009567999367)
XLA Ops:
  0.6 0.5 %collective-permute-start.3 = (f32[128,1024]{1,0:T(8,128)}, f32[128,1024]{1,0:T(8,128)S(1)}, u32[]{:S(2)}, u32[]{:S(2)}) collective-permute-start(f32[128,1024]{1,0:T(8,128)} %factor_mine.1), channel_id=1, source_target_pairs={{0,1},{1,0},{2,3},{3,2},{4,5},{5,4},{6,7},{7,6},{8,9},{9,8},{10,11... | collective-permute-start | bytes 1572872 | tf_op jit(solution)/shard_map/ppermute | solution.py:275
  1.1 1.0 %convert_element_type.21.refs_0_ = bf16[32,2048]{1,0:T(8,128)(2,1)S(1)} convert(f32[32,2048]{1,0:T(8,128)} %factor.1) | non-fusion elementwise | flops 65536 | bytes 393216 | tf_op jit(solution)/shard_map/convert_element_type | solution.py:280
  2.1 3.7 %collective-permute-start.2 = (bf16[32,2048]{1,0:T(8,128)(2,1)S(1)}, bf16[32,2048]{1,0:T(8,128)(2,1)S(1)}, u32[]{:S(2)}, u32[]{:S(2)}) collective-permute-start(bf16[32,2048]{1,0:T(8,128)(2,1)S(1)} %convert_element_type.21.refs_0_), channel_id=1, source_target_pairs={{0,8},{2,10},{4,12},{6,14},{8,0},{10,2},{12,4},{14,6},{1,9},{3,11}... | collective-permute-start | bytes 393224 | tf_op jit(solution)/shard_map/ppermute | solution.py:272
  5.8 1.6 %collective-permute-start.1 = (bf16[32,2048]{1,0:T(8,128)(2,1)S(1)}, bf16[32,2048]{1,0:T(8,128)(2,1)S(1)}, u32[]{:S(2)}, u32[]{:S(2)}) collective-permute-start(bf16[32,2048]{1,0:T(8,128)(2,1)S(1)} %convert_element_type.21.refs_0_), channel_id=1, source_target_pairs={{0,4},{2,6},{4,0},{6,2},{8,12},{10,14},{12,8},{14,10},{1,5},{3,7},... | collective-permute-start | bytes 393224 | tf_op jit(solution)/shard_map/ppermute | solution.py:272
  7.4 1.5 %collective-permute-start = (bf16[32,2048]{1,0:T(8,128)(2,1)S(1)}, bf16[32,2048]{1,0:T(8,128)(2,1)S(1)}, u32[]{:S(2)}, u32[]{:S(2)}) collective-permute-start(bf16[32,2048]{1,0:T(8,128)(2,1)S(1)} %convert_element_type.21.refs_0_), channel_id=1, source_target_pairs={{0,2},{2,0},{4,6},{6,4},{8,10},{10,8},{12,14},{14,12},{1,3},{3,1},... | collective-permute-start | bytes 393224 | tf_op jit(solution)/shard_map/ppermute | solution.py:272
  9.7 4.1 %shard_map.77 = (bf16[1024,2048]{1,0:T(8,128)(2,1)S(1)}, bf16[2048,1024]{1,0:T(8,128)(2,1)S(1)}) custom-call(s32[64]{0:T(128)} %bitcast.6, s32[64]{0:T(128)} %bitcast.7, s32[1]{0:T(128)} %bitcast.4.count, bf16[64,128,128]{2,1,0:T(8,128)(2,1)} %bitcast.5), custom_call_target="tpu_custom_call" | custom-call | tf_op jit(solution)/shard_map/pallas_call | solution.py:88
  13.9 1.1 %collective-permute-start.4 = (bf16[32,2048]{1,0:T(8,128)(2,1)S(1)}, bf16[32,2048]{1,0:T(8,128)(2,1)S(1)}, u32[]{:S(2)}, u32[]{:S(2)}) collective-permute-start(bf16[32,2048]{1,0:T(8,128)(2,1)S(1)} %collective-permute-done.refs_1_), channel_id=1, source_target_pairs={{0,4},{2,6},{4,0},{6,2},{8,12},{10,14},{12,8},{14,10},{1,5},{3,7},... | collective-permute-start | bytes 393224 | tf_op jit(solution)/shard_map/ppermute | solution.py:272
  15.0 1.5 %collective-permute-start.5 = (bf16[32,2048]{1,0:T(8,128)(2,1)S(1)}, bf16[32,2048]{1,0:T(8,128)(2,1)S(1)}, u32[]{:S(2)}, u32[]{:S(2)}) collective-permute-start(bf16[32,2048]{1,0:T(8,128)(2,1)S(1)} %collective-permute-done.2.refs_4_), channel_id=1, source_target_pairs={{0,2},{2,0},{4,6},{6,4},{8,10},{10,8},{12,14},{14,12},{1,3},{3,1},... | collective-permute-start | bytes 393224 | tf_op jit(solution)/shard_map/ppermute | solution.py:272
  16.5 0.4 collective-permute-done.6.refs_6_
  16.9 1.4 %collective-permute-start.7 = (bf16[32,2048]{1,0:T(8,128)(2,1)S(1)}, bf16[32,2048]{1,0:T(8,128)(2,1)S(1)}, u32[]{:S(2)}, u32[]{:S(2)}) collective-permute-start(bf16[32,2048]{1,0:T(8,128)(2,1)S(1)} %collective-permute-done.6.refs_6_), channel_id=1, source_target_pairs={{0,2},{2,0},{4,6},{6,4},{8,10},{10,8},{12,14},{14,12},{1,3},{3,1},... | collective-permute-start | bytes 393224 | tf_op jit(solution)/shard_map/ppermute | solution.py:272
  18.3 1.3 %collective-permute-done.4.refs_3_ = bf16[32,2048]{1,0:T(8,128)(2,1)S(1)} collective-permute-done((bf16[32,2048]{1,0:T(8,128)(2,1)S(1)}, bf16[32,2048]{1,0:T(8,128)(2,1)S(1)}, u32[]{:S(2)}, u32[]{:S(2)}) %collective-permute-start.4) | collective-permute-done | bytes 131104 | tf_op jit(solution)/shard_map/ppermute | solution.py:272
  19.6 1.4 %collective-permute-done.5.refs_5_ = bf16[32,2048]{1,0:T(8,128)(2,1)S(1)} collective-permute-done((bf16[32,2048]{1,0:T(8,128)(2,1)S(1)}, bf16[32,2048]{1,0:T(8,128)(2,1)S(1)}, u32[]{:S(2)}, u32[]{:S(2)}) %collective-permute-start.5) | collective-permute-done | bytes 131104 | tf_op jit(solution)/shard_map/ppermute | solution.py:272
  21.0 1.1 %shard_map.78 = (bf16[224,2048]{1,0:T(8,128)(2,1)S(1)}, f32[224,1024]{1,0:T(8,128)S(1)}, bf16[112,1024]{1,0:T(8,128)(2,1)S(1)}, bf16[112,1024]{1,0:T(8,128)(2,1)S(1)}) custom-call(bf16[2048,1024]{1,0:T(8,128)(2,1)S(1)} %get-tuple-element.36.turned, bf16[32,2048]{1,0:T(8,128)(2,1)S(1)} %convert_element_type.21.refs_0_, ...), custom_call_target="tpu_custom_call" | custom-call | bytes 16777216 | tf_op jit(solution)/shard_map/pallas_call | solution.py:301
  22.2 0.5 collective-permute-start.10
  22.8 1.2 %shard_map.79 = (bf16[256,2048]{1,0:T(8,128)(2,1)S(1)}, f32[96,1024]{1,0:T(8,128)S(1)}, bf16[96,1024]{1,0:T(8,128)(2,1)S(1)}) custom-call(bf16[2048,1024]{1,0:T(8,128)(2,1)S(1)} %get-tuple-element.36.turned, bf16[224,2048]{1,0:T(8,128)(2,1)S(1)} %get-tuple-element.41.first, bf16[32,2048]{1,0:T(8,128)(2,1)S(1)} %collective-permute-done.7.share), custom_call_target="tpu_custom_call" | custom-call | tf_op jit(solution)/shard_map/pallas_call | solution.py:315
  24.1 1.4 %collective-permute-done.8.other = bf16[96,1024]{1,0:T(8,128)(2,1)S(1)} collective-permute-done((bf16[96,1024]{1,0:T(8,128)(2,1)S(1)}, bf16[96,1024]{1,0:T(8,128)(2,1)S(1)}, u32[]{:S(2)}, u32[]{:S(2)}) %collective-permute-start.8) | collective-permute-done | bytes 196640 | tf_op jit(solution)/shard_map/ppermute | solution.py:275
  25.5 2.0 %shard_map.80 = (f32[128,1024]{1,0:T(8,128)S(1)}, bf16[256,1024]{1,0:T(8,128)(2,1)S(1)}, bf16[32,2048]{1,0:T(8,128)(2,1)S(1)}, bf16[384,128]{1,0:T(8,128)(2,1)S(1)}) custom-call(bf16[1024,2048]{1,0:T(8,128)(2,1)S(1)} %get-tuple-element.35.tile, f32[224,1024]{1,0:T(8,128)S(1)} %get-tuple-element.40.mine_first, f32[96,1024]{1,0:T(8,128)S(1)} %get-tuple-element.42.mine, ...), custom_call_target="tpu_custom_call" | custom-call | tf_op jit(solution)/shard_map/pallas_call | solution.py:331
  27.6 1.6 %collective-permute-start.17 = (bf16[32,2048]{1,0:T(8,128)(2,1)S(1)}, bf16[32,2048]{1,0:T(8,128)(2,1)S(1)}, u32[]{:S(2)}, u32[]{:S(2)}) collective-permute-start(bf16[32,2048]{1,0:T(8,128)(2,1)S(1)} %get-tuple-element.63), channel_id=1, source_target_pairs={{0,2},{2,0},{4,6},{6,4},{8,10},{10,8},{12,14},{14,12},{1,3},{3,1},... | collective-permute-start | bytes 393224 | tf_op jit(solution)/shard_map/ppermute | solution.py:272
  29.1 3.7 %collective-permute-start.11 = (bf16[384,128]{1,0:T(8,128)(2,1)S(1)}, bf16[384,128]{1,0:T(8,128)(2,1)S(1)}, u32[]{:S(2)}, u32[]{:S(2)}) collective-permute-start(bf16[384,128]{1,0:T(8,128)(2,1)S(1)} %get-tuple-element.49), channel_id=1, source_target_pairs={{0,8},{2,10},{4,12},{6,14},{8,0},{10,2},{12,4},{14,6},{1,9},{3,11}... | collective-permute-start | bytes 294920 | tf_op jit(solution)/shard_map/ppermute | solution.py:272
  32.8 1.1 %shard_map.81 = (bf16[64,2048]{1,0:T(8,128)(2,1)S(1)}, bf16[32,2048]{1,0:T(8,128)(2,1)S(1)}, f32[32,2048]{1,0:T(8,128)S(1)}, f32[32,2048]{1,0:T(8,128)S(1)}, f32...) custom-call(bf16[256,1024]{1,0:T(8,128)(2,1)S(1)} %get-tuple-element.47.low, bf16[1024,2048]{1,0:T(8,128)(2,1)S(1)} %get-tuple-element.35.tile), custom_call_target="tpu_custom_call" | custom-call | bytes 16777216 | tf_op jit(solution)/shard_map/pallas_call | solution.py:362
  34.0 0.6 %collective-permute-start.15 = (bf16[64,2048]{1,0:T(8,128)(2,1)S(1)}, bf16[64,2048]{1,0:T(8,128)(2,1)S(1)}, u32[]{:S(2)}, u32[]{:S(2)}) collective-permute-start(bf16[64,2048]{1,0:T(8,128)(2,1)S(1)} %get-tuple-element.60), channel_id=1, source_target_pairs={{0,2},{2,0},{4,6},{6,4},{8,10},{10,8},{12,14},{14,12},{1,3},{3,1},... | collective-permute-start | bytes 786440 | tf_op jit(solution)/shard_map/ppermute | solution.py:272
  34.6 0.5 collective-permute-start.18
  35.1 2.8 %collective-permute-done.11 = bf16[384,128]{1,0:T(8,128)(2,1)S(1)} collective-permute-done((bf16[384,128]{1,0:T(8,128)(2,1)S(1)}, bf16[384,128]{1,0:T(8,128)(2,1)S(1)}, u32[]{:S(2)}, u32[]{:S(2)}) %collective-permute-start.11) | collective-permute-done | bytes 98336 | tf_op jit(solution)/shard_map/ppermute | solution.py:272
  38.0 0.5 %collective-permute-start.14 = (bf16[32,2048]{1,0:T(8,128)(2,1)S(1)}, bf16[32,2048]{1,0:T(8,128)(2,1)S(1)}, u32[]{:S(2)}, u32[]{:S(2)}) collective-permute-start(bf16[32,2048]{1,0:T(8,128)(2,1)S(1)} %get-tuple-element.58), channel_id=1, source_target_pairs={{0,2},{2,0},{4,6},{6,4},{8,10},{10,8},{12,14},{14,12},{1,3},{3,1},... | collective-permute-start | bytes 393224 | tf_op jit(solution)/shard_map/ppermute | solution.py:272
  38.5 4.7 %collective-permute-done.15.refs_0_ = bf16[64,2048]{1,0:T(8,128)(2,1)S(1)} collective-permute-done((bf16[64,2048]{1,0:T(8,128)(2,1)S(1)}, bf16[64,2048]{1,0:T(8,128)(2,1)S(1)}, u32[]{:S(2)}, u32[]{:S(2)}) %collective-permute-start.15) | collective-permute-done | bytes 262176 | tf_op jit(solution)/shard_map/ppermute | solution.py:272
  43.5 0.8 %collective-permute-start.19 = (bf16[32,2048]{1,0:T(8,128)(2,1)S(1)}, bf16[32,2048]{1,0:T(8,128)(2,1)S(1)}, u32[]{:S(2)}, u32[]{:S(2)}) collective-permute-start(bf16[32,2048]{1,0:T(8,128)(2,1)S(1)} %shard_map.86), channel_id=1, source_target_pairs={{0,8},{2,10},{4,12},{6,14},{8,0},{10,2},{12,4},{14,6},{1,9},{3,11}... | collective-permute-start | bytes 393224 | tf_op jit(solution)/shard_map/ppermute | solution.py:272
  44.3 0.9 %collective-permute-start.13 = (bf16[384,128]{1,0:T(8,128)(2,1)S(1)}, bf16[384,128]{1,0:T(8,128)(2,1)S(1)}, u32[]{:S(2)}, u32[]{:S(2)}) collective-permute-start(bf16[384,128]{1,0:T(8,128)(2,1)S(1)} %add_convert_fusion.mine), channel_id=1, source_target_pairs={{0,2},{2,0},{4,6},{6,4},{8,10},{10,8},{12,14},{14,12},{1,3},{3,1},... | collective-permute-start | bytes 294920 | tf_op jit(solution)/shard_map/ppermute | solution.py:272
  45.2 0.8 %shard_map.82 = f32[128,1024]{1,0:T(8,128)} custom-call(f32[128,1024]{1,0:T(8,128)S(1)} %get-tuple-element.51.source), custom_call_target="tpu_custom_call" | custom-call | tf_op jit(solution)/shard_map/pallas_call | solution.py:392
  46.0 3.0 %collective-permute-done.13.other = bf16[384,128]{1,0:T(8,128)(2,1)S(1)} collective-permute-done((bf16[384,128]{1,0:T(8,128)(2,1)S(1)}, bf16[384,128]{1,0:T(8,128)(2,1)S(1)}, u32[]{:S(2)}, u32[]{:S(2)}) %collective-permute-start.13) | collective-permute-done | bytes 98336 | tf_op jit(solution)/shard_map/ppermute | solution.py:272
  49.0 0.4 shard_map.83
  49.4 0.4 collective-permute-done.16.refs_1_
  49.7 0.9 %shard_map.87 = f32[32,2048]{1,0:T(8,128)} custom-call(f32[8,128]{1,0:T(8,128)S(1)} %get-tuple-element.55.rate, f32[32,2048]{1,0:T(8,128)S(1)} %get-tuple-element.56.base, f32[32,2048]{1,0:T(8,128)S(1)} %get-tuple-element.57.own, bf16[32,2048]{1,0:T(8,128)(2,1)S(1)} %collective-permute-done.14.refs_0_, bf16[32,2048]{1,0:T(8,128)(2,1)S(1)} %collective-permute-done.16.refs_1_, ...), custom_call_target="tpu_custom_call" | custom-call | bytes 16777216 | tf_op jit(solution)/shard_map/pallas_call | solution.py:403
  (26 shorter events, 0.9 us)
Async XLA Ops:
  0.6 13.2 %collective-permute-start.3 = (f32[128,1024]{1,0:T(8,128)}, f32[128,1024]{1,0:T(8,128)S(1)}, u32[]{:S(2)}, u32[]{:S(2)}) collective-permute-start(f32[128,1024]{1,0:T(8,128)} %factor_mine.1), channel_id=1, source_target_pairs={{0,1},{1,0},{2,3},{3,2},{4,5},{5,4},{6,7},{7,6},{8,9},{9,8},{10,11... | collective-permute-start | bytes 1572872 | tf_op jit(solution)/shard_map/ppermute | solution.py:275
  2.1 11.7 %collective-permute-start.2 = (bf16[32,2048]{1,0:T(8,128)(2,1)S(1)}, bf16[32,2048]{1,0:T(8,128)(2,1)S(1)}, u32[]{:S(2)}, u32[]{:S(2)}) collective-permute-start(bf16[32,2048]{1,0:T(8,128)(2,1)S(1)} %convert_element_type.21.refs_0_), channel_id=1, source_target_pairs={{0,8},{2,10},{4,12},{6,14},{8,0},{10,2},{12,4},{14,6},{1,9},{3,11}... | collective-permute-start | bytes 393224 | tf_op jit(solution)/shard_map/ppermute | solution.py:272
  5.8 8.1 %collective-permute-start.1 = (bf16[32,2048]{1,0:T(8,128)(2,1)S(1)}, bf16[32,2048]{1,0:T(8,128)(2,1)S(1)}, u32[]{:S(2)}, u32[]{:S(2)}) collective-permute-start(bf16[32,2048]{1,0:T(8,128)(2,1)S(1)} %convert_element_type.21.refs_0_), channel_id=1, source_target_pairs={{0,4},{2,6},{4,0},{6,2},{8,12},{10,14},{12,8},{14,10},{1,5},{3,7},... | collective-permute-start | bytes 393224 | tf_op jit(solution)/shard_map/ppermute | solution.py:272
  7.4 6.5 %collective-permute-start = (bf16[32,2048]{1,0:T(8,128)(2,1)S(1)}, bf16[32,2048]{1,0:T(8,128)(2,1)S(1)}, u32[]{:S(2)}, u32[]{:S(2)}) collective-permute-start(bf16[32,2048]{1,0:T(8,128)(2,1)S(1)} %convert_element_type.21.refs_0_), channel_id=1, source_target_pairs={{0,2},{2,0},{4,6},{6,4},{8,10},{10,8},{12,14},{14,12},{1,3},{3,1},... | collective-permute-start | bytes 393224 | tf_op jit(solution)/shard_map/ppermute | solution.py:272
  8.9 8.0 %collective-permute-start.6 = (bf16[32,2048]{1,0:T(8,128)(2,1)S(1)}, bf16[32,2048]{1,0:T(8,128)(2,1)S(1)}, u32[]{:S(2)}, u32[]{:S(2)}) collective-permute-start(bf16[32,2048]{1,0:T(8,128)(2,1)S(1)} %convert_element_type.21.refs_0_), channel_id=1, source_target_pairs={{0,12},{2,14},{4,8},{6,10},{8,4},{10,6},{12,0},{14,2},{1,13},{3,15... | collective-permute-start | bytes 393224 | tf_op jit(solution)/shard_map/ppermute | solution.py:272
  13.9 11.7 %copy-start.1 = (f32[128,1024]{1,0:T(8,128)S(1)}, f32[128,1024]{1,0:T(8,128)}, u32[]{:S(2)}) copy-start(f32[128,1024]{1,0:T(8,128)} %factor_mine.1) | copy-start | bytes 1572868
  13.9 5.7 %collective-permute-start.4 = (bf16[32,2048]{1,0:T(8,128)(2,1)S(1)}, bf16[32,2048]{1,0:T(8,128)(2,1)S(1)}, u32[]{:S(2)}, u32[]{:S(2)}) collective-permute-start(bf16[32,2048]{1,0:T(8,128)(2,1)S(1)} %collective-permute-done.refs_1_), channel_id=1, source_target_pairs={{0,4},{2,6},{4,0},{6,2},{8,12},{10,14},{12,8},{14,10},{1,5},{3,7},... | collective-permute-start | bytes 393224 | tf_op jit(solution)/shard_map/ppermute | solution.py:272
  15.0 6.0 %collective-permute-start.5 = (bf16[32,2048]{1,0:T(8,128)(2,1)S(1)}, bf16[32,2048]{1,0:T(8,128)(2,1)S(1)}, u32[]{:S(2)}, u32[]{:S(2)}) collective-permute-start(bf16[32,2048]{1,0:T(8,128)(2,1)S(1)} %collective-permute-done.2.refs_4_), channel_id=1, source_target_pairs={{0,2},{2,0},{4,6},{6,4},{8,10},{10,8},{12,14},{14,12},{1,3},{3,1},... | collective-permute-start | bytes 393224 | tf_op jit(solution)/shard_map/ppermute | solution.py:272
  16.9 5.9 %collective-permute-start.7 = (bf16[32,2048]{1,0:T(8,128)(2,1)S(1)}, bf16[32,2048]{1,0:T(8,128)(2,1)S(1)}, u32[]{:S(2)}, u32[]{:S(2)}) collective-permute-start(bf16[32,2048]{1,0:T(8,128)(2,1)S(1)} %collective-permute-done.6.refs_6_), channel_id=1, source_target_pairs={{0,2},{2,0},{4,6},{6,4},{8,10},{10,8},{12,14},{14,12},{1,3},{3,1},... | collective-permute-start | bytes 393224 | tf_op jit(solution)/shard_map/ppermute | solution.py:272
  22.2 3.4 %collective-permute-start.9 = (bf16[112,1024]{1,0:T(8,128)(2,1)S(1)}, bf16[112,1024]{1,0:T(8,128)(2,1)S(1)}, u32[]{:S(2)}, u32[]{:S(2)}) collective-permute-start(bf16[112,1024]{1,0:T(8,128)(2,1)S(1)} %get-tuple-element.45), channel_id=1, source_target_pairs={{0,1},{1,0},{2,3},{3,2},{4,5},{5,4},{6,7},{7,6},{8,9},{9,8},{10,11... | collective-permute-start | bytes 688136 | tf_op jit(solution)/shard_map/ppermute | solution.py:275
  22.2 3.3 %collective-permute-start.10 = (bf16[112,1024]{1,0:T(8,128)(2,1)S(1)}, bf16[112,1024]{1,0:T(8,128)(2,1)S(1)}, u32[]{:S(2)}, u32[]{:S(2)}) collective-permute-start(bf16[112,1024]{1,0:T(8,128)(2,1)S(1)} %get-tuple-element.46), channel_id=1, source_target_pairs={{0,1},{1,0},{2,3},{3,2},{4,5},{5,4},{6,7},{7,6},{8,9},{9,8},{10,11... | collective-permute-start | bytes 688136 | tf_op jit(solution)/shard_map/ppermute | solution.py:275
  24.0 1.5 %collective-permute-start.8 = (bf16[96,1024]{1,0:T(8,128)(2,1)S(1)}, bf16[96,1024]{1,0:T(8,128)(2,1)S(1)}, u32[]{:S(2)}, u32[]{:S(2)}) collective-permute-start(bf16[96,1024]{1,0:T(8,128)(2,1)S(1)} %get-tuple-element.43), channel_id=1, source_target_pairs={{0,1},{1,0},{2,3},{3,2},{4,5},{5,4},{6,7},{7,6},{8,9},{9,8},{10,11... | collective-permute-start | bytes 589832 | tf_op jit(solution)/shard_map/ppermute | solution.py:275
  27.6 21.4 %copy-start = (f32[32,2048]{1,0:T(8,128)S(1)}, f32[32,2048]{1,0:T(8,128)}, u32[]{:S(2)}) copy-start(f32[32,2048]{1,0:T(8,128)} %factor.1) | copy-start | bytes 786436
  27.6 7.0 %collective-permute-start.17 = (bf16[32,2048]{1,0:T(8,128)(2,1)S(1)}, bf16[32,2048]{1,0:T(8,128)(2,1)S(1)}, u32[]{:S(2)}, u32[]{:S(2)}) collective-permute-start(bf16[32,2048]{1,0:T(8,128)(2,1)S(1)} %get-tuple-element.63), channel_id=1, source_target_pairs={{0,2},{2,0},{4,6},{6,4},{8,10},{10,8},{12,14},{14,12},{1,3},{3,1},... | collective-permute-start | bytes 393224 | tf_op jit(solution)/shard_map/ppermute | solution.py:272
  29.1 8.7 %collective-permute-start.11 = (bf16[384,128]{1,0:T(8,128)(2,1)S(1)}, bf16[384,128]{1,0:T(8,128)(2,1)S(1)}, u32[]{:S(2)}, u32[]{:S(2)}) collective-permute-start(bf16[384,128]{1,0:T(8,128)(2,1)S(1)} %get-tuple-element.49), channel_id=1, source_target_pairs={{0,8},{2,10},{4,12},{6,14},{8,0},{10,2},{12,4},{14,6},{1,9},{3,11}... | collective-permute-start | bytes 294920 | tf_op jit(solution)/shard_map/ppermute | solution.py:272
  34.0 9.3 %collective-permute-start.15 = (bf16[64,2048]{1,0:T(8,128)(2,1)S(1)}, bf16[64,2048]{1,0:T(8,128)(2,1)S(1)}, u32[]{:S(2)}, u32[]{:S(2)}) collective-permute-start(bf16[64,2048]{1,0:T(8,128)(2,1)S(1)} %get-tuple-element.60), channel_id=1, source_target_pairs={{0,2},{2,0},{4,6},{6,4},{8,10},{10,8},{12,14},{14,12},{1,3},{3,1},... | collective-permute-start | bytes 786440 | tf_op jit(solution)/shard_map/ppermute | solution.py:272
  34.6 8.7 %collective-permute-start.18 = (bf16[32,2048]{1,0:T(8,128)(2,1)S(1)}, bf16[32,2048]{1,0:T(8,128)(2,1)S(1)}, u32[]{:S(2)}, u32[]{:S(2)}) collective-permute-start(bf16[32,2048]{1,0:T(8,128)(2,1)S(1)} %shard_map.85), channel_id=1, source_target_pairs={{0,4},{2,6},{4,0},{6,2},{8,12},{10,14},{12,8},{14,10},{1,5},{3,7},... | collective-permute-start | bytes 393224 | tf_op jit(solution)/shard_map/ppermute | solution.py:272
  37.9 6.4 %collective-permute-start.12 = (bf16[384,128]{1,0:T(8,128)(2,1)S(1)}, bf16[384,128]{1,0:T(8,128)(2,1)S(1)}, u32[]{:S(2)}, u32[]{:S(2)}) collective-permute-start(bf16[384,128]{1,0:T(8,128)(2,1)S(1)} %add_convert_fusion.1), channel_id=1, source_target_pairs={{0,4},{2,6},{4,0},{6,2},{8,12},{10,14},{12,8},{14,10},{1,5},{3,7},... | collective-permute-start | bytes 294920 | tf_op jit(solution)/shard_map/ppermute | solution.py:272
  38.0 11.4 %collective-permute-start.14 = (bf16[32,2048]{1,0:T(8,128)(2,1)S(1)}, bf16[32,2048]{1,0:T(8,128)(2,1)S(1)}, u32[]{:S(2)}, u32[]{:S(2)}) collective-permute-start(bf16[32,2048]{1,0:T(8,128)(2,1)S(1)} %get-tuple-element.58), channel_id=1, source_target_pairs={{0,2},{2,0},{4,6},{6,4},{8,10},{10,8},{12,14},{14,12},{1,3},{3,1},... | collective-permute-start | bytes 393224 | tf_op jit(solution)/shard_map/ppermute | solution.py:272
  43.3 6.5 %collective-permute-start.16 = (bf16[32,2048]{1,0:T(8,128)(2,1)S(1)}, bf16[32,2048]{1,0:T(8,128)(2,1)S(1)}, u32[]{:S(2)}, u32[]{:S(2)}) collective-permute-start(bf16[32,2048]{1,0:T(8,128)(2,1)S(1)} %shard_map.84), channel_id=1, source_target_pairs={{0,4},{2,6},{4,0},{6,2},{8,12},{10,14},{12,8},{14,10},{1,5},{3,7},... | collective-permute-start | bytes 393224 | tf_op jit(solution)/shard_map/ppermute | solution.py:272
  43.5 6.3 %collective-permute-start.19 = (bf16[32,2048]{1,0:T(8,128)(2,1)S(1)}, bf16[32,2048]{1,0:T(8,128)(2,1)S(1)}, u32[]{:S(2)}, u32[]{:S(2)}) collective-permute-start(bf16[32,2048]{1,0:T(8,128)(2,1)S(1)} %shard_map.86), channel_id=1, source_target_pairs={{0,8},{2,10},{4,12},{6,14},{8,0},{10,2},{12,4},{14,6},{1,9},{3,11}... | collective-permute-start | bytes 393224 | tf_op jit(solution)/shard_map/ppermute | solution.py:272
  44.3 4.7 %collective-permute-start.13 = (bf16[384,128]{1,0:T(8,128)(2,1)S(1)}, bf16[384,128]{1,0:T(8,128)(2,1)S(1)}, u32[]{:S(2)}, u32[]{:S(2)}) collective-permute-start(bf16[384,128]{1,0:T(8,128)(2,1)S(1)} %add_convert_fusion.mine), channel_id=1, source_target_pairs={{0,2},{2,0},{4,6},{6,4},{8,10},{10,8},{12,14},{14,12},{1,3},{3,1},... | collective-permute-start | bytes 294920 | tf_op jit(solution)/shard_map/ppermute | solution.py:272

commit v14 on v13

--- a/solution.py
+++ b/solution.py
@@ -192,9 +192,7 @@
     cell_next[...] = updated[own]
     low[...] = updated[...].astype(jnp.bfloat16)
     if sends:
-        send, gram_out = sends
-        send[...] = coded(picked_product(picks, low, tile, chosen)[0])
-        gram_blocks(low, gram_out)
+        sends[0][...] = coded(picked_product(picks, low, tile, chosen)[0])
 
 
 def gram_blocks(low, out):
@@ -214,7 +212,7 @@
     return [product[n * size : (n + 1) * size] for n in range(len(picks))]
 
 
-def keep_body(picks, low, tile, send_pair, send, *rest):
+def keep_body(picks, low, tile, gram, send_pair, send, *rest):
     first, second, third, *kept = picked_product(picks, low, tile, rest[-1])
     size = first.shape[0]
     send_pair[:size] = coded(first)
@@ -222,6 +220,7 @@
     send[...] = coded(third)
     for out, part in zip(rest[:-1], kept):
         out[...] = part
+    gram_blocks(low, gram)
 
 
 def copy_body(source, out):
@@ -333,7 +332,7 @@
         (
             shape(cell_factor.shape, jnp.float32),
             shape((kdim, CELL_DEV), jnp.bfloat16),
-            *([wide(size, jnp.bfloat16), shape((3 * kdim // 2, kdim // 2), jnp.bfloat16)] if paired else []),
+            *([wide(size, jnp.bfloat16)] if paired else []),
         ),
         0,
         6 + n_parts,
@@ -359,9 +358,10 @@
         return (updated, jnp.maximum(gene_factor - rate_gene * (stepped - own_cols), 0.0))
 
     arrived = [swap(sends[0], 1)]
-    *parts, keep_third, keep_second, keep_near, own = call(
+    gram, *parts, keep_third, keep_second, keep_near, own = call(
         functools.partial(keep_body, sent + kept),
         (
+            shape((3 * kdim // 2, kdim // 2), jnp.bfloat16),
             wide(2 * size, jnp.bfloat16),
             wide(size, jnp.bfloat16),
             *[wide(size, jnp.float32) for _ in kept],
@@ -372,7 +372,6 @@
         AHEAD,
         [pltpu.VMEM((kdim - size, CELL_DEV), jnp.bfloat16)],
     )(next_low, tile)
-    gram = sends[1]
     arrived += [swap(part, 1) for part in parts]
 
     def add_up(which, keep, *parts):
@@ -385,6 +384,7 @@
     across = add_up(0, keep_second, arrived[1], through)
     gram = (gram.astype(jnp.float32) + gram_arrived.astype(jnp.float32)).astype(jnp.bfloat16)
     gram_arrived = swap(gram, 2)
+    gram_arrived, across = lax.optimization_barrier((gram_arrived, across))
     across = swap(across, 4)
     gram = (gram.astype(jnp.float32) + gram_arrived.astype(jnp.float32)).astype(jnp.bfloat16)
     partner = swap(gram, 1)

time: 50.9 us -> 52.9 us (1.039)
  waiting for transfers between devices: 15.4 us -> 17.4 us
    ppermute x16, waiting for transfers between devices: 14 us -> 15.9 us  [swap(): return lax.ppermute(value, 'cell', [(n, n ^ bits) for n in range(n_cell)])]
  transfers between devices with their start and end apart: 20 -> 20, of which waited for: 8 -> 12; matrix products, arithmetic and copies ran while one was open for 2% -> 2% of each run, Pallas kernels for 18% -> 17%
where the time goes in v14:
time: 52.9 us; the launch traced here: 52.6 us
  starting transfers between devices  21.3 us (40%)
  waiting for transfers between devices  17.4 us (33%)
  Pallas kernels  11.5 us (22%)
  between operations  1.44 us (3%)
  other arithmetic  1.02 us (2%)
    ppermute x16, starting transfers between devices, swap(): return lax.ppermute(value, 'cell', [(n, n ^ bits) for n in range(n_cell)])  20.1 us
    ppermute x16, waiting for transfers between devices, swap(): return lax.ppermute(value, 'cell', [(n, n ^ bits) for n in range(n_cell)])  15.9 us
    pallas_call x1, Pallas kernels, dense_tile(): pl.pallas_call(dense_body, out_shape=(shape((CELL_DEV, GENE_DEV), jnp.bfl...  4.09 us
    pallas_call x1, Pallas kernels, shards(): call(functools.partial(cell_body, order, [7], n_parts), (shape(cell_facto...  1.57 us
    ppermute x4, waiting for transfers between devices, swap_core(): return lax.ppermute(value, 'gene', [(0, 1), (1, 0)])  1.42 us
    pallas_call x1, Pallas kernels, shards(): call(functools.partial(keep_body, sent + kept), (shape((3 * kdim // 2, kd...  1.28 us
    pallas_call x1, Pallas kernels, shards(): call(functools.partial(second_body, order), (wide(kdim, jnp.bfloat16), sh...  1.21 us
    ppermute x4, starting transfers between devices, swap_core(): return lax.ppermute(value, 'gene', [(0, 1), (1, 0)])  1.18 us
  transfers between devices with their start and end apart: 20, of which 12 were waited for; matrix products, arithmetic and copies ran while one was open for 2% of the time, Pallas kernels for 17%

profile of v14, /device:TPU:0, one launch (start us, length us, event | category | flops | bytes accessed | tf_op | source)
XLA Modules:
  0.0 52.6 jit_solution(10932050999294865381)
XLA Ops:
  0.6 0.5 collective-permute-start.3
  1.1 1.0 %convert_element_type.21.refs_0_ = bf16[32,2048]{1,0:T(8,128)(2,1)S(1)} convert(f32[32,2048]{1,0:T(8,128)} %factor.1) | non-fusion elementwise | flops 65536 | bytes 393216 | tf_op jit(solution)/shard_map/convert_element_type | solution.py:279
  2.1 3.7 %collective-permute-start.2 = (bf16[32,2048]{1,0:T(8,128)(2,1)S(1)}, bf16[32,2048]{1,0:T(8,128)(2,1)S(1)}, u32[]{:S(2)}, u32[]{:S(2)}) collective-permute-start(bf16[32,2048]{1,0:T(8,128)(2,1)S(1)} %convert_element_type.21.refs_0_), channel_id=1, source_target_pairs={{0,8},{2,10},{4,12},{6,14},{8,0},{10,2},{12,4},{14,6},{1,9},{3,11}... | collective-permute-start | bytes 393224 | tf_op jit(solution)/shard_map/ppermute | solution.py:271
  5.8 1.6 %collective-permute-start.1 = (bf16[32,2048]{1,0:T(8,128)(2,1)S(1)}, bf16[32,2048]{1,0:T(8,128)(2,1)S(1)}, u32[]{:S(2)}, u32[]{:S(2)}) collective-permute-start(bf16[32,2048]{1,0:T(8,128)(2,1)S(1)} %convert_element_type.21.refs_0_), channel_id=1, source_target_pairs={{0,4},{2,6},{4,0},{6,2},{8,12},{10,14},{12,8},{14,10},{1,5},{3,7},... | collective-permute-start | bytes 393224 | tf_op jit(solution)/shard_map/ppermute | solution.py:271
  7.4 1.5 %collective-permute-start = (bf16[32,2048]{1,0:T(8,128)(2,1)S(1)}, bf16[32,2048]{1,0:T(8,128)(2,1)S(1)}, u32[]{:S(2)}, u32[]{:S(2)}) collective-permute-start(bf16[32,2048]{1,0:T(8,128)(2,1)S(1)} %convert_element_type.21.refs_0_), channel_id=1, source_target_pairs={{0,2},{2,0},{4,6},{6,4},{8,10},{10,8},{12,14},{14,12},{1,3},{3,1},... | collective-permute-start | bytes 393224 | tf_op jit(solution)/shard_map/ppermute | solution.py:271
  9.7 4.1 %shard_map.77 = (bf16[1024,2048]{1,0:T(8,128)(2,1)S(1)}, bf16[2048,1024]{1,0:T(8,128)(2,1)S(1)}) custom-call(s32[64]{0:T(128)} %bitcast.6, s32[64]{0:T(128)} %bitcast.7, s32[1]{0:T(128)} %bitcast.4.count, bf16[64,128,128]{2,1,0:T(8,128)(2,1)} %bitcast.5), custom_call_target="tpu_custom_call" | custom-call | tf_op jit(solution)/shard_map/pallas_call | solution.py:88
  13.9 1.1 %collective-permute-start.4 = (bf16[32,2048]{1,0:T(8,128)(2,1)S(1)}, bf16[32,2048]{1,0:T(8,128)(2,1)S(1)}, u32[]{:S(2)}, u32[]{:S(2)}) collective-permute-start(bf16[32,2048]{1,0:T(8,128)(2,1)S(1)} %collective-permute-done.refs_1_), channel_id=1, source_target_pairs={{0,4},{2,6},{4,0},{6,2},{8,12},{10,14},{12,8},{14,10},{1,5},{3,7},... | collective-permute-start | bytes 393224 | tf_op jit(solution)/shard_map/ppermute | solution.py:271
  15.0 1.5 %collective-permute-start.5 = (bf16[32,2048]{1,0:T(8,128)(2,1)S(1)}, bf16[32,2048]{1,0:T(8,128)(2,1)S(1)}, u32[]{:S(2)}, u32[]{:S(2)}) collective-permute-start(bf16[32,2048]{1,0:T(8,128)(2,1)S(1)} %collective-permute-done.2.refs_4_), channel_id=1, source_target_pairs={{0,2},{2,0},{4,6},{6,4},{8,10},{10,8},{12,14},{14,12},{1,3},{3,1},... | collective-permute-start | bytes 393224 | tf_op jit(solution)/shard_map/ppermute | solution.py:271
  16.8 1.5 %collective-permute-start.7 = (bf16[32,2048]{1,0:T(8,128)(2,1)S(1)}, bf16[32,2048]{1,0:T(8,128)(2,1)S(1)}, u32[]{:S(2)}, u32[]{:S(2)}) collective-permute-start(bf16[32,2048]{1,0:T(8,128)(2,1)S(1)} %collective-permute-done.6.refs_6_), channel_id=1, source_target_pairs={{0,2},{2,0},{4,6},{6,4},{8,10},{10,8},{12,14},{14,12},{1,3},{3,1},... | collective-permute-start | bytes 393224 | tf_op jit(solution)/shard_map/ppermute | solution.py:271
  18.3 1.3 %collective-permute-done.4.refs_3_ = bf16[32,2048]{1,0:T(8,128)(2,1)S(1)} collective-permute-done((bf16[32,2048]{1,0:T(8,128)(2,1)S(1)}, bf16[32,2048]{1,0:T(8,128)(2,1)S(1)}, u32[]{:S(2)}, u32[]{:S(2)}) %collective-permute-start.4) | collective-permute-done | bytes 131104 | tf_op jit(solution)/shard_map/ppermute | solution.py:271
  19.6 1.4 %collective-permute-done.5.refs_5_ = bf16[32,2048]{1,0:T(8,128)(2,1)S(1)} collective-permute-done((bf16[32,2048]{1,0:T(8,128)(2,1)S(1)}, bf16[32,2048]{1,0:T(8,128)(2,1)S(1)}, u32[]{:S(2)}, u32[]{:S(2)}) %collective-permute-start.5) | collective-permute-done | bytes 131104 | tf_op jit(solution)/shard_map/ppermute | solution.py:271
  21.0 1.1 %shard_map.78 = (bf16[224,2048]{1,0:T(8,128)(2,1)S(1)}, f32[224,1024]{1,0:T(8,128)S(1)}, bf16[112,1024]{1,0:T(8,128)(2,1)S(1)}, bf16[112,1024]{1,0:T(8,128)(2,1)S(1)}) custom-call(bf16[2048,1024]{1,0:T(8,128)(2,1)S(1)} %get-tuple-element.38.turned, bf16[32,2048]{1,0:T(8,128)(2,1)S(1)} %convert_element_type.21.refs_0_, ...), custom_call_target="tpu_custom_call" | custom-call | bytes 16777216 | tf_op jit(solution)/shard_map/pallas_call | solution.py:300
  22.2 0.5 collective-permute-start.10
  22.8 1.2 %shard_map.79 = (bf16[256,2048]{1,0:T(8,128)(2,1)S(1)}, f32[96,1024]{1,0:T(8,128)S(1)}, bf16[96,1024]{1,0:T(8,128)(2,1)S(1)}) custom-call(bf16[2048,1024]{1,0:T(8,128)(2,1)S(1)} %get-tuple-element.38.turned, bf16[224,2048]{1,0:T(8,128)(2,1)S(1)} %get-tuple-element.43.first, bf16[32,2048]{1,0:T(8,128)(2,1)S(1)} %collective-permute-done.7.share), custom_call_target="tpu_custom_call" | custom-call | tf_op jit(solution)/shard_map/pallas_call | solution.py:314
  24.1 1.4 %collective-permute-done.8.other = bf16[96,1024]{1,0:T(8,128)(2,1)S(1)} collective-permute-done((bf16[96,1024]{1,0:T(8,128)(2,1)S(1)}, bf16[96,1024]{1,0:T(8,128)(2,1)S(1)}, u32[]{:S(2)}, u32[]{:S(2)}) %collective-permute-start.8) | collective-permute-done | bytes 196640 | tf_op jit(solution)/shard_map/ppermute | solution.py:274
  25.5 1.6 %shard_map.80 = (f32[128,1024]{1,0:T(8,128)S(1)}, bf16[256,1024]{1,0:T(8,128)(2,1)S(1)}, bf16[32,2048]{1,0:T(8,128)(2,1)S(1)}) custom-call(bf16[1024,2048]{1,0:T(8,128)(2,1)S(1)} %get-tuple-element.37.tile, f32[224,1024]{1,0:T(8,128)S(1)} %get-tuple-element.42.mine_first, f32[96,1024]{1,0:T(8,128)S(1)} %get-tuple-element.44.mine, ...), custom_call_target="tpu_custom_call" | custom-call | tf_op jit(solution)/shard_map/pallas_call | solution.py:330
  27.1 1.6 %collective-permute-start.14 = (bf16[32,2048]{1,0:T(8,128)(2,1)S(1)}, bf16[32,2048]{1,0:T(8,128)(2,1)S(1)}, u32[]{:S(2)}, u32[]{:S(2)}) collective-permute-start(bf16[32,2048]{1,0:T(8,128)(2,1)S(1)} %get-tuple-element.55), channel_id=1, source_target_pairs={{0,2},{2,0},{4,6},{6,4},{8,10},{10,8},{12,14},{14,12},{1,3},{3,1},... | collective-permute-start | bytes 393224 | tf_op jit(solution)/shard_map/ppermute | solution.py:271
  28.7 1.3 %shard_map.81 = (bf16[384,128]{1,0:T(8,128)(2,1)S(1)}, bf16[64,2048]{1,0:T(8,128)(2,1)S(1)}, bf16[32,2048]{1,0:T(8,128)(2,1)S(1)}, f32[32,2048]{1,0:T(8,128)S(1)...) custom-call(bf16[256,1024]{1,0:T(8,128)(2,1)S(1)} %get-tuple-element.49.low, ...), custom_call_target="tpu_custom_call" | custom-call | bytes 16777216 | tf_op jit(solution)/shard_map/pallas_call | solution.py:361
  30.0 3.8 %collective-permute-start.11 = (bf16[384,128]{1,0:T(8,128)(2,1)S(1)}, bf16[384,128]{1,0:T(8,128)(2,1)S(1)}, u32[]{:S(2)}, u32[]{:S(2)}) collective-permute-start(bf16[384,128]{1,0:T(8,128)(2,1)S(1)} %get-tuple-element.51), channel_id=1, source_target_pairs={{0,8},{2,10},{4,12},{6,14},{8,0},{10,2},{12,4},{14,6},{1,9},{3,11}... | collective-permute-start | bytes 294920 | tf_op jit(solution)/shard_map/ppermute | solution.py:271
  33.7 0.5 %collective-permute-start.13 = (bf16[64,2048]{1,0:T(8,128)(2,1)S(1)}, bf16[64,2048]{1,0:T(8,128)(2,1)S(1)}, u32[]{:S(2)}, u32[]{:S(2)}) collective-permute-start(bf16[64,2048]{1,0:T(8,128)(2,1)S(1)} %get-tuple-element.53), channel_id=1, source_target_pairs={{0,2},{2,0},{4,6},{6,4},{8,10},{10,8},{12,14},{14,12},{1,3},{3,1},... | collective-permute-start | bytes 786440 | tf_op jit(solution)/shard_map/ppermute | solution.py:271
  34.6 4.1 %collective-permute-done.11 = bf16[384,128]{1,0:T(8,128)(2,1)S(1)} collective-permute-done((bf16[384,128]{1,0:T(8,128)(2,1)S(1)}, bf16[384,128]{1,0:T(8,128)(2,1)S(1)}, u32[]{:S(2)}, u32[]{:S(2)}) %collective-permute-start.11) | collective-permute-done | bytes 98336 | tf_op jit(solution)/shard_map/ppermute | solution.py:271
  38.9 0.6 %collective-permute-start.17 = (bf16[32,2048]{1,0:T(8,128)(2,1)S(1)}, bf16[32,2048]{1,0:T(8,128)(2,1)S(1)}, u32[]{:S(2)}, u32[]{:S(2)}) collective-permute-start(bf16[32,2048]{1,0:T(8,128)(2,1)S(1)} %get-tuple-element.65), channel_id=1, source_target_pairs={{0,2},{2,0},{4,6},{6,4},{8,10},{10,8},{12,14},{14,12},{1,3},{3,1},... | collective-permute-start | bytes 393224 | tf_op jit(solution)/shard_map/ppermute | solution.py:271
  39.5 1.5 %collective-permute-done.15.refs_1_ = bf16[32,2048]{1,0:T(8,128)(2,1)S(1)} collective-permute-done((bf16[32,2048]{1,0:T(8,128)(2,1)S(1)}, bf16[32,2048]{1,0:T(8,128)(2,1)S(1)}, u32[]{:S(2)}, u32[]{:S(2)}) %collective-permute-start.15) | collective-permute-done | bytes 131104 | tf_op jit(solution)/shard_map/ppermute | solution.py:271
  40.9 0.7 %collective-permute-done.13.refs_0_ = bf16[64,2048]{1,0:T(8,128)(2,1)S(1)} collective-permute-done((bf16[64,2048]{1,0:T(8,128)(2,1)S(1)}, bf16[64,2048]{1,0:T(8,128)(2,1)S(1)}, u32[]{:S(2)}, u32[]{:S(2)}) %collective-permute-start.13) | collective-permute-done | bytes 262176 | tf_op jit(solution)/shard_map/ppermute | solution.py:271
  41.7 1.8 %collective-permute-done.12 = bf16[384,128]{1,0:T(8,128)(2,1)S(1)} collective-permute-done((bf16[384,128]{1,0:T(8,128)(2,1)S(1)}, bf16[384,128]{1,0:T(8,128)(2,1)S(1)}, u32[]{:S(2)}, u32[]{:S(2)}) %collective-permute-start.12) | collective-permute-done | bytes 98336 | tf_op jit(solution)/shard_map/ppermute | solution.py:271
  43.5 1.5 %collective-permute-start.19 = (bf16[32,2048]{1,0:T(8,128)(2,1)S(1)}, bf16[32,2048]{1,0:T(8,128)(2,1)S(1)}, u32[]{:S(2)}, u32[]{:S(2)}) collective-permute-start(bf16[32,2048]{1,0:T(8,128)(2,1)S(1)} %shard_map.83), channel_id=1, source_target_pairs={{0,8},{2,10},{4,12},{6,14},{8,0},{10,2},{12,4},{14,6},{1,9},{3,11}... | collective-permute-start | bytes 393224 | tf_op jit(solution)/shard_map/ppermute | solution.py:271
  45.2 0.6 %collective-permute-start.16 = (bf16[384,128]{1,0:T(8,128)(2,1)S(1)}, bf16[384,128]{1,0:T(8,128)(2,1)S(1)}, u32[]{:S(2)}, u32[]{:S(2)}) collective-permute-start(bf16[384,128]{1,0:T(8,128)(2,1)S(1)} %add_convert_fusion.mine), channel_id=1, source_target_pairs={{0,2},{2,0},{4,6},{6,4},{8,10},{10,8},{12,14},{14,12},{1,3},{3,1},... | collective-permute-start | bytes 294920 | tf_op jit(solution)/shard_map/ppermute | solution.py:271
  45.8 0.8 %shard_map.84 = f32[128,1024]{1,0:T(8,128)} custom-call(f32[128,1024]{1,0:T(8,128)S(1)} %get-tuple-element.58.source), custom_call_target="tpu_custom_call" | custom-call | tf_op jit(solution)/shard_map/pallas_call | solution.py:392
  46.6 3.2 %collective-permute-done.16.other = bf16[384,128]{1,0:T(8,128)(2,1)S(1)} collective-permute-done((bf16[384,128]{1,0:T(8,128)(2,1)S(1)}, bf16[384,128]{1,0:T(8,128)(2,1)S(1)}, u32[]{:S(2)}, u32[]{:S(2)}) %collective-permute-start.16) | collective-permute-done | bytes 98336 | tf_op jit(solution)/shard_map/ppermute | solution.py:271
  50.3 1.1 %collective-permute-done.19.refs_2_ = bf16[32,2048]{1,0:T(8,128)(2,1)S(1)} collective-permute-done((bf16[32,2048]{1,0:T(8,128)(2,1)S(1)}, bf16[32,2048]{1,0:T(8,128)(2,1)S(1)}, u32[]{:S(2)}, u32[]{:S(2)}) %collective-permute-start.19) | collective-permute-done | bytes 131104 | tf_op jit(solution)/shard_map/ppermute | solution.py:271
  51.3 0.4 collective-permute-done.18.refs_1_
  51.8 0.9 %shard_map.87 = f32[32,2048]{1,0:T(8,128)} custom-call(f32[8,128]{1,0:T(8,128)S(1)} %get-tuple-element.62.rate, f32[32,2048]{1,0:T(8,128)S(1)} %get-tuple-element.63.base, f32[32,2048]{1,0:T(8,128)S(1)} %get-tuple-element.64.own, bf16[32,2048]{1,0:T(8,128)(2,1)S(1)} %collective-permute-done.17.refs_0_, bf16[32,2048]{1,0:T(8,128)(2,1)S(1)} %collective-permute-done.18.refs_1_, ...), custom_call_target="tpu_custom_call" | custom-call | bytes 16777216 | tf_op jit(solution)/shard_map/pallas_call | solution.py:403
  (26 shorter events, 1.9 us)
Async XLA Ops:
  0.6 13.2 %collective-permute-start.3 = (f32[128,1024]{1,0:T(8,128)}, f32[128,1024]{1,0:T(8,128)S(1)}, u32[]{:S(2)}, u32[]{:S(2)}) collective-permute-start(f32[128,1024]{1,0:T(8,128)} %factor_mine.1), channel_id=1, source_target_pairs={{0,1},{1,0},{2,3},{3,2},{4,5},{5,4},{6,7},{7,6},{8,9},{9,8},{10,11... | collective-permute-start | bytes 1572872 | tf_op jit(solution)/shard_map/ppermute | solution.py:274
  2.1 11.7 %collective-permute-start.2 = (bf16[32,2048]{1,0:T(8,128)(2,1)S(1)}, bf16[32,2048]{1,0:T(8,128)(2,1)S(1)}, u32[]{:S(2)}, u32[]{:S(2)}) collective-permute-start(bf16[32,2048]{1,0:T(8,128)(2,1)S(1)} %convert_element_type.21.refs_0_), channel_id=1, source_target_pairs={{0,8},{2,10},{4,12},{6,14},{8,0},{10,2},{12,4},{14,6},{1,9},{3,11}... | collective-permute-start | bytes 393224 | tf_op jit(solution)/shard_map/ppermute | solution.py:271
  5.8 8.1 %collective-permute-start.1 = (bf16[32,2048]{1,0:T(8,128)(2,1)S(1)}, bf16[32,2048]{1,0:T(8,128)(2,1)S(1)}, u32[]{:S(2)}, u32[]{:S(2)}) collective-permute-start(bf16[32,2048]{1,0:T(8,128)(2,1)S(1)} %convert_element_type.21.refs_0_), channel_id=1, source_target_pairs={{0,4},{2,6},{4,0},{6,2},{8,12},{10,14},{12,8},{14,10},{1,5},{3,7},... | collective-permute-start | bytes 393224 | tf_op jit(solution)/shard_map/ppermute | solution.py:271
  7.4 6.5 %collective-permute-start = (bf16[32,2048]{1,0:T(8,128)(2,1)S(1)}, bf16[32,2048]{1,0:T(8,128)(2,1)S(1)}, u32[]{:S(2)}, u32[]{:S(2)}) collective-permute-start(bf16[32,2048]{1,0:T(8,128)(2,1)S(1)} %convert_element_type.21.refs_0_), channel_id=1, source_target_pairs={{0,2},{2,0},{4,6},{6,4},{8,10},{10,8},{12,14},{14,12},{1,3},{3,1},... | collective-permute-start | bytes 393224 | tf_op jit(solution)/shard_map/ppermute | solution.py:271
  8.9 8.0 %collective-permute-start.6 = (bf16[32,2048]{1,0:T(8,128)(2,1)S(1)}, bf16[32,2048]{1,0:T(8,128)(2,1)S(1)}, u32[]{:S(2)}, u32[]{:S(2)}) collective-permute-start(bf16[32,2048]{1,0:T(8,128)(2,1)S(1)} %convert_element_type.21.refs_0_), channel_id=1, source_target_pairs={{0,12},{2,14},{4,8},{6,10},{8,4},{10,6},{12,0},{14,2},{1,13},{3,15... | collective-permute-start | bytes 393224 | tf_op jit(solution)/shard_map/ppermute | solution.py:271
  13.9 11.7 %copy-start.1 = (f32[128,1024]{1,0:T(8,128)S(1)}, f32[128,1024]{1,0:T(8,128)}, u32[]{:S(2)}) copy-start(f32[128,1024]{1,0:T(8,128)} %factor_mine.1) | copy-start | bytes 1572868
  13.9 5.7 %collective-permute-start.4 = (bf16[32,2048]{1,0:T(8,128)(2,1)S(1)}, bf16[32,2048]{1,0:T(8,128)(2,1)S(1)}, u32[]{:S(2)}, u32[]{:S(2)}) collective-permute-start(bf16[32,2048]{1,0:T(8,128)(2,1)S(1)} %collective-permute-done.refs_1_), channel_id=1, source_target_pairs={{0,4},{2,6},{4,0},{6,2},{8,12},{10,14},{12,8},{14,10},{1,5},{3,7},... | collective-permute-start | bytes 393224 | tf_op jit(solution)/shard_map/ppermute | solution.py:271
  15.0 6.0 %collective-permute-start.5 = (bf16[32,2048]{1,0:T(8,128)(2,1)S(1)}, bf16[32,2048]{1,0:T(8,128)(2,1)S(1)}, u32[]{:S(2)}, u32[]{:S(2)}) collective-permute-start(bf16[32,2048]{1,0:T(8,128)(2,1)S(1)} %collective-permute-done.2.refs_4_), channel_id=1, source_target_pairs={{0,2},{2,0},{4,6},{6,4},{8,10},{10,8},{12,14},{14,12},{1,3},{3,1},... | collective-permute-start | bytes 393224 | tf_op jit(solution)/shard_map/ppermute | solution.py:271
  16.8 5.9 %collective-permute-start.7 = (bf16[32,2048]{1,0:T(8,128)(2,1)S(1)}, bf16[32,2048]{1,0:T(8,128)(2,1)S(1)}, u32[]{:S(2)}, u32[]{:S(2)}) collective-permute-start(bf16[32,2048]{1,0:T(8,128)(2,1)S(1)} %collective-permute-done.6.refs_6_), channel_id=1, source_target_pairs={{0,2},{2,0},{4,6},{6,4},{8,10},{10,8},{12,14},{14,12},{1,3},{3,1},... | collective-permute-start | bytes 393224 | tf_op jit(solution)/shard_map/ppermute | solution.py:271
  22.2 3.4 %collective-permute-start.9 = (bf16[112,1024]{1,0:T(8,128)(2,1)S(1)}, bf16[112,1024]{1,0:T(8,128)(2,1)S(1)}, u32[]{:S(2)}, u32[]{:S(2)}) collective-permute-start(bf16[112,1024]{1,0:T(8,128)(2,1)S(1)} %get-tuple-element.47), channel_id=1, source_target_pairs={{0,1},{1,0},{2,3},{3,2},{4,5},{5,4},{6,7},{7,6},{8,9},{9,8},{10,11... | collective-permute-start | bytes 688136 | tf_op jit(solution)/shard_map/ppermute | solution.py:274
  22.2 3.3 %collective-permute-start.10 = (bf16[112,1024]{1,0:T(8,128)(2,1)S(1)}, bf16[112,1024]{1,0:T(8,128)(2,1)S(1)}, u32[]{:S(2)}, u32[]{:S(2)}) collective-permute-start(bf16[112,1024]{1,0:T(8,128)(2,1)S(1)} %get-tuple-element.48), channel_id=1, source_target_pairs={{0,1},{1,0},{2,3},{3,2},{4,5},{5,4},{6,7},{7,6},{8,9},{9,8},{10,11... | collective-permute-start | bytes 688136 | tf_op jit(solution)/shard_map/ppermute | solution.py:274
  24.0 1.5 %collective-permute-start.8 = (bf16[96,1024]{1,0:T(8,128)(2,1)S(1)}, bf16[96,1024]{1,0:T(8,128)(2,1)S(1)}, u32[]{:S(2)}, u32[]{:S(2)}) collective-permute-start(bf16[96,1024]{1,0:T(8,128)(2,1)S(1)} %get-tuple-element.45), channel_id=1, source_target_pairs={{0,1},{1,0},{2,3},{3,2},{4,5},{5,4},{6,7},{7,6},{8,9},{9,8},{10,11... | collective-permute-start | bytes 589832 | tf_op jit(solution)/shard_map/ppermute | solution.py:274
  27.1 22.8 %copy-start = (f32[32,2048]{1,0:T(8,128)S(1)}, f32[32,2048]{1,0:T(8,128)}, u32[]{:S(2)}) copy-start(f32[32,2048]{1,0:T(8,128)} %factor.1) | copy-start | bytes 786436
  27.1 7.1 %collective-permute-start.14 = (bf16[32,2048]{1,0:T(8,128)(2,1)S(1)}, bf16[32,2048]{1,0:T(8,128)(2,1)S(1)}, u32[]{:S(2)}, u32[]{:S(2)}) collective-permute-start(bf16[32,2048]{1,0:T(8,128)(2,1)S(1)} %get-tuple-element.55), channel_id=1, source_target_pairs={{0,2},{2,0},{4,6},{6,4},{8,10},{10,8},{12,14},{14,12},{1,3},{3,1},... | collective-permute-start | bytes 393224 | tf_op jit(solution)/shard_map/ppermute | solution.py:271
  30.0 8.8 %collective-permute-start.11 = (bf16[384,128]{1,0:T(8,128)(2,1)S(1)}, bf16[384,128]{1,0:T(8,128)(2,1)S(1)}, u32[]{:S(2)}, u32[]{:S(2)}) collective-permute-start(bf16[384,128]{1,0:T(8,128)(2,1)S(1)} %get-tuple-element.51), channel_id=1, source_target_pairs={{0,8},{2,10},{4,12},{6,14},{8,0},{10,2},{12,4},{14,6},{1,9},{3,11}... | collective-permute-start | bytes 294920 | tf_op jit(solution)/shard_map/ppermute | solution.py:271
  33.7 7.9 %collective-permute-start.13 = (bf16[64,2048]{1,0:T(8,128)(2,1)S(1)}, bf16[64,2048]{1,0:T(8,128)(2,1)S(1)}, u32[]{:S(2)}, u32[]{:S(2)}) collective-permute-start(bf16[64,2048]{1,0:T(8,128)(2,1)S(1)} %get-tuple-element.53), channel_id=1, source_target_pairs={{0,2},{2,0},{4,6},{6,4},{8,10},{10,8},{12,14},{14,12},{1,3},{3,1},... | collective-permute-start | bytes 786440 | tf_op jit(solution)/shard_map/ppermute | solution.py:271
  34.3 6.6 %collective-permute-start.15 = (bf16[32,2048]{1,0:T(8,128)(2,1)S(1)}, bf16[32,2048]{1,0:T(8,128)(2,1)S(1)}, u32[]{:S(2)}, u32[]{:S(2)}) collective-permute-start(bf16[32,2048]{1,0:T(8,128)(2,1)S(1)} %shard_map.82), channel_id=1, source_target_pairs={{0,4},{2,6},{4,0},{6,2},{8,12},{10,14},{12,8},{14,10},{1,5},{3,7},... | collective-permute-start | bytes 393224 | tf_op jit(solution)/shard_map/ppermute | solution.py:271
  38.8 4.7 %collective-permute-start.12 = (bf16[384,128]{1,0:T(8,128)(2,1)S(1)}, bf16[384,128]{1,0:T(8,128)(2,1)S(1)}, u32[]{:S(2)}, u32[]{:S(2)}) collective-permute-start(bf16[384,128]{1,0:T(8,128)(2,1)S(1)} %add_convert_fusion.1), channel_id=1, source_target_pairs={{0,4},{2,6},{4,0},{6,2},{8,12},{10,14},{12,8},{14,10},{1,5},{3,7},... | collective-permute-start | bytes 294920 | tf_op jit(solution)/shard_map/ppermute | solution.py:271
  38.9 11.4 %collective-permute-start.17 = (bf16[32,2048]{1,0:T(8,128)(2,1)S(1)}, bf16[32,2048]{1,0:T(8,128)(2,1)S(1)}, u32[]{:S(2)}, u32[]{:S(2)}) collective-permute-start(bf16[32,2048]{1,0:T(8,128)(2,1)S(1)} %get-tuple-element.65), channel_id=1, source_target_pairs={{0,2},{2,0},{4,6},{6,4},{8,10},{10,8},{12,14},{14,12},{1,3},{3,1},... | collective-permute-start | bytes 393224 | tf_op jit(solution)/shard_map/ppermute | solution.py:271
  43.5 7.9 %collective-permute-start.19 = (bf16[32,2048]{1,0:T(8,128)(2,1)S(1)}, bf16[32,2048]{1,0:T(8,128)(2,1)S(1)}, u32[]{:S(2)}, u32[]{:S(2)}) collective-permute-start(bf16[32,2048]{1,0:T(8,128)(2,1)S(1)} %shard_map.83), channel_id=1, source_target_pairs={{0,8},{2,10},{4,12},{6,14},{8,0},{10,2},{12,4},{14,6},{1,9},{3,11}... | collective-permute-start | bytes 393224 | tf_op jit(solution)/shard_map/ppermute | solution.py:271
  45.1 6.7 %collective-permute-start.18 = (bf16[32,2048]{1,0:T(8,128)(2,1)S(1)}, bf16[32,2048]{1,0:T(8,128)(2,1)S(1)}, u32[]{:S(2)}, u32[]{:S(2)}) collective-permute-start(bf16[32,2048]{1,0:T(8,128)(2,1)S(1)} %shard_map.86), channel_id=1, source_target_pairs={{0,4},{2,6},{4,0},{6,2},{8,12},{10,14},{12,8},{14,10},{1,5},{3,7},... | collective-permute-start | bytes 393224 | tf_op jit(solution)/shard_map/ppermute | solution.py:271
  45.2 4.7 %collective-permute-start.16 = (bf16[384,128]{1,0:T(8,128)(2,1)S(1)}, bf16[384,128]{1,0:T(8,128)(2,1)S(1)}, u32[]{:S(2)}, u32[]{:S(2)}) collective-permute-start(bf16[384,128]{1,0:T(8,128)(2,1)S(1)} %add_convert_fusion.mine), channel_id=1, source_target_pairs={{0,2},{2,0},{4,6},{6,4},{8,10},{10,8},{12,14},{14,12},{1,3},{3,1},... | collective-permute-start | bytes 294920 | tf_op jit(solution)/shard_map/ppermute | solution.py:271

commit v15 on v14

--- a/solution.py
+++ b/solution.py
@@ -235,7 +235,7 @@
     refs[-1][...] = coded(total)
 
 
-def base_body(mine, other, panel, factor, base, rate_out, gram):
+def base_body(mine, other, panel, factor, summed, base, rate_out, gram):
     half = mine.shape[0] // 3
     quarters = mine[...].astype(jnp.float32) + other[...].astype(jnp.float32)
     upper, side, lower = quarters[:half], quarters[half : 2 * half], quarters[2 * half :]
@@ -384,7 +384,7 @@
     across = add_up(0, keep_second, arrived[1], through)
     gram = (gram.astype(jnp.float32) + gram_arrived.astype(jnp.float32)).astype(jnp.bfloat16)
     gram_arrived = swap(gram, 2)
-    gram_arrived, across = lax.optimization_barrier((gram_arrived, across))
+    gram_arrived, summed = lax.optimization_barrier((gram_arrived, across))
     across = swap(across, 4)
     gram = (gram.astype(jnp.float32) + gram_arrived.astype(jnp.float32)).astype(jnp.bfloat16)
     partner = swap(gram, 1)
@@ -395,11 +395,11 @@
         base_body,
         (wide(size, jnp.float32), shape((8, 128), jnp.float32)),
         0,
-        4,
+        5,
         0,
         0,
         [pltpu.VMEM((kdim, kdim), jnp.float32)],
-    )(gram, partner, panel, gene_factor)
+    )(gram, partner, panel, gene_factor, summed)
     gene_next = call(last_body, wide(size, jnp.float32), 0, 6, 0, AHEAD)(
         rate, base, own, arrived[2], beside, across
     )

time: 52.9 us -> 51.4 us (0.972)
  waiting for transfers between devices: 17.4 us -> 15.4 us
    ppermute x16, waiting for transfers between devices: 15.9 us -> 14 us  [swap(): return lax.ppermute(value, 'cell', [(n, n ^ bits) for n in range(n_cell)])]
  transfers between devices with their start and end apart: 20 -> 20, of which waited for: 12 -> 11; matrix products, arithmetic and copies ran while one was open for 2% -> 2% of each run, Pallas kernels for 17% -> 18%
where the time goes in v15:
time: 51.4 us; the launch traced here: 51.1 us
  starting transfers between devices  21.7 us (42%)
  waiting for transfers between devices  15.4 us (30%)
  Pallas kernels  11.5 us (22%)
  between operations  1.43 us (3%)
  other arithmetic  1.02 us (2%)
    ppermute x16, starting transfers between devices, swap(): return lax.ppermute(value, 'cell', [(n, n ^ bits) for n in range(n_cell)])  20.6 us
    ppermute x16, waiting for transfers between devices, swap(): return lax.ppermute(value, 'cell', [(n, n ^ bits) for n in range(n_cell)])  14 us
    pallas_call x1, Pallas kernels, dense_tile(): pl.pallas_call(dense_body, out_shape=(shape((CELL_DEV, GENE_DEV), jnp.bfl...  4.09 us
    pallas_call x1, Pallas kernels, shards(): call(functools.partial(cell_body, order, [7], n_parts), (shape(cell_facto...  1.57 us
    ppermute x4, waiting for transfers between devices, swap_core(): return lax.ppermute(value, 'gene', [(0, 1), (1, 0)])  1.42 us
    pallas_call x1, Pallas kernels, shards(): call(functools.partial(keep_body, sent + kept), (shape((3 * kdim // 2, kd...  1.28 us
    pallas_call x1, Pallas kernels, shards(): call(functools.partial(second_body, order), (wide(kdim, jnp.bfloat16), sh...  1.21 us
    ppermute x4, starting transfers between devices, swap_core(): return lax.ppermute(value, 'gene', [(0, 1), (1, 0)])  1.18 us
  transfers between devices with their start and end apart: 20, of which 11 were waited for; matrix products, arithmetic and copies ran while one was open for 2% of the time, Pallas kernels for 18%

profile of v15, /device:TPU:0, one launch (start us, length us, event | category | flops | bytes accessed | tf_op | source)
XLA Modules:
  0.0 51.1 jit_solution(13642043831238748510)
XLA Ops:
  0.6 0.5 %collective-permute-start.3 = (f32[128,1024]{1,0:T(8,128)}, f32[128,1024]{1,0:T(8,128)S(1)}, u32[]{:S(2)}, u32[]{:S(2)}) collective-permute-start(f32[128,1024]{1,0:T(8,128)} %factor_mine.1), channel_id=1, source_target_pairs={{0,1},{1,0},{2,3},{3,2},{4,5},{5,4},{6,7},{7,6},{8,9},{9,8},{10,11... | collective-permute-start | bytes 1572872 | tf_op jit(solution)/shard_map/ppermute | solution.py:274
  1.1 1.0 %convert_element_type.21.refs_0_ = bf16[32,2048]{1,0:T(8,128)(2,1)S(1)} convert(f32[32,2048]{1,0:T(8,128)} %factor.1) | non-fusion elementwise | flops 65536 | bytes 393216 | tf_op jit(solution)/shard_map/convert_element_type | solution.py:279
  2.1 3.7 %collective-permute-start.2 = (bf16[32,2048]{1,0:T(8,128)(2,1)S(1)}, bf16[32,2048]{1,0:T(8,128)(2,1)S(1)}, u32[]{:S(2)}, u32[]{:S(2)}) collective-permute-start(bf16[32,2048]{1,0:T(8,128)(2,1)S(1)} %convert_element_type.21.refs_0_), channel_id=1, source_target_pairs={{0,8},{2,10},{4,12},{6,14},{8,0},{10,2},{12,4},{14,6},{1,9},{3,11}... | collective-permute-start | bytes 393224 | tf_op jit(solution)/shard_map/ppermute | solution.py:271
  5.8 1.6 %collective-permute-start.1 = (bf16[32,2048]{1,0:T(8,128)(2,1)S(1)}, bf16[32,2048]{1,0:T(8,128)(2,1)S(1)}, u32[]{:S(2)}, u32[]{:S(2)}) collective-permute-start(bf16[32,2048]{1,0:T(8,128)(2,1)S(1)} %convert_element_type.21.refs_0_), channel_id=1, source_target_pairs={{0,4},{2,6},{4,0},{6,2},{8,12},{10,14},{12,8},{14,10},{1,5},{3,7},... | collective-permute-start | bytes 393224 | tf_op jit(solution)/shard_map/ppermute | solution.py:271
  7.4 1.5 %collective-permute-start = (bf16[32,2048]{1,0:T(8,128)(2,1)S(1)}, bf16[32,2048]{1,0:T(8,128)(2,1)S(1)}, u32[]{:S(2)}, u32[]{:S(2)}) collective-permute-start(bf16[32,2048]{1,0:T(8,128)(2,1)S(1)} %convert_element_type.21.refs_0_), channel_id=1, source_target_pairs={{0,2},{2,0},{4,6},{6,4},{8,10},{10,8},{12,14},{14,12},{1,3},{3,1},... | collective-permute-start | bytes 393224 | tf_op jit(solution)/shard_map/ppermute | solution.py:271
  9.7 4.1 %shard_map.77 = (bf16[1024,2048]{1,0:T(8,128)(2,1)S(1)}, bf16[2048,1024]{1,0:T(8,128)(2,1)S(1)}) custom-call(s32[64]{0:T(128)} %bitcast.6, s32[64]{0:T(128)} %bitcast.7, s32[1]{0:T(128)} %bitcast.4.count, bf16[64,128,128]{2,1,0:T(8,128)(2,1)} %bitcast.5), custom_call_target="tpu_custom_call" | custom-call | tf_op jit(solution)/shard_map/pallas_call | solution.py:88
  13.9 1.1 %collective-permute-start.4 = (bf16[32,2048]{1,0:T(8,128)(2,1)S(1)}, bf16[32,2048]{1,0:T(8,128)(2,1)S(1)}, u32[]{:S(2)}, u32[]{:S(2)}) collective-permute-start(bf16[32,2048]{1,0:T(8,128)(2,1)S(1)} %collective-permute-done.refs_1_), channel_id=1, source_target_pairs={{0,4},{2,6},{4,0},{6,2},{8,12},{10,14},{12,8},{14,10},{1,5},{3,7},... | collective-permute-start | bytes 393224 | tf_op jit(solution)/shard_map/ppermute | solution.py:271
  15.0 1.5 %collective-permute-start.5 = (bf16[32,2048]{1,0:T(8,128)(2,1)S(1)}, bf16[32,2048]{1,0:T(8,128)(2,1)S(1)}, u32[]{:S(2)}, u32[]{:S(2)}) collective-permute-start(bf16[32,2048]{1,0:T(8,128)(2,1)S(1)} %collective-permute-done.2.refs_4_), channel_id=1, source_target_pairs={{0,2},{2,0},{4,6},{6,4},{8,10},{10,8},{12,14},{14,12},{1,3},{3,1},... | collective-permute-start | bytes 393224 | tf_op jit(solution)/shard_map/ppermute | solution.py:271
  16.5 0.4 collective-permute-done.6.refs_6_
  16.8 1.5 %collective-permute-start.7 = (bf16[32,2048]{1,0:T(8,128)(2,1)S(1)}, bf16[32,2048]{1,0:T(8,128)(2,1)S(1)}, u32[]{:S(2)}, u32[]{:S(2)}) collective-permute-start(bf16[32,2048]{1,0:T(8,128)(2,1)S(1)} %collective-permute-done.6.refs_6_), channel_id=1, source_target_pairs={{0,2},{2,0},{4,6},{6,4},{8,10},{10,8},{12,14},{14,12},{1,3},{3,1},... | collective-permute-start | bytes 393224 | tf_op jit(solution)/shard_map/ppermute | solution.py:271
  18.3 1.3 %collective-permute-done.4.refs_3_ = bf16[32,2048]{1,0:T(8,128)(2,1)S(1)} collective-permute-done((bf16[32,2048]{1,0:T(8,128)(2,1)S(1)}, bf16[32,2048]{1,0:T(8,128)(2,1)S(1)}, u32[]{:S(2)}, u32[]{:S(2)}) %collective-permute-start.4) | collective-permute-done | bytes 131104 | tf_op jit(solution)/shard_map/ppermute | solution.py:271
  19.6 1.4 %collective-permute-done.5.refs_5_ = bf16[32,2048]{1,0:T(8,128)(2,1)S(1)} collective-permute-done((bf16[32,2048]{1,0:T(8,128)(2,1)S(1)}, bf16[32,2048]{1,0:T(8,128)(2,1)S(1)}, u32[]{:S(2)}, u32[]{:S(2)}) %collective-permute-start.5) | collective-permute-done | bytes 131104 | tf_op jit(solution)/shard_map/ppermute | solution.py:271
  21.0 1.1 %shard_map.78 = (bf16[224,2048]{1,0:T(8,128)(2,1)S(1)}, f32[224,1024]{1,0:T(8,128)S(1)}, bf16[112,1024]{1,0:T(8,128)(2,1)S(1)}, bf16[112,1024]{1,0:T(8,128)(2,1)S(1)}) custom-call(bf16[2048,1024]{1,0:T(8,128)(2,1)S(1)} %get-tuple-element.38.turned, bf16[32,2048]{1,0:T(8,128)(2,1)S(1)} %convert_element_type.21.refs_0_, ...), custom_call_target="tpu_custom_call" | custom-call | bytes 16777216 | tf_op jit(solution)/shard_map/pallas_call | solution.py:300
  22.2 0.5 collective-permute-start.10
  22.8 1.2 %shard_map.79 = (bf16[256,2048]{1,0:T(8,128)(2,1)S(1)}, f32[96,1024]{1,0:T(8,128)S(1)}, bf16[96,1024]{1,0:T(8,128)(2,1)S(1)}) custom-call(bf16[2048,1024]{1,0:T(8,128)(2,1)S(1)} %get-tuple-element.38.turned, bf16[224,2048]{1,0:T(8,128)(2,1)S(1)} %get-tuple-element.43.first, bf16[32,2048]{1,0:T(8,128)(2,1)S(1)} %collective-permute-done.7.share), custom_call_target="tpu_custom_call" | custom-call | tf_op jit(solution)/shard_map/pallas_call | solution.py:314
  24.1 1.4 %collective-permute-done.8.other = bf16[96,1024]{1,0:T(8,128)(2,1)S(1)} collective-permute-done((bf16[96,1024]{1,0:T(8,128)(2,1)S(1)}, bf16[96,1024]{1,0:T(8,128)(2,1)S(1)}, u32[]{:S(2)}, u32[]{:S(2)}) %collective-permute-start.8) | collective-permute-done | bytes 196640 | tf_op jit(solution)/shard_map/ppermute | solution.py:274
  25.5 1.6 %shard_map.80 = (f32[128,1024]{1,0:T(8,128)S(1)}, bf16[256,1024]{1,0:T(8,128)(2,1)S(1)}, bf16[32,2048]{1,0:T(8,128)(2,1)S(1)}) custom-call(bf16[1024,2048]{1,0:T(8,128)(2,1)S(1)} %get-tuple-element.37.tile, f32[224,1024]{1,0:T(8,128)S(1)} %get-tuple-element.42.mine_first, f32[96,1024]{1,0:T(8,128)S(1)} %get-tuple-element.44.mine, ...), custom_call_target="tpu_custom_call" | custom-call | tf_op jit(solution)/shard_map/pallas_call | solution.py:330
  27.1 1.6 %collective-permute-start.14 = (bf16[32,2048]{1,0:T(8,128)(2,1)S(1)}, bf16[32,2048]{1,0:T(8,128)(2,1)S(1)}, u32[]{:S(2)}, u32[]{:S(2)}) collective-permute-start(bf16[32,2048]{1,0:T(8,128)(2,1)S(1)} %get-tuple-element.55), channel_id=1, source_target_pairs={{0,2},{2,0},{4,6},{6,4},{8,10},{10,8},{12,14},{14,12},{1,3},{3,1},... | collective-permute-start | bytes 393224 | tf_op jit(solution)/shard_map/ppermute | solution.py:271
  28.7 1.3 %shard_map.81 = (bf16[384,128]{1,0:T(8,128)(2,1)S(1)}, bf16[64,2048]{1,0:T(8,128)(2,1)S(1)}, bf16[32,2048]{1,0:T(8,128)(2,1)S(1)}, f32[32,2048]{1,0:T(8,128)S(1)...) custom-call(bf16[256,1024]{1,0:T(8,128)(2,1)S(1)} %get-tuple-element.49.low, ...), custom_call_target="tpu_custom_call" | custom-call | bytes 16777216 | tf_op jit(solution)/shard_map/pallas_call | solution.py:361
  30.0 3.8 %collective-permute-start.11 = (bf16[384,128]{1,0:T(8,128)(2,1)S(1)}, bf16[384,128]{1,0:T(8,128)(2,1)S(1)}, u32[]{:S(2)}, u32[]{:S(2)}) collective-permute-start(bf16[384,128]{1,0:T(8,128)(2,1)S(1)} %get-tuple-element.51), channel_id=1, source_target_pairs={{0,8},{2,10},{4,12},{6,14},{8,0},{10,2},{12,4},{14,6},{1,9},{3,11}... | collective-permute-start | bytes 294920 | tf_op jit(solution)/shard_map/ppermute | solution.py:271
  33.7 0.5 %collective-permute-start.13 = (bf16[64,2048]{1,0:T(8,128)(2,1)S(1)}, bf16[64,2048]{1,0:T(8,128)(2,1)S(1)}, u32[]{:S(2)}, u32[]{:S(2)}) collective-permute-start(bf16[64,2048]{1,0:T(8,128)(2,1)S(1)} %get-tuple-element.53), channel_id=1, source_target_pairs={{0,2},{2,0},{4,6},{6,4},{8,10},{10,8},{12,14},{14,12},{1,3},{3,1},... | collective-permute-start | bytes 786440 | tf_op jit(solution)/shard_map/ppermute | solution.py:271
  34.6 4.1 %collective-permute-done.11 = bf16[384,128]{1,0:T(8,128)(2,1)S(1)} collective-permute-done((bf16[384,128]{1,0:T(8,128)(2,1)S(1)}, bf16[384,128]{1,0:T(8,128)(2,1)S(1)}, u32[]{:S(2)}, u32[]{:S(2)}) %collective-permute-start.11) | collective-permute-done | bytes 98336 | tf_op jit(solution)/shard_map/ppermute | solution.py:271
  38.9 0.6 %collective-permute-start.17 = (bf16[32,2048]{1,0:T(8,128)(2,1)S(1)}, bf16[32,2048]{1,0:T(8,128)(2,1)S(1)}, u32[]{:S(2)}, u32[]{:S(2)}) collective-permute-start(bf16[32,2048]{1,0:T(8,128)(2,1)S(1)} %get-tuple-element.66), channel_id=1, source_target_pairs={{0,2},{2,0},{4,6},{6,4},{8,10},{10,8},{12,14},{14,12},{1,3},{3,1},... | collective-permute-start | bytes 393224 | tf_op jit(solution)/shard_map/ppermute | solution.py:271
  39.5 1.5 %collective-permute-done.15.refs_1_ = bf16[32,2048]{1,0:T(8,128)(2,1)S(1)} collective-permute-done((bf16[32,2048]{1,0:T(8,128)(2,1)S(1)}, bf16[32,2048]{1,0:T(8,128)(2,1)S(1)}, u32[]{:S(2)}, u32[]{:S(2)}) %collective-permute-start.15) | collective-permute-done | bytes 131104 | tf_op jit(solution)/shard_map/ppermute | solution.py:271
  40.9 0.7 %collective-permute-done.13.refs_0_ = bf16[64,2048]{1,0:T(8,128)(2,1)S(1)} collective-permute-done((bf16[64,2048]{1,0:T(8,128)(2,1)S(1)}, bf16[64,2048]{1,0:T(8,128)(2,1)S(1)}, u32[]{:S(2)}, u32[]{:S(2)}) %collective-permute-start.13) | collective-permute-done | bytes 262176 | tf_op jit(solution)/shard_map/ppermute | solution.py:271
  41.7 1.4 %collective-permute-start.19 = (bf16[32,2048]{1,0:T(8,128)(2,1)S(1)}, bf16[32,2048]{1,0:T(8,128)(2,1)S(1)}, u32[]{:S(2)}, u32[]{:S(2)}) collective-permute-start(bf16[32,2048]{1,0:T(8,128)(2,1)S(1)} %shard_map.83.summed), channel_id=1, source_target_pairs={{0,8},{2,10},{4,12},{6,14},{8,0},{10,2},{12,4},{14,6},{1,9},{3,11}... | collective-permute-start | bytes 393224 | tf_op jit(solution)/shard_map/ppermute | solution.py:271
  43.8 1.0 %collective-permute-start.16 = (bf16[384,128]{1,0:T(8,128)(2,1)S(1)}, bf16[384,128]{1,0:T(8,128)(2,1)S(1)}, u32[]{:S(2)}, u32[]{:S(2)}) collective-permute-start(bf16[384,128]{1,0:T(8,128)(2,1)S(1)} %add_convert_fusion.mine), channel_id=1, source_target_pairs={{0,2},{2,0},{4,6},{6,4},{8,10},{10,8},{12,14},{14,12},{1,3},{3,1},... | collective-permute-start | bytes 294920 | tf_op jit(solution)/shard_map/ppermute | solution.py:271
  44.8 0.8 %shard_map.84 = f32[128,1024]{1,0:T(8,128)} custom-call(f32[128,1024]{1,0:T(8,128)S(1)} %get-tuple-element.58.source), custom_call_target="tpu_custom_call" | custom-call | tf_op jit(solution)/shard_map/pallas_call | solution.py:392
  45.7 2.8 %collective-permute-done.16.other = bf16[384,128]{1,0:T(8,128)(2,1)S(1)} collective-permute-done((bf16[384,128]{1,0:T(8,128)(2,1)S(1)}, bf16[384,128]{1,0:T(8,128)(2,1)S(1)}, u32[]{:S(2)}, u32[]{:S(2)}) %collective-permute-start.16) | collective-permute-done | bytes 98336 | tf_op jit(solution)/shard_map/ppermute | solution.py:271
  48.5 0.4 shard_map.85
  48.9 1.4 %collective-permute-done.18.refs_1_ = bf16[32,2048]{1,0:T(8,128)(2,1)S(1)} collective-permute-done((bf16[32,2048]{1,0:T(8,128)(2,1)S(1)}, bf16[32,2048]{1,0:T(8,128)(2,1)S(1)}, u32[]{:S(2)}, u32[]{:S(2)}) %collective-permute-start.18) | collective-permute-done | bytes 131104 | tf_op jit(solution)/shard_map/ppermute | solution.py:271
  50.3 0.9 %shard_map.87 = f32[32,2048]{1,0:T(8,128)} custom-call(f32[8,128]{1,0:T(8,128)S(1)} %get-tuple-element.63.rate, f32[32,2048]{1,0:T(8,128)S(1)} %get-tuple-element.64.base, f32[32,2048]{1,0:T(8,128)S(1)} %get-tuple-element.65.own, bf16[32,2048]{1,0:T(8,128)(2,1)S(1)} %collective-permute-done.17.refs_0_, bf16[32,2048]{1,0:T(8,128)(2,1)S(1)} %collective-permute-done.18.refs_1_, ...), custom_call_target="tpu_custom_call" | custom-call | bytes 16777216 | tf_op jit(solution)/shard_map/pallas_call | solution.py:403
  (26 shorter events, 1.7 us)
Async XLA Ops:
  0.6 13.2 %collective-permute-start.3 = (f32[128,1024]{1,0:T(8,128)}, f32[128,1024]{1,0:T(8,128)S(1)}, u32[]{:S(2)}, u32[]{:S(2)}) collective-permute-start(f32[128,1024]{1,0:T(8,128)} %factor_mine.1), channel_id=1, source_target_pairs={{0,1},{1,0},{2,3},{3,2},{4,5},{5,4},{6,7},{7,6},{8,9},{9,8},{10,11... | collective-permute-start | bytes 1572872 | tf_op jit(solution)/shard_map/ppermute | solution.py:274
  2.1 11.7 %collective-permute-start.2 = (bf16[32,2048]{1,0:T(8,128)(2,1)S(1)}, bf16[32,2048]{1,0:T(8,128)(2,1)S(1)}, u32[]{:S(2)}, u32[]{:S(2)}) collective-permute-start(bf16[32,2048]{1,0:T(8,128)(2,1)S(1)} %convert_element_type.21.refs_0_), channel_id=1, source_target_pairs={{0,8},{2,10},{4,12},{6,14},{8,0},{10,2},{12,4},{14,6},{1,9},{3,11}... | collective-permute-start | bytes 393224 | tf_op jit(solution)/shard_map/ppermute | solution.py:271
  5.8 8.1 %collective-permute-start.1 = (bf16[32,2048]{1,0:T(8,128)(2,1)S(1)}, bf16[32,2048]{1,0:T(8,128)(2,1)S(1)}, u32[]{:S(2)}, u32[]{:S(2)}) collective-permute-start(bf16[32,2048]{1,0:T(8,128)(2,1)S(1)} %convert_element_type.21.refs_0_), channel_id=1, source_target_pairs={{0,4},{2,6},{4,0},{6,2},{8,12},{10,14},{12,8},{14,10},{1,5},{3,7},... | collective-permute-start | bytes 393224 | tf_op jit(solution)/shard_map/ppermute | solution.py:271
  7.4 6.5 %collective-permute-start = (bf16[32,2048]{1,0:T(8,128)(2,1)S(1)}, bf16[32,2048]{1,0:T(8,128)(2,1)S(1)}, u32[]{:S(2)}, u32[]{:S(2)}) collective-permute-start(bf16[32,2048]{1,0:T(8,128)(2,1)S(1)} %convert_element_type.21.refs_0_), channel_id=1, source_target_pairs={{0,2},{2,0},{4,6},{6,4},{8,10},{10,8},{12,14},{14,12},{1,3},{3,1},... | collective-permute-start | bytes 393224 | tf_op jit(solution)/shard_map/ppermute | solution.py:271
  8.9 8.0 %collective-permute-start.6 = (bf16[32,2048]{1,0:T(8,128)(2,1)S(1)}, bf16[32,2048]{1,0:T(8,128)(2,1)S(1)}, u32[]{:S(2)}, u32[]{:S(2)}) collective-permute-start(bf16[32,2048]{1,0:T(8,128)(2,1)S(1)} %convert_element_type.21.refs_0_), channel_id=1, source_target_pairs={{0,12},{2,14},{4,8},{6,10},{8,4},{10,6},{12,0},{14,2},{1,13},{3,15... | collective-permute-start | bytes 393224 | tf_op jit(solution)/shard_map/ppermute | solution.py:271
  13.9 11.7 %copy-start.1 = (f32[128,1024]{1,0:T(8,128)S(1)}, f32[128,1024]{1,0:T(8,128)}, u32[]{:S(2)}) copy-start(f32[128,1024]{1,0:T(8,128)} %factor_mine.1) | copy-start | bytes 1572868
  13.9 5.7 %collective-permute-start.4 = (bf16[32,2048]{1,0:T(8,128)(2,1)S(1)}, bf16[32,2048]{1,0:T(8,128)(2,1)S(1)}, u32[]{:S(2)}, u32[]{:S(2)}) collective-permute-start(bf16[32,2048]{1,0:T(8,128)(2,1)S(1)} %collective-permute-done.refs_1_), channel_id=1, source_target_pairs={{0,4},{2,6},{4,0},{6,2},{8,12},{10,14},{12,8},{14,10},{1,5},{3,7},... | collective-permute-start | bytes 393224 | tf_op jit(solution)/shard_map/ppermute | solution.py:271
  15.0 6.0 %collective-permute-start.5 = (bf16[32,2048]{1,0:T(8,128)(2,1)S(1)}, bf16[32,2048]{1,0:T(8,128)(2,1)S(1)}, u32[]{:S(2)}, u32[]{:S(2)}) collective-permute-start(bf16[32,2048]{1,0:T(8,128)(2,1)S(1)} %collective-permute-done.2.refs_4_), channel_id=1, source_target_pairs={{0,2},{2,0},{4,6},{6,4},{8,10},{10,8},{12,14},{14,12},{1,3},{3,1},... | collective-permute-start | bytes 393224 | tf_op jit(solution)/shard_map/ppermute | solution.py:271
  16.8 5.9 %collective-permute-start.7 = (bf16[32,2048]{1,0:T(8,128)(2,1)S(1)}, bf16[32,2048]{1,0:T(8,128)(2,1)S(1)}, u32[]{:S(2)}, u32[]{:S(2)}) collective-permute-start(bf16[32,2048]{1,0:T(8,128)(2,1)S(1)} %collective-permute-done.6.refs_6_), channel_id=1, source_target_pairs={{0,2},{2,0},{4,6},{6,4},{8,10},{10,8},{12,14},{14,12},{1,3},{3,1},... | collective-permute-start | bytes 393224 | tf_op jit(solution)/shard_map/ppermute | solution.py:271
  22.2 3.4 %collective-permute-start.9 = (bf16[112,1024]{1,0:T(8,128)(2,1)S(1)}, bf16[112,1024]{1,0:T(8,128)(2,1)S(1)}, u32[]{:S(2)}, u32[]{:S(2)}) collective-permute-start(bf16[112,1024]{1,0:T(8,128)(2,1)S(1)} %get-tuple-element.47), channel_id=1, source_target_pairs={{0,1},{1,0},{2,3},{3,2},{4,5},{5,4},{6,7},{7,6},{8,9},{9,8},{10,11... | collective-permute-start | bytes 688136 | tf_op jit(solution)/shard_map/ppermute | solution.py:274
  22.2 3.3 %collective-permute-start.10 = (bf16[112,1024]{1,0:T(8,128)(2,1)S(1)}, bf16[112,1024]{1,0:T(8,128)(2,1)S(1)}, u32[]{:S(2)}, u32[]{:S(2)}) collective-permute-start(bf16[112,1024]{1,0:T(8,128)(2,1)S(1)} %get-tuple-element.48), channel_id=1, source_target_pairs={{0,1},{1,0},{2,3},{3,2},{4,5},{5,4},{6,7},{7,6},{8,9},{9,8},{10,11... | collective-permute-start | bytes 688136 | tf_op jit(solution)/shard_map/ppermute | solution.py:274
  24.0 1.5 %collective-permute-start.8 = (bf16[96,1024]{1,0:T(8,128)(2,1)S(1)}, bf16[96,1024]{1,0:T(8,128)(2,1)S(1)}, u32[]{:S(2)}, u32[]{:S(2)}) collective-permute-start(bf16[96,1024]{1,0:T(8,128)(2,1)S(1)} %get-tuple-element.45), channel_id=1, source_target_pairs={{0,1},{1,0},{2,3},{3,2},{4,5},{5,4},{6,7},{7,6},{8,9},{9,8},{10,11... | collective-permute-start | bytes 589832 | tf_op jit(solution)/shard_map/ppermute | solution.py:274
  27.1 21.4 %copy-start = (f32[32,2048]{1,0:T(8,128)S(1)}, f32[32,2048]{1,0:T(8,128)}, u32[]{:S(2)}) copy-start(f32[32,2048]{1,0:T(8,128)} %factor.1) | copy-start | bytes 786436
  27.1 7.1 %collective-permute-start.14 = (bf16[32,2048]{1,0:T(8,128)(2,1)S(1)}, bf16[32,2048]{1,0:T(8,128)(2,1)S(1)}, u32[]{:S(2)}, u32[]{:S(2)}) collective-permute-start(bf16[32,2048]{1,0:T(8,128)(2,1)S(1)} %get-tuple-element.55), channel_id=1, source_target_pairs={{0,2},{2,0},{4,6},{6,4},{8,10},{10,8},{12,14},{14,12},{1,3},{3,1},... | collective-permute-start | bytes 393224 | tf_op jit(solution)/shard_map/ppermute | solution.py:271
  30.0 8.8 %collective-permute-start.11 = (bf16[384,128]{1,0:T(8,128)(2,1)S(1)}, bf16[384,128]{1,0:T(8,128)(2,1)S(1)}, u32[]{:S(2)}, u32[]{:S(2)}) collective-permute-start(bf16[384,128]{1,0:T(8,128)(2,1)S(1)} %get-tuple-element.51), channel_id=1, source_target_pairs={{0,8},{2,10},{4,12},{6,14},{8,0},{10,2},{12,4},{14,6},{1,9},{3,11}... | collective-permute-start | bytes 294920 | tf_op jit(solution)/shard_map/ppermute | solution.py:271
  33.7 7.9 %collective-permute-start.13 = (bf16[64,2048]{1,0:T(8,128)(2,1)S(1)}, bf16[64,2048]{1,0:T(8,128)(2,1)S(1)}, u32[]{:S(2)}, u32[]{:S(2)}) collective-permute-start(bf16[64,2048]{1,0:T(8,128)(2,1)S(1)} %get-tuple-element.53), channel_id=1, source_target_pairs={{0,2},{2,0},{4,6},{6,4},{8,10},{10,8},{12,14},{14,12},{1,3},{3,1},... | collective-permute-start | bytes 786440 | tf_op jit(solution)/shard_map/ppermute | solution.py:271
  34.3 6.6 %collective-permute-start.15 = (bf16[32,2048]{1,0:T(8,128)(2,1)S(1)}, bf16[32,2048]{1,0:T(8,128)(2,1)S(1)}, u32[]{:S(2)}, u32[]{:S(2)}) collective-permute-start(bf16[32,2048]{1,0:T(8,128)(2,1)S(1)} %shard_map.82), channel_id=1, source_target_pairs={{0,4},{2,6},{4,0},{6,2},{8,12},{10,14},{12,8},{14,10},{1,5},{3,7},... | collective-permute-start | bytes 393224 | tf_op jit(solution)/shard_map/ppermute | solution.py:271
  38.8 4.7 %collective-permute-start.12 = (bf16[384,128]{1,0:T(8,128)(2,1)S(1)}, bf16[384,128]{1,0:T(8,128)(2,1)S(1)}, u32[]{:S(2)}, u32[]{:S(2)}) collective-permute-start(bf16[384,128]{1,0:T(8,128)(2,1)S(1)} %add_convert_fusion.1), channel_id=1, source_target_pairs={{0,4},{2,6},{4,0},{6,2},{8,12},{10,14},{12,8},{14,10},{1,5},{3,7},... | collective-permute-start | bytes 294920 | tf_op jit(solution)/shard_map/ppermute | solution.py:271
  38.9 10.0 %collective-permute-start.17 = (bf16[32,2048]{1,0:T(8,128)(2,1)S(1)}, bf16[32,2048]{1,0:T(8,128)(2,1)S(1)}, u32[]{:S(2)}, u32[]{:S(2)}) collective-permute-start(bf16[32,2048]{1,0:T(8,128)(2,1)S(1)} %get-tuple-element.66), channel_id=1, source_target_pairs={{0,2},{2,0},{4,6},{6,4},{8,10},{10,8},{12,14},{14,12},{1,3},{3,1},... | collective-permute-start | bytes 393224 | tf_op jit(solution)/shard_map/ppermute | solution.py:271
  41.7 8.5 %collective-permute-start.19 = (bf16[32,2048]{1,0:T(8,128)(2,1)S(1)}, bf16[32,2048]{1,0:T(8,128)(2,1)S(1)}, u32[]{:S(2)}, u32[]{:S(2)}) collective-permute-start(bf16[32,2048]{1,0:T(8,128)(2,1)S(1)} %shard_map.83.summed), channel_id=1, source_target_pairs={{0,8},{2,10},{4,12},{6,14},{8,0},{10,2},{12,4},{14,6},{1,9},{3,11}... | collective-permute-start | bytes 393224 | tf_op jit(solution)/shard_map/ppermute | solution.py:271
  43.5 6.7 %collective-permute-start.18 = (bf16[32,2048]{1,0:T(8,128)(2,1)S(1)}, bf16[32,2048]{1,0:T(8,128)(2,1)S(1)}, u32[]{:S(2)}, u32[]{:S(2)}) collective-permute-start(bf16[32,2048]{1,0:T(8,128)(2,1)S(1)} %shard_map.86), channel_id=1, source_target_pairs={{0,4},{2,6},{4,0},{6,2},{8,12},{10,14},{12,8},{14,10},{1,5},{3,7},... | collective-permute-start | bytes 393224 | tf_op jit(solution)/shard_map/ppermute | solution.py:271
  43.8 4.7 %collective-permute-start.16 = (bf16[384,128]{1,0:T(8,128)(2,1)S(1)}, bf16[384,128]{1,0:T(8,128)(2,1)S(1)}, u32[]{:S(2)}, u32[]{:S(2)}) collective-permute-start(bf16[384,128]{1,0:T(8,128)(2,1)S(1)} %add_convert_fusion.mine), channel_id=1, source_target_pairs={{0,2},{2,0},{4,6},{6,4},{8,10},{10,8},{12,14},{14,12},{1,3},{3,1},... | collective-permute-start | bytes 294920 | tf_op jit(solution)/shard_map/ppermute | solution.py:271

commit v16 on v13

--- a/solution.py
+++ b/solution.py
@@ -236,7 +236,7 @@
     refs[-1][...] = coded(total)
 
 
-def base_body(mine, other, panel, factor, base, rate_out, gram):
+def base_body(mine, other, panel, factor, summed, base, rate_out, gram):
     half = mine.shape[0] // 3
     quarters = mine[...].astype(jnp.float32) + other[...].astype(jnp.float32)
     upper, side, lower = quarters[:half], quarters[half : 2 * half], quarters[2 * half :]
@@ -385,6 +385,7 @@
     across = add_up(0, keep_second, arrived[1], through)
     gram = (gram.astype(jnp.float32) + gram_arrived.astype(jnp.float32)).astype(jnp.bfloat16)
     gram_arrived = swap(gram, 2)
+    gram_arrived, summed = lax.optimization_barrier((gram_arrived, across))
     across = swap(across, 4)
     gram = (gram.astype(jnp.float32) + gram_arrived.astype(jnp.float32)).astype(jnp.bfloat16)
     partner = swap(gram, 1)
@@ -395,11 +396,11 @@
         base_body,
         (wide(size, jnp.float32), shape((8, 128), jnp.float32)),
         0,
-        4,
+        5,
         0,
         0,
         [pltpu.VMEM((kdim, kdim), jnp.float32)],
-    )(gram, partner, panel, gene_factor)
+    )(gram, partner, panel, gene_factor, summed)
     gene_next = call(last_body, wide(size, jnp.float32), 0, 6, 0, AHEAD)(
         rate, base, own, arrived[2], beside, across
     )

time: 50.9 us -> 51.3 us (level)
  transfers between devices with their start and end apart: 20 -> 20, of which waited for: 8 -> 9; matrix products, arithmetic and copies ran while one was open for 2% -> 2% of each run, Pallas kernels for 18% -> 18%
where the time goes in v16:
time: 51.3 us; the launch traced here: 51 us
  starting transfers between devices  20.9 us (41%)
  waiting for transfers between devices  15.7 us (31%)
  Pallas kernels  11.8 us (23%)
  between operations  1.45 us (3%)
  other arithmetic  1.02 us (2%)
    ppermute x16, starting transfers between devices, swap(): return lax.ppermute(value, 'cell', [(n, n ^ bits) for n in range(n_cell)])  19.7 us
    ppermute x16, waiting for transfers between devices, swap(): return lax.ppermute(value, 'cell', [(n, n ^ bits) for n in range(n_cell)])  14.3 us
    pallas_call x1, Pallas kernels, dense_tile(): pl.pallas_call(dense_body, out_shape=(shape((CELL_DEV, GENE_DEV), jnp.bfl...  4.09 us
    pallas_call x1, Pallas kernels, shards(): call(functools.partial(cell_body, order, [7], n_parts), (shape(cell_facto...  2.03 us
    ppermute x4, waiting for transfers between devices, swap_core(): return lax.ppermute(value, 'gene', [(0, 1), (1, 0)])  1.41 us
    pallas_call x1, Pallas kernels, shards(): call(functools.partial(second_body, order), (wide(kdim, jnp.bfloat16), sh...  1.21 us
    ppermute x4, starting transfers between devices, swap_core(): return lax.ppermute(value, 'gene', [(0, 1), (1, 0)])  1.19 us
    pallas_call x1, Pallas kernels, shards(): call(functools.partial(first_body, n_parts), (wide(first_rows, jnp.bfloat...  1.14 us
  transfers between devices with their start and end apart: 20, of which 9 were waited for; matrix products, arithmetic and copies ran while one was open for 2% of the time, Pallas kernels for 18%

profile of v16, /device:TPU:0, one launch (start us, length us, event | category | flops | bytes accessed | tf_op | source)
XLA Modules:
  0.0 51.0 jit_solution(15697524693957145207)
XLA Ops:
  0.6 0.5 %collective-permute-start.3 = (f32[128,1024]{1,0:T(8,128)}, f32[128,1024]{1,0:T(8,128)S(1)}, u32[]{:S(2)}, u32[]{:S(2)}) collective-permute-start(f32[128,1024]{1,0:T(8,128)} %factor_mine.1), channel_id=1, source_target_pairs={{0,1},{1,0},{2,3},{3,2},{4,5},{5,4},{6,7},{7,6},{8,9},{9,8},{10,11... | collective-permute-start | bytes 1572872 | tf_op jit(solution)/shard_map/ppermute | solution.py:275
  1.1 1.0 %convert_element_type.21.refs_0_ = bf16[32,2048]{1,0:T(8,128)(2,1)S(1)} convert(f32[32,2048]{1,0:T(8,128)} %factor.1) | non-fusion elementwise | flops 65536 | bytes 393216 | tf_op jit(solution)/shard_map/convert_element_type | solution.py:280
  2.1 3.7 %collective-permute-start.2 = (bf16[32,2048]{1,0:T(8,128)(2,1)S(1)}, bf16[32,2048]{1,0:T(8,128)(2,1)S(1)}, u32[]{:S(2)}, u32[]{:S(2)}) collective-permute-start(bf16[32,2048]{1,0:T(8,128)(2,1)S(1)} %convert_element_type.21.refs_0_), channel_id=1, source_target_pairs={{0,8},{2,10},{4,12},{6,14},{8,0},{10,2},{12,4},{14,6},{1,9},{3,11}... | collective-permute-start | bytes 393224 | tf_op jit(solution)/shard_map/ppermute | solution.py:272
  5.8 1.6 %collective-permute-start.1 = (bf16[32,2048]{1,0:T(8,128)(2,1)S(1)}, bf16[32,2048]{1,0:T(8,128)(2,1)S(1)}, u32[]{:S(2)}, u32[]{:S(2)}) collective-permute-start(bf16[32,2048]{1,0:T(8,128)(2,1)S(1)} %convert_element_type.21.refs_0_), channel_id=1, source_target_pairs={{0,4},{2,6},{4,0},{6,2},{8,12},{10,14},{12,8},{14,10},{1,5},{3,7},... | collective-permute-start | bytes 393224 | tf_op jit(solution)/shard_map/ppermute | solution.py:272
  7.4 1.5 %collective-permute-start = (bf16[32,2048]{1,0:T(8,128)(2,1)S(1)}, bf16[32,2048]{1,0:T(8,128)(2,1)S(1)}, u32[]{:S(2)}, u32[]{:S(2)}) collective-permute-start(bf16[32,2048]{1,0:T(8,128)(2,1)S(1)} %convert_element_type.21.refs_0_), channel_id=1, source_target_pairs={{0,2},{2,0},{4,6},{6,4},{8,10},{10,8},{12,14},{14,12},{1,3},{3,1},... | collective-permute-start | bytes 393224 | tf_op jit(solution)/shard_map/ppermute | solution.py:272
  9.7 4.1 %shard_map.77 = (bf16[1024,2048]{1,0:T(8,128)(2,1)S(1)}, bf16[2048,1024]{1,0:T(8,128)(2,1)S(1)}) custom-call(s32[64]{0:T(128)} %bitcast.6, s32[64]{0:T(128)} %bitcast.7, s32[1]{0:T(128)} %bitcast.4.count, bf16[64,128,128]{2,1,0:T(8,128)(2,1)} %bitcast.5), custom_call_target="tpu_custom_call" | custom-call | tf_op jit(solution)/shard_map/pallas_call | solution.py:88
  13.9 1.1 %collective-permute-start.4 = (bf16[32,2048]{1,0:T(8,128)(2,1)S(1)}, bf16[32,2048]{1,0:T(8,128)(2,1)S(1)}, u32[]{:S(2)}, u32[]{:S(2)}) collective-permute-start(bf16[32,2048]{1,0:T(8,128)(2,1)S(1)} %collective-permute-done.refs_1_), channel_id=1, source_target_pairs={{0,4},{2,6},{4,0},{6,2},{8,12},{10,14},{12,8},{14,10},{1,5},{3,7},... | collective-permute-start | bytes 393224 | tf_op jit(solution)/shard_map/ppermute | solution.py:272
  15.0 1.5 %collective-permute-start.5 = (bf16[32,2048]{1,0:T(8,128)(2,1)S(1)}, bf16[32,2048]{1,0:T(8,128)(2,1)S(1)}, u32[]{:S(2)}, u32[]{:S(2)}) collective-permute-start(bf16[32,2048]{1,0:T(8,128)(2,1)S(1)} %collective-permute-done.2.refs_4_), channel_id=1, source_target_pairs={{0,2},{2,0},{4,6},{6,4},{8,10},{10,8},{12,14},{14,12},{1,3},{3,1},... | collective-permute-start | bytes 393224 | tf_op jit(solution)/shard_map/ppermute | solution.py:272
  16.9 1.4 %collective-permute-start.7 = (bf16[32,2048]{1,0:T(8,128)(2,1)S(1)}, bf16[32,2048]{1,0:T(8,128)(2,1)S(1)}, u32[]{:S(2)}, u32[]{:S(2)}) collective-permute-start(bf16[32,2048]{1,0:T(8,128)(2,1)S(1)} %collective-permute-done.6.refs_6_), channel_id=1, source_target_pairs={{0,2},{2,0},{4,6},{6,4},{8,10},{10,8},{12,14},{14,12},{1,3},{3,1},... | collective-permute-start | bytes 393224 | tf_op jit(solution)/shard_map/ppermute | solution.py:272
  18.3 1.3 %collective-permute-done.4.refs_3_ = bf16[32,2048]{1,0:T(8,128)(2,1)S(1)} collective-permute-done((bf16[32,2048]{1,0:T(8,128)(2,1)S(1)}, bf16[32,2048]{1,0:T(8,128)(2,1)S(1)}, u32[]{:S(2)}, u32[]{:S(2)}) %collective-permute-start.4) | collective-permute-done | bytes 131104 | tf_op jit(solution)/shard_map/ppermute | solution.py:272
  19.6 1.4 %collective-permute-done.5.refs_5_ = bf16[32,2048]{1,0:T(8,128)(2,1)S(1)} collective-permute-done((bf16[32,2048]{1,0:T(8,128)(2,1)S(1)}, bf16[32,2048]{1,0:T(8,128)(2,1)S(1)}, u32[]{:S(2)}, u32[]{:S(2)}) %collective-permute-start.5) | collective-permute-done | bytes 131104 | tf_op jit(solution)/shard_map/ppermute | solution.py:272
  21.0 1.1 %shard_map.78 = (bf16[224,2048]{1,0:T(8,128)(2,1)S(1)}, f32[224,1024]{1,0:T(8,128)S(1)}, bf16[112,1024]{1,0:T(8,128)(2,1)S(1)}, bf16[112,1024]{1,0:T(8,128)(2,1)S(1)}) custom-call(bf16[2048,1024]{1,0:T(8,128)(2,1)S(1)} %get-tuple-element.38.turned, bf16[32,2048]{1,0:T(8,128)(2,1)S(1)} %convert_element_type.21.refs_0_, ...), custom_call_target="tpu_custom_call" | custom-call | bytes 16777216 | tf_op jit(solution)/shard_map/pallas_call | solution.py:301
  22.2 0.5 collective-permute-start.10
  22.8 1.2 %shard_map.79 = (bf16[256,2048]{1,0:T(8,128)(2,1)S(1)}, f32[96,1024]{1,0:T(8,128)S(1)}, bf16[96,1024]{1,0:T(8,128)(2,1)S(1)}) custom-call(bf16[2048,1024]{1,0:T(8,128)(2,1)S(1)} %get-tuple-element.38.turned, bf16[224,2048]{1,0:T(8,128)(2,1)S(1)} %get-tuple-element.43.first, bf16[32,2048]{1,0:T(8,128)(2,1)S(1)} %collective-permute-done.7.share), custom_call_target="tpu_custom_call" | custom-call | tf_op jit(solution)/shard_map/pallas_call | solution.py:315
  24.1 1.4 %collective-permute-done.8.other = bf16[96,1024]{1,0:T(8,128)(2,1)S(1)} collective-permute-done((bf16[96,1024]{1,0:T(8,128)(2,1)S(1)}, bf16[96,1024]{1,0:T(8,128)(2,1)S(1)}, u32[]{:S(2)}, u32[]{:S(2)}) %collective-permute-start.8) | collective-permute-done | bytes 196640 | tf_op jit(solution)/shard_map/ppermute | solution.py:275
  25.5 2.0 %shard_map.80 = (f32[128,1024]{1,0:T(8,128)S(1)}, bf16[256,1024]{1,0:T(8,128)(2,1)S(1)}, bf16[32,2048]{1,0:T(8,128)(2,1)S(1)}, bf16[384,128]{1,0:T(8,128)(2,1)S(1)}) custom-call(bf16[1024,2048]{1,0:T(8,128)(2,1)S(1)} %get-tuple-element.37.tile, f32[224,1024]{1,0:T(8,128)S(1)} %get-tuple-element.42.mine_first, f32[96,1024]{1,0:T(8,128)S(1)} %get-tuple-element.44.mine, ...), custom_call_target="tpu_custom_call" | custom-call | tf_op jit(solution)/shard_map/pallas_call | solution.py:331
  27.6 1.6 %collective-permute-start.14 = (bf16[32,2048]{1,0:T(8,128)(2,1)S(1)}, bf16[32,2048]{1,0:T(8,128)(2,1)S(1)}, u32[]{:S(2)}, u32[]{:S(2)}) collective-permute-start(bf16[32,2048]{1,0:T(8,128)(2,1)S(1)} %get-tuple-element.55), channel_id=1, source_target_pairs={{0,2},{2,0},{4,6},{6,4},{8,10},{10,8},{12,14},{14,12},{1,3},{3,1},... | collective-permute-start | bytes 393224 | tf_op jit(solution)/shard_map/ppermute | solution.py:272
  29.1 3.7 %collective-permute-start.11 = (bf16[384,128]{1,0:T(8,128)(2,1)S(1)}, bf16[384,128]{1,0:T(8,128)(2,1)S(1)}, u32[]{:S(2)}, u32[]{:S(2)}) collective-permute-start(bf16[384,128]{1,0:T(8,128)(2,1)S(1)} %get-tuple-element.51), channel_id=1, source_target_pairs={{0,8},{2,10},{4,12},{6,14},{8,0},{10,2},{12,4},{14,6},{1,9},{3,11}... | collective-permute-start | bytes 294920 | tf_op jit(solution)/shard_map/ppermute | solution.py:272
  32.8 1.1 %shard_map.81 = (bf16[64,2048]{1,0:T(8,128)(2,1)S(1)}, bf16[32,2048]{1,0:T(8,128)(2,1)S(1)}, f32[32,2048]{1,0:T(8,128)S(1)}, f32[32,2048]{1,0:T(8,128)S(1)}, f32...) custom-call(bf16[256,1024]{1,0:T(8,128)(2,1)S(1)} %get-tuple-element.49.low, bf16[1024,2048]{1,0:T(8,128)(2,1)S(1)} %get-tuple-element.37.tile), custom_call_target="tpu_custom_call" | custom-call | bytes 16777216 | tf_op jit(solution)/shard_map/pallas_call | solution.py:362
  34.0 0.6 %collective-permute-start.13 = (bf16[64,2048]{1,0:T(8,128)(2,1)S(1)}, bf16[64,2048]{1,0:T(8,128)(2,1)S(1)}, u32[]{:S(2)}, u32[]{:S(2)}) collective-permute-start(bf16[64,2048]{1,0:T(8,128)(2,1)S(1)} %get-tuple-element.53), channel_id=1, source_target_pairs={{0,2},{2,0},{4,6},{6,4},{8,10},{10,8},{12,14},{14,12},{1,3},{3,1},... | collective-permute-start | bytes 786440 | tf_op jit(solution)/shard_map/ppermute | solution.py:272
  34.6 0.5 collective-permute-start.15
  35.1 2.8 %collective-permute-done.11 = bf16[384,128]{1,0:T(8,128)(2,1)S(1)} collective-permute-done((bf16[384,128]{1,0:T(8,128)(2,1)S(1)}, bf16[384,128]{1,0:T(8,128)(2,1)S(1)}, u32[]{:S(2)}, u32[]{:S(2)}) %collective-permute-start.11) | collective-permute-done | bytes 98336 | tf_op jit(solution)/shard_map/ppermute | solution.py:272
  38.0 0.5 %collective-permute-start.17 = (bf16[32,2048]{1,0:T(8,128)(2,1)S(1)}, bf16[32,2048]{1,0:T(8,128)(2,1)S(1)}, u32[]{:S(2)}, u32[]{:S(2)}) collective-permute-start(bf16[32,2048]{1,0:T(8,128)(2,1)S(1)} %get-tuple-element.66), channel_id=1, source_target_pairs={{0,2},{2,0},{4,6},{6,4},{8,10},{10,8},{12,14},{14,12},{1,3},{3,1},... | collective-permute-start | bytes 393224 | tf_op jit(solution)/shard_map/ppermute | solution.py:272
  38.5 2.3 %collective-permute-done.15.refs_1_ = bf16[32,2048]{1,0:T(8,128)(2,1)S(1)} collective-permute-done((bf16[32,2048]{1,0:T(8,128)(2,1)S(1)}, bf16[32,2048]{1,0:T(8,128)(2,1)S(1)}, u32[]{:S(2)}, u32[]{:S(2)}) %collective-permute-start.15) | collective-permute-done | bytes 131104 | tf_op jit(solution)/shard_map/ppermute | solution.py:272
  40.8 2.5 %collective-permute-done.13.refs_0_ = bf16[64,2048]{1,0:T(8,128)(2,1)S(1)} collective-permute-done((bf16[64,2048]{1,0:T(8,128)(2,1)S(1)}, bf16[64,2048]{1,0:T(8,128)(2,1)S(1)}, u32[]{:S(2)}, u32[]{:S(2)}) %collective-permute-start.13) | collective-permute-done | bytes 262176 | tf_op jit(solution)/shard_map/ppermute | solution.py:272
  43.5 0.8 %collective-permute-start.18 = (bf16[32,2048]{1,0:T(8,128)(2,1)S(1)}, bf16[32,2048]{1,0:T(8,128)(2,1)S(1)}, u32[]{:S(2)}, u32[]{:S(2)}) collective-permute-start(bf16[32,2048]{1,0:T(8,128)(2,1)S(1)} %shard_map.86), channel_id=1, source_target_pairs={{0,4},{2,6},{4,0},{6,2},{8,12},{10,14},{12,8},{14,10},{1,5},{3,7},... | collective-permute-start | bytes 393224 | tf_op jit(solution)/shard_map/ppermute | solution.py:272
  44.3 0.9 %collective-permute-start.16 = (bf16[384,128]{1,0:T(8,128)(2,1)S(1)}, bf16[384,128]{1,0:T(8,128)(2,1)S(1)}, u32[]{:S(2)}, u32[]{:S(2)}) collective-permute-start(bf16[384,128]{1,0:T(8,128)(2,1)S(1)} %add_convert_fusion.mine), channel_id=1, source_target_pairs={{0,2},{2,0},{4,6},{6,4},{8,10},{10,8},{12,14},{14,12},{1,3},{3,1},... | collective-permute-start | bytes 294920 | tf_op jit(solution)/shard_map/ppermute | solution.py:272
  45.2 0.8 %shard_map.84 = f32[128,1024]{1,0:T(8,128)} custom-call(f32[128,1024]{1,0:T(8,128)S(1)} %get-tuple-element.58.source), custom_call_target="tpu_custom_call" | custom-call | tf_op jit(solution)/shard_map/pallas_call | solution.py:393
  46.0 3.0 %collective-permute-done.16.other = bf16[384,128]{1,0:T(8,128)(2,1)S(1)} collective-permute-done((bf16[384,128]{1,0:T(8,128)(2,1)S(1)}, bf16[384,128]{1,0:T(8,128)(2,1)S(1)}, u32[]{:S(2)}, u32[]{:S(2)}) %collective-permute-start.16) | collective-permute-done | bytes 98336 | tf_op jit(solution)/shard_map/ppermute | solution.py:272
  49.0 0.4 shard_map.85
  49.4 0.7 %collective-permute-done.18.refs_1_ = bf16[32,2048]{1,0:T(8,128)(2,1)S(1)} collective-permute-done((bf16[32,2048]{1,0:T(8,128)(2,1)S(1)}, bf16[32,2048]{1,0:T(8,128)(2,1)S(1)}, u32[]{:S(2)}, u32[]{:S(2)}) %collective-permute-start.18) | collective-permute-done | bytes 131104 | tf_op jit(solution)/shard_map/ppermute | solution.py:272
  50.1 0.9 %shard_map.87 = f32[32,2048]{1,0:T(8,128)} custom-call(f32[8,128]{1,0:T(8,128)S(1)} %get-tuple-element.63.rate, f32[32,2048]{1,0:T(8,128)S(1)} %get-tuple-element.64.base, f32[32,2048]{1,0:T(8,128)S(1)} %get-tuple-element.65.own, bf16[32,2048]{1,0:T(8,128)(2,1)S(1)} %collective-permute-done.17.refs_0_, bf16[32,2048]{1,0:T(8,128)(2,1)S(1)} %collective-permute-done.18.refs_1_, ...), custom_call_target="tpu_custom_call" | custom-call | bytes 16777216 | tf_op jit(solution)/shard_map/pallas_call | solution.py:404
  (26 shorter events, 1.2 us)
Async XLA Ops:
  0.6 13.2 %collective-permute-start.3 = (f32[128,1024]{1,0:T(8,128)}, f32[128,1024]{1,0:T(8,128)S(1)}, u32[]{:S(2)}, u32[]{:S(2)}) collective-permute-start(f32[128,1024]{1,0:T(8,128)} %factor_mine.1), channel_id=1, source_target_pairs={{0,1},{1,0},{2,3},{3,2},{4,5},{5,4},{6,7},{7,6},{8,9},{9,8},{10,11... | collective-permute-start | bytes 1572872 | tf_op jit(solution)/shard_map/ppermute | solution.py:275
  2.1 11.7 %collective-permute-start.2 = (bf16[32,2048]{1,0:T(8,128)(2,1)S(1)}, bf16[32,2048]{1,0:T(8,128)(2,1)S(1)}, u32[]{:S(2)}, u32[]{:S(2)}) collective-permute-start(bf16[32,2048]{1,0:T(8,128)(2,1)S(1)} %convert_element_type.21.refs_0_), channel_id=1, source_target_pairs={{0,8},{2,10},{4,12},{6,14},{8,0},{10,2},{12,4},{14,6},{1,9},{3,11}... | collective-permute-start | bytes 393224 | tf_op jit(solution)/shard_map/ppermute | solution.py:272
  5.8 8.1 %collective-permute-start.1 = (bf16[32,2048]{1,0:T(8,128)(2,1)S(1)}, bf16[32,2048]{1,0:T(8,128)(2,1)S(1)}, u32[]{:S(2)}, u32[]{:S(2)}) collective-permute-start(bf16[32,2048]{1,0:T(8,128)(2,1)S(1)} %convert_element_type.21.refs_0_), channel_id=1, source_target_pairs={{0,4},{2,6},{4,0},{6,2},{8,12},{10,14},{12,8},{14,10},{1,5},{3,7},... | collective-permute-start | bytes 393224 | tf_op jit(solution)/shard_map/ppermute | solution.py:272
  7.4 6.5 %collective-permute-start = (bf16[32,2048]{1,0:T(8,128)(2,1)S(1)}, bf16[32,2048]{1,0:T(8,128)(2,1)S(1)}, u32[]{:S(2)}, u32[]{:S(2)}) collective-permute-start(bf16[32,2048]{1,0:T(8,128)(2,1)S(1)} %convert_element_type.21.refs_0_), channel_id=1, source_target_pairs={{0,2},{2,0},{4,6},{6,4},{8,10},{10,8},{12,14},{14,12},{1,3},{3,1},... | collective-permute-start | bytes 393224 | tf_op jit(solution)/shard_map/ppermute | solution.py:272
  8.9 8.0 %collective-permute-start.6 = (bf16[32,2048]{1,0:T(8,128)(2,1)S(1)}, bf16[32,2048]{1,0:T(8,128)(2,1)S(1)}, u32[]{:S(2)}, u32[]{:S(2)}) collective-permute-start(bf16[32,2048]{1,0:T(8,128)(2,1)S(1)} %convert_element_type.21.refs_0_), channel_id=1, source_target_pairs={{0,12},{2,14},{4,8},{6,10},{8,4},{10,6},{12,0},{14,2},{1,13},{3,15... | collective-permute-start | bytes 393224 | tf_op jit(solution)/shard_map/ppermute | solution.py:272
  13.9 11.7 %copy-start.1 = (f32[128,1024]{1,0:T(8,128)S(1)}, f32[128,1024]{1,0:T(8,128)}, u32[]{:S(2)}) copy-start(f32[128,1024]{1,0:T(8,128)} %factor_mine.1) | copy-start | bytes 1572868
  13.9 5.7 %collective-permute-start.4 = (bf16[32,2048]{1,0:T(8,128)(2,1)S(1)}, bf16[32,2048]{1,0:T(8,128)(2,1)S(1)}, u32[]{:S(2)}, u32[]{:S(2)}) collective-permute-start(bf16[32,2048]{1,0:T(8,128)(2,1)S(1)} %collective-permute-done.refs_1_), channel_id=1, source_target_pairs={{0,4},{2,6},{4,0},{6,2},{8,12},{10,14},{12,8},{14,10},{1,5},{3,7},... | collective-permute-start | bytes 393224 | tf_op jit(solution)/shard_map/ppermute | solution.py:272
  15.0 6.0 %collective-permute-start.5 = (bf16[32,2048]{1,0:T(8,128)(2,1)S(1)}, bf16[32,2048]{1,0:T(8,128)(2,1)S(1)}, u32[]{:S(2)}, u32[]{:S(2)}) collective-permute-start(bf16[32,2048]{1,0:T(8,128)(2,1)S(1)} %collective-permute-done.2.refs_4_), channel_id=1, source_target_pairs={{0,2},{2,0},{4,6},{6,4},{8,10},{10,8},{12,14},{14,12},{1,3},{3,1},... | collective-permute-start | bytes 393224 | tf_op jit(solution)/shard_map/ppermute | solution.py:272
  16.9 5.9 %collective-permute-start.7 = (bf16[32,2048]{1,0:T(8,128)(2,1)S(1)}, bf16[32,2048]{1,0:T(8,128)(2,1)S(1)}, u32[]{:S(2)}, u32[]{:S(2)}) collective-permute-start(bf16[32,2048]{1,0:T(8,128)(2,1)S(1)} %collective-permute-done.6.refs_6_), channel_id=1, source_target_pairs={{0,2},{2,0},{4,6},{6,4},{8,10},{10,8},{12,14},{14,12},{1,3},{3,1},... | collective-permute-start | bytes 393224 | tf_op jit(solution)/shard_map/ppermute | solution.py:272
  22.2 3.4 %collective-permute-start.9 = (bf16[112,1024]{1,0:T(8,128)(2,1)S(1)}, bf16[112,1024]{1,0:T(8,128)(2,1)S(1)}, u32[]{:S(2)}, u32[]{:S(2)}) collective-permute-start(bf16[112,1024]{1,0:T(8,128)(2,1)S(1)} %get-tuple-element.47), channel_id=1, source_target_pairs={{0,1},{1,0},{2,3},{3,2},{4,5},{5,4},{6,7},{7,6},{8,9},{9,8},{10,11... | collective-permute-start | bytes 688136 | tf_op jit(solution)/shard_map/ppermute | solution.py:275
  22.2 3.3 %collective-permute-start.10 = (bf16[112,1024]{1,0:T(8,128)(2,1)S(1)}, bf16[112,1024]{1,0:T(8,128)(2,1)S(1)}, u32[]{:S(2)}, u32[]{:S(2)}) collective-permute-start(bf16[112,1024]{1,0:T(8,128)(2,1)S(1)} %get-tuple-element.48), channel_id=1, source_target_pairs={{0,1},{1,0},{2,3},{3,2},{4,5},{5,4},{6,7},{7,6},{8,9},{9,8},{10,11... | collective-permute-start | bytes 688136 | tf_op jit(solution)/shard_map/ppermute | solution.py:275
  24.0 1.5 %collective-permute-start.8 = (bf16[96,1024]{1,0:T(8,128)(2,1)S(1)}, bf16[96,1024]{1,0:T(8,128)(2,1)S(1)}, u32[]{:S(2)}, u32[]{:S(2)}) collective-permute-start(bf16[96,1024]{1,0:T(8,128)(2,1)S(1)} %get-tuple-element.45), channel_id=1, source_target_pairs={{0,1},{1,0},{2,3},{3,2},{4,5},{5,4},{6,7},{7,6},{8,9},{9,8},{10,11... | collective-permute-start | bytes 589832 | tf_op jit(solution)/shard_map/ppermute | solution.py:275
  27.6 21.4 %copy-start = (f32[32,2048]{1,0:T(8,128)S(1)}, f32[32,2048]{1,0:T(8,128)}, u32[]{:S(2)}) copy-start(f32[32,2048]{1,0:T(8,128)} %factor.1) | copy-start | bytes 786436
  27.6 7.0 %collective-permute-start.14 = (bf16[32,2048]{1,0:T(8,128)(2,1)S(1)}, bf16[32,2048]{1,0:T(8,128)(2,1)S(1)}, u32[]{:S(2)}, u32[]{:S(2)}) collective-permute-start(bf16[32,2048]{1,0:T(8,128)(2,1)S(1)} %get-tuple-element.55), channel_id=1, source_target_pairs={{0,2},{2,0},{4,6},{6,4},{8,10},{10,8},{12,14},{14,12},{1,3},{3,1},... | collective-permute-start | bytes 393224 | tf_op jit(solution)/shard_map/ppermute | solution.py:272
  29.1 8.7 %collective-permute-start.11 = (bf16[384,128]{1,0:T(8,128)(2,1)S(1)}, bf16[384,128]{1,0:T(8,128)(2,1)S(1)}, u32[]{:S(2)}, u32[]{:S(2)}) collective-permute-start(bf16[384,128]{1,0:T(8,128)(2,1)S(1)} %get-tuple-element.51), channel_id=1, source_target_pairs={{0,8},{2,10},{4,12},{6,14},{8,0},{10,2},{12,4},{14,6},{1,9},{3,11}... | collective-permute-start | bytes 294920 | tf_op jit(solution)/shard_map/ppermute | solution.py:272
  34.0 9.3 %collective-permute-start.13 = (bf16[64,2048]{1,0:T(8,128)(2,1)S(1)}, bf16[64,2048]{1,0:T(8,128)(2,1)S(1)}, u32[]{:S(2)}, u32[]{:S(2)}) collective-permute-start(bf16[64,2048]{1,0:T(8,128)(2,1)S(1)} %get-tuple-element.53), channel_id=1, source_target_pairs={{0,2},{2,0},{4,6},{6,4},{8,10},{10,8},{12,14},{14,12},{1,3},{3,1},... | collective-permute-start | bytes 786440 | tf_op jit(solution)/shard_map/ppermute | solution.py:272
  34.6 6.1 %collective-permute-start.15 = (bf16[32,2048]{1,0:T(8,128)(2,1)S(1)}, bf16[32,2048]{1,0:T(8,128)(2,1)S(1)}, u32[]{:S(2)}, u32[]{:S(2)}) collective-permute-start(bf16[32,2048]{1,0:T(8,128)(2,1)S(1)} %shard_map.82), channel_id=1, source_target_pairs={{0,4},{2,6},{4,0},{6,2},{8,12},{10,14},{12,8},{14,10},{1,5},{3,7},... | collective-permute-start | bytes 393224 | tf_op jit(solution)/shard_map/ppermute | solution.py:272
  37.9 5.5 %collective-permute-start.12 = (bf16[384,128]{1,0:T(8,128)(2,1)S(1)}, bf16[384,128]{1,0:T(8,128)(2,1)S(1)}, u32[]{:S(2)}, u32[]{:S(2)}) collective-permute-start(bf16[384,128]{1,0:T(8,128)(2,1)S(1)} %add_convert_fusion.1), channel_id=1, source_target_pairs={{0,4},{2,6},{4,0},{6,2},{8,12},{10,14},{12,8},{14,10},{1,5},{3,7},... | collective-permute-start | bytes 294920 | tf_op jit(solution)/shard_map/ppermute | solution.py:272
  38.0 11.4 %collective-permute-start.17 = (bf16[32,2048]{1,0:T(8,128)(2,1)S(1)}, bf16[32,2048]{1,0:T(8,128)(2,1)S(1)}, u32[]{:S(2)}, u32[]{:S(2)}) collective-permute-start(bf16[32,2048]{1,0:T(8,128)(2,1)S(1)} %get-tuple-element.66), channel_id=1, source_target_pairs={{0,2},{2,0},{4,6},{6,4},{8,10},{10,8},{12,14},{14,12},{1,3},{3,1},... | collective-permute-start | bytes 393224 | tf_op jit(solution)/shard_map/ppermute | solution.py:272
  43.3 6.8 %collective-permute-start.19 = (bf16[32,2048]{1,0:T(8,128)(2,1)S(1)}, bf16[32,2048]{1,0:T(8,128)(2,1)S(1)}, u32[]{:S(2)}, u32[]{:S(2)}) collective-permute-start(bf16[32,2048]{1,0:T(8,128)(2,1)S(1)} %shard_map.83.summed), channel_id=1, source_target_pairs={{0,8},{2,10},{4,12},{6,14},{8,0},{10,2},{12,4},{14,6},{1,9},{3,11}... | collective-permute-start | bytes 393224 | tf_op jit(solution)/shard_map/ppermute | solution.py:272
  43.5 6.6 %collective-permute-start.18 = (bf16[32,2048]{1,0:T(8,128)(2,1)S(1)}, bf16[32,2048]{1,0:T(8,128)(2,1)S(1)}, u32[]{:S(2)}, u32[]{:S(2)}) collective-permute-start(bf16[32,2048]{1,0:T(8,128)(2,1)S(1)} %shard_map.86), channel_id=1, source_target_pairs={{0,4},{2,6},{4,0},{6,2},{8,12},{10,14},{12,8},{14,10},{1,5},{3,7},... | collective-permute-start | bytes 393224 | tf_op jit(solution)/shard_map/ppermute | solution.py:272
  44.3 4.7 %collective-permute-start.16 = (bf16[384,128]{1,0:T(8,128)(2,1)S(1)}, bf16[384,128]{1,0:T(8,128)(2,1)S(1)}, u32[]{:S(2)}, u32[]{:S(2)}) collective-permute-start(bf16[384,128]{1,0:T(8,128)(2,1)S(1)} %add_convert_fusion.mine), channel_id=1, source_target_pairs={{0,2},{2,0},{4,6},{6,4},{8,10},{10,8},{12,14},{14,12},{1,3},{3,1},... | collective-permute-start | bytes 294920 | tf_op jit(solution)/shard_map/ppermute | solution.py:272

commit v17 on v14

--- a/solution.py
+++ b/solution.py
@@ -384,7 +384,6 @@
     across = add_up(0, keep_second, arrived[1], through)
     gram = (gram.astype(jnp.float32) + gram_arrived.astype(jnp.float32)).astype(jnp.bfloat16)
     gram_arrived = swap(gram, 2)
-    gram_arrived, across = lax.optimization_barrier((gram_arrived, across))
     across = swap(across, 4)
     gram = (gram.astype(jnp.float32) + gram_arrived.astype(jnp.float32)).astype(jnp.bfloat16)
     partner = swap(gram, 1)

time: 52.9 us -> 51.3 us (0.970)
  waiting for transfers between devices: 17.4 us -> 15.7 us
    ppermute x16, waiting for transfers between devices: 15.9 us -> 14.2 us  [swap(): return lax.ppermute(value, 'cell', [(n, n ^ bits) for n in range(n_cell)])]
  transfers between devices with their start and end apart: 20 -> 20, of which waited for: 12 -> 10; matrix products, arithmetic and copies ran while one was open for 2% -> 2% of each run, Pallas kernels for 17% -> 18%
where the time goes in v17:
time: 51.3 us; the launch traced here: 51 us
  starting transfers between devices  21.3 us (42%)
  waiting for transfers between devices  15.7 us (31%)
  Pallas kernels  11.5 us (22%)
  between operations  1.46 us (3%)
  other arithmetic  1.02 us (2%)
    ppermute x16, starting transfers between devices, swap(): return lax.ppermute(value, 'cell', [(n, n ^ bits) for n in range(n_cell)])  20.1 us
    ppermute x16, waiting for transfers between devices, swap(): return lax.ppermute(value, 'cell', [(n, n ^ bits) for n in range(n_cell)])  14.2 us
    pallas_call x1, Pallas kernels, dense_tile(): pl.pallas_call(dense_body, out_shape=(shape((CELL_DEV, GENE_DEV), jnp.bfl...  4.09 us
    pallas_call x1, Pallas kernels, shards(): call(functools.partial(cell_body, order, [7], n_parts), (shape(cell_facto...  1.57 us
    ppermute x4, waiting for transfers between devices, swap_core(): return lax.ppermute(value, 'gene', [(0, 1), (1, 0)])  1.42 us
    pallas_call x1, Pallas kernels, shards(): call(functools.partial(keep_body, sent + kept), (shape((3 * kdim // 2, kd...  1.28 us
    pallas_call x1, Pallas kernels, shards(): call(functools.partial(second_body, order), (wide(kdim, jnp.bfloat16), sh...  1.21 us
    ppermute x4, starting transfers between devices, swap_core(): return lax.ppermute(value, 'gene', [(0, 1), (1, 0)])  1.18 us
  transfers between devices with their start and end apart: 20, of which 10 were waited for; matrix products, arithmetic and copies ran while one was open for 2% of the time, Pallas kernels for 18%

profile of v17, /device:TPU:0, one launch (start us, length us, event | category | flops | bytes accessed | tf_op | source)
XLA Modules:
  0.0 51.0 jit_solution(4153892505594139075)
XLA Ops:
  0.6 0.5 %collective-permute-start.3 = (f32[128,1024]{1,0:T(8,128)}, f32[128,1024]{1,0:T(8,128)S(1)}, u32[]{:S(2)}, u32[]{:S(2)}) collective-permute-start(f32[128,1024]{1,0:T(8,128)} %factor_mine.1), channel_id=1, source_target_pairs={{0,1},{1,0},{2,3},{3,2},{4,5},{5,4},{6,7},{7,6},{8,9},{9,8},{10,11... | collective-permute-start | bytes 1572872 | tf_op jit(solution)/shard_map/ppermute | solution.py:274
  1.1 1.0 %convert_element_type.21.refs_0_ = bf16[32,2048]{1,0:T(8,128)(2,1)S(1)} convert(f32[32,2048]{1,0:T(8,128)} %factor.1) | non-fusion elementwise | flops 65536 | bytes 393216 | tf_op jit(solution)/shard_map/convert_element_type | solution.py:279
  2.1 3.7 %collective-permute-start.2 = (bf16[32,2048]{1,0:T(8,128)(2,1)S(1)}, bf16[32,2048]{1,0:T(8,128)(2,1)S(1)}, u32[]{:S(2)}, u32[]{:S(2)}) collective-permute-start(bf16[32,2048]{1,0:T(8,128)(2,1)S(1)} %convert_element_type.21.refs_0_), channel_id=1, source_target_pairs={{0,8},{2,10},{4,12},{6,14},{8,0},{10,2},{12,4},{14,6},{1,9},{3,11}... | collective-permute-start | bytes 393224 | tf_op jit(solution)/shard_map/ppermute | solution.py:271
  5.8 1.6 %collective-permute-start.1 = (bf16[32,2048]{1,0:T(8,128)(2,1)S(1)}, bf16[32,2048]{1,0:T(8,128)(2,1)S(1)}, u32[]{:S(2)}, u32[]{:S(2)}) collective-permute-start(bf16[32,2048]{1,0:T(8,128)(2,1)S(1)} %convert_element_type.21.refs_0_), channel_id=1, source_target_pairs={{0,4},{2,6},{4,0},{6,2},{8,12},{10,14},{12,8},{14,10},{1,5},{3,7},... | collective-permute-start | bytes 393224 | tf_op jit(solution)/shard_map/ppermute | solution.py:271
  7.4 1.5 %collective-permute-start = (bf16[32,2048]{1,0:T(8,128)(2,1)S(1)}, bf16[32,2048]{1,0:T(8,128)(2,1)S(1)}, u32[]{:S(2)}, u32[]{:S(2)}) collective-permute-start(bf16[32,2048]{1,0:T(8,128)(2,1)S(1)} %convert_element_type.21.refs_0_), channel_id=1, source_target_pairs={{0,2},{2,0},{4,6},{6,4},{8,10},{10,8},{12,14},{14,12},{1,3},{3,1},... | collective-permute-start | bytes 393224 | tf_op jit(solution)/shard_map/ppermute | solution.py:271
  9.7 4.1 %shard_map.77 = (bf16[1024,2048]{1,0:T(8,128)(2,1)S(1)}, bf16[2048,1024]{1,0:T(8,128)(2,1)S(1)}) custom-call(s32[64]{0:T(128)} %bitcast.6, s32[64]{0:T(128)} %bitcast.7, s32[1]{0:T(128)} %bitcast.4.count, bf16[64,128,128]{2,1,0:T(8,128)(2,1)} %bitcast.5), custom_call_target="tpu_custom_call" | custom-call | tf_op jit(solution)/shard_map/pallas_call | solution.py:88
  13.9 1.1 %collective-permute-start.4 = (bf16[32,2048]{1,0:T(8,128)(2,1)S(1)}, bf16[32,2048]{1,0:T(8,128)(2,1)S(1)}, u32[]{:S(2)}, u32[]{:S(2)}) collective-permute-start(bf16[32,2048]{1,0:T(8,128)(2,1)S(1)} %collective-permute-done.refs_1_), channel_id=1, source_target_pairs={{0,4},{2,6},{4,0},{6,2},{8,12},{10,14},{12,8},{14,10},{1,5},{3,7},... | collective-permute-start | bytes 393224 | tf_op jit(solution)/shard_map/ppermute | solution.py:271
  15.0 1.5 %collective-permute-start.5 = (bf16[32,2048]{1,0:T(8,128)(2,1)S(1)}, bf16[32,2048]{1,0:T(8,128)(2,1)S(1)}, u32[]{:S(2)}, u32[]{:S(2)}) collective-permute-start(bf16[32,2048]{1,0:T(8,128)(2,1)S(1)} %collective-permute-done.2.refs_4_), channel_id=1, source_target_pairs={{0,2},{2,0},{4,6},{6,4},{8,10},{10,8},{12,14},{14,12},{1,3},{3,1},... | collective-permute-start | bytes 393224 | tf_op jit(solution)/shard_map/ppermute | solution.py:271
  16.5 0.4 collective-permute-done.6.refs_6_
  16.9 1.4 %collective-permute-start.7 = (bf16[32,2048]{1,0:T(8,128)(2,1)S(1)}, bf16[32,2048]{1,0:T(8,128)(2,1)S(1)}, u32[]{:S(2)}, u32[]{:S(2)}) collective-permute-start(bf16[32,2048]{1,0:T(8,128)(2,1)S(1)} %collective-permute-done.6.refs_6_), channel_id=1, source_target_pairs={{0,2},{2,0},{4,6},{6,4},{8,10},{10,8},{12,14},{14,12},{1,3},{3,1},... | collective-permute-start | bytes 393224 | tf_op jit(solution)/shard_map/ppermute | solution.py:271
  18.3 1.3 %collective-permute-done.4.refs_3_ = bf16[32,2048]{1,0:T(8,128)(2,1)S(1)} collective-permute-done((bf16[32,2048]{1,0:T(8,128)(2,1)S(1)}, bf16[32,2048]{1,0:T(8,128)(2,1)S(1)}, u32[]{:S(2)}, u32[]{:S(2)}) %collective-permute-start.4) | collective-permute-done | bytes 131104 | tf_op jit(solution)/shard_map/ppermute | solution.py:271
  19.6 1.4 %collective-permute-done.5.refs_5_ = bf16[32,2048]{1,0:T(8,128)(2,1)S(1)} collective-permute-done((bf16[32,2048]{1,0:T(8,128)(2,1)S(1)}, bf16[32,2048]{1,0:T(8,128)(2,1)S(1)}, u32[]{:S(2)}, u32[]{:S(2)}) %collective-permute-start.5) | collective-permute-done | bytes 131104 | tf_op jit(solution)/shard_map/ppermute | solution.py:271
  21.0 1.1 %shard_map.78 = (bf16[224,2048]{1,0:T(8,128)(2,1)S(1)}, f32[224,1024]{1,0:T(8,128)S(1)}, bf16[112,1024]{1,0:T(8,128)(2,1)S(1)}, bf16[112,1024]{1,0:T(8,128)(2,1)S(1)}) custom-call(bf16[2048,1024]{1,0:T(8,128)(2,1)S(1)} %get-tuple-element.36.turned, bf16[32,2048]{1,0:T(8,128)(2,1)S(1)} %convert_element_type.21.refs_0_, ...), custom_call_target="tpu_custom_call" | custom-call | bytes 16777216 | tf_op jit(solution)/shard_map/pallas_call | solution.py:300
  22.2 0.5 collective-permute-start.10
  22.8 1.2 %shard_map.79 = (bf16[256,2048]{1,0:T(8,128)(2,1)S(1)}, f32[96,1024]{1,0:T(8,128)S(1)}, bf16[96,1024]{1,0:T(8,128)(2,1)S(1)}) custom-call(bf16[2048,1024]{1,0:T(8,128)(2,1)S(1)} %get-tuple-element.36.turned, bf16[224,2048]{1,0:T(8,128)(2,1)S(1)} %get-tuple-element.41.first, bf16[32,2048]{1,0:T(8,128)(2,1)S(1)} %collective-permute-done.7.share), custom_call_target="tpu_custom_call" | custom-call | tf_op jit(solution)/shard_map/pallas_call | solution.py:314
  24.1 1.4 %collective-permute-done.8.other = bf16[96,1024]{1,0:T(8,128)(2,1)S(1)} collective-permute-done((bf16[96,1024]{1,0:T(8,128)(2,1)S(1)}, bf16[96,1024]{1,0:T(8,128)(2,1)S(1)}, u32[]{:S(2)}, u32[]{:S(2)}) %collective-permute-start.8) | collective-permute-done | bytes 196640 | tf_op jit(solution)/shard_map/ppermute | solution.py:274
  25.5 1.6 %shard_map.80 = (f32[128,1024]{1,0:T(8,128)S(1)}, bf16[256,1024]{1,0:T(8,128)(2,1)S(1)}, bf16[32,2048]{1,0:T(8,128)(2,1)S(1)}) custom-call(bf16[1024,2048]{1,0:T(8,128)(2,1)S(1)} %get-tuple-element.35.tile, f32[224,1024]{1,0:T(8,128)S(1)} %get-tuple-element.40.mine_first, f32[96,1024]{1,0:T(8,128)S(1)} %get-tuple-element.42.mine, ...), custom_call_target="tpu_custom_call" | custom-call | tf_op jit(solution)/shard_map/pallas_call | solution.py:330
  27.1 1.6 %collective-permute-start.17 = (bf16[32,2048]{1,0:T(8,128)(2,1)S(1)}, bf16[32,2048]{1,0:T(8,128)(2,1)S(1)}, u32[]{:S(2)}, u32[]{:S(2)}) collective-permute-start(bf16[32,2048]{1,0:T(8,128)(2,1)S(1)} %get-tuple-element.63), channel_id=1, source_target_pairs={{0,2},{2,0},{4,6},{6,4},{8,10},{10,8},{12,14},{14,12},{1,3},{3,1},... | collective-permute-start | bytes 393224 | tf_op jit(solution)/shard_map/ppermute | solution.py:271
  28.7 1.3 %shard_map.81 = (bf16[384,128]{1,0:T(8,128)(2,1)S(1)}, bf16[64,2048]{1,0:T(8,128)(2,1)S(1)}, bf16[32,2048]{1,0:T(8,128)(2,1)S(1)}, f32[32,2048]{1,0:T(8,128)S(1)...) custom-call(bf16[256,1024]{1,0:T(8,128)(2,1)S(1)} %get-tuple-element.47.low, ...), custom_call_target="tpu_custom_call" | custom-call | bytes 16777216 | tf_op jit(solution)/shard_map/pallas_call | solution.py:361
  30.0 3.8 %collective-permute-start.11 = (bf16[384,128]{1,0:T(8,128)(2,1)S(1)}, bf16[384,128]{1,0:T(8,128)(2,1)S(1)}, u32[]{:S(2)}, u32[]{:S(2)}) collective-permute-start(bf16[384,128]{1,0:T(8,128)(2,1)S(1)} %get-tuple-element.49), channel_id=1, source_target_pairs={{0,8},{2,10},{4,12},{6,14},{8,0},{10,2},{12,4},{14,6},{1,9},{3,11}... | collective-permute-start | bytes 294920 | tf_op jit(solution)/shard_map/ppermute | solution.py:271
  33.7 0.5 %collective-permute-start.15 = (bf16[64,2048]{1,0:T(8,128)(2,1)S(1)}, bf16[64,2048]{1,0:T(8,128)(2,1)S(1)}, u32[]{:S(2)}, u32[]{:S(2)}) collective-permute-start(bf16[64,2048]{1,0:T(8,128)(2,1)S(1)} %get-tuple-element.60), channel_id=1, source_target_pairs={{0,2},{2,0},{4,6},{6,4},{8,10},{10,8},{12,14},{14,12},{1,3},{3,1},... | collective-permute-start | bytes 786440 | tf_op jit(solution)/shard_map/ppermute | solution.py:271
  34.6 4.1 %collective-permute-done.11 = bf16[384,128]{1,0:T(8,128)(2,1)S(1)} collective-permute-done((bf16[384,128]{1,0:T(8,128)(2,1)S(1)}, bf16[384,128]{1,0:T(8,128)(2,1)S(1)}, u32[]{:S(2)}, u32[]{:S(2)}) %collective-permute-start.11) | collective-permute-done | bytes 98336 | tf_op jit(solution)/shard_map/ppermute | solution.py:271
  38.9 0.6 %collective-permute-start.14 = (bf16[32,2048]{1,0:T(8,128)(2,1)S(1)}, bf16[32,2048]{1,0:T(8,128)(2,1)S(1)}, u32[]{:S(2)}, u32[]{:S(2)}) collective-permute-start(bf16[32,2048]{1,0:T(8,128)(2,1)S(1)} %get-tuple-element.58), channel_id=1, source_target_pairs={{0,2},{2,0},{4,6},{6,4},{8,10},{10,8},{12,14},{14,12},{1,3},{3,1},... | collective-permute-start | bytes 393224 | tf_op jit(solution)/shard_map/ppermute | solution.py:271
  39.5 2.2 %collective-permute-done.15.refs_0_ = bf16[64,2048]{1,0:T(8,128)(2,1)S(1)} collective-permute-done((bf16[64,2048]{1,0:T(8,128)(2,1)S(1)}, bf16[64,2048]{1,0:T(8,128)(2,1)S(1)}, u32[]{:S(2)}, u32[]{:S(2)}) %collective-permute-start.15) | collective-permute-done | bytes 262176 | tf_op jit(solution)/shard_map/ppermute | solution.py:271
  41.9 1.4 %collective-permute-start.19 = (bf16[32,2048]{1,0:T(8,128)(2,1)S(1)}, bf16[32,2048]{1,0:T(8,128)(2,1)S(1)}, u32[]{:S(2)}, u32[]{:S(2)}) collective-permute-start(bf16[32,2048]{1,0:T(8,128)(2,1)S(1)} %shard_map.86), channel_id=1, source_target_pairs={{0,8},{2,10},{4,12},{6,14},{8,0},{10,2},{12,4},{14,6},{1,9},{3,11}... | collective-permute-start | bytes 393224 | tf_op jit(solution)/shard_map/ppermute | solution.py:271
  43.3 0.8 %collective-permute-done.12 = bf16[384,128]{1,0:T(8,128)(2,1)S(1)} collective-permute-done((bf16[384,128]{1,0:T(8,128)(2,1)S(1)}, bf16[384,128]{1,0:T(8,128)(2,1)S(1)}, u32[]{:S(2)}, u32[]{:S(2)}) %collective-permute-start.12) | collective-permute-done | bytes 98336 | tf_op jit(solution)/shard_map/ppermute | solution.py:271
  44.1 0.8 %collective-permute-start.13 = (bf16[384,128]{1,0:T(8,128)(2,1)S(1)}, bf16[384,128]{1,0:T(8,128)(2,1)S(1)}, u32[]{:S(2)}, u32[]{:S(2)}) collective-permute-start(bf16[384,128]{1,0:T(8,128)(2,1)S(1)} %add_convert_fusion.mine), channel_id=1, source_target_pairs={{0,2},{2,0},{4,6},{6,4},{8,10},{10,8},{12,14},{14,12},{1,3},{3,1},... | collective-permute-start | bytes 294920 | tf_op jit(solution)/shard_map/ppermute | solution.py:271
  44.9 0.8 %shard_map.82 = f32[128,1024]{1,0:T(8,128)} custom-call(f32[128,1024]{1,0:T(8,128)S(1)} %get-tuple-element.51.source), custom_call_target="tpu_custom_call" | custom-call | tf_op jit(solution)/shard_map/pallas_call | solution.py:391
  45.8 3.1 %collective-permute-done.13.other = bf16[384,128]{1,0:T(8,128)(2,1)S(1)} collective-permute-done((bf16[384,128]{1,0:T(8,128)(2,1)S(1)}, bf16[384,128]{1,0:T(8,128)(2,1)S(1)}, u32[]{:S(2)}, u32[]{:S(2)}) %collective-permute-start.13) | collective-permute-done | bytes 98336 | tf_op jit(solution)/shard_map/ppermute | solution.py:271
  48.8 0.4 shard_map.83
  49.2 0.9 %collective-permute-done.19.refs_2_ = bf16[32,2048]{1,0:T(8,128)(2,1)S(1)} collective-permute-done((bf16[32,2048]{1,0:T(8,128)(2,1)S(1)}, bf16[32,2048]{1,0:T(8,128)(2,1)S(1)}, u32[]{:S(2)}, u32[]{:S(2)}) %collective-permute-start.19) | collective-permute-done | bytes 131104 | tf_op jit(solution)/shard_map/ppermute | solution.py:271
  50.1 0.9 %shard_map.87 = f32[32,2048]{1,0:T(8,128)} custom-call(f32[8,128]{1,0:T(8,128)S(1)} %get-tuple-element.55.rate, f32[32,2048]{1,0:T(8,128)S(1)} %get-tuple-element.56.base, f32[32,2048]{1,0:T(8,128)S(1)} %get-tuple-element.57.own, bf16[32,2048]{1,0:T(8,128)(2,1)S(1)} %collective-permute-done.14.refs_0_, bf16[32,2048]{1,0:T(8,128)(2,1)S(1)} %collective-permute-done.16.refs_1_, ...), custom_call_target="tpu_custom_call" | custom-call | bytes 16777216 | tf_op jit(solution)/shard_map/pallas_call | solution.py:402
  (26 shorter events, 1.2 us)
Async XLA Ops:
  0.6 13.2 %collective-permute-start.3 = (f32[128,1024]{1,0:T(8,128)}, f32[128,1024]{1,0:T(8,128)S(1)}, u32[]{:S(2)}, u32[]{:S(2)}) collective-permute-start(f32[128,1024]{1,0:T(8,128)} %factor_mine.1), channel_id=1, source_target_pairs={{0,1},{1,0},{2,3},{3,2},{4,5},{5,4},{6,7},{7,6},{8,9},{9,8},{10,11... | collective-permute-start | bytes 1572872 | tf_op jit(solution)/shard_map/ppermute | solution.py:274
  2.1 11.7 %collective-permute-start.2 = (bf16[32,2048]{1,0:T(8,128)(2,1)S(1)}, bf16[32,2048]{1,0:T(8,128)(2,1)S(1)}, u32[]{:S(2)}, u32[]{:S(2)}) collective-permute-start(bf16[32,2048]{1,0:T(8,128)(2,1)S(1)} %convert_element_type.21.refs_0_), channel_id=1, source_target_pairs={{0,8},{2,10},{4,12},{6,14},{8,0},{10,2},{12,4},{14,6},{1,9},{3,11}... | collective-permute-start | bytes 393224 | tf_op jit(solution)/shard_map/ppermute | solution.py:271
  5.8 8.1 %collective-permute-start.1 = (bf16[32,2048]{1,0:T(8,128)(2,1)S(1)}, bf16[32,2048]{1,0:T(8,128)(2,1)S(1)}, u32[]{:S(2)}, u32[]{:S(2)}) collective-permute-start(bf16[32,2048]{1,0:T(8,128)(2,1)S(1)} %convert_element_type.21.refs_0_), channel_id=1, source_target_pairs={{0,4},{2,6},{4,0},{6,2},{8,12},{10,14},{12,8},{14,10},{1,5},{3,7},... | collective-permute-start | bytes 393224 | tf_op jit(solution)/shard_map/ppermute | solution.py:271
  7.4 6.5 %collective-permute-start = (bf16[32,2048]{1,0:T(8,128)(2,1)S(1)}, bf16[32,2048]{1,0:T(8,128)(2,1)S(1)}, u32[]{:S(2)}, u32[]{:S(2)}) collective-permute-start(bf16[32,2048]{1,0:T(8,128)(2,1)S(1)} %convert_element_type.21.refs_0_), channel_id=1, source_target_pairs={{0,2},{2,0},{4,6},{6,4},{8,10},{10,8},{12,14},{14,12},{1,3},{3,1},... | collective-permute-start | bytes 393224 | tf_op jit(solution)/shard_map/ppermute | solution.py:271
  8.9 8.0 %collective-permute-start.6 = (bf16[32,2048]{1,0:T(8,128)(2,1)S(1)}, bf16[32,2048]{1,0:T(8,128)(2,1)S(1)}, u32[]{:S(2)}, u32[]{:S(2)}) collective-permute-start(bf16[32,2048]{1,0:T(8,128)(2,1)S(1)} %convert_element_type.21.refs_0_), channel_id=1, source_target_pairs={{0,12},{2,14},{4,8},{6,10},{8,4},{10,6},{12,0},{14,2},{1,13},{3,15... | collective-permute-start | bytes 393224 | tf_op jit(solution)/shard_map/ppermute | solution.py:271
  13.9 11.7 %copy-start.1 = (f32[128,1024]{1,0:T(8,128)S(1)}, f32[128,1024]{1,0:T(8,128)}, u32[]{:S(2)}) copy-start(f32[128,1024]{1,0:T(8,128)} %factor_mine.1) | copy-start | bytes 1572868
  13.9 5.7 %collective-permute-start.4 = (bf16[32,2048]{1,0:T(8,128)(2,1)S(1)}, bf16[32,2048]{1,0:T(8,128)(2,1)S(1)}, u32[]{:S(2)}, u32[]{:S(2)}) collective-permute-start(bf16[32,2048]{1,0:T(8,128)(2,1)S(1)} %collective-permute-done.refs_1_), channel_id=1, source_target_pairs={{0,4},{2,6},{4,0},{6,2},{8,12},{10,14},{12,8},{14,10},{1,5},{3,7},... | collective-permute-start | bytes 393224 | tf_op jit(solution)/shard_map/ppermute | solution.py:271
  15.0 6.0 %collective-permute-start.5 = (bf16[32,2048]{1,0:T(8,128)(2,1)S(1)}, bf16[32,2048]{1,0:T(8,128)(2,1)S(1)}, u32[]{:S(2)}, u32[]{:S(2)}) collective-permute-start(bf16[32,2048]{1,0:T(8,128)(2,1)S(1)} %collective-permute-done.2.refs_4_), channel_id=1, source_target_pairs={{0,2},{2,0},{4,6},{6,4},{8,10},{10,8},{12,14},{14,12},{1,3},{3,1},... | collective-permute-start | bytes 393224 | tf_op jit(solution)/shard_map/ppermute | solution.py:271
  16.9 5.9 %collective-permute-start.7 = (bf16[32,2048]{1,0:T(8,128)(2,1)S(1)}, bf16[32,2048]{1,0:T(8,128)(2,1)S(1)}, u32[]{:S(2)}, u32[]{:S(2)}) collective-permute-start(bf16[32,2048]{1,0:T(8,128)(2,1)S(1)} %collective-permute-done.6.refs_6_), channel_id=1, source_target_pairs={{0,2},{2,0},{4,6},{6,4},{8,10},{10,8},{12,14},{14,12},{1,3},{3,1},... | collective-permute-start | bytes 393224 | tf_op jit(solution)/shard_map/ppermute | solution.py:271
  22.2 3.4 %collective-permute-start.9 = (bf16[112,1024]{1,0:T(8,128)(2,1)S(1)}, bf16[112,1024]{1,0:T(8,128)(2,1)S(1)}, u32[]{:S(2)}, u32[]{:S(2)}) collective-permute-start(bf16[112,1024]{1,0:T(8,128)(2,1)S(1)} %get-tuple-element.45), channel_id=1, source_target_pairs={{0,1},{1,0},{2,3},{3,2},{4,5},{5,4},{6,7},{7,6},{8,9},{9,8},{10,11... | collective-permute-start | bytes 688136 | tf_op jit(solution)/shard_map/ppermute | solution.py:274
  22.2 3.3 %collective-permute-start.10 = (bf16[112,1024]{1,0:T(8,128)(2,1)S(1)}, bf16[112,1024]{1,0:T(8,128)(2,1)S(1)}, u32[]{:S(2)}, u32[]{:S(2)}) collective-permute-start(bf16[112,1024]{1,0:T(8,128)(2,1)S(1)} %get-tuple-element.46), channel_id=1, source_target_pairs={{0,1},{1,0},{2,3},{3,2},{4,5},{5,4},{6,7},{7,6},{8,9},{9,8},{10,11... | collective-permute-start | bytes 688136 | tf_op jit(solution)/shard_map/ppermute | solution.py:274
  24.0 1.5 %collective-permute-start.8 = (bf16[96,1024]{1,0:T(8,128)(2,1)S(1)}, bf16[96,1024]{1,0:T(8,128)(2,1)S(1)}, u32[]{:S(2)}, u32[]{:S(2)}) collective-permute-start(bf16[96,1024]{1,0:T(8,128)(2,1)S(1)} %get-tuple-element.43), channel_id=1, source_target_pairs={{0,1},{1,0},{2,3},{3,2},{4,5},{5,4},{6,7},{7,6},{8,9},{9,8},{10,11... | collective-permute-start | bytes 589832 | tf_op jit(solution)/shard_map/ppermute | solution.py:274
  27.1 21.7 %copy-start = (f32[32,2048]{1,0:T(8,128)S(1)}, f32[32,2048]{1,0:T(8,128)}, u32[]{:S(2)}) copy-start(f32[32,2048]{1,0:T(8,128)} %factor.1) | copy-start | bytes 786436
  27.1 7.1 %collective-permute-start.17 = (bf16[32,2048]{1,0:T(8,128)(2,1)S(1)}, bf16[32,2048]{1,0:T(8,128)(2,1)S(1)}, u32[]{:S(2)}, u32[]{:S(2)}) collective-permute-start(bf16[32,2048]{1,0:T(8,128)(2,1)S(1)} %get-tuple-element.63), channel_id=1, source_target_pairs={{0,2},{2,0},{4,6},{6,4},{8,10},{10,8},{12,14},{14,12},{1,3},{3,1},... | collective-permute-start | bytes 393224 | tf_op jit(solution)/shard_map/ppermute | solution.py:271
  30.0 8.8 %collective-permute-start.11 = (bf16[384,128]{1,0:T(8,128)(2,1)S(1)}, bf16[384,128]{1,0:T(8,128)(2,1)S(1)}, u32[]{:S(2)}, u32[]{:S(2)}) collective-permute-start(bf16[384,128]{1,0:T(8,128)(2,1)S(1)} %get-tuple-element.49), channel_id=1, source_target_pairs={{0,8},{2,10},{4,12},{6,14},{8,0},{10,2},{12,4},{14,6},{1,9},{3,11}... | collective-permute-start | bytes 294920 | tf_op jit(solution)/shard_map/ppermute | solution.py:271
  33.7 7.9 %collective-permute-start.15 = (bf16[64,2048]{1,0:T(8,128)(2,1)S(1)}, bf16[64,2048]{1,0:T(8,128)(2,1)S(1)}, u32[]{:S(2)}, u32[]{:S(2)}) collective-permute-start(bf16[64,2048]{1,0:T(8,128)(2,1)S(1)} %get-tuple-element.60), channel_id=1, source_target_pairs={{0,2},{2,0},{4,6},{6,4},{8,10},{10,8},{12,14},{14,12},{1,3},{3,1},... | collective-permute-start | bytes 786440 | tf_op jit(solution)/shard_map/ppermute | solution.py:271
  34.3 7.5 %collective-permute-start.18 = (bf16[32,2048]{1,0:T(8,128)(2,1)S(1)}, bf16[32,2048]{1,0:T(8,128)(2,1)S(1)}, u32[]{:S(2)}, u32[]{:S(2)}) collective-permute-start(bf16[32,2048]{1,0:T(8,128)(2,1)S(1)} %shard_map.85), channel_id=1, source_target_pairs={{0,4},{2,6},{4,0},{6,2},{8,12},{10,14},{12,8},{14,10},{1,5},{3,7},... | collective-permute-start | bytes 393224 | tf_op jit(solution)/shard_map/ppermute | solution.py:271
  38.8 5.3 %collective-permute-start.12 = (bf16[384,128]{1,0:T(8,128)(2,1)S(1)}, bf16[384,128]{1,0:T(8,128)(2,1)S(1)}, u32[]{:S(2)}, u32[]{:S(2)}) collective-permute-start(bf16[384,128]{1,0:T(8,128)(2,1)S(1)} %add_convert_fusion.1), channel_id=1, source_target_pairs={{0,4},{2,6},{4,0},{6,2},{8,12},{10,14},{12,8},{14,10},{1,5},{3,7},... | collective-permute-start | bytes 294920 | tf_op jit(solution)/shard_map/ppermute | solution.py:271
  38.9 10.3 %collective-permute-start.14 = (bf16[32,2048]{1,0:T(8,128)(2,1)S(1)}, bf16[32,2048]{1,0:T(8,128)(2,1)S(1)}, u32[]{:S(2)}, u32[]{:S(2)}) collective-permute-start(bf16[32,2048]{1,0:T(8,128)(2,1)S(1)} %get-tuple-element.58), channel_id=1, source_target_pairs={{0,2},{2,0},{4,6},{6,4},{8,10},{10,8},{12,14},{14,12},{1,3},{3,1},... | collective-permute-start | bytes 393224 | tf_op jit(solution)/shard_map/ppermute | solution.py:271
  41.7 7.5 %collective-permute-start.16 = (bf16[32,2048]{1,0:T(8,128)(2,1)S(1)}, bf16[32,2048]{1,0:T(8,128)(2,1)S(1)}, u32[]{:S(2)}, u32[]{:S(2)}) collective-permute-start(bf16[32,2048]{1,0:T(8,128)(2,1)S(1)} %shard_map.84), channel_id=1, source_target_pairs={{0,4},{2,6},{4,0},{6,2},{8,12},{10,14},{12,8},{14,10},{1,5},{3,7},... | collective-permute-start | bytes 393224 | tf_op jit(solution)/shard_map/ppermute | solution.py:271
  41.9 8.3 %collective-permute-start.19 = (bf16[32,2048]{1,0:T(8,128)(2,1)S(1)}, bf16[32,2048]{1,0:T(8,128)(2,1)S(1)}, u32[]{:S(2)}, u32[]{:S(2)}) collective-permute-start(bf16[32,2048]{1,0:T(8,128)(2,1)S(1)} %shard_map.86), channel_id=1, source_target_pairs={{0,8},{2,10},{4,12},{6,14},{8,0},{10,2},{12,4},{14,6},{1,9},{3,11}... | collective-permute-start | bytes 393224 | tf_op jit(solution)/shard_map/ppermute | solution.py:271
  44.1 4.7 %collective-permute-start.13 = (bf16[384,128]{1,0:T(8,128)(2,1)S(1)}, bf16[384,128]{1,0:T(8,128)(2,1)S(1)}, u32[]{:S(2)}, u32[]{:S(2)}) collective-permute-start(bf16[384,128]{1,0:T(8,128)(2,1)S(1)} %add_convert_fusion.mine), channel_id=1, source_target_pairs={{0,2},{2,0},{4,6},{6,4},{8,10},{10,8},{12,14},{14,12},{1,3},{3,1},... | collective-permute-start | bytes 294920 | tf_op jit(solution)/shard_map/ppermute | solution.py:271
